TPU v7x, 512 devices: a whole 4x4x16 slice. The times are simulated.
512 devices in a mesh: ctx: 64 (over x_hi, z, core), heads: 8 (over x_lo, y).
Axes of the slice: x: 4 (x_hi: 2, x_lo: 2; x = x_hi * 2 + x_lo), y: 4, z: 16, core: 2. Of those that a mesh axis runs over, the one named last changes fastest.
Arguments:
- queries: bfloat16 [8192, 4096], P('ctx', 'heads'), may hold values from -9 to 9
- keys: bfloat16 [8192, 1024], P('ctx', 'heads'), may hold values from -3 to 3
- values: bfloat16 [8192, 1024], P('ctx', 'heads'), may hold values from -6 to 6
- outputs: bfloat16 [8192, 4096], P(('ctx', 'heads')), may hold values from -6 to 6
- out_grad: bfloat16 [8192, 4096], P(('ctx', 'heads')), may hold values from -6 to 6
- lse: float32 [8192, 32], P('ctx', 'heads'), as said below
- positions: int32 [8192], P('ctx'), may hold values from 0 to 8191, as said below
Outputs:
- query_grad: bfloat16 [8192, 4096], P('ctx', 'heads')
- key_grad: bfloat16 [8192, 1024], P('ctx', 'heads')
- value_grad: bfloat16 [8192, 1024], P('ctx', 'heads')
Inputs may be any that keep to these rules, and one draw needn't show every extreme that they name: A permutation of 0 to 8191. Rows d * 128 to (d + 1) * 128 - 1 hold two runs of 64 consecutive positions, blocks c and 127 - c of size 64 for some c, in either order. lse[i, h] = log of the sum over all 8192 tokens j of exp(S[i, j]) for head h, with S as in the first step from the given queries, keys and positions (masked entries at -1e30 included).
All inputs are finite; a program needn't handle non-finite values.
Results may differ from a plain program's by a relative error of at most 0.0049.
Values may be sent and summed in bfloat16 or wider, within the bound.
No kernel may reach another device: no remote copies, remote signals or barrier semaphores. Data moves between devices by JAX's collectives and lax.ppermute only.
A program may use at most 64 MiB of HBM per device.

v0:
```python
import math

import jax
import jax.numpy as jnp
from jax import lax
from jax.sharding import PartitionSpec as P

HEAD_SIZE = 128


def passed_along(block, axis, distance):
    devices = range(lax.axis_size(axis))
    route = [((i - distance) % len(devices), i) for i in devices]
    return lax.ppermute(block, axis, route)


def shards(queries, keys, values, outputs, out_grad, lse, positions):
    cycle_size = lax.axis_size("ctx")
    own_index = lax.axis_index("ctx")
    all_pos = lax.all_gather(positions, "ctx", axis=0, tiled=True)
    out_local, grad_local = (
        lax.all_to_all(outputs, "heads", split_axis=1, concat_axis=0, tiled=True),
        lax.all_to_all(out_grad, "heads", split_axis=1, concat_axis=0, tiled=True),
    )
    tok_rows = queries.shape[0]
    kv_heads = keys.shape[1] // HEAD_SIZE
    query_group = queries.shape[1] // keys.shape[1]
    scale = 1.0 / math.sqrt(HEAD_SIZE)

    def to_rows(array):
        shaped = array.reshape(tok_rows, kv_heads, query_group, HEAD_SIZE).transpose(1, 2, 0, 3)
        return shaped.reshape(kv_heads, query_group * tok_rows, HEAD_SIZE)

    def heads_first(block):
        return block.reshape(block.shape[0], kv_heads, HEAD_SIZE).transpose(1, 0, 2)

    query_rows = to_rows(queries)
    grad_rows = to_rows(grad_local)
    out_rows = to_rows(out_local)
    delta = jnp.sum(out_rows.astype(jnp.float32) * grad_rows.astype(jnp.float32), axis=-1)
    saved_lse = (
        lse.reshape(tok_rows, kv_heads, query_group)
        .transpose(1, 2, 0)
        .reshape(kv_heads, query_group * tok_rows)
    )
    query_pos = jnp.tile(positions, query_group)

    def masked_scores(key_block, key_pos):
        scores = (
            jnp.einsum(
                "gqd,gkd->gqk",
                query_rows,
                heads_first(key_block),
                preferred_element_type=jnp.float32,
            )
            * scale
        )
        return jnp.where(key_pos[None, None, :] <= query_pos[None, :, None], scores, -1e30)

    def visit(turn_index, key_block, value_block, dq_acc, dk_acc, dv_acc):
        owner = (own_index - turn_index) % cycle_size
        key_pos = lax.dynamic_slice_in_dim(all_pos, owner * tok_rows, tok_rows)
        scores = masked_scores(key_block, key_pos)
        probs = jnp.exp(scores - saved_lse[..., None])
        probs_b = probs.astype(jnp.bfloat16)
        key_heads = heads_first(key_block)
        value_heads = heads_first(value_block)
        dprob = jnp.einsum(
            "gqd,gkd->gqk", grad_rows, value_heads, preferred_element_type=jnp.float32
        )
        dscore = (probs * (dprob - delta[..., None])).astype(jnp.bfloat16)
        dq_acc = dq_acc + jnp.einsum(
            "gqk,gkd->gqd", dscore, key_heads, preferred_element_type=jnp.float32
        )
        dk_acc = dk_acc + jnp.einsum(
            "gqk,gqd->gkd", dscore, query_rows, preferred_element_type=jnp.float32
        )
        dv_acc = dv_acc + jnp.einsum(
            "gqk,gqd->gkd", probs_b, grad_rows, preferred_element_type=jnp.float32
        )
        return (dq_acc, dk_acc, dv_acc)

    def send_back(dk_acc, dv_acc):
        return passed_along((dk_acc, dv_acc), "ctx", 1)

    dq_start = jnp.zeros((kv_heads, query_group * tok_rows, HEAD_SIZE), jnp.float32)
    kv_start = jnp.zeros((kv_heads, tok_rows, HEAD_SIZE), jnp.float32)

    def moving_turn(turn_index, carry):
        key_block, value_block, dq_acc, dk_acc, dv_acc = carry
        dq_acc, dk_acc, dv_acc = visit(turn_index, key_block, value_block, dq_acc, dk_acc, dv_acc)
        key_block, value_block = passed_along((key_block, value_block), "ctx", 1)
        dk_acc, dv_acc = send_back(dk_acc, dv_acc)
        return (key_block, value_block, dq_acc, dk_acc, dv_acc)

    key_block, value_block, dq_acc, dk_acc, dv_acc = lax.fori_loop(
        0, cycle_size - 1, moving_turn, (keys, values, dq_start, kv_start, kv_start)
    )
    dq_acc, dk_acc, dv_acc = visit(cycle_size - 1, key_block, value_block, dq_acc, dk_acc, dv_acc)
    dk_acc, dv_acc = send_back(dk_acc, dv_acc)
    query_grad = (
        (dq_acc * scale).reshape(kv_heads, query_group, tok_rows, HEAD_SIZE).transpose(2, 0, 1, 3)
    )
    query_grad = query_grad.reshape(tok_rows, kv_heads * query_group * HEAD_SIZE).astype(
        jnp.bfloat16
    )
    key_grad = (
        (dk_acc * scale)
        .transpose(1, 0, 2)
        .reshape(tok_rows, kv_heads * HEAD_SIZE)
        .astype(jnp.bfloat16)
    )
    value_grad = (
        dv_acc.transpose(1, 0, 2).reshape(tok_rows, kv_heads * HEAD_SIZE).astype(jnp.bfloat16)
    )
    return (query_grad, key_grad, value_grad)


def solution(mesh):
    return jax.shard_map(
        shards,
        mesh=mesh,
        in_specs=(
            P("ctx", "heads"),
            P("ctx", "heads"),
            P("ctx", "heads"),
            P(("ctx", "heads"), None),
            P(("ctx", "heads"), None),
            P("ctx", "heads"),
            P("ctx"),
        ),
        out_specs=(P("ctx", "heads"), P("ctx", "heads"), P("ctx", "heads")),
        check_vma=False,
    )
```

profile of v0, /device:TPU:6, one launch (start us, length us, event | category | flops | bytes accessed | tf_op | source)
XLA Modules:
  0.0 1125.4 jit_solution(15405561834560199279)
XLA Ops:
  2.2 6.1 all-to-all-start.1
  8.9 81.2 %all-gather = s32[64,1,128]{2,1,0:T(1,128)S(1)} all-gather(s32[1,1,128]{2,1,0:T(1,128)S(1)} %bitcast.168), channel_id=1, replica_groups=mesh['ctx'=64,'heads'=8] {'ctx'}, dimensions={0}, use_global_device_ids=true | all-gather | bytes 33280 | tf_op jit(solution)/shard_map/all_gather | solution.py:20
  91.8 5.7 all-to-all-start
  97.6 5.1 all-to-all-done
  103.9 1008.4 %while.24 = (s32[]{:T(128)}, bf16[128,128]{1,0:T(8,128)(2,1)S(1)}, bf16[128,128]{1,0:T(8,128)(2,1)S(1)}, f32[1,512,128]{2,1,0:T(8,128)S(1)}, f32[1,128,128]{2,1,...) while((s32[]{:T(128)}, bf16[128,128]{1,0:T(8,128)(2,1)S(1)}, ...), condition=%wide.region_2.3_spmd.clone, body=%wide.region_1.2_spmd.clone.sunk | while | flops 84574224 | bytes 3516930 | solution.py:96
  114.7 3.1 collective-permute-done.2
  130.7 3.1 collective-permute-done.2
  146.7 3.1 collective-permute-done.2
  162.7 3.1 collective-permute-done.2
  178.7 3.1 collective-permute-done.2
  210.7 3.1 collective-permute-done.2
  226.7 3.1 collective-permute-done.2
  274.8 3.1 collective-permute-done.2
  322.8 3.1 collective-permute-done.2
  370.8 3.1 collective-permute-done.2
  418.8 3.1 collective-permute-done.2
  466.8 3.1 collective-permute-done.2
  514.8 3.1 collective-permute-done.2
  562.9 3.1 collective-permute-done.2
  610.9 3.1 collective-permute-done.2
  642.9 3.1 collective-permute-done.2
  658.9 3.1 collective-permute-done.2
  706.9 3.1 collective-permute-done.2
  754.9 3.1 collective-permute-done.2
  802.9 3.1 collective-permute-done.2
  851.0 3.1 collective-permute-done.2
  899.0 3.1 collective-permute-done.2
  947.0 3.1 collective-permute-done.2
  995.0 3.1 collective-permute-done.2
  1043.0 3.1 collective-permute-done.2
  1091.0 3.1 collective-permute-done.2
  1117.9 3.6 collective-permute-done.5
  (1087 shorter events, 935.3 us)
Async XLA Ops:
  2.2 89.6 %all-to-all-start.1 = ((bf16[16,8,512]{2,0,1:T(8,128)(2,1)}), bf16[16,8,512]{2,0,1:T(8,128)(2,1)S(1)}, u32[]{:S(2)}, u32[]{:S(2)}) async-start(bf16[16,8,512]{2,0,1:T(8,128)(2,1)} %bitcast.117), calls=%async_computation.1 | async-start | bytes 262144 | tf_op jit(solution)/shard_map/all_to_all | solution.py:22
  91.8 10.9 all-to-all-start
  108.6 9.2 collective-permute-start.2
  110.7 9.2 collective-permute-start.3
  156.6 9.2 collective-permute-start.2
  158.7 9.2 collective-permute-start.3
  204.6 9.2 collective-permute-start.2
  206.8 9.2 collective-permute-start.3
  236.6 9.2 collective-permute-start.2
  252.6 9.2 collective-permute-start.2
  254.8 9.2 collective-permute-start.3
  284.6 9.2 collective-permute-start.2
  300.6 9.2 collective-permute-start.2
  302.8 9.2 collective-permute-start.3
  332.6 9.2 collective-permute-start.2
  348.6 9.2 collective-permute-start.2
  350.8 9.2 collective-permute-start.3
  380.7 9.2 collective-permute-start.2
  446.8 9.2 collective-permute-start.3
  494.9 9.2 collective-permute-start.3
  542.9 9.2 collective-permute-start.3
  636.7 9.2 collective-permute-start.2
  684.8 9.2 collective-permute-start.2
  716.8 9.2 collective-permute-start.2
  732.8 9.2 collective-permute-start.2
  764.8 9.2 collective-permute-start.2
  780.8 9.2 collective-permute-start.2
  812.8 9.2 collective-permute-start.2
  879.0 9.2 collective-permute-start.3
  927.0 9.2 collective-permute-start.3
  975.0 9.2 collective-permute-start.3
  1023.0 9.2 collective-permute-start.3
  (231 other events, 2115.2 us)
where the time goes:
time: 1140 us; the launch traced here: 1130 us
  starting transfers between devices  499 us (44%)
  waiting for transfers between devices  455 us (40%)
  blocking collectives  81.2 us (7%)
  matrix products  68.9 us (6%)
  local copies, waits for them, and re-layouts  11.8 us (1%)
    ppermute x254, starting transfers between devices, passed_along(): return lax.ppermute(block, axis, route)  487 us
    ppermute x254, waiting for transfers between devices, passed_along(): return lax.ppermute(block, axis, route)  450 us
    all_gather x1, blocking collectives, shards(): all_pos = lax.all_gather(positions, 'ctx', axis=0, tiled=True)  81.2 us
  transfers between devices with their start and end apart: 256, of which 192 were waited for; matrix products, arithmetic and copies ran while one was open for 7% of the time, Pallas kernels for 0%

commit v1 on v0

v1 whole, which is shorter than its diff:
```python
import math

import jax
import jax.numpy as jnp
from jax import lax
from jax.experimental import pallas as pl
from jax.experimental.pallas import tpu as pltpu
from jax.sharding import PartitionSpec as P

HEAD = 128
BLK = 64
TOK = 2 * BLK
GROUP = 4
ROWS = GROUP * BLK
SET = 4
LOG2E = math.log2(math.e)
SCALE = 1.0 / math.sqrt(HEAD)
FAR = 1e30
F32 = jnp.float32
BF16 = jnp.bfloat16
FOLD = None


def dot_nt(a, b):
    return lax.dot_general(a, b, (((1,), (1,)), ((), ())), preferred_element_type=F32)


def dot_nn(a, b):
    return lax.dot_general(a, b, (((1,), (0,)), ((), ())), preferred_element_type=F32)


def dot_tn(a, b):
    return lax.dot_general(a, b, (((0,), (0,)), ((), ())), preferred_element_type=F32)


def backward(x_ref, xx_ref, y_ref, s_ref, p_ref, m_ref, h1_ref, h2_ref, *rest):
    own_out, p_out, m_out, h1_out, h2_out, dq_out, dq_core_out, acc, dq_acc = rest
    seen = lax.broadcasted_iota(jnp.int32, (BLK, ROWS), 0) <= (
        lax.broadcasted_iota(jnp.int32, (BLK, ROWS), 1) % BLK
    )
    acc[...] = jnp.zeros_like(acc)

    def grads(scores, dprob, lse, delta):
        probs = jnp.exp2(scores * (SCALE * LOG2E) - lse)
        dscore = probs * (dprob - delta)
        return probs.astype(BF16), dscore.astype(BF16)

    def row_vectors(table):
        return [
            jnp.concatenate([table[h : h + 1, s : s + BLK] for h in range(GROUP)], axis=1)
            for s in (0, BLK)
        ]

    def half_rows(block):
        return [
            jnp.concatenate(
                [block[s : s + BLK, h * HEAD : (h + 1) * HEAD] for h in range(GROUP)], axis=0
            )
            for s in (0, BLK)
        ]

    def query_side(block):
        wide = GROUP * HEAD
        tail = jnp.transpose(block[:, wide : wide + HEAD].astype(F32))
        lse = tail[0:8, :] + tail[8:16, :] + tail[16:24, :]
        c_row, swapped = tail[24:25, :], tail[25:26, :] > 0.5
        tail = jnp.transpose(block[:, 2 * wide + HEAD :].astype(F32))
        delta = tail[0:8, :] + tail[8:16, :] + tail[16:24, :]
        d0, d1 = row_vectors(delta)
        g0, g1 = half_rows(block[:, wide + HEAD : 2 * wide + HEAD])
        two = jnp.concatenate([swapped, swapped], axis=1)
        tall = jnp.broadcast_to(swapped, (ROWS, HEAD))
        return (
            c_row,
            row_vectors(lse * LOG2E),
            (jnp.where(two, d1, d0), jnp.where(two, d0, d1)),
            half_rows(block[:, :wide]),
            (jnp.where(tall, g1, g0), jnp.where(tall, g0, g1)),
        )

    def pick(i, j):
        if i < 3:
            return (s_ref, p_ref, m_ref)[i][:, j]
        return jnp.concatenate([h1_ref[:, j], h2_ref[:, j]], axis=0)

    def flat(x):
        return x.reshape(SET * BLK, HEAD)

    def visit(block, e, own=False):
        own_c, lse, delta, q, g = query_side(block)
        (lse_early, lse_late), (delta_early, delta_late) = lse, delta
        q_late, g_late = q[1], g[1]
        q_both = jnp.concatenate(q, axis=1)
        g_both = jnp.concatenate(g, axis=1)
        dq_a = jnp.zeros((HEAD, ROWS), F32)
        dq_b = jnp.zeros((2 * HEAD, ROWS), F32)
        for i in range(4):
            c = pick(i, slice(4 * BLK, 4 * BLK + 16)).astype(F32)[:, 0:1, :]
            before = c < own_c[None]
            after = c > own_c[None]
            wide = jnp.broadcast_to(before, (SET, BLK, HEAD))
            k_early, k_late, v_early, v_late = [
                pick(i, slice(j * BLK, (j + 1) * BLK)) for j in range(4)
            ]
            k_both = jnp.concatenate(
                [flat(jnp.where(wide, k_early, 0)), flat(jnp.where(wide, 0, k_late))], axis=1
            )
            v_both = jnp.concatenate(
                [flat(jnp.where(wide, v_early, 0)), flat(jnp.where(wide, 0, v_late))], axis=1
            )
            k_early, v_early = flat(k_early), flat(v_early)
            before2 = jnp.concatenate([before, before], axis=2)
            after2 = jnp.concatenate([after, after], axis=2)
            lse_b = jnp.where(before2, lse_early[None], jnp.where(after2, lse_late[None], FAR))
            delta_b = jnp.where(before2, delta_early[None], delta_late[None])
            lse_b = jnp.broadcast_to(lse_b, (SET, BLK, ROWS)).reshape(SET * BLK, ROWS)
            delta_b = jnp.broadcast_to(delta_b, (SET, BLK, ROWS)).reshape(SET * BLK, ROWS)

            p_a, ds_a = grads(
                dot_nt(k_early, q_late), dot_nt(v_early, g_late), lse_late, delta_late
            )
            p_b, ds_b = grads(dot_nt(k_both, q_both), dot_nt(v_both, g_both), lse_b, delta_b)
            dv_a, dk_a = dot_nn(p_a, g_late), dot_nn(ds_a, q_late)
            dv_b, dk_b = dot_nn(p_b, g_both), dot_nn(ds_b, q_both)
            dq_a = dq_a + dot_tn(k_early, ds_a)
            dq_b = dq_b + dot_tn(k_both, ds_b)
            for j, one, two in ((0, dk_a, dk_b), (2, dv_a, dv_b)):
                one = one.reshape(SET, BLK, HEAD)
                two = two.reshape(SET, BLK, 2 * HEAD)
                acc[i, :, j * BLK : (j + 1) * BLK] += one + jnp.where(wide, two[:, :, :HEAD], 0.0)
                acc[i, :, (j + 1) * BLK : (j + 2) * BLK] += jnp.where(
                    wide, 0.0, two[:, :, HEAD:]
                )
        dq = [dq_b[:HEAD], dq_b[HEAD:] + dq_a]
        if own:
            for i in range(2):
                at = slice(i * BLK, (i + 1) * BLK)
                k, v = s_ref[0, at], s_ref[0, (2 + i) * BLK : (3 + i) * BLK]
                scores = jnp.where(seen, dot_nt(k, q[i]), -FAR)
                p, ds = grads(scores, dot_nt(v, g[i]), lse[i], delta[i])
                acc[0, 0, at] += dot_nn(ds, q[i])
                acc[0, 0, (2 + i) * BLK : (3 + i) * BLK] += dot_nn(p, g[i])
                dq[i] = dq[i] + dot_tn(k, ds)
        for i in range(2):
            grad = jnp.transpose(dq[i]) * SCALE
            for h in range(GROUP):
                dq_acc[e, i * BLK : (i + 1) * BLK, h * HEAD : (h + 1) * HEAD] = grad[
                    h * BLK : (h + 1) * BLK
                ]

    visit(x_ref[...], 0, own=True)
    visit(xx_ref[...], 1)

    @pl.loop(0, 2)
    def _(e):
        visit(y_ref[e], e + 2)

    dq_out[...] = dq_acc[:2]
    dq_core_out[...] = dq_acc[2:].astype(BF16)
    acc[:, :, : 2 * BLK] = acc[:, :, : 2 * BLK] * SCALE
    own_out[...] = acc[0]
    p_out[...] = acc[1].astype(BF16)
    m_out[...] = acc[2].astype(BF16)
    h1_out[...] = acc[3, :2].astype(BF16)
    h2_out[...] = acc[3, 2:].astype(BF16)


def bf16_terms(x):
    hi = lax.reduce_precision(x, 8, 7)
    rest = x - hi
    mid = lax.reduce_precision(rest, 8, 7)
    return [hi.astype(BF16), mid.astype(BF16), (rest - mid).astype(BF16)]


def tail_of(x, *flags):
    lead = x.shape[:-1]
    gap = jnp.zeros(lead + (8 - GROUP,), BF16)
    parts = [part for term in bf16_terms(x) for part in (term, gap)]
    parts += [jnp.broadcast_to(f.astype(BF16), lead + (1,)) for f in flags]
    parts.append(jnp.zeros(lead + (HEAD - 24 - len(flags),), BF16))
    return jnp.concatenate(parts, axis=-1)


HEADS = ("xl", "y")


def shifted(x, by):
    n = lax.axis_size("z")
    return lax.ppermute(x, "z", [(i, (i + by) % n) for i in range(n)])


def swapped_with(x, axis):
    return lax.ppermute(x, axis, [(0, 1), (1, 0)])


def shards(queries, keys, values, outputs, out_grad, lse, positions):
    n_heads = lax.axis_size(HEADS)
    quarter = lax.axis_size("z") // 4
    first, second = positions[0], positions[BLK]
    swapped = (first > second).astype(jnp.int32)
    c = jnp.minimum(first, second) // BLK

    def early_then_late(x):
        return jnp.where(swapped == 1, jnp.concatenate([x[BLK:], x[:BLK]]), x)

    own = jnp.concatenate(
        [
            early_then_late(keys),
            early_then_late(values),
            jnp.broadcast_to(c.astype(BF16), (16, HEAD)),
        ]
    )
    far = shifted(own, 2 * quarter)
    s_set = jnp.stack([own, shifted(own, quarter), shifted(own, -quarter), far])
    p_set, m_set = shifted(s_set, 1), shifted(s_set, -1)
    h1 = shifted(s_set[:2], 2)
    h2 = shifted(jnp.stack([s_set[0], s_set[2]]), -2)

    tok = out_grad.shape[0]
    delta = jnp.sum(
        (outputs.astype(F32) * out_grad.astype(F32)).reshape(tok, n_heads, GROUP, HEAD), axis=-1
    )
    send = jnp.concatenate(
        [out_grad.reshape(tok, n_heads, GROUP * HEAD), tail_of(delta)], axis=-1
    ).transpose(1, 0, 2)
    grad = lax.all_to_all(send, HEADS, split_axis=0, concat_axis=0, tiled=True)
    own_q = early_then_late(jnp.concatenate([queries, tail_of(lse, c, swapped)], axis=1))
    x = jnp.concatenate([own_q, grad.reshape(TOK, (GROUP + 1) * HEAD)], axis=1)
    xx = swapped_with(x, "xh")
    y = swapped_with(jnp.stack([x, xx]), "core")

    vmem = pl.BlockSpec(memory_space=pltpu.VMEM)
    four, two = (SET, 4 * BLK, HEAD), (2, 4 * BLK, HEAD)
    own_g, p_g, m_g, h1_g, h2_g, dq, dq_core = pl.pallas_call(
        backward,
        out_shape=(
            jax.ShapeDtypeStruct(four, F32),
            jax.ShapeDtypeStruct(four, BF16),
            jax.ShapeDtypeStruct(four, BF16),
            jax.ShapeDtypeStruct(two, BF16),
            jax.ShapeDtypeStruct(two, BF16),
            jax.ShapeDtypeStruct((2, TOK, GROUP * HEAD), F32),
            jax.ShapeDtypeStruct((2, TOK, GROUP * HEAD), BF16),
        ),
        in_specs=[vmem] * 8,
        out_specs=[vmem] * 7,
        scratch_shapes=[
            pltpu.VMEM((4,) + four, F32),
            pltpu.VMEM((4, TOK, GROUP * HEAD), F32),
        ],
        compiler_params=pltpu.CompilerParams(vmem_limit_bytes=40 * 1024 * 1024),
        name="backward",
    )(x, xx, y, s_set, p_set, m_set, h1, h2)

    p_in, m_in = shifted(p_g, -1).astype(F32), shifted(m_g, 1).astype(F32)
    h1_in, h2_in = shifted(h1_g, -2).astype(F32), shifted(h2_g, 2).astype(F32)
    total = own_g + p_in + m_in
    mine = total[0] + h1_in[0] + h2_in[0]
    back = shifted((total[3]).astype(BF16), 2 * quarter).astype(F32)
    left = shifted((total[1] + h1_in[1]).astype(BF16), -quarter).astype(F32)
    right = shifted((total[2] + h2_in[1]).astype(BF16), quarter).astype(F32)
    mine = mine + left + right + back

    dq = dq + swapped_with(dq_core, "core").astype(F32)
    dq = dq[0] + swapped_with(dq[1].astype(BF16), "xh").astype(F32)
    return (
        early_then_late(dq).astype(BF16),
        early_then_late(mine[:TOK]).astype(BF16),
        early_then_late(mine[TOK:]).astype(BF16),
    )


def solution(mesh):
    shape = FOLD or (2, 16, 2, 2, 4)
    split = jax.sharding.Mesh(mesh.devices.reshape(shape), ("xh", "z", "core", "xl", "y"))
    ctx, heads = ("xh", "z", "core"), ("xl", "y")
    return jax.shard_map(
        shards,
        mesh=split,
        in_specs=(
            P(ctx, heads),
            P(ctx, heads),
            P(ctx, heads),
            P(ctx + heads, None),
            P(ctx + heads, None),
            P(ctx, heads),
            P(ctx),
        ),
        out_specs=(P(ctx, heads), P(ctx, heads), P(ctx, heads)),
        check_vma=False,
    )
```

time: 1140 us -> 140 us (0.12); the launches traced: 1130 us -> 140 us
  waiting for transfers between devices: 455 us -> 29.8 us
  starting transfers between devices: 499 us -> 91.5 us
  blocking collectives: 81.2 us -> 0 us
  matrix products: 68.9 us -> 0 us
    ppermute x254 -> x18, waiting for transfers between devices: 450 us -> 29.8 us  [the longest x14 24.2 us: shifted(): return lax.ppermute(x, 'z', [(i, (i + by) % n) for i in range(n)])]
    ppermute x254 -> x18, starting transfers between devices: 487 us -> 85.4 us  [the longest x14 71.6 us: shifted(): return lax.ppermute(x, 'z', [(i, (i + by) % n) for i in range(n)])]
    all_gather x1 -> x0, blocking collectives: 81.2 us -> none  [shards(): all_pos = lax.all_gather(positions, 'ctx', axis=0, tiled=True)]
    dot_general x320 -> x0, matrix products: 68.9 us -> none  [the longest x64 14.8 us: visit(): jnp.einsum('gqk,gqd->gkd', probs_b, grad_rows, preferred_element_type=jnp...]
  transfers between devices with their start and end apart: 256 -> 19, of which waited for: 192 -> 8; matrix products, arithmetic and copies ran while one was open for 7% -> 2% of each run, Pallas kernels for 0% -> 0%
where the time goes in v1:
time: 140 us
  starting transfers between devices  91.5 us (65%)
  waiting for transfers between devices  29.8 us (21%)
  Pallas kernels  7.04 us (5%)
  local copies, waits for them, and re-layouts  5.29 us (4%)
  between operations  3.76 us (3%)
  other arithmetic  2.27 us (2%)
    ppermute x14, starting transfers between devices, shifted(): return lax.ppermute(x, 'z', [(i, (i + by) % n) for i in range(n)])  71.6 us
    ppermute x14, waiting for transfers between devices, shifted(): return lax.ppermute(x, 'z', [(i, (i + by) % n) for i in range(n)])  24.2 us
    ppermute x4, starting transfers between devices, swapped_with(): return lax.ppermute(x, axis, [(0, 1), (1, 0)])  13.7 us
    pallas_call x1, Pallas kernels, shards(): pl.pallas_call(backward, out_shape=(jax.ShapeDtypeStruct(four, F32), jax....  7.04 us
    all_to_all x1, starting transfers between devices, shards(): grad = lax.all_to_all(send, HEADS, split_axis=0, concat_axis=0, tiled=True)  6.06 us
    ppermute x4, waiting for transfers between devices, swapped_with(): return lax.ppermute(x, axis, [(0, 1), (1, 0)])  5.61 us
  transfers between devices with their start and end apart: 19, of which 8 were waited for; matrix products, arithmetic and copies ran while one was open for 2% of the time, Pallas kernels for 0%

profile of v1, /device:TPU:6, one launch (start us, length us, event | category | flops | bytes accessed | tf_op | source)
XLA Modules:
  0.0 139.6 jit_solution(17466450184991974668)
XLA Ops:
  0.7 1.0 copy.30
  2.7 0.8 concatenate.33
  3.5 6.1 %all-to-all-start = ((bf16[8,16,640]{2,1,0:T(8,128)(2,1)}), bf16[8,16,640]{2,1,0:T(8,128)(2,1)S(1)}, u32[]{:S(2)}, u32[]{:S(2)}) async-start(bf16[8,16,640]{2,1,0:T(8,128)(2,1)} %bitcast.3), calls=%async_computation | async-start | bytes 327680 | tf_op jit(solution)/shard_map/all_to_all | solution.py:226
  13.3 0.8 copy-done.4
  14.3 0.7 copy-done.1
  15.1 6.6 %collective-permute-start = (bf16[128,1280]{1,0:T(8,128)(2,1)S(1)}, bf16[128,1280]{1,0:T(8,128)(2,1)S(1)}, u32[]{:S(2)}, u32[]{:S(2)}) collective-permute-start(bf16[128,1280]{1,0:T(8,128)(2,1)S(1)} %get-tuple-element.20.x_ref), channel_id=1, source_target_pairs={{0,256},{256,0},{1,257},{257,1},{2,258},{258,2},{3,259},{259,3},{4... | collective-permute-start | bytes 983048 | tf_op jit(solution)/shard_map/ppermute | solution.py:193
  21.8 5.6 %collective-permute-done.xx_ref = bf16[128,1280]{1,0:T(8,128)(2,1)S(1)} collective-permute-done((bf16[128,1280]{1,0:T(8,128)(2,1)S(1)}, bf16[128,1280]{1,0:T(8,128)(2,1)S(1)}, u32[]{:S(2)}, u32[]{:S(2)}) %collective-permute-start) | collective-permute-done | bytes 327712 | tf_op jit(solution)/shard_map/ppermute | solution.py:193
  27.4 1.9 %collective-permute-start.1 = (bf16[2,128,1280]{2,1,0:T(8,128)(2,1)S(1)}, bf16[2,128,1280]{2,1,0:T(8,128)(2,1)S(1)}, u32[]{:S(2)}, u32[]{:S(2)}) collective-permute-start(bf16[2,128,1280]{2,1,0:T(8,128)(2,1)S(1)} %pad_maximum_fusion), channel_id=1, source_target_pairs={{0,8},{8,0},{1,9},{9,1},{2,10},{10,2},{3,11},{11,3},{4,12},{12,4},... | collective-permute-start | bytes 1966088 | tf_op jit(solution)/shard_map/ppermute | solution.py:193
  29.5 12.7 %collective-permute-start.3 = (bf16[272,128]{1,0:T(8,128)(2,1)S(1)}, bf16[272,128]{1,0:T(8,128)(2,1)S(1)}, u32[]{:S(2)}, u32[]{:S(2)}) collective-permute-start(bf16[272,128]{1,0:T(8,128)(2,1)S(1)} %get-tuple-element.30), channel_id=1, source_target_pairs={{0,192},{16,208},{32,224},{48,240},{64,0},{80,16},{96,32},{112,48}... | collective-permute-start | bytes 208904 | tf_op jit(solution)/shard_map/ppermute | solution.py:189
  42.2 1.9 %collective-permute-start.2 = (bf16[272,128]{1,0:T(8,128)(2,1)S(1)}, bf16[272,128]{1,0:T(8,128)(2,1)S(1)}, u32[]{:S(2)}, u32[]{:S(2)}) collective-permute-start(bf16[272,128]{1,0:T(8,128)(2,1)S(1)} %get-tuple-element.30), channel_id=1, source_target_pairs={{0,64},{16,80},{32,96},{48,112},{64,128},{80,144},{96,160},{112,17... | collective-permute-start | bytes 208904 | tf_op jit(solution)/shard_map/ppermute | solution.py:189
  44.2 10.8 %collective-permute-start.4 = (bf16[272,128]{1,0:T(8,128)(2,1)S(1)}, bf16[272,128]{1,0:T(8,128)(2,1)S(1)}, u32[]{:S(2)}, u32[]{:S(2)}) collective-permute-start(bf16[272,128]{1,0:T(8,128)(2,1)S(1)} %get-tuple-element.30), channel_id=1, source_target_pairs={{0,128},{16,144},{32,160},{48,176},{64,192},{80,208},{96,224},{112... | collective-permute-start | bytes 208904 | tf_op jit(solution)/shard_map/ppermute | solution.py:189
  55.0 5.4 %collective-permute-done.4 = bf16[272,128]{1,0:T(8,128)(2,1)S(1)} collective-permute-done((bf16[272,128]{1,0:T(8,128)(2,1)S(1)}, bf16[272,128]{1,0:T(8,128)(2,1)S(1)}, u32[]{:S(2)}, u32[]{:S(2)}) %collective-permute-start.4) | collective-permute-done | bytes 69664 | tf_op jit(solution)/shard_map/ppermute | solution.py:189
  60.5 8.2 %collective-permute-start.6 = (bf16[4,272,128]{2,1,0:T(8,128)(2,1)S(1)}, bf16[4,272,128]{2,1,0:T(8,128)(2,1)S(1)}, u32[]{:S(2)}, u32[]{:S(2)}) collective-permute-start(bf16[4,272,128]{2,1,0:T(8,128)(2,1)S(1)} %pad_maximum_fusion.2.s_ref), channel_id=1, source_target_pairs={{0,240},{16,0},{32,16},{48,32},{64,48},{80,64},{96,80},{112,96},{1... | collective-permute-start | bytes 835592 | tf_op jit(solution)/shard_map/ppermute | solution.py:189
  68.7 1.9 %collective-permute-start.5 = (bf16[4,272,128]{2,1,0:T(8,128)(2,1)S(1)}, bf16[4,272,128]{2,1,0:T(8,128)(2,1)S(1)}, u32[]{:S(2)}, u32[]{:S(2)}) collective-permute-start(bf16[4,272,128]{2,1,0:T(8,128)(2,1)S(1)} %pad_maximum_fusion.2.s_ref), channel_id=1, source_target_pairs={{0,16},{16,32},{32,48},{48,64},{64,80},{80,96},{96,112},{112,128},... | collective-permute-start | bytes 835592 | tf_op jit(solution)/shard_map/ppermute | solution.py:189
  70.6 3.4 %collective-permute-start.8 = (bf16[2,272,128]{2,1,0:T(8,128)(2,1)S(1)}, bf16[2,272,128]{2,1,0:T(8,128)(2,1)S(1)}, u32[]{:S(2)}, u32[]{:S(2)}) collective-permute-start(bf16[2,272,128]{2,1,0:T(8,128)(2,1)S(1)} %get-tuple-element.27), channel_id=1, source_target_pairs={{0,224},{16,240},{32,0},{48,16},{64,32},{80,48},{96,64},{112,80},{... | collective-permute-start | bytes 417800 | tf_op jit(solution)/shard_map/ppermute | solution.py:189
  74.0 3.4 %collective-permute-start.7 = (bf16[2,272,128]{2,1,0:T(8,128)(2,1)S(1)}, bf16[2,272,128]{2,1,0:T(8,128)(2,1)S(1)}, u32[]{:S(2)}, u32[]{:S(2)}) collective-permute-start(bf16[2,272,128]{2,1,0:T(8,128)(2,1)S(1)} %get-tuple-element.28), channel_id=1, source_target_pairs={{0,32},{16,48},{32,64},{48,80},{64,96},{80,112},{96,128},{112,144}... | collective-permute-start | bytes 417800 | tf_op jit(solution)/shard_map/ppermute | solution.py:189
  77.4 3.9 %collective-permute-done.8.h2_ref = bf16[2,272,128]{2,1,0:T(8,128)(2,1)S(1)} collective-permute-done((bf16[2,272,128]{2,1,0:T(8,128)(2,1)S(1)}, bf16[2,272,128]{2,1,0:T(8,128)(2,1)S(1)}, u32[]{:S(2)}, u32[]{:S(2)}) %collective-permute-start.8) | collective-permute-done | bytes 139296 | tf_op jit(solution)/shard_map/ppermute | solution.py:189
  81.3 4.7 %collective-permute-done.7.h1_ref = bf16[2,272,128]{2,1,0:T(8,128)(2,1)S(1)} collective-permute-done((bf16[2,272,128]{2,1,0:T(8,128)(2,1)S(1)}, bf16[2,272,128]{2,1,0:T(8,128)(2,1)S(1)}, u32[]{:S(2)}, u32[]{:S(2)}) %collective-permute-start.7) | collective-permute-done | bytes 139296 | tf_op jit(solution)/shard_map/ppermute | solution.py:189
  86.0 7.0 %backward.1 = (f32[4,256,128]{2,1,0:T(8,128)S(1)}, bf16[4,256,128]{2,1,0:T(8,128)(2,1)S(1)}, bf16[4,256,128]{2,1,0:T(8,128)(2,1)S(1)}, bf16[2,256,128]{2,1,0:T(8...) custom-call(bf16[128,1280]{1,0:T(8,128)(2,1)S(1)} %get-tuple-element., ...), custom_call_target="tpu_custom_call" | custom-call | tf_op jit(solution)/shard_map/backward/pallas_call | solution.py:234
  93.1 2.7 %collective-permute-start.11 = (bf16[4,256,128]{2,1,0:T(8,128)(2,1)S(1)}, bf16[4,256,128]{2,1,0:T(8,128)(2,1)S(1)}, u32[]{:S(2)}, u32[]{:S(2)}) collective-permute-start(bf16[4,256,128]{2,1,0:T(8,128)(2,1)S(1)} %get-tuple-element.13), channel_id=1, source_target_pairs={{0,240},{16,0},{32,16},{48,32},{64,48},{80,64},{96,80},{112,96},{1... | collective-permute-start | bytes 786440 | tf_op jit(solution)/shard_map/ppermute | solution.py:189
  95.8 3.8 %collective-permute-start.12 = (bf16[4,256,128]{2,1,0:T(8,128)(2,1)S(1)}, bf16[4,256,128]{2,1,0:T(8,128)(2,1)S(1)}, u32[]{:S(2)}, u32[]{:S(2)}) collective-permute-start(bf16[4,256,128]{2,1,0:T(8,128)(2,1)S(1)} %get-tuple-element.14), channel_id=1, source_target_pairs={{0,16},{16,32},{32,48},{48,64},{64,80},{80,96},{96,112},{112,128},... | collective-permute-start | bytes 786440 | tf_op jit(solution)/shard_map/ppermute | solution.py:189
  99.6 2.5 %collective-permute-start.13 = (bf16[2,256,128]{2,1,0:T(8,128)(2,1)S(1)}, bf16[2,256,128]{2,1,0:T(8,128)(2,1)S(1)}, u32[]{:S(2)}, u32[]{:S(2)}) collective-permute-start(bf16[2,256,128]{2,1,0:T(8,128)(2,1)S(1)} %get-tuple-element.15), channel_id=1, source_target_pairs={{0,224},{16,240},{32,0},{48,16},{64,32},{80,48},{96,64},{112,80},{... | collective-permute-start | bytes 393224 | tf_op jit(solution)/shard_map/ppermute | solution.py:189
  102.1 4.3 %collective-permute-start.14 = (bf16[2,256,128]{2,1,0:T(8,128)(2,1)S(1)}, bf16[2,256,128]{2,1,0:T(8,128)(2,1)S(1)}, u32[]{:S(2)}, u32[]{:S(2)}) collective-permute-start(bf16[2,256,128]{2,1,0:T(8,128)(2,1)S(1)} %get-tuple-element.16), channel_id=1, source_target_pairs={{0,32},{16,48},{32,64},{48,80},{64,96},{80,112},{96,128},{112,144}... | collective-permute-start | bytes 393224 | tf_op jit(solution)/shard_map/ppermute | solution.py:189
  106.3 1.9 %collective-permute-start.9 = (bf16[2,128,512]{2,1,0:T(8,128)(2,1)S(1)}, bf16[2,128,512]{2,1,0:T(8,128)(2,1)S(1)}, u32[]{:S(2)}, u32[]{:S(2)}) collective-permute-start(bf16[2,128,512]{2,1,0:T(8,128)(2,1)S(1)} %get-tuple-element.11), channel_id=1, source_target_pairs={{0,8},{8,0},{1,9},{9,1},{2,10},{10,2},{3,11},{11,3},{4,12},{12,4},... | collective-permute-start | bytes 786440 | tf_op jit(solution)/shard_map/ppermute | solution.py:193
  108.3 2.6 %collective-permute-done.13 = bf16[2,256,128]{2,1,0:T(8,128)(2,1)S(1)} collective-permute-done((bf16[2,256,128]{2,1,0:T(8,128)(2,1)S(1)}, bf16[2,256,128]{2,1,0:T(8,128)(2,1)S(1)}, u32[]{:S(2)}, u32[]{:S(2)}) %collective-permute-start.13) | collective-permute-done | bytes 131104 | tf_op jit(solution)/shard_map/ppermute | solution.py:189
  110.9 2.4 %collective-permute-done.14 = bf16[2,256,128]{2,1,0:T(8,128)(2,1)S(1)} collective-permute-done((bf16[2,256,128]{2,1,0:T(8,128)(2,1)S(1)}, bf16[2,256,128]{2,1,0:T(8,128)(2,1)S(1)}, u32[]{:S(2)}, u32[]{:S(2)}) %collective-permute-start.14) | collective-permute-done | bytes 131104 | tf_op jit(solution)/shard_map/ppermute | solution.py:189
  113.4 5.0 %collective-permute-start.17 = (bf16[256,128]{1,0:T(8,128)(2,1)S(1)}, bf16[256,128]{1,0:T(8,128)(2,1)S(1)}, u32[]{:S(2)}, u32[]{:S(2)}) collective-permute-start(bf16[256,128]{1,0:T(8,128)(2,1)S(1)} %fusion.12), channel_id=1, source_target_pairs={{0,128},{16,144},{32,160},{48,176},{64,192},{80,208},{96,224},{112... | collective-permute-start | bytes 196616 | tf_op jit(solution)/shard_map/ppermute | solution.py:189
  118.5 9.1 %collective-permute-start.15 = (bf16[256,128]{1,0:T(8,128)(2,1)S(1)}, bf16[256,128]{1,0:T(8,128)(2,1)S(1)}, u32[]{:S(2)}, u32[]{:S(2)}) collective-permute-start(bf16[256,128]{1,0:T(8,128)(2,1)S(1)} %get-tuple-element.17), channel_id=1, source_target_pairs={{0,192},{16,208},{32,224},{48,240},{64,0},{80,16},{96,32},{112,48}... | collective-permute-start | bytes 196616 | tf_op jit(solution)/shard_map/ppermute | solution.py:189
  127.6 1.9 %collective-permute-start.16 = (bf16[256,128]{1,0:T(8,128)(2,1)S(1)}, bf16[256,128]{1,0:T(8,128)(2,1)S(1)}, u32[]{:S(2)}, u32[]{:S(2)}) collective-permute-start(bf16[256,128]{1,0:T(8,128)(2,1)S(1)} %get-tuple-element.18), channel_id=1, source_target_pairs={{0,64},{16,80},{32,96},{48,112},{64,128},{80,144},{96,160},{112,17... | collective-permute-start | bytes 196616 | tf_op jit(solution)/shard_map/ppermute | solution.py:189
  129.7 3.3 %collective-permute-start.10 = (bf16[128,512]{1,0:T(8,128)(2,1)S(1)}, bf16[128,512]{1,0:T(8,128)(2,1)S(1)}, u32[]{:S(2)}, u32[]{:S(2)}) collective-permute-start(bf16[128,512]{1,0:T(8,128)(2,1)S(1)} %fusion.2), channel_id=1, source_target_pairs={{0,256},{256,0},{1,257},{257,1},{2,258},{258,2},{3,259},{259,3},{4... | collective-permute-start | bytes 393224 | tf_op jit(solution)/shard_map/ppermute | solution.py:193
  133.0 3.3 %collective-permute-done.15 = bf16[256,128]{1,0:T(8,128)(2,1)S(1)} collective-permute-done((bf16[256,128]{1,0:T(8,128)(2,1)S(1)}, bf16[256,128]{1,0:T(8,128)(2,1)S(1)}, u32[]{:S(2)}, u32[]{:S(2)}) %collective-permute-start.15) | collective-permute-done | bytes 65568 | tf_op jit(solution)/shard_map/ppermute | solution.py:189
  136.2 1.9 %collective-permute-done.16 = bf16[256,128]{1,0:T(8,128)(2,1)S(1)} collective-permute-done((bf16[256,128]{1,0:T(8,128)(2,1)S(1)}, bf16[256,128]{1,0:T(8,128)(2,1)S(1)}, u32[]{:S(2)}, u32[]{:S(2)}) %collective-permute-start.16) | collective-permute-done | bytes 65568 | tf_op jit(solution)/shard_map/ppermute | solution.py:189
  (69 shorter events, 4.3 us)
Async XLA Ops:
  0.6 1.0 copy-start
  0.6 1.0 copy-start.3
  3.5 6.1 %copy-start.6 = (s32[128]{0:T(128)S(1)}, s32[128]{0:T(128)}, u32[]{:S(2)}) copy-start(s32[128]{0:T(128)} %param.13) | copy-start | bytes 1540
  3.5 11.6 %all-to-all-start = ((bf16[8,16,640]{2,1,0:T(8,128)(2,1)}), bf16[8,16,640]{2,1,0:T(8,128)(2,1)S(1)}, u32[]{:S(2)}, u32[]{:S(2)}) async-start(bf16[8,16,640]{2,1,0:T(8,128)(2,1)} %bitcast.3), calls=%async_computation | async-start | bytes 327680 | tf_op jit(solution)/shard_map/all_to_all | solution.py:226
  11.4 1.3 copy-start.5
  13.2 0.9 copy-start.4
  14.3 0.8 copy-start.1
  15.0 6.7 %copy-start.2 = (bf16[128,128]{1,0:T(8,128)(2,1)S(1)}, bf16[128,128]{1,0:T(8,128)(2,1)}, u32[]{:S(2)}) copy-start(bf16[128,128]{1,0:T(8,128)(2,1)} %param.9) | copy-start | bytes 98308
  15.1 12.3 %collective-permute-start = (bf16[128,1280]{1,0:T(8,128)(2,1)S(1)}, bf16[128,1280]{1,0:T(8,128)(2,1)S(1)}, u32[]{:S(2)}, u32[]{:S(2)}) collective-permute-start(bf16[128,1280]{1,0:T(8,128)(2,1)S(1)} %get-tuple-element.20.x_ref), channel_id=1, source_target_pairs={{0,256},{256,0},{1,257},{257,1},{2,258},{258,2},{3,259},{259,3},{4... | collective-permute-start | bytes 983048 | tf_op jit(solution)/shard_map/ppermute | solution.py:193
  27.4 58.6 %collective-permute-start.1 = (bf16[2,128,1280]{2,1,0:T(8,128)(2,1)S(1)}, bf16[2,128,1280]{2,1,0:T(8,128)(2,1)S(1)}, u32[]{:S(2)}, u32[]{:S(2)}) collective-permute-start(bf16[2,128,1280]{2,1,0:T(8,128)(2,1)S(1)} %pad_maximum_fusion), channel_id=1, source_target_pairs={{0,8},{8,0},{1,9},{9,1},{2,10},{10,2},{3,11},{11,3},{4,12},{12,4},... | collective-permute-start | bytes 1966088 | tf_op jit(solution)/shard_map/ppermute | solution.py:193
  29.5 25.5 %collective-permute-start.3 = (bf16[272,128]{1,0:T(8,128)(2,1)S(1)}, bf16[272,128]{1,0:T(8,128)(2,1)S(1)}, u32[]{:S(2)}, u32[]{:S(2)}) collective-permute-start(bf16[272,128]{1,0:T(8,128)(2,1)S(1)} %get-tuple-element.30), channel_id=1, source_target_pairs={{0,192},{16,208},{32,224},{48,240},{64,0},{80,16},{96,32},{112,48}... | collective-permute-start | bytes 208904 | tf_op jit(solution)/shard_map/ppermute | solution.py:189
  42.2 12.8 %collective-permute-start.2 = (bf16[272,128]{1,0:T(8,128)(2,1)S(1)}, bf16[272,128]{1,0:T(8,128)(2,1)S(1)}, u32[]{:S(2)}, u32[]{:S(2)}) collective-permute-start(bf16[272,128]{1,0:T(8,128)(2,1)S(1)} %get-tuple-element.30), channel_id=1, source_target_pairs={{0,64},{16,80},{32,96},{48,112},{64,128},{80,144},{96,160},{112,17... | collective-permute-start | bytes 208904 | tf_op jit(solution)/shard_map/ppermute | solution.py:189
  44.2 16.3 %collective-permute-start.4 = (bf16[272,128]{1,0:T(8,128)(2,1)S(1)}, bf16[272,128]{1,0:T(8,128)(2,1)S(1)}, u32[]{:S(2)}, u32[]{:S(2)}) collective-permute-start(bf16[272,128]{1,0:T(8,128)(2,1)S(1)} %get-tuple-element.30), channel_id=1, source_target_pairs={{0,128},{16,144},{32,160},{48,176},{64,192},{80,208},{96,224},{112... | collective-permute-start | bytes 208904 | tf_op jit(solution)/shard_map/ppermute | solution.py:189
  60.5 25.5 %collective-permute-start.6 = (bf16[4,272,128]{2,1,0:T(8,128)(2,1)S(1)}, bf16[4,272,128]{2,1,0:T(8,128)(2,1)S(1)}, u32[]{:S(2)}, u32[]{:S(2)}) collective-permute-start(bf16[4,272,128]{2,1,0:T(8,128)(2,1)S(1)} %pad_maximum_fusion.2.s_ref), channel_id=1, source_target_pairs={{0,240},{16,0},{32,16},{48,32},{64,48},{80,64},{96,80},{112,96},{1... | collective-permute-start | bytes 835592 | tf_op jit(solution)/shard_map/ppermute | solution.py:189
  68.7 17.3 %collective-permute-start.5 = (bf16[4,272,128]{2,1,0:T(8,128)(2,1)S(1)}, bf16[4,272,128]{2,1,0:T(8,128)(2,1)S(1)}, u32[]{:S(2)}, u32[]{:S(2)}) collective-permute-start(bf16[4,272,128]{2,1,0:T(8,128)(2,1)S(1)} %pad_maximum_fusion.2.s_ref), channel_id=1, source_target_pairs={{0,16},{16,32},{32,48},{48,64},{64,80},{80,96},{96,112},{112,128},... | collective-permute-start | bytes 835592 | tf_op jit(solution)/shard_map/ppermute | solution.py:189
  70.6 10.6 %collective-permute-start.8 = (bf16[2,272,128]{2,1,0:T(8,128)(2,1)S(1)}, bf16[2,272,128]{2,1,0:T(8,128)(2,1)S(1)}, u32[]{:S(2)}, u32[]{:S(2)}) collective-permute-start(bf16[2,272,128]{2,1,0:T(8,128)(2,1)S(1)} %get-tuple-element.27), channel_id=1, source_target_pairs={{0,224},{16,240},{32,0},{48,16},{64,32},{80,48},{96,64},{112,80},{... | collective-permute-start | bytes 417800 | tf_op jit(solution)/shard_map/ppermute | solution.py:189
  74.0 12.0 %collective-permute-start.7 = (bf16[2,272,128]{2,1,0:T(8,128)(2,1)S(1)}, bf16[2,272,128]{2,1,0:T(8,128)(2,1)S(1)}, u32[]{:S(2)}, u32[]{:S(2)}) collective-permute-start(bf16[2,272,128]{2,1,0:T(8,128)(2,1)S(1)} %get-tuple-element.28), channel_id=1, source_target_pairs={{0,32},{16,48},{32,64},{48,80},{64,96},{80,112},{96,128},{112,144}... | collective-permute-start | bytes 417800 | tf_op jit(solution)/shard_map/ppermute | solution.py:189
  93.1 20.2 %collective-permute-start.11 = (bf16[4,256,128]{2,1,0:T(8,128)(2,1)S(1)}, bf16[4,256,128]{2,1,0:T(8,128)(2,1)S(1)}, u32[]{:S(2)}, u32[]{:S(2)}) collective-permute-start(bf16[4,256,128]{2,1,0:T(8,128)(2,1)S(1)} %get-tuple-element.13), channel_id=1, source_target_pairs={{0,240},{16,0},{32,16},{48,32},{64,48},{80,64},{96,80},{112,96},{1... | collective-permute-start | bytes 786440 | tf_op jit(solution)/shard_map/ppermute | solution.py:189
  95.8 17.5 %collective-permute-start.12 = (bf16[4,256,128]{2,1,0:T(8,128)(2,1)S(1)}, bf16[4,256,128]{2,1,0:T(8,128)(2,1)S(1)}, u32[]{:S(2)}, u32[]{:S(2)}) collective-permute-start(bf16[4,256,128]{2,1,0:T(8,128)(2,1)S(1)} %get-tuple-element.14), channel_id=1, source_target_pairs={{0,16},{16,32},{32,48},{48,64},{64,80},{80,96},{96,112},{112,128},... | collective-permute-start | bytes 786440 | tf_op jit(solution)/shard_map/ppermute | solution.py:189
  99.6 11.3 %collective-permute-start.13 = (bf16[2,256,128]{2,1,0:T(8,128)(2,1)S(1)}, bf16[2,256,128]{2,1,0:T(8,128)(2,1)S(1)}, u32[]{:S(2)}, u32[]{:S(2)}) collective-permute-start(bf16[2,256,128]{2,1,0:T(8,128)(2,1)S(1)} %get-tuple-element.15), channel_id=1, source_target_pairs={{0,224},{16,240},{32,0},{48,16},{64,32},{80,48},{96,64},{112,80},{... | collective-permute-start | bytes 393224 | tf_op jit(solution)/shard_map/ppermute | solution.py:189
  102.1 11.2 %collective-permute-start.14 = (bf16[2,256,128]{2,1,0:T(8,128)(2,1)S(1)}, bf16[2,256,128]{2,1,0:T(8,128)(2,1)S(1)}, u32[]{:S(2)}, u32[]{:S(2)}) collective-permute-start(bf16[2,256,128]{2,1,0:T(8,128)(2,1)S(1)} %get-tuple-element.16), channel_id=1, source_target_pairs={{0,32},{16,48},{32,64},{48,80},{64,96},{80,112},{96,128},{112,144}... | collective-permute-start | bytes 393224 | tf_op jit(solution)/shard_map/ppermute | solution.py:189
  106.3 23.2 %collective-permute-start.9 = (bf16[2,128,512]{2,1,0:T(8,128)(2,1)S(1)}, bf16[2,128,512]{2,1,0:T(8,128)(2,1)S(1)}, u32[]{:S(2)}, u32[]{:S(2)}) collective-permute-start(bf16[2,128,512]{2,1,0:T(8,128)(2,1)S(1)} %get-tuple-element.11), channel_id=1, source_target_pairs={{0,8},{8,0},{1,9},{9,1},{2,10},{10,2},{3,11},{11,3},{4,12},{12,4},... | collective-permute-start | bytes 786440 | tf_op jit(solution)/shard_map/ppermute | solution.py:193
  113.4 19.6 %collective-permute-start.17 = (bf16[256,128]{1,0:T(8,128)(2,1)S(1)}, bf16[256,128]{1,0:T(8,128)(2,1)S(1)}, u32[]{:S(2)}, u32[]{:S(2)}) collective-permute-start(bf16[256,128]{1,0:T(8,128)(2,1)S(1)} %fusion.12), channel_id=1, source_target_pairs={{0,128},{16,144},{32,160},{48,176},{64,192},{80,208},{96,224},{112... | collective-permute-start | bytes 196616 | tf_op jit(solution)/shard_map/ppermute | solution.py:189
  118.5 17.8 %collective-permute-start.15 = (bf16[256,128]{1,0:T(8,128)(2,1)S(1)}, bf16[256,128]{1,0:T(8,128)(2,1)S(1)}, u32[]{:S(2)}, u32[]{:S(2)}) collective-permute-start(bf16[256,128]{1,0:T(8,128)(2,1)S(1)} %get-tuple-element.17), channel_id=1, source_target_pairs={{0,192},{16,208},{32,224},{48,240},{64,0},{80,16},{96,32},{112,48}... | collective-permute-start | bytes 196616 | tf_op jit(solution)/shard_map/ppermute | solution.py:189
  127.6 10.5 %collective-permute-start.16 = (bf16[256,128]{1,0:T(8,128)(2,1)S(1)}, bf16[256,128]{1,0:T(8,128)(2,1)S(1)}, u32[]{:S(2)}, u32[]{:S(2)}) collective-permute-start(bf16[256,128]{1,0:T(8,128)(2,1)S(1)} %get-tuple-element.18), channel_id=1, source_target_pairs={{0,64},{16,80},{32,96},{48,112},{64,128},{80,144},{96,160},{112,17... | collective-permute-start | bytes 196616 | tf_op jit(solution)/shard_map/ppermute | solution.py:189
  129.7 9.2 %collective-permute-start.10 = (bf16[128,512]{1,0:T(8,128)(2,1)S(1)}, bf16[128,512]{1,0:T(8,128)(2,1)S(1)}, u32[]{:S(2)}, u32[]{:S(2)}) collective-permute-start(bf16[128,512]{1,0:T(8,128)(2,1)S(1)} %fusion.2), channel_id=1, source_target_pairs={{0,256},{256,0},{1,257},{257,1},{2,258},{258,2},{3,259},{259,3},{4... | collective-permute-start | bytes 393224 | tf_op jit(solution)/shard_map/ppermute | solution.py:193

commit v2 on v1

--- a/solution.py
+++ b/solution.py
@@ -33,8 +33,8 @@
     return lax.dot_general(a, b, (((0,), (0,)), ((), ())), preferred_element_type=F32)
 
 
-def backward(x_ref, xx_ref, y_ref, s_ref, p_ref, m_ref, h1_ref, h2_ref, *rest):
-    own_out, p_out, m_out, h1_out, h2_out, dq_out, dq_core_out, acc, dq_acc = rest
+def backward(info, x_ref, y_ref, s_ref, p_ref, m_ref, h_ref, *rest):
+    own_out, p_out, m_out, h_out, dq_out, dq_core_out, acc, dq_acc = rest
     seen = lax.broadcasted_iota(jnp.int32, (BLK, ROWS), 0) <= (
         lax.broadcasted_iota(jnp.int32, (BLK, ROWS), 1) % BLK
     )
@@ -79,9 +79,7 @@
         )
 
     def pick(i, j):
-        if i < 3:
-            return (s_ref, p_ref, m_ref)[i][:, j]
-        return jnp.concatenate([h1_ref[:, j], h2_ref[:, j]], axis=0)
+        return (s_ref, p_ref, m_ref, h_ref)[i][:, j]
 
     def flat(x):
         return x.reshape(SET * BLK, HEAD)
@@ -133,13 +131,14 @@
                 )
         dq = [dq_b[:HEAD], dq_b[HEAD:] + dq_a]
         if own:
+            mine = info[0]
             for i in range(2):
                 at = slice(i * BLK, (i + 1) * BLK)
-                k, v = s_ref[0, at], s_ref[0, (2 + i) * BLK : (3 + i) * BLK]
+                k, v = s_ref[mine, at], s_ref[mine, (2 + i) * BLK : (3 + i) * BLK]
                 scores = jnp.where(seen, dot_nt(k, q[i]), -FAR)
                 p, ds = grads(scores, dot_nt(v, g[i]), lse[i], delta[i])
-                acc[0, 0, at] += dot_nn(ds, q[i])
-                acc[0, 0, (2 + i) * BLK : (3 + i) * BLK] += dot_nn(p, g[i])
+                acc[0, mine, at] += dot_nn(ds, q[i])
+                acc[0, mine, (2 + i) * BLK : (3 + i) * BLK] += dot_nn(p, g[i])
                 dq[i] = dq[i] + dot_tn(k, ds)
         for i in range(2):
             grad = jnp.transpose(dq[i]) * SCALE
@@ -148,8 +147,8 @@
                     h * BLK : (h + 1) * BLK
                 ]
 
-    visit(x_ref[...], 0, own=True)
-    visit(xx_ref[...], 1)
+    visit(x_ref[0], 0, own=True)
+    visit(x_ref[1], 1)
 
     @pl.loop(0, 2)
     def _(e):
@@ -161,8 +160,15 @@
     own_out[...] = acc[0]
     p_out[...] = acc[1].astype(BF16)
     m_out[...] = acc[2].astype(BF16)
-    h1_out[...] = acc[3, :2].astype(BF16)
-    h2_out[...] = acc[3, 2:].astype(BF16)
+    h_out[...] = acc[3].astype(BF16)
+
+
+def join(info, own_ref, other_ref, grad_ref, after_ref, x_ref):
+    wide = (GROUP + 1) * HEAD
+    x_ref[0, :, :wide] = own_ref[...]
+    x_ref[1, :, :wide] = other_ref[...]
+    x_ref[0, :, wide:] = grad_ref[info[1]]
+    x_ref[1, :, wide:] = grad_ref[1 - info[1]]
 
 
 def bf16_terms(x):
@@ -182,11 +188,28 @@
 
 
 HEADS = ("xl", "y")
-
-
-def shifted(x, by):
-    n = lax.axis_size("z")
-    return lax.ppermute(x, "z", [(i, (i + by) % n) for i in range(n)])
+RING = ("zq", "zr")
+
+
+def along_ring(x, to):
+    n = lax.axis_size(RING)
+    return lax.ppermute(x, RING, [(i, to(i) % n) for i in range(n)])
+
+
+def plus(i):
+    return i + 1
+
+
+def minus(i):
+    return i - 1
+
+
+def two_on(i):
+    return i + 2 if i % 2 == 0 else i - 2
+
+
+def two_back(i):
+    return i - 2 if i % 2 == 0 else i + 2
 
 
 def swapped_with(x, axis):
@@ -195,7 +218,6 @@
 
 def shards(queries, keys, values, outputs, out_grad, lse, positions):
     n_heads = lax.axis_size(HEADS)
-    quarter = lax.axis_size("z") // 4
     first, second = positions[0], positions[BLK]
     swapped = (first > second).astype(jnp.int32)
     c = jnp.minimum(first, second) // BLK
@@ -210,56 +232,63 @@
             jnp.broadcast_to(c.astype(BF16), (16, HEAD)),
         ]
     )
-    far = shifted(own, 2 * quarter)
-    s_set = jnp.stack([own, shifted(own, quarter), shifted(own, -quarter), far])
-    p_set, m_set = shifted(s_set, 1), shifted(s_set, -1)
-    h1 = shifted(s_set[:2], 2)
-    h2 = shifted(jnp.stack([s_set[0], s_set[2]]), -2)
+    s_set = lax.all_to_all(
+        jnp.broadcast_to(own[None], (SET,) + own.shape), "zq", split_axis=0, concat_axis=0, tiled=True
+    )
+    h_set = along_ring(s_set, two_on)
+    p_set, m_set = along_ring(s_set, plus), along_ring(s_set, minus)
 
     tok = out_grad.shape[0]
+    wide = (GROUP + 1) * HEAD
     delta = jnp.sum(
         (outputs.astype(F32) * out_grad.astype(F32)).reshape(tok, n_heads, GROUP, HEAD), axis=-1
     )
     send = jnp.concatenate(
         [out_grad.reshape(tok, n_heads, GROUP * HEAD), tail_of(delta)], axis=-1
     ).transpose(1, 0, 2)
-    grad = lax.all_to_all(send, HEADS, split_axis=0, concat_axis=0, tiled=True)
+    send = jnp.concatenate([send, send])
+    grad = lax.all_to_all(send, ("xh",) + HEADS, split_axis=0, concat_axis=0, tiled=True)
+    grad = grad.reshape(2, TOK, wide)
     own_q = early_then_late(jnp.concatenate([queries, tail_of(lse, c, swapped)], axis=1))
-    x = jnp.concatenate([own_q, grad.reshape(TOK, (GROUP + 1) * HEAD)], axis=1)
-    xx = swapped_with(x, "xh")
-    y = swapped_with(jnp.stack([x, xx]), "core")
-
+    other_q = swapped_with(own_q, "xh")
+    info = jnp.stack([lax.axis_index("zq"), lax.axis_index("xh")]).astype(jnp.int32)
+    smem = pl.BlockSpec(memory_space=pltpu.SMEM)
     vmem = pl.BlockSpec(memory_space=pltpu.VMEM)
-    four, two = (SET, 4 * BLK, HEAD), (2, 4 * BLK, HEAD)
-    own_g, p_g, m_g, h1_g, h2_g, dq, dq_core = pl.pallas_call(
+    x = pl.pallas_call(
+        join,
+        out_shape=jax.ShapeDtypeStruct((2, TOK, 2 * wide), BF16),
+        in_specs=[smem, vmem, vmem, vmem, pl.BlockSpec(memory_space=pl.ANY)],
+        out_specs=vmem,
+        name="join",
+    )(info, own_q, other_q, grad, s_set)
+    y = swapped_with(x, "core")
+
+    four, dq_shape = (SET, 4 * BLK, HEAD), (2, TOK, GROUP * HEAD)
+    own_g, p_g, m_g, h_g, dq, dq_core = pl.pallas_call(
         backward,
         out_shape=(
             jax.ShapeDtypeStruct(four, F32),
             jax.ShapeDtypeStruct(four, BF16),
             jax.ShapeDtypeStruct(four, BF16),
-            jax.ShapeDtypeStruct(two, BF16),
-            jax.ShapeDtypeStruct(two, BF16),
-            jax.ShapeDtypeStruct((2, TOK, GROUP * HEAD), F32),
-            jax.ShapeDtypeStruct((2, TOK, GROUP * HEAD), BF16),
+            jax.ShapeDtypeStruct(four, BF16),
+            jax.ShapeDtypeStruct(dq_shape, F32),
+            jax.ShapeDtypeStruct(dq_shape, BF16),
         ),
-        in_specs=[vmem] * 8,
-        out_specs=[vmem] * 7,
+        in_specs=[smem] + [vmem] * 6,
+        out_specs=[vmem] * 6,
         scratch_shapes=[
             pltpu.VMEM((4,) + four, F32),
             pltpu.VMEM((4, TOK, GROUP * HEAD), F32),
         ],
         compiler_params=pltpu.CompilerParams(vmem_limit_bytes=40 * 1024 * 1024),
         name="backward",
-    )(x, xx, y, s_set, p_set, m_set, h1, h2)
-
-    p_in, m_in = shifted(p_g, -1).astype(F32), shifted(m_g, 1).astype(F32)
-    h1_in, h2_in = shifted(h1_g, -2).astype(F32), shifted(h2_g, 2).astype(F32)
-    total = own_g + p_in + m_in
-    mine = total[0] + h1_in[0] + h2_in[0]
-    back = shifted((total[3]).astype(BF16), 2 * quarter).astype(F32)
-    left = shifted((total[1] + h1_in[1]).astype(BF16), -quarter).astype(F32)
-    right = shifted((total[2] + h2_in[1]).astype(BF16), quarter).astype(F32)
-    mine = mine + left + right + back
+    )(info, x, y, s_set, p_set, m_set, h_set)
+
+    h_in = along_ring(h_g, two_back).astype(F32)
+    p_in, m_in = along_ring(p_g, minus).astype(F32), along_ring(m_g, plus).astype(F32)
+    total = (own_g + p_in + m_in + h_in).astype(BF16)
+    mine = lax.all_to_all(total, "zq", split_axis=0, concat_axis=0, tiled=True)
+    mine = jnp.sum(mine.astype(F32), axis=0)
 
     dq = dq + swapped_with(dq_core, "core").astype(F32)
     dq = dq[0] + swapped_with(dq[1].astype(BF16), "xh").astype(F32)
@@ -271,9 +300,9 @@
 
 
 def solution(mesh):
-    shape = FOLD or (2, 16, 2, 2, 4)
-    split = jax.sharding.Mesh(mesh.devices.reshape(shape), ("xh", "z", "core", "xl", "y"))
-    ctx, heads = ("xh", "z", "core"), ("xl", "y")
+    shape = FOLD or (2, 4, 4, 2, 2, 4)
+    split = jax.sharding.Mesh(mesh.devices.reshape(shape), ("xh", "zq", "zr", "core", "xl", "y"))
+    ctx, heads = ("xh", "zq", "zr", "core"), ("xl", "y")
     return jax.shard_map(
         shards,
         mesh=split,

time: 140 us -> 136 us (0.971)
  the two profiles are of different devices: /device:TPU:6 before, /device:TPU:33 now
where the time goes in v2:
time: 136 us; the launch traced here: 135 us
  starting transfers between devices  55.2 us (41%)
  waiting for transfers between devices  53.1 us (39%)
  Pallas kernels  9.65 us (7%)
  local copies, waits for them, and re-layouts  8.91 us (7%)
  other arithmetic  4.07 us (3%)
  between operations  3.64 us (3%)
    all_to_all x1, waiting for transfers between devices, shards(): mine = lax.all_to_all(total, 'zq', split_axis=0, concat_axis=0, tiled=True)  18 us
    ppermute x6, waiting for transfers between devices, along_ring(): return lax.ppermute(x, RING, [(i, to(i) % n) for i in range(n)])  17.5 us
    ppermute x6, starting transfers between devices, along_ring(): return lax.ppermute(x, RING, [(i, to(i) % n) for i in range(n)])  17 us
    all_to_all x1, starting transfers between devices, shards(): lax.all_to_all(jnp.broadcast_to(own[None], (SET,) + own.shape), 'zq', spl...  13.9 us
    ppermute x4, starting transfers between devices, swapped_with(): return lax.ppermute(x, axis, [(0, 1), (1, 0)])  13.2 us
    all_to_all x1, waiting for transfers between devices, shards(): lax.all_to_all(jnp.broadcast_to(own[None], (SET,) + own.shape), 'zq', spl...  11 us
    pallas_call x1, Pallas kernels, shards(): pl.pallas_call(backward, out_shape=(jax.ShapeDtypeStruct(four, F32), jax....  7.59 us
    all_to_all x1, starting transfers between devices, shards(): lax.all_to_all(send, ('xh',) + HEADS, split_axis=0, concat_axis=0, tiled=...  6.89 us
  transfers between devices with their start and end apart: 13, of which 8 were waited for; matrix products, arithmetic and copies ran while one was open for 3% of the time, Pallas kernels for 0%

profile of v2, /device:TPU:33, one launch (start us, length us, event | category | flops | bytes accessed | tf_op | source)
XLA Modules:
  0.0 134.6 jit_solution(9409652656933828733)
XLA Ops:
  0.7 1.0 copy.30
  2.8 0.8 pad_maximum_fusion
  3.6 6.9 %all-to-all-start = ((bf16[16,16,640]{2,1,0:T(8,128)(2,1)}), bf16[16,16,640]{2,1,0:T(8,128)(2,1)S(1)}, u32[]{:S(2)}, u32[]{:S(2)}) async-start(bf16[16,16,640]{2,1,0:T(8,128)(2,1)} %pad_maximum_fusion), calls=%async_computation | async-start | bytes 655360 | tf_op jit(solution)/shard_map/all_to_all | solution.py:250
  12.4 0.7 copy-done.9
  15.7 2.6 %all-to-all-done = bf16[16,16,640]{2,1,0:T(8,128)(2,1)S(1)} async-done(((bf16[16,16,640]{2,1,0:T(8,128)(2,1)}), bf16[16,16,640]{2,1,0:T(8,128)(2,1)S(1)}, u32[]{:S(2)}, u32[]{:S(2)}) %all-to-all-start) | async-done | bytes 327712 | tf_op jit(solution)/shard_map/all_to_all | solution.py:250
  18.3 0.8 broadcast_in_dim.34
  19.2 13.9 %all-to-all-start.1 = ((bf16[4,272,128]{2,1,0:T(8,128)(2,1)}), bf16[4,272,128]{2,1,0:T(8,128)(2,1)S(1)}, u32[]{:S(2)}, u32[]{:S(2)}) async-start(bf16[4,272,128]{2,1,0:T(8,128)(2,1)} %broadcast_in_dim.34), calls=%async_computation.1 | async-start | bytes 557056 | tf_op jit(solution)/shard_map/all_to_all | solution.py:235
  33.1 0.8 copy-done.11
  34.2 3.0 %collective-permute-start = (bf16[128,640]{1,0:T(8,128)(2,1)S(1)}, bf16[128,640]{1,0:T(8,128)(2,1)S(1)}, u32[]{:S(2)}, u32[]{:S(2)}) collective-permute-start(bf16[128,640]{1,0:T(8,128)(2,1)S(1)} %maximum_select_fusion.1.own_ref), channel_id=1, source_target_pairs={{0,256},{256,0},{1,257},{257,1},{2,258},{258,2},{3,259},{259,3},{4... | collective-permute-start | bytes 491528 | tf_op jit(solution)/shard_map/ppermute | solution.py:216
  37.8 3.9 %collective-permute-done.other_ref = bf16[128,640]{1,0:T(8,128)(2,1)S(1)} collective-permute-done((bf16[128,640]{1,0:T(8,128)(2,1)S(1)}, bf16[128,640]{1,0:T(8,128)(2,1)S(1)}, u32[]{:S(2)}, u32[]{:S(2)}) %collective-permute-start) | collective-permute-done | bytes 163872 | tf_op jit(solution)/shard_map/ppermute | solution.py:216
  41.8 11.0 %all-to-all-done.1.after_ref.s_ref = bf16[4,272,128]{2,1,0:T(8,128)(2,1)S(1)} async-done(((bf16[4,272,128]{2,1,0:T(8,128)(2,1)}), bf16[4,272,128]{2,1,0:T(8,128)(2,1)S(1)}, u32[]{:S(2)}, u32[]{:S(2)}) %all-to-all-start.1) | async-done | bytes 278560 | tf_op jit(solution)/shard_map/all_to_all | solution.py:235
  52.8 0.7 copy-done.1
  53.5 2.1 %join.1.x_ref = bf16[2,128,1280]{2,1,0:T(8,128)(2,1)} custom-call(s32[2]{0:T(128)} %pad_add_fusion.info, bf16[128,640]{1,0:T(8,128)(2,1)} %copy-done.5, bf16[128,640]{1,0:T(8,128)(2,1)} %copy-done.7, bf16[2,128,640]{2,1,0:T(8,128)(2,1)} %bitcast.17, bf16[4,272,128]{2,1,0:T(8,128)(2,1)} %copy-done.1), custom_call_target="tpu_custom_call" | custom-call | tf_op jit(solution)/shard_map/join/pallas_call | solution.py:257
  55.5 4.7 %collective-permute-start.1 = (bf16[2,128,1280]{2,1,0:T(8,128)(2,1)}, bf16[2,128,1280]{2,1,0:T(8,128)(2,1)S(1)}, u32[]{:S(2)}, u32[]{:S(2)}) collective-permute-start(bf16[2,128,1280]{2,1,0:T(8,128)(2,1)} %join.1.x_ref), channel_id=1, source_target_pairs={{0,8},{8,0},{1,9},{9,1},{2,10},{10,2},{3,11},{11,3},{4,12},{12,4},... | collective-permute-start | bytes 1966088 | tf_op jit(solution)/shard_map/ppermute | solution.py:216
  60.3 2.7 %collective-permute-start.4 = (bf16[4,272,128]{2,1,0:T(8,128)(2,1)}, bf16[4,272,128]{2,1,0:T(8,128)(2,1)S(1)}, u32[]{:S(2)}, u32[]{:S(2)}) collective-permute-start(bf16[4,272,128]{2,1,0:T(8,128)(2,1)} %copy-done.1), channel_id=1, source_target_pairs={{0,32},{16,240},{32,64},{48,16},{64,96},{80,48},{96,128},{112,80},... | collective-permute-start | bytes 835592 | tf_op jit(solution)/shard_map/ppermute | solution.py:196
  63.0 3.0 %collective-permute-start.3 = (bf16[4,272,128]{2,1,0:T(8,128)(2,1)}, bf16[4,272,128]{2,1,0:T(8,128)(2,1)S(1)}, u32[]{:S(2)}, u32[]{:S(2)}) collective-permute-start(bf16[4,272,128]{2,1,0:T(8,128)(2,1)} %copy-done.1), channel_id=1, source_target_pairs={{0,240},{16,0},{32,16},{48,32},{64,48},{80,64},{96,80},{112,96},{1... | collective-permute-start | bytes 835592 | tf_op jit(solution)/shard_map/ppermute | solution.py:196
  66.0 2.3 %collective-permute-start.2 = (bf16[4,272,128]{2,1,0:T(8,128)(2,1)}, bf16[4,272,128]{2,1,0:T(8,128)(2,1)S(1)}, u32[]{:S(2)}, u32[]{:S(2)}) collective-permute-start(bf16[4,272,128]{2,1,0:T(8,128)(2,1)} %copy-done.1), channel_id=1, source_target_pairs={{0,16},{16,32},{32,48},{48,64},{64,80},{80,96},{96,112},{112,128},... | collective-permute-start | bytes 835592 | tf_op jit(solution)/shard_map/ppermute | solution.py:196
  68.3 3.3 %collective-permute-done.4.h_ref = bf16[4,272,128]{2,1,0:T(8,128)(2,1)S(1)} collective-permute-done((bf16[4,272,128]{2,1,0:T(8,128)(2,1)}, bf16[4,272,128]{2,1,0:T(8,128)(2,1)S(1)}, u32[]{:S(2)}, u32[]{:S(2)}) %collective-permute-start.4) | collective-permute-done | bytes 278560 | tf_op jit(solution)/shard_map/ppermute | solution.py:196
  71.6 6.3 %collective-permute-done.3.m_ref = bf16[4,272,128]{2,1,0:T(8,128)(2,1)S(1)} collective-permute-done((bf16[4,272,128]{2,1,0:T(8,128)(2,1)}, bf16[4,272,128]{2,1,0:T(8,128)(2,1)S(1)}, u32[]{:S(2)}, u32[]{:S(2)}) %collective-permute-start.3) | collective-permute-done | bytes 278560 | tf_op jit(solution)/shard_map/ppermute | solution.py:196
  77.9 1.1 copy-done
  78.9 1.0 copy-done.2
  79.9 7.6 %backward.1 = (f32[4,256,128]{2,1,0:T(8,128)S(1)}, bf16[4,256,128]{2,1,0:T(8,128)(2,1)S(1)}, bf16[4,256,128]{2,1,0:T(8,128)(2,1)S(1)}, bf16[4,256,128]{2,1,0:T(8...) custom-call(s32[2]{0:T(128)S(1)} %copy-done.3, bf16[2,128,1280]{2,1,0:T(8,128)(2,1)S(1)} %copy-done, ...), custom_call_target="tpu_custom_call" | custom-call | tf_op jit(solution)/shard_map/backward/pallas_call | solution.py:267
  87.5 2.4 %collective-permute-start.5 = (bf16[2,128,512]{2,1,0:T(8,128)(2,1)S(1)}, bf16[2,128,512]{2,1,0:T(8,128)(2,1)S(1)}, u32[]{:S(2)}, u32[]{:S(2)}) collective-permute-start(bf16[2,128,512]{2,1,0:T(8,128)(2,1)S(1)} %get-tuple-element.10), channel_id=1, source_target_pairs={{0,8},{8,0},{1,9},{9,1},{2,10},{10,2},{3,11},{11,3},{4,12},{12,4},... | collective-permute-start | bytes 786440 | tf_op jit(solution)/shard_map/ppermute | solution.py:216
  89.9 2.0 %collective-permute-start.7 = (bf16[4,256,128]{2,1,0:T(8,128)(2,1)S(1)}, bf16[4,256,128]{2,1,0:T(8,128)(2,1)S(1)}, u32[]{:S(2)}, u32[]{:S(2)}) collective-permute-start(bf16[4,256,128]{2,1,0:T(8,128)(2,1)S(1)} %get-tuple-element.12), channel_id=1, source_target_pairs={{0,240},{16,0},{32,16},{48,32},{64,48},{80,64},{96,80},{112,96},{1... | collective-permute-start | bytes 786440 | tf_op jit(solution)/shard_map/ppermute | solution.py:196
  91.9 3.3 %collective-permute-start.8 = (bf16[4,256,128]{2,1,0:T(8,128)(2,1)S(1)}, bf16[4,256,128]{2,1,0:T(8,128)(2,1)S(1)}, u32[]{:S(2)}, u32[]{:S(2)}) collective-permute-start(bf16[4,256,128]{2,1,0:T(8,128)(2,1)S(1)} %get-tuple-element.13), channel_id=1, source_target_pairs={{0,16},{16,32},{32,48},{48,64},{64,80},{80,96},{96,112},{112,128},... | collective-permute-start | bytes 786440 | tf_op jit(solution)/shard_map/ppermute | solution.py:196
  95.2 3.7 %collective-permute-start.9 = (bf16[4,256,128]{2,1,0:T(8,128)(2,1)S(1)}, bf16[4,256,128]{2,1,0:T(8,128)(2,1)S(1)}, u32[]{:S(2)}, u32[]{:S(2)}) collective-permute-start(bf16[4,256,128]{2,1,0:T(8,128)(2,1)S(1)} %get-tuple-element.14), channel_id=1, source_target_pairs={{0,224},{16,48},{32,0},{48,80},{64,32},{80,112},{96,64},{112,144},... | collective-permute-start | bytes 786440 | tf_op jit(solution)/shard_map/ppermute | solution.py:196
  99.0 3.1 %collective-permute-start.6 = (bf16[128,512]{1,0:T(8,128)(2,1)S(1)}, bf16[128,512]{1,0:T(8,128)(2,1)S(1)}, u32[]{:S(2)}, u32[]{:S(2)}) collective-permute-start(bf16[128,512]{1,0:T(8,128)(2,1)S(1)} %fusion.2), channel_id=1, source_target_pairs={{0,256},{256,0},{1,257},{257,1},{2,258},{258,2},{3,259},{259,3},{4... | collective-permute-start | bytes 393224 | tf_op jit(solution)/shard_map/ppermute | solution.py:216
  102.4 7.7 %collective-permute-done.9 = bf16[4,256,128]{2,1,0:T(8,128)(2,1)S(1)} collective-permute-done((bf16[4,256,128]{2,1,0:T(8,128)(2,1)S(1)}, bf16[4,256,128]{2,1,0:T(8,128)(2,1)S(1)}, u32[]{:S(2)}, u32[]{:S(2)}) %collective-permute-start.9) | collective-permute-done | bytes 262176 | tf_op jit(solution)/shard_map/ppermute | solution.py:196
  110.1 0.8 add_convert_fusion
  110.9 4.2 %all-to-all-start.2 = ((bf16[4,256,128]{2,1,0:T(8,128)(2,1)}), bf16[4,256,128]{2,1,0:T(8,128)(2,1)S(1)}, u32[]{:S(2)}, u32[]{:S(2)}) async-start(bf16[4,256,128]{2,1,0:T(8,128)(2,1)} %add_convert_fusion), calls=%async_computation.2 | async-start | bytes 524288 | tf_op jit(solution)/shard_map/all_to_all | solution.py:290
  115.2 0.7 fusion.1
  115.9 18.0 %all-to-all-done.2 = bf16[4,256,128]{2,1,0:T(8,128)(2,1)S(1)} async-done(((bf16[4,256,128]{2,1,0:T(8,128)(2,1)}), bf16[4,256,128]{2,1,0:T(8,128)(2,1)S(1)}, u32[]{:S(2)}, u32[]{:S(2)}) %all-to-all-start.2) | async-done | bytes 262176 | tf_op jit(solution)/shard_map/all_to_all | solution.py:290
  (67 shorter events, 5.0 us)
Async XLA Ops:
  0.6 1.0 copy-start.6
  0.6 1.0 copy-start.10
  3.6 6.9 %copy-start.13 = (s32[128]{0:T(128)S(1)}, s32[128]{0:T(128)}, u32[]{:S(2)}) copy-start(s32[128]{0:T(128)} %param.13) | copy-start | bytes 1540
  3.6 8.8 %copy-start.8 = (bf16[128,128]{1,0:T(8,128)(2,1)S(1)}, bf16[128,128]{1,0:T(8,128)(2,1)}, u32[]{:S(2)}) copy-start(bf16[128,128]{1,0:T(8,128)(2,1)} %param.8) | copy-start | bytes 98308
  3.6 14.7 %all-to-all-start = ((bf16[16,16,640]{2,1,0:T(8,128)(2,1)}), bf16[16,16,640]{2,1,0:T(8,128)(2,1)S(1)}, u32[]{:S(2)}, u32[]{:S(2)}) async-start(bf16[16,16,640]{2,1,0:T(8,128)(2,1)} %pad_maximum_fusion), calls=%async_computation | async-start | bytes 655360 | tf_op jit(solution)/shard_map/all_to_all | solution.py:250
  12.4 0.8 copy-start.9
  13.2 0.7 copy-start.12
  18.3 0.8 copy-start.4
  19.2 33.6 %all-to-all-start.1 = ((bf16[4,272,128]{2,1,0:T(8,128)(2,1)}), bf16[4,272,128]{2,1,0:T(8,128)(2,1)S(1)}, u32[]{:S(2)}, u32[]{:S(2)}) async-start(bf16[4,272,128]{2,1,0:T(8,128)(2,1)} %broadcast_in_dim.34), calls=%async_computation.1 | async-start | bytes 557056 | tf_op jit(solution)/shard_map/all_to_all | solution.py:235
  33.1 0.9 copy-start.11
  34.2 18.6 %copy-start.5 = (bf16[128,640]{1,0:T(8,128)(2,1)}, bf16[128,640]{1,0:T(8,128)(2,1)S(1)}, u32[]{:S(2)}) copy-start(bf16[128,640]{1,0:T(8,128)(2,1)S(1)} %maximum_select_fusion.1.own_ref) | copy-start | bytes 491524
  34.2 7.6 %collective-permute-start = (bf16[128,640]{1,0:T(8,128)(2,1)S(1)}, bf16[128,640]{1,0:T(8,128)(2,1)S(1)}, u32[]{:S(2)}, u32[]{:S(2)}) collective-permute-start(bf16[128,640]{1,0:T(8,128)(2,1)S(1)} %maximum_select_fusion.1.own_ref), channel_id=1, source_target_pairs={{0,256},{256,0},{1,257},{257,1},{2,258},{258,2},{3,259},{259,3},{4... | collective-permute-start | bytes 491528 | tf_op jit(solution)/shard_map/ppermute | solution.py:216
  41.8 11.0 %copy-start.7 = (bf16[128,640]{1,0:T(8,128)(2,1)}, bf16[128,640]{1,0:T(8,128)(2,1)S(1)}, u32[]{:S(2)}) copy-start(bf16[128,640]{1,0:T(8,128)(2,1)S(1)} %collective-permute-done.other_ref) | copy-start | bytes 491524
  52.8 0.7 copy-start.1
  53.5 24.4 %copy-start.3 = (s32[2]{0:T(128)S(1)}, s32[2]{0:T(128)}, u32[]{:S(2)}) copy-start(s32[2]{0:T(128)} %pad_add_fusion.info) | copy-start | bytes 28
  55.5 22.3 %collective-permute-start.1 = (bf16[2,128,1280]{2,1,0:T(8,128)(2,1)}, bf16[2,128,1280]{2,1,0:T(8,128)(2,1)S(1)}, u32[]{:S(2)}, u32[]{:S(2)}) collective-permute-start(bf16[2,128,1280]{2,1,0:T(8,128)(2,1)} %join.1.x_ref), channel_id=1, source_target_pairs={{0,8},{8,0},{1,9},{9,1},{2,10},{10,2},{3,11},{11,3},{4,12},{12,4},... | collective-permute-start | bytes 1966088 | tf_op jit(solution)/shard_map/ppermute | solution.py:216
  60.3 11.3 %collective-permute-start.4 = (bf16[4,272,128]{2,1,0:T(8,128)(2,1)}, bf16[4,272,128]{2,1,0:T(8,128)(2,1)S(1)}, u32[]{:S(2)}, u32[]{:S(2)}) collective-permute-start(bf16[4,272,128]{2,1,0:T(8,128)(2,1)} %copy-done.1), channel_id=1, source_target_pairs={{0,32},{16,240},{32,64},{48,16},{64,96},{80,48},{96,128},{112,80},... | collective-permute-start | bytes 835592 | tf_op jit(solution)/shard_map/ppermute | solution.py:196
  63.0 14.8 %collective-permute-start.3 = (bf16[4,272,128]{2,1,0:T(8,128)(2,1)}, bf16[4,272,128]{2,1,0:T(8,128)(2,1)S(1)}, u32[]{:S(2)}, u32[]{:S(2)}) collective-permute-start(bf16[4,272,128]{2,1,0:T(8,128)(2,1)} %copy-done.1), channel_id=1, source_target_pairs={{0,240},{16,0},{32,16},{48,32},{64,48},{80,64},{96,80},{112,96},{1... | collective-permute-start | bytes 835592 | tf_op jit(solution)/shard_map/ppermute | solution.py:196
  66.0 11.8 %collective-permute-start.2 = (bf16[4,272,128]{2,1,0:T(8,128)(2,1)}, bf16[4,272,128]{2,1,0:T(8,128)(2,1)S(1)}, u32[]{:S(2)}, u32[]{:S(2)}) collective-permute-start(bf16[4,272,128]{2,1,0:T(8,128)(2,1)} %copy-done.1), channel_id=1, source_target_pairs={{0,16},{16,32},{32,48},{48,64},{64,80},{80,96},{96,112},{112,128},... | collective-permute-start | bytes 835592 | tf_op jit(solution)/shard_map/ppermute | solution.py:196
  77.9 1.1 copy-start
  78.9 1.0 copy-start.2
  87.5 11.4 %collective-permute-start.5 = (bf16[2,128,512]{2,1,0:T(8,128)(2,1)S(1)}, bf16[2,128,512]{2,1,0:T(8,128)(2,1)S(1)}, u32[]{:S(2)}, u32[]{:S(2)}) collective-permute-start(bf16[2,128,512]{2,1,0:T(8,128)(2,1)S(1)} %get-tuple-element.10), channel_id=1, source_target_pairs={{0,8},{8,0},{1,9},{9,1},{2,10},{10,2},{3,11},{11,3},{4,12},{12,4},... | collective-permute-start | bytes 786440 | tf_op jit(solution)/shard_map/ppermute | solution.py:216
  89.9 12.2 %collective-permute-start.7 = (bf16[4,256,128]{2,1,0:T(8,128)(2,1)S(1)}, bf16[4,256,128]{2,1,0:T(8,128)(2,1)S(1)}, u32[]{:S(2)}, u32[]{:S(2)}) collective-permute-start(bf16[4,256,128]{2,1,0:T(8,128)(2,1)S(1)} %get-tuple-element.12), channel_id=1, source_target_pairs={{0,240},{16,0},{32,16},{48,32},{64,48},{80,64},{96,80},{112,96},{1... | collective-permute-start | bytes 786440 | tf_op jit(solution)/shard_map/ppermute | solution.py:196
  91.9 10.5 %collective-permute-start.8 = (bf16[4,256,128]{2,1,0:T(8,128)(2,1)S(1)}, bf16[4,256,128]{2,1,0:T(8,128)(2,1)S(1)}, u32[]{:S(2)}, u32[]{:S(2)}) collective-permute-start(bf16[4,256,128]{2,1,0:T(8,128)(2,1)S(1)} %get-tuple-element.13), channel_id=1, source_target_pairs={{0,16},{16,32},{32,48},{48,64},{64,80},{80,96},{96,112},{112,128},... | collective-permute-start | bytes 786440 | tf_op jit(solution)/shard_map/ppermute | solution.py:196
  95.2 14.9 %collective-permute-start.9 = (bf16[4,256,128]{2,1,0:T(8,128)(2,1)S(1)}, bf16[4,256,128]{2,1,0:T(8,128)(2,1)S(1)}, u32[]{:S(2)}, u32[]{:S(2)}) collective-permute-start(bf16[4,256,128]{2,1,0:T(8,128)(2,1)S(1)} %get-tuple-element.14), channel_id=1, source_target_pairs={{0,224},{16,48},{32,0},{48,80},{64,32},{80,112},{96,64},{112,144},... | collective-permute-start | bytes 786440 | tf_op jit(solution)/shard_map/ppermute | solution.py:196
  99.0 16.1 %collective-permute-start.6 = (bf16[128,512]{1,0:T(8,128)(2,1)S(1)}, bf16[128,512]{1,0:T(8,128)(2,1)S(1)}, u32[]{:S(2)}, u32[]{:S(2)}) collective-permute-start(bf16[128,512]{1,0:T(8,128)(2,1)S(1)} %fusion.2), channel_id=1, source_target_pairs={{0,256},{256,0},{1,257},{257,1},{2,258},{258,2},{3,259},{259,3},{4... | collective-permute-start | bytes 393224 | tf_op jit(solution)/shard_map/ppermute | solution.py:216
  110.9 23.0 %all-to-all-start.2 = ((bf16[4,256,128]{2,1,0:T(8,128)(2,1)}), bf16[4,256,128]{2,1,0:T(8,128)(2,1)S(1)}, u32[]{:S(2)}, u32[]{:S(2)}) async-start(bf16[4,256,128]{2,1,0:T(8,128)(2,1)} %add_convert_fusion), calls=%async_computation.2 | async-start | bytes 524288 | tf_op jit(solution)/shard_map/all_to_all | solution.py:290

commit v3 on v1

--- a/solution.py
+++ b/solution.py
@@ -13,6 +13,7 @@
 GROUP = 4
 ROWS = GROUP * BLK
 SET = 4
+NEAR = 5
 LOG2E = math.log2(math.e)
 SCALE = 1.0 / math.sqrt(HEAD)
 FAR = 1e30
@@ -33,8 +34,12 @@
     return lax.dot_general(a, b, (((0,), (0,)), ((), ())), preferred_element_type=F32)
 
 
-def backward(x_ref, xx_ref, y_ref, s_ref, p_ref, m_ref, h1_ref, h2_ref, *rest):
-    own_out, p_out, m_out, h1_out, h2_out, dq_out, dq_core_out, acc, dq_acc = rest
+def backward(x_ref, y_ref, s_ref, p_ref, m_ref, e_ref, *rest):
+    own_out, p_out, m_out, e_out, dq_out, dq_core_out, kv, acc, dq_acc = rest
+    kv[:NEAR] = s_ref[...]
+    kv[NEAR : 2 * NEAR] = p_ref[...]
+    kv[2 * NEAR : 3 * NEAR] = m_ref[...]
+    kv[3 * NEAR] = e_ref[...]
     seen = lax.broadcasted_iota(jnp.int32, (BLK, ROWS), 0) <= (
         lax.broadcasted_iota(jnp.int32, (BLK, ROWS), 1) % BLK
     )
@@ -79,9 +84,7 @@
         )
 
     def pick(i, j):
-        if i < 3:
-            return (s_ref, p_ref, m_ref)[i][:, j]
-        return jnp.concatenate([h1_ref[:, j], h2_ref[:, j]], axis=0)
+        return kv[i * SET : (i + 1) * SET, j]
 
     def flat(x):
         return x.reshape(SET * BLK, HEAD)
@@ -127,19 +130,19 @@
             for j, one, two in ((0, dk_a, dk_b), (2, dv_a, dv_b)):
                 one = one.reshape(SET, BLK, HEAD)
                 two = two.reshape(SET, BLK, 2 * HEAD)
-                acc[i, :, j * BLK : (j + 1) * BLK] += one + jnp.where(wide, two[:, :, :HEAD], 0.0)
-                acc[i, :, (j + 1) * BLK : (j + 2) * BLK] += jnp.where(
+                acc[i * SET : (i + 1) * SET, j * BLK : (j + 1) * BLK] += one + jnp.where(wide, two[:, :, :HEAD], 0.0)
+                acc[i * SET : (i + 1) * SET, (j + 1) * BLK : (j + 2) * BLK] += jnp.where(
                     wide, 0.0, two[:, :, HEAD:]
                 )
         dq = [dq_b[:HEAD], dq_b[HEAD:] + dq_a]
         if own:
             for i in range(2):
                 at = slice(i * BLK, (i + 1) * BLK)
-                k, v = s_ref[0, at], s_ref[0, (2 + i) * BLK : (3 + i) * BLK]
+                k, v = kv[0, at], kv[0, (2 + i) * BLK : (3 + i) * BLK]
                 scores = jnp.where(seen, dot_nt(k, q[i]), -FAR)
                 p, ds = grads(scores, dot_nt(v, g[i]), lse[i], delta[i])
-                acc[0, 0, at] += dot_nn(ds, q[i])
-                acc[0, 0, (2 + i) * BLK : (3 + i) * BLK] += dot_nn(p, g[i])
+                acc[0, at] += dot_nn(ds, q[i])
+                acc[0, (2 + i) * BLK : (3 + i) * BLK] += dot_nn(p, g[i])
                 dq[i] = dq[i] + dot_tn(k, ds)
         for i in range(2):
             grad = jnp.transpose(dq[i]) * SCALE
@@ -148,37 +151,83 @@
                     h * BLK : (h + 1) * BLK
                 ]
 
-    visit(x_ref[...], 0, own=True)
-    visit(xx_ref[...], 1)
+    visit(x_ref[0], 0, own=True)
+    visit(x_ref[1], 1)
 
     @pl.loop(0, 2)
     def _(e):
         visit(y_ref[e], e + 2)
 
     dq_out[...] = dq_acc[:2]
-    dq_core_out[...] = dq_acc[2:].astype(BF16)
-    acc[:, :, : 2 * BLK] = acc[:, :, : 2 * BLK] * SCALE
-    own_out[...] = acc[0]
-    p_out[...] = acc[1].astype(BF16)
-    m_out[...] = acc[2].astype(BF16)
-    h1_out[...] = acc[3, :2].astype(BF16)
-    h2_out[...] = acc[3, 2:].astype(BF16)
-
-
-def bf16_terms(x):
-    hi = lax.reduce_precision(x, 8, 7)
-    rest = x - hi
-    mid = lax.reduce_precision(rest, 8, 7)
-    return [hi.astype(BF16), mid.astype(BF16), (rest - mid).astype(BF16)]
-
-
-def tail_of(x, *flags):
-    lead = x.shape[:-1]
-    gap = jnp.zeros(lead + (8 - GROUP,), BF16)
-    parts = [part for term in bf16_terms(x) for part in (term, gap)]
-    parts += [jnp.broadcast_to(f.astype(BF16), lead + (1,)) for f in flags]
-    parts.append(jnp.zeros(lead + (HEAD - 24 - len(flags),), BF16))
-    return jnp.concatenate(parts, axis=-1)
+    dq_core_out[...] = dq_acc[2:]
+    for j, factor in ((slice(0, 2 * BLK), SCALE), (slice(2 * BLK, 4 * BLK), 1.0)):
+        own_out[:, j] = acc[:NEAR, j] * factor
+        p_out[:, j] = (acc[NEAR : 2 * NEAR, j] * factor).astype(BF16)
+        m_out[:, j] = (acc[2 * NEAR : 3 * NEAR, j] * factor).astype(BF16)
+        e_out[j] = (acc[3 * NEAR, j] * factor).astype(BF16)
+
+
+def in_terms(x, lanes):
+    out = jnp.zeros(lanes.shape, F32)
+    for h in range(GROUP):
+        rest = x[h]
+        for n in range(3):
+            term = rest.astype(BF16).astype(F32)
+            out = jnp.where(lanes == 8 * n + h, term, out)
+            rest = rest - term
+    return out
+
+
+def pack_keys(pos, k_ref, v_ref, out):
+    start = pl.multiple_of(jnp.where(pos[0] > pos[BLK], BLK, 0), BLK)
+    other = pl.multiple_of(BLK - start, BLK)
+    out[:BLK] = k_ref[pl.ds(start, BLK), :]
+    out[BLK : 2 * BLK] = k_ref[pl.ds(other, BLK), :]
+    out[2 * BLK : 3 * BLK] = v_ref[pl.ds(start, BLK), :]
+    out[3 * BLK : 4 * BLK] = v_ref[pl.ds(other, BLK), :]
+    c = jnp.minimum(pos[0], pos[BLK]) // BLK
+    out[4 * BLK :] = jnp.full((16, HEAD), c, jnp.int32).astype(F32).astype(BF16)
+
+
+def pack_queries(pos, q_ref, lse_ref, o_ref, g_ref, q_out, g_out):
+    wide = GROUP * HEAD
+    swapped = pos[0] > pos[BLK]
+    start = pl.multiple_of(jnp.where(swapped, BLK, 0), BLK)
+    lanes = lax.broadcasted_iota(jnp.int32, (BLK, HEAD), 1)
+    c = jnp.minimum(pos[0], pos[BLK]) // BLK
+    for i in range(2):
+        rows = pl.ds(start if i == 0 else pl.multiple_of(BLK - start, BLK), BLK)
+        q_out[i * BLK : (i + 1) * BLK, :wide] = q_ref[rows, :]
+        lse = lse_ref[rows, :]
+        tail = in_terms([lse[:, h : h + 1] for h in range(GROUP)], lanes)
+        tail = jnp.where(lanes == 24, c.astype(F32), tail)
+        tail = jnp.where(lanes == 25, swapped.astype(F32), tail)
+        q_out[i * BLK : (i + 1) * BLK, wide:] = tail.astype(BF16)
+    n_heads = g_ref.shape[1] // wide
+    lanes = lax.broadcasted_iota(jnp.int32, (g_ref.shape[0], HEAD), 1)
+    for d in range(n_heads):
+        g = g_ref[:, d * wide : (d + 1) * wide]
+        product = g.astype(F32) * o_ref[:, d * wide : (d + 1) * wide].astype(F32)
+        delta = [
+            jnp.sum(product[:, h * HEAD : (h + 1) * HEAD], axis=1, keepdims=True)
+            for h in range(GROUP)
+        ]
+        tail = in_terms(delta, lanes).astype(BF16)
+        for twin in range(2):
+            g_out[twin * n_heads + d, :, :wide] = g
+            g_out[twin * n_heads + d, :, wide:] = tail
+
+
+def join(info, own_ref, other_ref, grad_ref, after_ref, x_ref):
+    wide = (GROUP + 1) * HEAD
+    x_ref[0, :, :wide] = own_ref[...]
+    x_ref[1, :, :wide] = other_ref[...]
+    x_ref[0, :, wide:] = grad_ref[info[0]]
+    x_ref[1, :, wide:] = grad_ref[1 - info[0]]
+
+
+def narrow(dq_ref, after_ref, out):
+    out[...] = dq_ref[...].astype(BF16)
 
 
 HEADS = ("xl", "y")
@@ -189,78 +238,106 @@
     return lax.ppermute(x, "z", [(i, (i + by) % n) for i in range(n)])
 
 
+def by_parity(x, even):
+    n = lax.axis_size("z")
+    return lax.ppermute(x, "z", [(i, (i + (even if i % 2 == 0 else -even)) % n) for i in range(n)])
+
+
 def swapped_with(x, axis):
     return lax.ppermute(x, axis, [(0, 1), (1, 0)])
 
 
+def local_call(body, out_shape, mib, name):
+    vmem, smem = pl.BlockSpec(memory_space=pltpu.VMEM), pl.BlockSpec(memory_space=pltpu.SMEM)
+
+    def call(*args, scratch=()):
+        return pl.pallas_call(
+            body,
+            out_shape=out_shape,
+            in_specs=[smem if a.dtype == jnp.int32 else vmem for a in args],
+            out_specs=jax.tree.map(lambda _: vmem, out_shape),
+            scratch_shapes=scratch,
+            compiler_params=pltpu.CompilerParams(vmem_limit_bytes=mib * 1024 * 1024),
+            name=name,
+        )(*args)
+
+    return call
+
+
 def shards(queries, keys, values, outputs, out_grad, lse, positions):
     n_heads = lax.axis_size(HEADS)
-    quarter = lax.axis_size("z") // 4
-    first, second = positions[0], positions[BLK]
-    swapped = (first > second).astype(jnp.int32)
-    c = jnp.minimum(first, second) // BLK
+    even = lax.axis_index("z") % 2 == 0
+    swapped = positions[0] > positions[BLK]
+    wide = (GROUP + 1) * HEAD
+    like = jax.ShapeDtypeStruct
 
     def early_then_late(x):
-        return jnp.where(swapped == 1, jnp.concatenate([x[BLK:], x[:BLK]]), x)
-
-    own = jnp.concatenate(
-        [
-            early_then_late(keys),
-            early_then_late(values),
-            jnp.broadcast_to(c.astype(BF16), (16, HEAD)),
-        ]
-    )
-    far = shifted(own, 2 * quarter)
-    s_set = jnp.stack([own, shifted(own, quarter), shifted(own, -quarter), far])
+        return jnp.where(swapped, jnp.concatenate([x[BLK:], x[:BLK]]), x)
+
+    own = local_call(pack_keys, like((4 * BLK + 16, HEAD), BF16), 4, "pack_keys")(
+        positions, keys, values
+    )
+    far = [shifted(own, by) for by in (6, -6, 3, -3)]
+    s_set = jnp.stack([own] + far)
     p_set, m_set = shifted(s_set, 1), shifted(s_set, -1)
-    h1 = shifted(s_set[:2], 2)
-    h2 = shifted(jnp.stack([s_set[0], s_set[2]]), -2)
-
-    tok = out_grad.shape[0]
-    delta = jnp.sum(
-        (outputs.astype(F32) * out_grad.astype(F32)).reshape(tok, n_heads, GROUP, HEAD), axis=-1
-    )
-    send = jnp.concatenate(
-        [out_grad.reshape(tok, n_heads, GROUP * HEAD), tail_of(delta)], axis=-1
-    ).transpose(1, 0, 2)
-    grad = lax.all_to_all(send, HEADS, split_axis=0, concat_axis=0, tiled=True)
-    own_q = early_then_late(jnp.concatenate([queries, tail_of(lse, c, swapped)], axis=1))
-    x = jnp.concatenate([own_q, grad.reshape(TOK, (GROUP + 1) * HEAD)], axis=1)
-    xx = swapped_with(x, "xh")
-    y = swapped_with(jnp.stack([x, xx]), "core")
-
-    vmem = pl.BlockSpec(memory_space=pltpu.VMEM)
-    four, two = (SET, 4 * BLK, HEAD), (2, 4 * BLK, HEAD)
-    own_g, p_g, m_g, h1_g, h2_g, dq, dq_core = pl.pallas_call(
+    e_one = by_parity(jnp.where(even, far[1], far[0]), -2)
+
+    own_q, send = local_call(
+        pack_queries,
+        (like((TOK, wide), BF16), like((2 * n_heads, TOK // n_heads, wide), BF16)),
+        8,
+        "pack_queries",
+    )(positions, queries, lse, outputs, out_grad)
+    grad = lax.all_to_all(send, ("xh",) + HEADS, split_axis=0, concat_axis=0, tiled=True)
+    other_q = swapped_with(own_q, "xh")
+    info = lax.axis_index("xh").astype(jnp.int32).reshape(1)
+    x = local_call(join, like((2, TOK, 2 * wide), BF16), 4, "join")(
+        info, own_q, other_q, grad.reshape(2, TOK, wide), far[2]
+    )
+    y = swapped_with(x, "core")
+
+    five, one = (NEAR, 4 * BLK, HEAD), (4 * BLK, HEAD)
+    dq_shape = (2, TOK, GROUP * HEAD)
+    own_g, p_g, m_g, e_g, dq, dq_core = local_call(
         backward,
-        out_shape=(
-            jax.ShapeDtypeStruct(four, F32),
-            jax.ShapeDtypeStruct(four, BF16),
-            jax.ShapeDtypeStruct(four, BF16),
-            jax.ShapeDtypeStruct(two, BF16),
-            jax.ShapeDtypeStruct(two, BF16),
-            jax.ShapeDtypeStruct((2, TOK, GROUP * HEAD), F32),
-            jax.ShapeDtypeStruct((2, TOK, GROUP * HEAD), BF16),
+        (
+            like(five, F32),
+            like(five, BF16),
+            like(five, BF16),
+            like(one, BF16),
+            like(dq_shape, F32),
+            like(dq_shape, F32),
         ),
-        in_specs=[vmem] * 8,
-        out_specs=[vmem] * 7,
-        scratch_shapes=[
-            pltpu.VMEM((4,) + four, F32),
+        20,
+        "backward",
+    )(
+        x,
+        y,
+        s_set,
+        p_set,
+        m_set,
+        e_one,
+        scratch=[
+            pltpu.VMEM((3 * NEAR + 1, 4 * BLK + 16, HEAD), BF16),
+            pltpu.VMEM((3 * NEAR + 1,) + one, F32),
             pltpu.VMEM((4, TOK, GROUP * HEAD), F32),
         ],
-        compiler_params=pltpu.CompilerParams(vmem_limit_bytes=40 * 1024 * 1024),
-        name="backward",
-    )(x, xx, y, s_set, p_set, m_set, h1, h2)
-
-    p_in, m_in = shifted(p_g, -1).astype(F32), shifted(m_g, 1).astype(F32)
-    h1_in, h2_in = shifted(h1_g, -2).astype(F32), shifted(h2_g, 2).astype(F32)
-    total = own_g + p_in + m_in
-    mine = total[0] + h1_in[0] + h2_in[0]
-    back = shifted((total[3]).astype(BF16), 2 * quarter).astype(F32)
-    left = shifted((total[1] + h1_in[1]).astype(BF16), -quarter).astype(F32)
-    right = shifted((total[2] + h2_in[1]).astype(BF16), quarter).astype(F32)
-    mine = mine + left + right + back
-
+    )
+
+    p_in, m_in = shifted(p_g, -1), shifted(m_g, 1)
+    e_in = by_parity(e_g, 2).astype(F32)
+    total = own_g + p_in.astype(F32) + m_in.astype(F32)
+    parts = [
+        total[1] + jnp.where(even, 0.0, e_in),
+        total[2] + jnp.where(even, e_in, 0.0),
+        total[3],
+        total[4],
+    ]
+    mine = total[0]
+    for part, by in zip(parts, (-6, 6, -3, 3)):
+        mine = mine + shifted(part.astype(BF16), by).astype(F32)
+
+    dq_core = local_call(narrow, like(dq_shape, BF16), 4, "narrow")(dq_core, m_in)
     dq = dq + swapped_with(dq_core, "core").astype(F32)
     dq = dq[0] + swapped_with(dq[1].astype(BF16), "xh").astype(F32)
     return (

time: 140 us -> 133 us (0.950); the launches traced: 140 us -> 131 us
  starting transfers between devices: 91.5 us -> 86 us
  waiting for transfers between devices: 29.8 us -> 26.5 us
  Pallas kernels: 7.04 us -> 9.22 us
  between operations: 3.76 us -> 2.33 us
    ppermute x14 -> x12, waiting for transfers between devices: 24.2 us -> 8.98 us  [shifted(): return lax.ppermute(x, 'z', [(i, (i + by) % n) for i in range(n)])]
    ppermute x14 -> x12, starting transfers between devices: 71.6 us -> 59.9 us  [shifted(): return lax.ppermute(x, 'z', [(i, (i + by) % n) for i in range(n)])]
    ppermute x0 -> x2, starting transfers between devices: none -> 8.14 us  [by_parity(): lax.ppermute(x, 'z', [(i, (i + (even if i % 2 == 0 else -even)) % n) for...]
    all_to_all x1, waiting for transfers between devices: 0.01 us -> 6.71 us  [shards(): lax.all_to_all(send, ('xh',) + HEADS, split_axis=0, concat_axis=0, tiled=...]
    ppermute x0 -> x2, waiting for transfers between devices: none -> 6.7 us  [by_parity(): lax.ppermute(x, 'z', [(i, (i + (even if i % 2 == 0 else -even)) % n) for...]
    ppermute x4, starting transfers between devices: 13.7 us -> 10.7 us  [swapped_with(): return lax.ppermute(x, axis, [(0, 1), (1, 0)])]
    unnamed x15 -> x21, local copies, waits for them, and re-layouts: 1.68 us -> 4.14 us
    pallas_call x1 -> x5, Pallas kernels: 7.04 us -> 9.22 us  [call(): pl.pallas_call(body, out_shape=out_shape, in_specs=[smem if a.dtype == jn...]
  transfers between devices with their start and end apart: 19 -> 19, of which waited for: 8 -> 7; matrix products, arithmetic and copies ran while one was open for 2% -> 1% of each run, Pallas kernels for 0% -> 1%
where the time goes in v3:
time: 133 us; the launch traced here: 131 us
  starting transfers between devices  86 us (65%)
  waiting for transfers between devices  26.5 us (20%)
  Pallas kernels  9.22 us (7%)
  local copies, waits for them, and re-layouts  4.79 us (4%)
  between operations  2.33 us (2%)
  other arithmetic  1.65 us (1%)
    ppermute x12, starting transfers between devices, shifted(): return lax.ppermute(x, 'z', [(i, (i + by) % n) for i in range(n)])  59.9 us
    ppermute x4, starting transfers between devices, swapped_with(): return lax.ppermute(x, axis, [(0, 1), (1, 0)])  10.7 us
    pallas_call x5, Pallas kernels, call(): pl.pallas_call(body, out_shape=out_shape, in_specs=[smem if a.dtype == jn...  9.22 us
    ppermute x12, waiting for transfers between devices, shifted(): return lax.ppermute(x, 'z', [(i, (i + by) % n) for i in range(n)])  8.98 us
    ppermute x2, starting transfers between devices, by_parity(): lax.ppermute(x, 'z', [(i, (i + (even if i % 2 == 0 else -even)) % n) for...  8.14 us
    all_to_all x1, starting transfers between devices, shards(): lax.all_to_all(send, ('xh',) + HEADS, split_axis=0, concat_axis=0, tiled=...  7.17 us
    all_to_all x1, waiting for transfers between devices, shards(): lax.all_to_all(send, ('xh',) + HEADS, split_axis=0, concat_axis=0, tiled=...  6.71 us
    ppermute x2, waiting for transfers between devices, by_parity(): lax.ppermute(x, 'z', [(i, (i + (even if i % 2 == 0 else -even)) % n) for...  6.7 us
  transfers between devices with their start and end apart: 19, of which 7 were waited for; matrix products, arithmetic and copies ran while one was open for 1% of the time, Pallas kernels for 1%

profile of v3, /device:TPU:6, one launch (start us, length us, event | category | flops | bytes accessed | tf_op | source)
XLA Modules:
  0.0 130.5 jit_solution(3299823254864118973)
XLA Ops:
  0.6 0.7 copy-done.3
  1.4 0.8 copy-done.4
  3.4 11.8 %collective-permute-start.3 = (bf16[272,128]{1,0:T(8,128)(2,1)S(1)}, bf16[272,128]{1,0:T(8,128)(2,1)S(1)}, u32[]{:S(2)}, u32[]{:S(2)}) collective-permute-start(bf16[272,128]{1,0:T(8,128)(2,1)S(1)} %pack_keys.1), channel_id=1, source_target_pairs={{0,96},{16,112},{32,128},{48,144},{64,160},{80,176},{96,192},{112,... | collective-permute-start | bytes 208904 | tf_op jit(solution)/shard_map/ppermute | solution.py:238
  15.2 5.0 %collective-permute-start.4 = (bf16[272,128]{1,0:T(8,128)(2,1)S(1)}, bf16[272,128]{1,0:T(8,128)(2,1)S(1)}, u32[]{:S(2)}, u32[]{:S(2)}) collective-permute-start(bf16[272,128]{1,0:T(8,128)(2,1)S(1)} %pack_keys.1), channel_id=1, source_target_pairs={{0,160},{16,176},{32,192},{48,208},{64,224},{80,240},{96,0},{112,1... | collective-permute-start | bytes 208904 | tf_op jit(solution)/shard_map/ppermute | solution.py:238
  20.2 3.8 %collective-permute-start.1 = (bf16[272,128]{1,0:T(8,128)(2,1)S(1)}, bf16[272,128]{1,0:T(8,128)(2,1)S(1)}, u32[]{:S(2)}, u32[]{:S(2)}) collective-permute-start(bf16[272,128]{1,0:T(8,128)(2,1)S(1)} %pack_keys.1), channel_id=1, source_target_pairs={{0,48},{16,64},{32,80},{48,96},{64,112},{80,128},{96,144},{112,160... | collective-permute-start | bytes 208904 | tf_op jit(solution)/shard_map/ppermute | solution.py:238
  24.0 6.4 %collective-permute-start.5 = (bf16[272,128]{1,0:T(8,128)(2,1)S(1)}, bf16[272,128]{1,0:T(8,128)(2,1)S(1)}, u32[]{:S(2)}, u32[]{:S(2)}) collective-permute-start(bf16[272,128]{1,0:T(8,128)(2,1)S(1)} %pack_keys.1), channel_id=1, source_target_pairs={{0,208},{16,224},{32,240},{48,0},{64,16},{80,32},{96,48},{112,64},... | collective-permute-start | bytes 208904 | tf_op jit(solution)/shard_map/ppermute | solution.py:238
  30.5 0.9 copy-done.1
  31.4 0.9 copy-done.2
  32.3 1.6 %pack_queries.1 = (bf16[128,640]{1,0:T(8,128)(2,1)S(1)}, bf16[16,16,640]{2,1,0:T(8,128)(2,1)}) custom-call(s32[128]{0:T(128)S(1)} %copy-done.6, bf16[128,512]{1,0:T(8,128)(2,1)S(1)} %copy-done, f32[128,4]{1,0:T(8,128)S(1)} %copy.10.lse_ref, bf16[16,4096]{1,0:T(8,128)(2,1)S(1)} %copy-done.1, bf16[16,4096]{1,0:T(8,128)(2,1)S(1)} %copy-done.2), custom_call_target="tpu_custom_call" | custom-call | tf_op jit(solution)/shard_map/pack_queries/pallas_call | solution.py:254
  33.9 3.3 %collective-permute-start = (bf16[128,640]{1,0:T(8,128)(2,1)S(1)}, bf16[128,640]{1,0:T(8,128)(2,1)S(1)}, u32[]{:S(2)}, u32[]{:S(2)}) collective-permute-start(bf16[128,640]{1,0:T(8,128)(2,1)S(1)} %get-tuple-element.11.own_ref), channel_id=1, source_target_pairs={{0,256},{256,0},{1,257},{257,1},{2,258},{258,2},{3,259},{259,3},{4... | collective-permute-start | bytes 491528 | tf_op jit(solution)/shard_map/ppermute | solution.py:247
  37.2 7.2 %all-to-all-start = ((bf16[16,16,640]{2,1,0:T(8,128)(2,1)}), bf16[16,16,640]{2,1,0:T(8,128)(2,1)S(1)}, u32[]{:S(2)}, u32[]{:S(2)}) async-start(bf16[16,16,640]{2,1,0:T(8,128)(2,1)} %get-tuple-element.12), calls=%async_computation | async-start | bytes 655360 | tf_op jit(solution)/shard_map/all_to_all | solution.py:291
  44.5 6.7 %all-to-all-done = bf16[16,16,640]{2,1,0:T(8,128)(2,1)S(1)} async-done(((bf16[16,16,640]{2,1,0:T(8,128)(2,1)}), bf16[16,16,640]{2,1,0:T(8,128)(2,1)S(1)}, u32[]{:S(2)}, u32[]{:S(2)}) %all-to-all-start) | async-done | bytes 327712 | tf_op jit(solution)/shard_map/all_to_all | solution.py:291
  51.2 1.9 %collective-permute-start.2 = (bf16[2,128,1280]{2,1,0:T(8,128)(2,1)S(1)}, bf16[2,128,1280]{2,1,0:T(8,128)(2,1)S(1)}, u32[]{:S(2)}, u32[]{:S(2)}) collective-permute-start(bf16[2,128,1280]{2,1,0:T(8,128)(2,1)S(1)} %join.1.x_ref), channel_id=1, source_target_pairs={{0,8},{8,0},{1,9},{9,1},{2,10},{10,2},{3,11},{11,3},{4,12},{12,4},... | collective-permute-start | bytes 1966088 | tf_op jit(solution)/shard_map/ppermute | solution.py:247
  53.2 1.9 %collective-permute-start.6 = (bf16[5,272,128]{2,1,0:T(8,128)(2,1)S(1)}, bf16[5,272,128]{2,1,0:T(8,128)(2,1)S(1)}, u32[]{:S(2)}, u32[]{:S(2)}) collective-permute-start(bf16[5,272,128]{2,1,0:T(8,128)(2,1)S(1)} %bitcast_dynamic-update-slice_fusion.s_ref), channel_id=1, source_target_pairs={{0,16},{16,32},{32,48},{48,64},{64,80},{80,96},{96,112},{112,128},... | collective-permute-start | bytes 1044488 | tf_op jit(solution)/shard_map/ppermute | solution.py:238
  55.2 5.1 %collective-permute-start.7 = (bf16[5,272,128]{2,1,0:T(8,128)(2,1)S(1)}, bf16[5,272,128]{2,1,0:T(8,128)(2,1)S(1)}, u32[]{:S(2)}, u32[]{:S(2)}) collective-permute-start(bf16[5,272,128]{2,1,0:T(8,128)(2,1)S(1)} %bitcast_dynamic-update-slice_fusion.s_ref), channel_id=1, source_target_pairs={{0,240},{16,0},{32,16},{48,32},{64,48},{80,64},{96,80},{112,96},{1... | collective-permute-start | bytes 1044488 | tf_op jit(solution)/shard_map/ppermute | solution.py:238
  60.3 4.3 %collective-permute-start.8 = (bf16[272,128]{1,0:T(8,128)(2,1)S(1)}, bf16[272,128]{1,0:T(8,128)(2,1)S(1)}, u32[]{:S(2)}, u32[]{:S(2)}) collective-permute-start(bf16[272,128]{1,0:T(8,128)(2,1)S(1)} %broadcast_select_fusion), channel_id=1, source_target_pairs={{0,224},{16,48},{32,0},{48,80},{64,32},{80,112},{96,64},{112,144},... | collective-permute-start | bytes 208904 | tf_op jit(solution)/shard_map/ppermute | solution.py:243
  64.6 5.0 %collective-permute-done.8.e_ref = bf16[272,128]{1,0:T(8,128)(2,1)S(1)} collective-permute-done((bf16[272,128]{1,0:T(8,128)(2,1)S(1)}, bf16[272,128]{1,0:T(8,128)(2,1)S(1)}, u32[]{:S(2)}, u32[]{:S(2)}) %collective-permute-start.8) | collective-permute-done | bytes 69664 | tf_op jit(solution)/shard_map/ppermute | solution.py:243
  69.6 7.0 %backward.1 = (f32[5,256,128]{2,1,0:T(8,128)S(1)}, bf16[5,256,128]{2,1,0:T(8,128)(2,1)S(1)}, bf16[5,256,128]{2,1,0:T(8,128)(2,1)S(1)}, bf16[256,128]{1,0:T(8,128...) custom-call(bf16[2,128,1280]{2,1,0:T(8,128)(2,1)S(1)} %join.1.x_ref, ...), custom_call_target="tpu_custom_call" | custom-call | tf_op jit(solution)/shard_map/backward/pallas_call | solution.py:254
  76.6 4.8 %collective-permute-start.12 = (bf16[5,256,128]{2,1,0:T(8,128)(2,1)S(1)}, bf16[5,256,128]{2,1,0:T(8,128)(2,1)S(1)}, u32[]{:S(2)}, u32[]{:S(2)}) collective-permute-start(bf16[5,256,128]{2,1,0:T(8,128)(2,1)S(1)} %get-tuple-element.17), channel_id=1, source_target_pairs={{0,240},{16,0},{32,16},{48,32},{64,48},{80,64},{96,80},{112,96},{1... | collective-permute-start | bytes 983048 | tf_op jit(solution)/shard_map/ppermute | solution.py:238
  81.4 1.9 %collective-permute-start.9 = (bf16[5,256,128]{2,1,0:T(8,128)(2,1)S(1)}, bf16[5,256,128]{2,1,0:T(8,128)(2,1)S(1)}, u32[]{:S(2)}, u32[]{:S(2)}) collective-permute-start(bf16[5,256,128]{2,1,0:T(8,128)(2,1)S(1)} %get-tuple-element.15), channel_id=1, source_target_pairs={{0,16},{16,32},{32,48},{48,64},{64,80},{80,96},{96,112},{112,128},... | collective-permute-start | bytes 983048 | tf_op jit(solution)/shard_map/ppermute | solution.py:238
  83.3 3.9 %collective-permute-start.13 = (bf16[256,128]{1,0:T(8,128)(2,1)S(1)}, bf16[256,128]{1,0:T(8,128)(2,1)S(1)}, u32[]{:S(2)}, u32[]{:S(2)}) collective-permute-start(bf16[256,128]{1,0:T(8,128)(2,1)S(1)} %get-tuple-element.18), channel_id=1, source_target_pairs={{0,32},{16,240},{32,64},{48,16},{64,96},{80,48},{96,128},{112,80},... | collective-permute-start | bytes 196616 | tf_op jit(solution)/shard_map/ppermute | solution.py:243
  87.5 5.8 %collective-permute-done.9.after_ref = bf16[5,256,128]{2,1,0:T(8,128)(2,1)S(1)} collective-permute-done((bf16[5,256,128]{2,1,0:T(8,128)(2,1)S(1)}, bf16[5,256,128]{2,1,0:T(8,128)(2,1)S(1)}, u32[]{:S(2)}, u32[]{:S(2)}) %collective-permute-start.9) | collective-permute-done | bytes 327712 | tf_op jit(solution)/shard_map/ppermute | solution.py:238
  93.4 1.8 %collective-permute-done.13 = bf16[256,128]{1,0:T(8,128)(2,1)S(1)} collective-permute-done((bf16[256,128]{1,0:T(8,128)(2,1)S(1)}, bf16[256,128]{1,0:T(8,128)(2,1)S(1)}, u32[]{:S(2)}, u32[]{:S(2)}) %collective-permute-start.13) | collective-permute-done | bytes 65568 | tf_op jit(solution)/shard_map/ppermute | solution.py:243
  95.2 7.2 %collective-permute-start.14 = (bf16[256,128]{1,0:T(8,128)(2,1)S(1)}, bf16[256,128]{1,0:T(8,128)(2,1)S(1)}, u32[]{:S(2)}, u32[]{:S(2)}) collective-permute-start(bf16[256,128]{1,0:T(8,128)(2,1)S(1)} %get-tuple-element.21), channel_id=1, source_target_pairs={{0,160},{16,176},{32,192},{48,208},{64,224},{80,240},{96,0},{112,1... | collective-permute-start | bytes 196616 | tf_op jit(solution)/shard_map/ppermute | solution.py:238
  102.4 4.3 %collective-permute-start.15 = (bf16[256,128]{1,0:T(8,128)(2,1)S(1)}, bf16[256,128]{1,0:T(8,128)(2,1)S(1)}, u32[]{:S(2)}, u32[]{:S(2)}) collective-permute-start(bf16[256,128]{1,0:T(8,128)(2,1)S(1)} %get-tuple-element.22), channel_id=1, source_target_pairs={{0,96},{16,112},{32,128},{48,144},{64,160},{80,176},{96,192},{112,... | collective-permute-start | bytes 196616 | tf_op jit(solution)/shard_map/ppermute | solution.py:238
  106.8 3.2 %collective-permute-start.16 = (bf16[256,128]{1,0:T(8,128)(2,1)S(1)}, bf16[256,128]{1,0:T(8,128)(2,1)S(1)}, u32[]{:S(2)}, u32[]{:S(2)}) collective-permute-start(bf16[256,128]{1,0:T(8,128)(2,1)S(1)} %get-tuple-element.23), channel_id=1, source_target_pairs={{0,208},{16,224},{32,240},{48,0},{64,16},{80,32},{96,48},{112,64},... | collective-permute-start | bytes 196616 | tf_op jit(solution)/shard_map/ppermute | solution.py:238
  110.0 4.4 %collective-permute-start.17 = (bf16[256,128]{1,0:T(8,128)(2,1)S(1)}, bf16[256,128]{1,0:T(8,128)(2,1)S(1)}, u32[]{:S(2)}, u32[]{:S(2)}) collective-permute-start(bf16[256,128]{1,0:T(8,128)(2,1)S(1)} %get-tuple-element.24), channel_id=1, source_target_pairs={{0,48},{16,64},{32,80},{48,96},{64,112},{80,128},{96,144},{112,160... | collective-permute-start | bytes 196616 | tf_op jit(solution)/shard_map/ppermute | solution.py:238
  116.3 1.9 %collective-permute-start.10 = (bf16[2,128,512]{2,1,0:T(8,128)(2,1)S(1)}, bf16[2,128,512]{2,1,0:T(8,128)(2,1)S(1)}, u32[]{:S(2)}, u32[]{:S(2)}) collective-permute-start(bf16[2,128,512]{2,1,0:T(8,128)(2,1)S(1)} %narrow.1), channel_id=1, source_target_pairs={{0,8},{8,0},{1,9},{9,1},{2,10},{10,2},{3,11},{11,3},{4,12},{12,4},... | collective-permute-start | bytes 786440 | tf_op jit(solution)/shard_map/ppermute | solution.py:247
  118.3 2.9 %collective-permute-done.17 = bf16[256,128]{1,0:T(8,128)(2,1)S(1)} collective-permute-done((bf16[256,128]{1,0:T(8,128)(2,1)S(1)}, bf16[256,128]{1,0:T(8,128)(2,1)S(1)}, u32[]{:S(2)}, u32[]{:S(2)}) %collective-permute-start.17) | collective-permute-done | bytes 65568 | tf_op jit(solution)/shard_map/ppermute | solution.py:238
  121.4 3.6 %collective-permute-start.11 = (bf16[128,512]{1,0:T(8,128)(2,1)S(1)}, bf16[128,512]{1,0:T(8,128)(2,1)S(1)}, u32[]{:S(2)}, u32[]{:S(2)}) collective-permute-start(bf16[128,512]{1,0:T(8,128)(2,1)S(1)} %fusion.6), channel_id=1, source_target_pairs={{0,256},{256,0},{1,257},{257,1},{2,258},{258,2},{3,259},{259,3},{4... | collective-permute-start | bytes 393224 | tf_op jit(solution)/shard_map/ppermute | solution.py:247
  125.6 4.1 %collective-permute-done.11 = bf16[128,512]{1,0:T(8,128)(2,1)S(1)} collective-permute-done((bf16[128,512]{1,0:T(8,128)(2,1)S(1)}, bf16[128,512]{1,0:T(8,128)(2,1)S(1)}, u32[]{:S(2)}, u32[]{:S(2)}) %collective-permute-start.11) | collective-permute-done | bytes 131104 | tf_op jit(solution)/shard_map/ppermute | solution.py:247
  129.8 0.7 fusion.1
  (46 shorter events, 3.4 us)
Async XLA Ops:
  0.6 0.8 copy-start.3
  1.4 0.8 copy-start.4
  2.1 0.7 copy-start.5
  2.8 27.6 %copy-start.7 = (f32[128,4]{0,1:T(4,128)S(1)}, f32[128,4]{0,1:T(4,128)}, u32[]{:S(2)}) copy-start(f32[128,4]{0,1:T(4,128)} %param.12) | copy-start | bytes 6148
  2.8 27.7 %copy-start = (bf16[128,512]{1,0:T(8,128)(2,1)S(1)}, bf16[128,512]{1,0:T(8,128)(2,1)}, u32[]{:S(2)}) copy-start(bf16[128,512]{1,0:T(8,128)(2,1)} %q_ref.1) | copy-start | bytes 393220
  3.4 27.1 %copy-start.6 = (s32[128]{0:T(128)S(1)}, s32[128]{0:T(128)}, u32[]{:S(2)}) copy-start(s32[128]{0:T(128)} %pos.3) | copy-start | bytes 1540
  3.4 41.0 %collective-permute-start.3 = (bf16[272,128]{1,0:T(8,128)(2,1)S(1)}, bf16[272,128]{1,0:T(8,128)(2,1)S(1)}, u32[]{:S(2)}, u32[]{:S(2)}) collective-permute-start(bf16[272,128]{1,0:T(8,128)(2,1)S(1)} %pack_keys.1), channel_id=1, source_target_pairs={{0,96},{16,112},{32,128},{48,144},{64,160},{80,176},{96,192},{112,... | collective-permute-start | bytes 208904 | tf_op jit(solution)/shard_map/ppermute | solution.py:238
  15.2 29.2 %collective-permute-start.4 = (bf16[272,128]{1,0:T(8,128)(2,1)S(1)}, bf16[272,128]{1,0:T(8,128)(2,1)S(1)}, u32[]{:S(2)}, u32[]{:S(2)}) collective-permute-start(bf16[272,128]{1,0:T(8,128)(2,1)S(1)} %pack_keys.1), channel_id=1, source_target_pairs={{0,160},{16,176},{32,192},{48,208},{64,224},{80,240},{96,0},{112,1... | collective-permute-start | bytes 208904 | tf_op jit(solution)/shard_map/ppermute | solution.py:238
  20.2 24.3 %collective-permute-start.1 = (bf16[272,128]{1,0:T(8,128)(2,1)S(1)}, bf16[272,128]{1,0:T(8,128)(2,1)S(1)}, u32[]{:S(2)}, u32[]{:S(2)}) collective-permute-start(bf16[272,128]{1,0:T(8,128)(2,1)S(1)} %pack_keys.1), channel_id=1, source_target_pairs={{0,48},{16,64},{32,80},{48,96},{64,112},{80,128},{96,144},{112,160... | collective-permute-start | bytes 208904 | tf_op jit(solution)/shard_map/ppermute | solution.py:238
  24.0 29.2 %collective-permute-start.5 = (bf16[272,128]{1,0:T(8,128)(2,1)S(1)}, bf16[272,128]{1,0:T(8,128)(2,1)S(1)}, u32[]{:S(2)}, u32[]{:S(2)}) collective-permute-start(bf16[272,128]{1,0:T(8,128)(2,1)S(1)} %pack_keys.1), channel_id=1, source_target_pairs={{0,208},{16,224},{32,240},{48,0},{64,16},{80,32},{96,48},{112,64},... | collective-permute-start | bytes 208904 | tf_op jit(solution)/shard_map/ppermute | solution.py:238
  30.5 0.9 copy-start.1
  31.4 0.9 copy-start.2
  33.9 10.6 %collective-permute-start = (bf16[128,640]{1,0:T(8,128)(2,1)S(1)}, bf16[128,640]{1,0:T(8,128)(2,1)S(1)}, u32[]{:S(2)}, u32[]{:S(2)}) collective-permute-start(bf16[128,640]{1,0:T(8,128)(2,1)S(1)} %get-tuple-element.11.own_ref), channel_id=1, source_target_pairs={{0,256},{256,0},{1,257},{257,1},{2,258},{258,2},{3,259},{259,3},{4... | collective-permute-start | bytes 491528 | tf_op jit(solution)/shard_map/ppermute | solution.py:247
  37.2 14.0 %all-to-all-start = ((bf16[16,16,640]{2,1,0:T(8,128)(2,1)}), bf16[16,16,640]{2,1,0:T(8,128)(2,1)S(1)}, u32[]{:S(2)}, u32[]{:S(2)}) async-start(bf16[16,16,640]{2,1,0:T(8,128)(2,1)} %get-tuple-element.12), calls=%async_computation | async-start | bytes 655360 | tf_op jit(solution)/shard_map/all_to_all | solution.py:291
  51.2 18.3 %collective-permute-start.2 = (bf16[2,128,1280]{2,1,0:T(8,128)(2,1)S(1)}, bf16[2,128,1280]{2,1,0:T(8,128)(2,1)S(1)}, u32[]{:S(2)}, u32[]{:S(2)}) collective-permute-start(bf16[2,128,1280]{2,1,0:T(8,128)(2,1)S(1)} %join.1.x_ref), channel_id=1, source_target_pairs={{0,8},{8,0},{1,9},{9,1},{2,10},{10,2},{3,11},{11,3},{4,12},{12,4},... | collective-permute-start | bytes 1966088 | tf_op jit(solution)/shard_map/ppermute | solution.py:247
  53.2 16.3 %collective-permute-start.6 = (bf16[5,272,128]{2,1,0:T(8,128)(2,1)S(1)}, bf16[5,272,128]{2,1,0:T(8,128)(2,1)S(1)}, u32[]{:S(2)}, u32[]{:S(2)}) collective-permute-start(bf16[5,272,128]{2,1,0:T(8,128)(2,1)S(1)} %bitcast_dynamic-update-slice_fusion.s_ref), channel_id=1, source_target_pairs={{0,16},{16,32},{32,48},{48,64},{64,80},{80,96},{96,112},{112,128},... | collective-permute-start | bytes 1044488 | tf_op jit(solution)/shard_map/ppermute | solution.py:238
  55.2 14.4 %collective-permute-start.7 = (bf16[5,272,128]{2,1,0:T(8,128)(2,1)S(1)}, bf16[5,272,128]{2,1,0:T(8,128)(2,1)S(1)}, u32[]{:S(2)}, u32[]{:S(2)}) collective-permute-start(bf16[5,272,128]{2,1,0:T(8,128)(2,1)S(1)} %bitcast_dynamic-update-slice_fusion.s_ref), channel_id=1, source_target_pairs={{0,240},{16,0},{32,16},{48,32},{64,48},{80,64},{96,80},{112,96},{1... | collective-permute-start | bytes 1044488 | tf_op jit(solution)/shard_map/ppermute | solution.py:238
  60.3 9.2 %collective-permute-start.8 = (bf16[272,128]{1,0:T(8,128)(2,1)S(1)}, bf16[272,128]{1,0:T(8,128)(2,1)S(1)}, u32[]{:S(2)}, u32[]{:S(2)}) collective-permute-start(bf16[272,128]{1,0:T(8,128)(2,1)S(1)} %broadcast_select_fusion), channel_id=1, source_target_pairs={{0,224},{16,48},{32,0},{48,80},{64,32},{80,112},{96,64},{112,144},... | collective-permute-start | bytes 208904 | tf_op jit(solution)/shard_map/ppermute | solution.py:243
  76.6 10.9 %collective-permute-start.12 = (bf16[5,256,128]{2,1,0:T(8,128)(2,1)S(1)}, bf16[5,256,128]{2,1,0:T(8,128)(2,1)S(1)}, u32[]{:S(2)}, u32[]{:S(2)}) collective-permute-start(bf16[5,256,128]{2,1,0:T(8,128)(2,1)S(1)} %get-tuple-element.17), channel_id=1, source_target_pairs={{0,240},{16,0},{32,16},{48,32},{64,48},{80,64},{96,80},{112,96},{1... | collective-permute-start | bytes 983048 | tf_op jit(solution)/shard_map/ppermute | solution.py:238
  81.4 11.8 %collective-permute-start.9 = (bf16[5,256,128]{2,1,0:T(8,128)(2,1)S(1)}, bf16[5,256,128]{2,1,0:T(8,128)(2,1)S(1)}, u32[]{:S(2)}, u32[]{:S(2)}) collective-permute-start(bf16[5,256,128]{2,1,0:T(8,128)(2,1)S(1)} %get-tuple-element.15), channel_id=1, source_target_pairs={{0,16},{16,32},{32,48},{48,64},{64,80},{80,96},{96,112},{112,128},... | collective-permute-start | bytes 983048 | tf_op jit(solution)/shard_map/ppermute | solution.py:238
  83.3 11.8 %collective-permute-start.13 = (bf16[256,128]{1,0:T(8,128)(2,1)S(1)}, bf16[256,128]{1,0:T(8,128)(2,1)S(1)}, u32[]{:S(2)}, u32[]{:S(2)}) collective-permute-start(bf16[256,128]{1,0:T(8,128)(2,1)S(1)} %get-tuple-element.18), channel_id=1, source_target_pairs={{0,32},{16,240},{32,64},{48,16},{64,96},{80,48},{96,128},{112,80},... | collective-permute-start | bytes 196616 | tf_op jit(solution)/shard_map/ppermute | solution.py:243
  95.2 23.1 %collective-permute-start.14 = (bf16[256,128]{1,0:T(8,128)(2,1)S(1)}, bf16[256,128]{1,0:T(8,128)(2,1)S(1)}, u32[]{:S(2)}, u32[]{:S(2)}) collective-permute-start(bf16[256,128]{1,0:T(8,128)(2,1)S(1)} %get-tuple-element.21), channel_id=1, source_target_pairs={{0,160},{16,176},{32,192},{48,208},{64,224},{80,240},{96,0},{112,1... | collective-permute-start | bytes 196616 | tf_op jit(solution)/shard_map/ppermute | solution.py:238
  102.4 15.9 %collective-permute-start.15 = (bf16[256,128]{1,0:T(8,128)(2,1)S(1)}, bf16[256,128]{1,0:T(8,128)(2,1)S(1)}, u32[]{:S(2)}, u32[]{:S(2)}) collective-permute-start(bf16[256,128]{1,0:T(8,128)(2,1)S(1)} %get-tuple-element.22), channel_id=1, source_target_pairs={{0,96},{16,112},{32,128},{48,144},{64,160},{80,176},{96,192},{112,... | collective-permute-start | bytes 196616 | tf_op jit(solution)/shard_map/ppermute | solution.py:238
  106.8 11.5 %collective-permute-start.16 = (bf16[256,128]{1,0:T(8,128)(2,1)S(1)}, bf16[256,128]{1,0:T(8,128)(2,1)S(1)}, u32[]{:S(2)}, u32[]{:S(2)}) collective-permute-start(bf16[256,128]{1,0:T(8,128)(2,1)S(1)} %get-tuple-element.23), channel_id=1, source_target_pairs={{0,208},{16,224},{32,240},{48,0},{64,16},{80,32},{96,48},{112,64},... | collective-permute-start | bytes 196616 | tf_op jit(solution)/shard_map/ppermute | solution.py:238
  110.0 11.2 %collective-permute-start.17 = (bf16[256,128]{1,0:T(8,128)(2,1)S(1)}, bf16[256,128]{1,0:T(8,128)(2,1)S(1)}, u32[]{:S(2)}, u32[]{:S(2)}) collective-permute-start(bf16[256,128]{1,0:T(8,128)(2,1)S(1)} %get-tuple-element.24), channel_id=1, source_target_pairs={{0,48},{16,64},{32,80},{48,96},{64,112},{80,128},{96,144},{112,160... | collective-permute-start | bytes 196616 | tf_op jit(solution)/shard_map/ppermute | solution.py:238
  116.3 4.9 %collective-permute-start.10 = (bf16[2,128,512]{2,1,0:T(8,128)(2,1)S(1)}, bf16[2,128,512]{2,1,0:T(8,128)(2,1)S(1)}, u32[]{:S(2)}, u32[]{:S(2)}) collective-permute-start(bf16[2,128,512]{2,1,0:T(8,128)(2,1)S(1)} %narrow.1), channel_id=1, source_target_pairs={{0,8},{8,0},{1,9},{9,1},{2,10},{10,2},{3,11},{11,3},{4,12},{12,4},... | collective-permute-start | bytes 786440 | tf_op jit(solution)/shard_map/ppermute | solution.py:247
  121.4 8.4 %collective-permute-start.11 = (bf16[128,512]{1,0:T(8,128)(2,1)S(1)}, bf16[128,512]{1,0:T(8,128)(2,1)S(1)}, u32[]{:S(2)}, u32[]{:S(2)}) collective-permute-start(bf16[128,512]{1,0:T(8,128)(2,1)S(1)} %fusion.6), channel_id=1, source_target_pairs={{0,256},{256,0},{1,257},{257,1},{2,258},{258,2},{3,259},{259,3},{4... | collective-permute-start | bytes 393224 | tf_op jit(solution)/shard_map/ppermute | solution.py:247

commit v4 on v3

--- a/solution.py
+++ b/solution.py
@@ -12,8 +12,7 @@
 TOK = 2 * BLK
 GROUP = 4
 ROWS = GROUP * BLK
-SET = 4
-NEAR = 5
+NEAR = 3
 LOG2E = math.log2(math.e)
 SCALE = 1.0 / math.sqrt(HEAD)
 FAR = 1e30
@@ -34,16 +33,10 @@
     return lax.dot_general(a, b, (((0,), (0,)), ((), ())), preferred_element_type=F32)
 
 
-def backward(x_ref, y_ref, s_ref, p_ref, m_ref, e_ref, *rest):
-    own_out, p_out, m_out, e_out, dq_out, dq_core_out, kv, acc, dq_acc = rest
-    kv[:NEAR] = s_ref[...]
-    kv[NEAR : 2 * NEAR] = p_ref[...]
-    kv[2 * NEAR : 3 * NEAR] = m_ref[...]
-    kv[3 * NEAR] = e_ref[...]
+def backward(x_ref, y_ref, kv, acc, dq_acc, tiles, own):
     seen = lax.broadcasted_iota(jnp.int32, (BLK, ROWS), 0) <= (
         lax.broadcasted_iota(jnp.int32, (BLK, ROWS), 1) % BLK
     )
-    acc[...] = jnp.zeros_like(acc)
 
     def grads(scores, dprob, lse, delta):
         probs = jnp.exp2(scores * (SCALE * LOG2E) - lse)
@@ -83,11 +76,8 @@
             (jnp.where(tall, g1, g0), jnp.where(tall, g0, g1)),
         )
 
-    def pick(i, j):
-        return kv[i * SET : (i + 1) * SET, j]
-
     def flat(x):
-        return x.reshape(SET * BLK, HEAD)
+        return x.reshape(x.shape[0] * x.shape[1], x.shape[2])
 
     def visit(block, e, own=False):
         own_c, lse, delta, q, g = query_side(block)
@@ -97,14 +87,17 @@
         g_both = jnp.concatenate(g, axis=1)
         dq_a = jnp.zeros((HEAD, ROWS), F32)
         dq_b = jnp.zeros((2 * HEAD, ROWS), F32)
-        for i in range(4):
-            c = pick(i, slice(4 * BLK, 4 * BLK + 16)).astype(F32)[:, 0:1, :]
+        for first, last in tiles:
+            size = last - first
+
+            def pick(j):
+                return kv[first:last, j * BLK : (j + 1) * BLK]
+
+            c = kv[first:last, 4 * BLK : 4 * BLK + 16].astype(F32)[:, 0:1, :]
             before = c < own_c[None]
             after = c > own_c[None]
-            wide = jnp.broadcast_to(before, (SET, BLK, HEAD))
-            k_early, k_late, v_early, v_late = [
-                pick(i, slice(j * BLK, (j + 1) * BLK)) for j in range(4)
-            ]
+            wide = jnp.broadcast_to(before, (size, BLK, HEAD))
+            k_early, k_late, v_early, v_late = [pick(j) for j in range(4)]
             k_both = jnp.concatenate(
                 [flat(jnp.where(wide, k_early, 0)), flat(jnp.where(wide, 0, k_late))], axis=1
             )
@@ -116,8 +109,8 @@
             after2 = jnp.concatenate([after, after], axis=2)
             lse_b = jnp.where(before2, lse_early[None], jnp.where(after2, lse_late[None], FAR))
             delta_b = jnp.where(before2, delta_early[None], delta_late[None])
-            lse_b = jnp.broadcast_to(lse_b, (SET, BLK, ROWS)).reshape(SET * BLK, ROWS)
-            delta_b = jnp.broadcast_to(delta_b, (SET, BLK, ROWS)).reshape(SET * BLK, ROWS)
+            lse_b = jnp.broadcast_to(lse_b, (size, BLK, ROWS)).reshape(size * BLK, ROWS)
+            delta_b = jnp.broadcast_to(delta_b, (size, BLK, ROWS)).reshape(size * BLK, ROWS)
 
             p_a, ds_a = grads(
                 dot_nt(k_early, q_late), dot_nt(v_early, g_late), lse_late, delta_late
@@ -128,10 +121,10 @@
             dq_a = dq_a + dot_tn(k_early, ds_a)
             dq_b = dq_b + dot_tn(k_both, ds_b)
             for j, one, two in ((0, dk_a, dk_b), (2, dv_a, dv_b)):
-                one = one.reshape(SET, BLK, HEAD)
-                two = two.reshape(SET, BLK, 2 * HEAD)
-                acc[i * SET : (i + 1) * SET, j * BLK : (j + 1) * BLK] += one + jnp.where(wide, two[:, :, :HEAD], 0.0)
-                acc[i * SET : (i + 1) * SET, (j + 1) * BLK : (j + 2) * BLK] += jnp.where(
+                one = one.reshape(size, BLK, HEAD)
+                two = two.reshape(size, BLK, 2 * HEAD)
+                acc[first:last, j * BLK : (j + 1) * BLK] += one + jnp.where(wide, two[:, :, :HEAD], 0.0)
+                acc[first:last, (j + 1) * BLK : (j + 2) * BLK] += jnp.where(
                     wide, 0.0, two[:, :, HEAD:]
                 )
         dq = [dq_b[:HEAD], dq_b[HEAD:] + dq_a]
@@ -147,24 +140,47 @@
         for i in range(2):
             grad = jnp.transpose(dq[i]) * SCALE
             for h in range(GROUP):
-                dq_acc[e, i * BLK : (i + 1) * BLK, h * HEAD : (h + 1) * HEAD] = grad[
+                dq_acc[e, i * BLK : (i + 1) * BLK, h * HEAD : (h + 1) * HEAD] += grad[
                     h * BLK : (h + 1) * BLK
                 ]
 
-    visit(x_ref[0], 0, own=True)
+    acc[...] = jnp.zeros_like(acc)
+    visit(x_ref[0], 0, own=own)
     visit(x_ref[1], 1)
 
     @pl.loop(0, 2)
     def _(e):
         visit(y_ref[e], e + 2)
 
-    dq_out[...] = dq_acc[:2]
-    dq_core_out[...] = dq_acc[2:]
-    for j, factor in ((slice(0, 2 * BLK), SCALE), (slice(2 * BLK, 4 * BLK), 1.0)):
-        own_out[:, j] = acc[:NEAR, j] * factor
-        p_out[:, j] = (acc[NEAR : 2 * NEAR, j] * factor).astype(BF16)
-        m_out[:, j] = (acc[2 * NEAR : 3 * NEAR, j] * factor).astype(BF16)
-        e_out[j] = (acc[3 * NEAR, j] * factor).astype(BF16)
+
+def scaled(acc, rows):
+    return jnp.concatenate([acc[rows, : 2 * BLK] * SCALE, acc[rows, 2 * BLK :]], axis=-2)
+
+
+def with_nearest(x_ref, y_ref, s_ref, p_ref, m_ref, e_ref, *rest):
+    own_out, p_out, m_out, e_out, dq_out, kv, acc = rest
+    kv[:NEAR] = s_ref[...]
+    kv[NEAR : 2 * NEAR] = p_ref[...]
+    kv[2 * NEAR : 3 * NEAR] = m_ref[...]
+    kv[3 * NEAR] = e_ref[...]
+    dq_out[...] = jnp.zeros_like(dq_out)
+    backward(x_ref, y_ref, kv, acc, dq_out, ((0, 5), (5, 10)), True)
+    own_out[...] = scaled(acc, slice(0, NEAR))
+    p_out[...] = scaled(acc, slice(NEAR, 2 * NEAR)).astype(BF16)
+    m_out[...] = scaled(acc, slice(2 * NEAR, 3 * NEAR)).astype(BF16)
+    e_out[...] = scaled(acc, 3 * NEAR).astype(BF16)
+
+
+def with_next(x_ref, y_ref, p_ref, m_ref, dq_ref, *rest):
+    p_out, m_out, dq_out, dq_core_out, kv, acc, dq = rest
+    kv[:NEAR] = p_ref[...]
+    kv[NEAR:] = m_ref[...]
+    dq[...] = dq_ref[...]
+    backward(x_ref, y_ref, kv, acc, dq, ((0, 3), (3, 6)), False)
+    p_out[...] = scaled(acc, slice(0, NEAR)).astype(BF16)
+    m_out[...] = scaled(acc, slice(NEAR, 2 * NEAR)).astype(BF16)
+    dq_out[...] = dq[:2]
+    dq_core_out[...] = dq[2:].astype(BF16)
 
 
 def in_terms(x, lanes):
@@ -218,16 +234,42 @@
             g_out[twin * n_heads + d, :, wide:] = tail
 
 
-def join(info, own_ref, other_ref, grad_ref, after_ref, x_ref):
+def join(info, own_ref, plus_ref, minus_ref, q_ref, qx_ref, grad_ref, s_out, e_out, x_out):
+    s_out[0] = own_ref[...]
+    s_out[1] = plus_ref[...]
+    s_out[2] = minus_ref[...]
+    e_out[...] = jnp.where(info[1] == 0, minus_ref[...], plus_ref[...])
     wide = (GROUP + 1) * HEAD
-    x_ref[0, :, :wide] = own_ref[...]
-    x_ref[1, :, :wide] = other_ref[...]
-    x_ref[0, :, wide:] = grad_ref[info[0]]
-    x_ref[1, :, wide:] = grad_ref[1 - info[0]]
-
-
-def narrow(dq_ref, after_ref, out):
-    out[...] = dq_ref[...].astype(BF16)
+    x_out[0, :, :wide] = q_ref[...]
+    x_out[1, :, :wide] = qx_ref[...]
+    x_out[0, :, wide:] = grad_ref[info[0]]
+    x_out[1, :, wide:] = grad_ref[1 - info[0]]
+
+
+def sum_near(info, own_ref, p1, m1, p2, m2, e_ref, dq_ref, core_ref, *outs):
+    own_out, plus_out, minus_out, dq_out, dqx_out = outs
+    extra = e_ref[...].astype(F32)
+    even = info[1] == 0
+    for i, out in enumerate((own_out, plus_out, minus_out)):
+        total = own_ref[i]
+        for ref in (p1, m1, p2, m2):
+            total = total + ref[i].astype(F32)
+        if i:
+            total = total + jnp.where(even == (i == 2), extra, 0.0)
+        out[...] = total.astype(out.dtype)
+    dq_out[...] = dq_ref[0] + core_ref[0].astype(F32)
+    dqx_out[...] = (dq_ref[1] + core_ref[1].astype(F32)).astype(BF16)
+
+
+def finish(pos, own_ref, plus_ref, minus_ref, dq_ref, dqx_ref, q_out, k_out, v_out):
+    start = pl.multiple_of(jnp.where(pos[0] > pos[BLK], BLK, 0), BLK)
+    total = own_ref[...] + plus_ref[...].astype(F32) + minus_ref[...].astype(F32)
+    dq = dq_ref[...] + dqx_ref[...].astype(F32)
+    for i in range(2):
+        rows = pl.ds(start if i == 0 else pl.multiple_of(BLK - start, BLK), BLK)
+        q_out[rows, :] = dq[i * BLK : (i + 1) * BLK].astype(BF16)
+        k_out[rows, :] = total[i * BLK : (i + 1) * BLK].astype(BF16)
+        v_out[rows, :] = total[(2 + i) * BLK : (3 + i) * BLK].astype(BF16)
 
 
 HEADS = ("xl", "y")
@@ -247,18 +289,21 @@
     return lax.ppermute(x, axis, [(0, 1), (1, 0)])
 
 
-def local_call(body, out_shape, mib, name):
+def local_call(body, out_shape, mib, stream_in=False, stream_out=False):
     vmem, smem = pl.BlockSpec(memory_space=pltpu.VMEM), pl.BlockSpec(memory_space=pltpu.SMEM)
+    free = pl.BlockSpec()
 
     def call(*args, scratch=()):
         return pl.pallas_call(
             body,
             out_shape=out_shape,
-            in_specs=[smem if a.dtype == jnp.int32 else vmem for a in args],
-            out_specs=jax.tree.map(lambda _: vmem, out_shape),
+            in_specs=[
+                smem if a.dtype == jnp.int32 else free if stream_in else vmem for a in args
+            ],
+            out_specs=jax.tree.map(lambda _: free if stream_out else vmem, out_shape),
             scratch_shapes=scratch,
             compiler_params=pltpu.CompilerParams(vmem_limit_bytes=mib * 1024 * 1024),
-            name=name,
+            name=body.__name__,
         )(*args)
 
     return call
@@ -266,85 +311,91 @@
 
 def shards(queries, keys, values, outputs, out_grad, lse, positions):
     n_heads = lax.axis_size(HEADS)
-    even = lax.axis_index("z") % 2 == 0
-    swapped = positions[0] > positions[BLK]
     wide = (GROUP + 1) * HEAD
-    like = jax.ShapeDtypeStruct
-
-    def early_then_late(x):
-        return jnp.where(swapped, jnp.concatenate([x[BLK:], x[:BLK]]), x)
-
-    own = local_call(pack_keys, like((4 * BLK + 16, HEAD), BF16), 4, "pack_keys")(
-        positions, keys, values
-    )
-    far = [shifted(own, by) for by in (6, -6, 3, -3)]
-    s_set = jnp.stack([own] + far)
-    p_set, m_set = shifted(s_set, 1), shifted(s_set, -1)
-    e_one = by_parity(jnp.where(even, far[1], far[0]), -2)
+    info = jnp.stack([lax.axis_index("xh"), lax.axis_index("z") % 2]).astype(jnp.int32)
+
+    def like(shape, dtype=BF16):
+        return jax.ShapeDtypeStruct(shape, dtype)
+
+    packed, block = (4 * BLK + 16, HEAD), (4 * BLK, HEAD)
+    own = local_call(pack_keys, like(packed), 56, stream_in=True)(positions, keys, values)
+    plus, minus = shifted(own, -5), shifted(own, 5)
 
     own_q, send = local_call(
         pack_queries,
-        (like((TOK, wide), BF16), like((2 * n_heads, TOK // n_heads, wide), BF16)),
-        8,
-        "pack_queries",
+        (like((TOK, wide)), like((2 * n_heads, TOK // n_heads, wide))),
+        56,
+        stream_in=True,
     )(positions, queries, lse, outputs, out_grad)
     grad = lax.all_to_all(send, ("xh",) + HEADS, split_axis=0, concat_axis=0, tiled=True)
     other_q = swapped_with(own_q, "xh")
-    info = lax.axis_index("xh").astype(jnp.int32).reshape(1)
-    x = local_call(join, like((2, TOK, 2 * wide), BF16), 4, "join")(
-        info, own_q, other_q, grad.reshape(2, TOK, wide), far[2]
-    )
+    s_set, e_one, x = local_call(
+        join, (like((NEAR,) + packed), like(packed), like((2, TOK, 2 * wide))), 8, stream_in=True
+    )(info, own, plus, minus, own_q, other_q, grad.reshape(2, TOK, wide))
+    p1, m1, p2, m2 = [shifted(s_set, by) for by in (1, -1, 2, -2)]
+    e_one = by_parity(e_one, 3)
     y = swapped_with(x, "core")
 
-    five, one = (NEAR, 4 * BLK, HEAD), (4 * BLK, HEAD)
-    dq_shape = (2, TOK, GROUP * HEAD)
-    own_g, p_g, m_g, e_g, dq, dq_core = local_call(
-        backward,
+    near, dq_shape = (NEAR,) + block, (2, TOK, GROUP * HEAD)
+    own_g, p1_g, m1_g, e_g, dq = local_call(
+        with_nearest,
         (
-            like(five, F32),
-            like(five, BF16),
-            like(five, BF16),
-            like(one, BF16),
-            like(dq_shape, F32),
-            like(dq_shape, F32),
+            like(near, F32),
+            like(near),
+            like(near),
+            like(block),
+            like((4,) + dq_shape[1:], F32),
         ),
-        20,
-        "backward",
+        16,
     )(
         x,
         y,
         s_set,
-        p_set,
-        m_set,
+        p1,
+        m1,
         e_one,
         scratch=[
-            pltpu.VMEM((3 * NEAR + 1, 4 * BLK + 16, HEAD), BF16),
-            pltpu.VMEM((3 * NEAR + 1,) + one, F32),
-            pltpu.VMEM((4, TOK, GROUP * HEAD), F32),
+            pltpu.VMEM((3 * NEAR + 1,) + packed, BF16),
+            pltpu.VMEM((3 * NEAR + 1,) + block, F32),
         ],
     )
-
-    p_in, m_in = shifted(p_g, -1), shifted(m_g, 1)
-    e_in = by_parity(e_g, 2).astype(F32)
-    total = own_g + p_in.astype(F32) + m_in.astype(F32)
-    parts = [
-        total[1] + jnp.where(even, 0.0, e_in),
-        total[2] + jnp.where(even, e_in, 0.0),
-        total[3],
-        total[4],
-    ]
-    mine = total[0]
-    for part, by in zip(parts, (-6, 6, -3, 3)):
-        mine = mine + shifted(part.astype(BF16), by).astype(F32)
-
-    dq_core = local_call(narrow, like(dq_shape, BF16), 4, "narrow")(dq_core, m_in)
-    dq = dq + swapped_with(dq_core, "core").astype(F32)
-    dq = dq[0] + swapped_with(dq[1].astype(BF16), "xh").astype(F32)
-    return (
-        early_then_late(dq).astype(BF16),
-        early_then_late(mine[:TOK]).astype(BF16),
-        early_then_late(mine[TOK:]).astype(BF16),
+    p2_g, m2_g, dq, dq_core = local_call(
+        with_next, (like(near), like(near), like(dq_shape, F32), like(dq_shape)), 16
+    )(
+        x,
+        y,
+        p2,
+        m2,
+        dq,
+        scratch=[
+            pltpu.VMEM((2 * NEAR,) + packed, BF16),
+            pltpu.VMEM((2 * NEAR,) + block, F32),
+            pltpu.VMEM((4,) + dq_shape[1:], F32),
+        ],
     )
+
+    p1_in, m1_in, e_in = shifted(p1_g, -1), shifted(m1_g, 1), by_parity(e_g, 3)
+    p2_in, m2_in = shifted(p2_g, -2), shifted(m2_g, 2)
+    dq_core = swapped_with(dq_core, "core")
+    own_g, plus_g, minus_g, dq, dqx = local_call(
+        sum_near,
+        (
+            like(block, F32),
+            like(block),
+            like(block),
+            like(dq_shape[1:], F32),
+            like(dq_shape[1:]),
+        ),
+        8,
+    )(info, own_g, p1_in, m1_in, p2_in, m2_in, e_in, dq, dq_core)
+    plus_g, minus_g = shifted(plus_g, 5), shifted(minus_g, -5)
+    dqx = swapped_with(dqx, "xh")
+    return local_call(
+        finish,
+        (like(queries.shape), like(keys.shape), like(values.shape)),
+        8,
+        stream_out=True,
+    )(positions, own_g, plus_g, minus_g, dq, dqx)
 
 
 def solution(mesh):

time: 133 us -> 133 us (level); the launches traced: 131 us -> 132 us
  Pallas kernels: 9.22 us -> 15.5 us
  local copies, waits for them, and re-layouts: 4.79 us -> 2.96 us
  other arithmetic: 1.65 us -> 0.08 us
  between operations: 2.33 us -> 0.89 us
    ppermute x12, waiting for transfers between devices: 8.98 us -> 25.8 us  [shifted(): return lax.ppermute(x, 'z', [(i, (i + by) % n) for i in range(n)])]
    ppermute x12, starting transfers between devices: 59.9 us -> 51.5 us  [shifted(): return lax.ppermute(x, 'z', [(i, (i + by) % n) for i in range(n)])]
    ppermute x2, starting transfers between devices: 8.14 us -> 15.1 us  [by_parity(): lax.ppermute(x, 'z', [(i, (i + (even if i % 2 == 0 else -even)) % n) for...]
    all_to_all x1, waiting for transfers between devices: 6.71 us -> 0.01 us  [shards(): lax.all_to_all(send, ('xh',) + HEADS, split_axis=0, concat_axis=0, tiled=...]
    ppermute x2, waiting for transfers between devices: 6.7 us -> 0.01 us  [by_parity(): lax.ppermute(x, 'z', [(i, (i + (even if i % 2 == 0 else -even)) % n) for...]
    pallas_call x5 -> x7, Pallas kernels: 9.22 us -> 15.5 us  [call(): pl.pallas_call(body, out_shape=out_shape, in_specs=[smem if a.dtype == jn...]
    ppermute x4, waiting for transfers between devices: 4.15 us -> 0.01 us  [swapped_with(): return lax.ppermute(x, axis, [(0, 1), (1, 0)])]
    all_to_all x1, starting transfers between devices: 7.17 us -> 9.39 us  [shards(): lax.all_to_all(send, ('xh',) + HEADS, split_axis=0, concat_axis=0, tiled=...]
  transfers between devices with their start and end apart: 19 -> 19, of which waited for: 7 -> 7; matrix products, arithmetic and copies ran while one was open for 1% -> 0% of each run, Pallas kernels for 1% -> 8%
where the time goes in v4:
time: 133 us; the launch traced here: 132 us
  starting transfers between devices  87.1 us (65%)
  waiting for transfers between devices  25.8 us (19%)
  Pallas kernels  15.5 us (12%)
  local copies, waits for them, and re-layouts  2.96 us (2%)
    ppermute x12, starting transfers between devices, shifted(): return lax.ppermute(x, 'z', [(i, (i + by) % n) for i in range(n)])  51.5 us
    ppermute x12, waiting for transfers between devices, shifted(): return lax.ppermute(x, 'z', [(i, (i + by) % n) for i in range(n)])  25.8 us
    pallas_call x7, Pallas kernels, call(): pl.pallas_call(body, out_shape=out_shape, in_specs=[smem if a.dtype == jn...  15.5 us
    ppermute x2, starting transfers between devices, by_parity(): lax.ppermute(x, 'z', [(i, (i + (even if i % 2 == 0 else -even)) % n) for...  15.1 us
    ppermute x4, starting transfers between devices, swapped_with(): return lax.ppermute(x, axis, [(0, 1), (1, 0)])  11.1 us
    all_to_all x1, starting transfers between devices, shards(): lax.all_to_all(send, ('xh',) + HEADS, split_axis=0, concat_axis=0, tiled=...  9.39 us
    unnamed x7, local copies, waits for them, and re-layouts  2.96 us
  transfers between devices with their start and end apart: 19, of which 7 were waited for; matrix products, arithmetic and copies ran while one was open for 0% of the time, Pallas kernels for 8%

profile of v4, /device:TPU:6, one launch (start us, length us, event | category | flops | bytes accessed | tf_op | source)
XLA Modules:
  0.0 132.4 jit_solution(13016635183562968962)
XLA Ops:
  0.6 1.4 %copy.10.lse_ref = f32[128,4]{1,0:T(8,128)} copy(f32[128,4]{0,1:T(4,128)} %param.12) | data formatting | bytes 4096 | tf_op args[5]
  2.0 2.1 %pack_queries.1 = (bf16[128,640]{1,0:T(8,128)(2,1)}, bf16[16,16,640]{2,1,0:T(8,128)(2,1)}) custom-call(s32[128]{0:T(128)} %pos.5, bf16[128,512]{1,0:T(8,128)(2,1)} %q_ref.1, f32[128,4]{1,0:T(8,128)} %copy.10.lse_ref, bf16[16,4096]{1,0:T(8,128)(2,1)} %o_ref.1, bf16[16,4096]{1,0:T(8,128)(2,1)} %g_ref.1), custom_call_target="tpu_custom_call" | custom-call | tf_op jit(solution)/shard_map/pack_queries/pallas_call | solution.py:297
  4.2 9.4 %all-to-all-start = ((bf16[16,16,640]{2,1,0:T(8,128)(2,1)}), bf16[16,16,640]{2,1,0:T(8,128)(2,1)S(1)}, u32[]{:S(2)}, u32[]{:S(2)}) async-start(bf16[16,16,640]{2,1,0:T(8,128)(2,1)} %get-tuple-element.23), calls=%async_computation | async-start | bytes 655360 | tf_op jit(solution)/shard_map/all_to_all | solution.py:330
  13.5 3.3 %collective-permute-start.2 = (bf16[128,640]{1,0:T(8,128)(2,1)S(1)}, bf16[128,640]{1,0:T(8,128)(2,1)S(1)}, u32[]{:S(2)}, u32[]{:S(2)}) collective-permute-start(bf16[128,640]{1,0:T(8,128)(2,1)S(1)} %copy-done.1), channel_id=1, source_target_pairs={{0,256},{256,0},{1,257},{257,1},{2,258},{258,2},{3,259},{259,3},{4... | collective-permute-start | bytes 491528 | tf_op jit(solution)/shard_map/ppermute | solution.py:289
  16.9 1.4 %pack_keys.1.own_ref = bf16[272,128]{1,0:T(8,128)(2,1)} custom-call(s32[128]{0:T(128)} %pos.5, bf16[128,128]{1,0:T(8,128)(2,1)} %k_ref.1, bf16[128,128]{1,0:T(8,128)(2,1)} %v_ref.1), custom_call_target="tpu_custom_call" | custom-call | tf_op jit(solution)/shard_map/pack_keys/pallas_call | solution.py:297
  18.3 8.7 %collective-permute-start.1 = (bf16[272,128]{1,0:T(8,128)(2,1)}, bf16[272,128]{1,0:T(8,128)(2,1)S(1)}, u32[]{:S(2)}, u32[]{:S(2)}) collective-permute-start(bf16[272,128]{1,0:T(8,128)(2,1)} %pack_keys.1.own_ref), channel_id=1, source_target_pairs={{0,80},{16,96},{32,112},{48,128},{64,144},{80,160},{96,176},{112,1... | collective-permute-start | bytes 208904 | tf_op jit(solution)/shard_map/ppermute | solution.py:280
  27.0 5.9 %collective-permute-start = (bf16[272,128]{1,0:T(8,128)(2,1)}, bf16[272,128]{1,0:T(8,128)(2,1)S(1)}, u32[]{:S(2)}, u32[]{:S(2)}) collective-permute-start(bf16[272,128]{1,0:T(8,128)(2,1)} %pack_keys.1.own_ref), channel_id=1, source_target_pairs={{0,176},{16,192},{32,208},{48,224},{64,240},{80,0},{96,16},{112,32... | collective-permute-start | bytes 208904 | tf_op jit(solution)/shard_map/ppermute | solution.py:280
  33.5 6.4 %collective-permute-done.plus_ref = bf16[272,128]{1,0:T(8,128)(2,1)S(1)} collective-permute-done((bf16[272,128]{1,0:T(8,128)(2,1)}, bf16[272,128]{1,0:T(8,128)(2,1)S(1)}, u32[]{:S(2)}, u32[]{:S(2)}) %collective-permute-start) | collective-permute-done | bytes 69664 | tf_op jit(solution)/shard_map/ppermute | solution.py:280
  39.8 0.9 copy-done
  41.4 1.9 %collective-permute-start.3 = (bf16[2,128,1280]{2,1,0:T(8,128)(2,1)S(1)}, bf16[2,128,1280]{2,1,0:T(8,128)(2,1)S(1)}, u32[]{:S(2)}, u32[]{:S(2)}) collective-permute-start(bf16[2,128,1280]{2,1,0:T(8,128)(2,1)S(1)} %get-tuple-element.24.x_ref), channel_id=1, source_target_pairs={{0,8},{8,0},{1,9},{9,1},{2,10},{10,2},{3,11},{11,3},{4,12},{12,4},... | collective-permute-start | bytes 1966088 | tf_op jit(solution)/shard_map/ppermute | solution.py:289
  43.3 10.5 %collective-permute-start.6 = (bf16[272,128]{1,0:T(8,128)(2,1)S(1)}, bf16[272,128]{1,0:T(8,128)(2,1)S(1)}, u32[]{:S(2)}, u32[]{:S(2)}) collective-permute-start(bf16[272,128]{1,0:T(8,128)(2,1)S(1)} %get-tuple-element.26), channel_id=1, source_target_pairs={{0,48},{16,224},{32,80},{48,0},{64,112},{80,32},{96,144},{112,64},... | collective-permute-start | bytes 208904 | tf_op jit(solution)/shard_map/ppermute | solution.py:285
  53.8 1.9 %collective-permute-start.5 = (bf16[3,272,128]{2,1,0:T(8,128)(2,1)S(1)}, bf16[3,272,128]{2,1,0:T(8,128)(2,1)S(1)}, u32[]{:S(2)}, u32[]{:S(2)}) collective-permute-start(bf16[3,272,128]{2,1,0:T(8,128)(2,1)S(1)} %get-tuple-element.25.s_ref), channel_id=1, source_target_pairs={{0,240},{16,0},{32,16},{48,32},{64,48},{80,64},{96,80},{112,96},{1... | collective-permute-start | bytes 626696 | tf_op jit(solution)/shard_map/ppermute | solution.py:280
  55.7 3.9 %collective-permute-start.4 = (bf16[3,272,128]{2,1,0:T(8,128)(2,1)S(1)}, bf16[3,272,128]{2,1,0:T(8,128)(2,1)S(1)}, u32[]{:S(2)}, u32[]{:S(2)}) collective-permute-start(bf16[3,272,128]{2,1,0:T(8,128)(2,1)S(1)} %get-tuple-element.25.s_ref), channel_id=1, source_target_pairs={{0,16},{16,32},{32,48},{48,64},{64,80},{80,96},{96,112},{112,128},... | collective-permute-start | bytes 626696 | tf_op jit(solution)/shard_map/ppermute | solution.py:280
  59.6 1.9 %collective-permute-start.10 = (bf16[3,272,128]{2,1,0:T(8,128)(2,1)S(1)}, bf16[3,272,128]{2,1,0:T(8,128)(2,1)S(1)}, u32[]{:S(2)}, u32[]{:S(2)}) collective-permute-start(bf16[3,272,128]{2,1,0:T(8,128)(2,1)S(1)} %get-tuple-element.25.s_ref), channel_id=1, source_target_pairs={{0,224},{16,240},{32,0},{48,16},{64,32},{80,48},{96,64},{112,80},{... | collective-permute-start | bytes 626696 | tf_op jit(solution)/shard_map/ppermute | solution.py:280
  61.6 4.8 %collective-permute-start.9 = (bf16[3,272,128]{2,1,0:T(8,128)(2,1)S(1)}, bf16[3,272,128]{2,1,0:T(8,128)(2,1)S(1)}, u32[]{:S(2)}, u32[]{:S(2)}) collective-permute-start(bf16[3,272,128]{2,1,0:T(8,128)(2,1)S(1)} %get-tuple-element.25.s_ref), channel_id=1, source_target_pairs={{0,32},{16,48},{32,64},{48,80},{64,96},{80,112},{96,128},{112,144}... | collective-permute-start | bytes 626696 | tf_op jit(solution)/shard_map/ppermute | solution.py:280
  66.4 5.5 %with_nearest.1 = (f32[3,256,128]{2,1,0:T(8,128)S(1)}, bf16[3,256,128]{2,1,0:T(8,128)(2,1)S(1)}, bf16[3,256,128]{2,1,0:T(8,128)(2,1)S(1)}, bf16[256,128]{1,0:T(8,128)(2,1)S(1)}, f32[4,128,512]{2,1,0:T(8,128)S(1)}) custom-call(bf16[2,128,1280]{2,1,0:T(8,128)(2,1)S(1)} %get-tuple-element.24.x_ref, bf16[2,128,1280]{2,1,0:T(8,128)(2,1)S(1)} %collective-permute-done.3.y_ref, ...), custom_call_target="tpu_custom_call" | custom-call | tf_op jit(solution)/shard_map/with_nearest/pallas_call | solution.py:297
  71.9 4.6 %collective-permute-start.13 = (bf16[256,128]{1,0:T(8,128)(2,1)S(1)}, bf16[256,128]{1,0:T(8,128)(2,1)S(1)}, u32[]{:S(2)}, u32[]{:S(2)}) collective-permute-start(bf16[256,128]{1,0:T(8,128)(2,1)S(1)} %get-tuple-element.33), channel_id=1, source_target_pairs={{0,48},{16,224},{32,80},{48,0},{64,112},{80,32},{96,144},{112,64},... | collective-permute-start | bytes 196616 | tf_op jit(solution)/shard_map/ppermute | solution.py:285
  76.9 3.9 %with_next.1 = (bf16[3,256,128]{2,1,0:T(8,128)(2,1)S(1)}, bf16[3,256,128]{2,1,0:T(8,128)(2,1)S(1)}, f32[2,128,512]{2,1,0:T(8,128)S(1)}, bf16[2,128,512]{2,1,0:T(8,128)(2,1)S(1)}) custom-call(bf16[2,128,1280]{2,1,0:T(8,128)(2,1)S(1)} %get-tuple-element.24.x_ref, bf16[2,128,1280]{2,1,0:T(8,128)(2,1)S(1)} %collective-permute-done.3.y_ref, ...), custom_call_target="tpu_custom_call" | custom-call | tf_op jit(solution)/shard_map/with_next/pallas_call | solution.py:297
  80.8 1.9 %collective-permute-start.14 = (bf16[2,128,512]{2,1,0:T(8,128)(2,1)S(1)}, bf16[2,128,512]{2,1,0:T(8,128)(2,1)S(1)}, u32[]{:S(2)}, u32[]{:S(2)}) collective-permute-start(bf16[2,128,512]{2,1,0:T(8,128)(2,1)S(1)} %get-tuple-element.35), channel_id=1, source_target_pairs={{0,8},{8,0},{1,9},{9,1},{2,10},{10,2},{3,11},{11,3},{4,12},{12,4},... | collective-permute-start | bytes 786440 | tf_op jit(solution)/shard_map/ppermute | solution.py:289
  82.7 2.2 %collective-permute-start.7 = (bf16[3,256,128]{2,1,0:T(8,128)(2,1)S(1)}, bf16[3,256,128]{2,1,0:T(8,128)(2,1)S(1)}, u32[]{:S(2)}, u32[]{:S(2)}) collective-permute-start(bf16[3,256,128]{2,1,0:T(8,128)(2,1)S(1)} %get-tuple-element.28), channel_id=1, source_target_pairs={{0,240},{16,0},{32,16},{48,32},{64,48},{80,64},{96,80},{112,96},{1... | collective-permute-start | bytes 589832 | tf_op jit(solution)/shard_map/ppermute | solution.py:280
  84.9 3.7 %collective-permute-start.8 = (bf16[3,256,128]{2,1,0:T(8,128)(2,1)S(1)}, bf16[3,256,128]{2,1,0:T(8,128)(2,1)S(1)}, u32[]{:S(2)}, u32[]{:S(2)}) collective-permute-start(bf16[3,256,128]{2,1,0:T(8,128)(2,1)S(1)} %get-tuple-element.29), channel_id=1, source_target_pairs={{0,16},{16,32},{32,48},{48,64},{64,80},{80,96},{96,112},{112,128},... | collective-permute-start | bytes 589832 | tf_op jit(solution)/shard_map/ppermute | solution.py:280
  88.5 2.8 %collective-permute-start.11 = (bf16[3,256,128]{2,1,0:T(8,128)(2,1)S(1)}, bf16[3,256,128]{2,1,0:T(8,128)(2,1)S(1)}, u32[]{:S(2)}, u32[]{:S(2)}) collective-permute-start(bf16[3,256,128]{2,1,0:T(8,128)(2,1)S(1)} %get-tuple-element.31), channel_id=1, source_target_pairs={{0,224},{16,240},{32,0},{48,16},{64,32},{80,48},{96,64},{112,80},{... | collective-permute-start | bytes 589832 | tf_op jit(solution)/shard_map/ppermute | solution.py:280
  91.4 3.9 %collective-permute-start.12 = (bf16[3,256,128]{2,1,0:T(8,128)(2,1)S(1)}, bf16[3,256,128]{2,1,0:T(8,128)(2,1)S(1)}, u32[]{:S(2)}, u32[]{:S(2)}) collective-permute-start(bf16[3,256,128]{2,1,0:T(8,128)(2,1)S(1)} %get-tuple-element.32), channel_id=1, source_target_pairs={{0,32},{16,48},{32,64},{48,80},{64,96},{80,112},{96,128},{112,144}... | collective-permute-start | bytes 589832 | tf_op jit(solution)/shard_map/ppermute | solution.py:280
  95.3 5.9 %collective-permute-done.11.p2 = bf16[3,256,128]{2,1,0:T(8,128)(2,1)S(1)} collective-permute-done((bf16[3,256,128]{2,1,0:T(8,128)(2,1)S(1)}, bf16[3,256,128]{2,1,0:T(8,128)(2,1)S(1)}, u32[]{:S(2)}, u32[]{:S(2)}) %collective-permute-start.11) | collective-permute-done | bytes 196640 | tf_op jit(solution)/shard_map/ppermute | solution.py:280
  101.3 5.1 %collective-permute-done.12.m2 = bf16[3,256,128]{2,1,0:T(8,128)(2,1)S(1)} collective-permute-done((bf16[3,256,128]{2,1,0:T(8,128)(2,1)S(1)}, bf16[3,256,128]{2,1,0:T(8,128)(2,1)S(1)}, u32[]{:S(2)}, u32[]{:S(2)}) %collective-permute-start.12) | collective-permute-done | bytes 196640 | tf_op jit(solution)/shard_map/ppermute | solution.py:280
  106.4 0.7 sum_near.1
  107.1 4.0 %collective-permute-start.17 = (bf16[128,512]{1,0:T(8,128)(2,1)S(1)}, bf16[128,512]{1,0:T(8,128)(2,1)S(1)}, u32[]{:S(2)}, u32[]{:S(2)}) collective-permute-start(bf16[128,512]{1,0:T(8,128)(2,1)S(1)} %get-tuple-element.40), channel_id=1, source_target_pairs={{0,256},{256,0},{1,257},{257,1},{2,258},{258,2},{3,259},{259,3},{4... | collective-permute-start | bytes 393224 | tf_op jit(solution)/shard_map/ppermute | solution.py:289
  111.1 6.4 %collective-permute-start.15 = (bf16[256,128]{1,0:T(8,128)(2,1)S(1)}, bf16[256,128]{1,0:T(8,128)(2,1)S(1)}, u32[]{:S(2)}, u32[]{:S(2)}) collective-permute-start(bf16[256,128]{1,0:T(8,128)(2,1)S(1)} %get-tuple-element.37), channel_id=1, source_target_pairs={{0,80},{16,96},{32,112},{48,128},{64,144},{80,160},{96,176},{112,1... | collective-permute-start | bytes 196616 | tf_op jit(solution)/shard_map/ppermute | solution.py:280
  117.5 5.5 %collective-permute-start.16 = (bf16[256,128]{1,0:T(8,128)(2,1)S(1)}, bf16[256,128]{1,0:T(8,128)(2,1)S(1)}, u32[]{:S(2)}, u32[]{:S(2)}) collective-permute-start(bf16[256,128]{1,0:T(8,128)(2,1)S(1)} %get-tuple-element.38), channel_id=1, source_target_pairs={{0,176},{16,192},{32,208},{48,224},{64,240},{80,0},{96,16},{112,32... | collective-permute-start | bytes 196616 | tf_op jit(solution)/shard_map/ppermute | solution.py:280
  123.0 1.9 %collective-permute-done.15.plus_ref = bf16[256,128]{1,0:T(8,128)(2,1)S(1)} collective-permute-done((bf16[256,128]{1,0:T(8,128)(2,1)S(1)}, bf16[256,128]{1,0:T(8,128)(2,1)S(1)}, u32[]{:S(2)}, u32[]{:S(2)}) %collective-permute-start.15) | collective-permute-done | bytes 65568 | tf_op jit(solution)/shard_map/ppermute | solution.py:280
  124.9 5.6 %collective-permute-done.16.minus_ref = bf16[256,128]{1,0:T(8,128)(2,1)S(1)} collective-permute-done((bf16[256,128]{1,0:T(8,128)(2,1)S(1)}, bf16[256,128]{1,0:T(8,128)(2,1)S(1)}, u32[]{:S(2)}, u32[]{:S(2)}) %collective-permute-start.16) | collective-permute-done | bytes 65568 | tf_op jit(solution)/shard_map/ppermute | solution.py:280
  131.2 1.2 finish.1
  (21 shorter events, 2.2 us)
Async XLA Ops:
  4.2 9.4 %copy-start.1 = (bf16[128,640]{1,0:T(8,128)(2,1)S(1)}, bf16[128,640]{1,0:T(8,128)(2,1)}, u32[]{:S(2)}) copy-start(bf16[128,640]{1,0:T(8,128)(2,1)} %get-tuple-element.22.q_ref) | copy-start | bytes 491524
  4.2 35.7 %all-to-all-start = ((bf16[16,16,640]{2,1,0:T(8,128)(2,1)}), bf16[16,16,640]{2,1,0:T(8,128)(2,1)S(1)}, u32[]{:S(2)}, u32[]{:S(2)}) async-start(bf16[16,16,640]{2,1,0:T(8,128)(2,1)} %get-tuple-element.23), calls=%async_computation | async-start | bytes 655360 | tf_op jit(solution)/shard_map/all_to_all | solution.py:330
  13.5 26.3 %collective-permute-start.2 = (bf16[128,640]{1,0:T(8,128)(2,1)S(1)}, bf16[128,640]{1,0:T(8,128)(2,1)S(1)}, u32[]{:S(2)}, u32[]{:S(2)}) collective-permute-start(bf16[128,640]{1,0:T(8,128)(2,1)S(1)} %copy-done.1), channel_id=1, source_target_pairs={{0,256},{256,0},{1,257},{257,1},{2,258},{258,2},{3,259},{259,3},{4... | collective-permute-start | bytes 491528 | tf_op jit(solution)/shard_map/ppermute | solution.py:289
  18.3 15.2 %collective-permute-start.1 = (bf16[272,128]{1,0:T(8,128)(2,1)}, bf16[272,128]{1,0:T(8,128)(2,1)S(1)}, u32[]{:S(2)}, u32[]{:S(2)}) collective-permute-start(bf16[272,128]{1,0:T(8,128)(2,1)} %pack_keys.1.own_ref), channel_id=1, source_target_pairs={{0,80},{16,96},{32,112},{48,128},{64,144},{80,160},{96,176},{112,1... | collective-permute-start | bytes 208904 | tf_op jit(solution)/shard_map/ppermute | solution.py:280
  27.0 12.9 %collective-permute-start = (bf16[272,128]{1,0:T(8,128)(2,1)}, bf16[272,128]{1,0:T(8,128)(2,1)S(1)}, u32[]{:S(2)}, u32[]{:S(2)}) collective-permute-start(bf16[272,128]{1,0:T(8,128)(2,1)} %pack_keys.1.own_ref), channel_id=1, source_target_pairs={{0,176},{16,192},{32,208},{48,224},{64,240},{80,0},{96,16},{112,32... | collective-permute-start | bytes 208904 | tf_op jit(solution)/shard_map/ppermute | solution.py:280
  39.8 0.9 copy-start
  41.4 25.0 %collective-permute-start.3 = (bf16[2,128,1280]{2,1,0:T(8,128)(2,1)S(1)}, bf16[2,128,1280]{2,1,0:T(8,128)(2,1)S(1)}, u32[]{:S(2)}, u32[]{:S(2)}) collective-permute-start(bf16[2,128,1280]{2,1,0:T(8,128)(2,1)S(1)} %get-tuple-element.24.x_ref), channel_id=1, source_target_pairs={{0,8},{8,0},{1,9},{9,1},{2,10},{10,2},{3,11},{11,3},{4,12},{12,4},... | collective-permute-start | bytes 1966088 | tf_op jit(solution)/shard_map/ppermute | solution.py:289
  43.3 18.3 %collective-permute-start.6 = (bf16[272,128]{1,0:T(8,128)(2,1)S(1)}, bf16[272,128]{1,0:T(8,128)(2,1)S(1)}, u32[]{:S(2)}, u32[]{:S(2)}) collective-permute-start(bf16[272,128]{1,0:T(8,128)(2,1)S(1)} %get-tuple-element.26), channel_id=1, source_target_pairs={{0,48},{16,224},{32,80},{48,0},{64,112},{80,32},{96,144},{112,64},... | collective-permute-start | bytes 208904 | tf_op jit(solution)/shard_map/ppermute | solution.py:285
  53.8 12.6 %collective-permute-start.5 = (bf16[3,272,128]{2,1,0:T(8,128)(2,1)S(1)}, bf16[3,272,128]{2,1,0:T(8,128)(2,1)S(1)}, u32[]{:S(2)}, u32[]{:S(2)}) collective-permute-start(bf16[3,272,128]{2,1,0:T(8,128)(2,1)S(1)} %get-tuple-element.25.s_ref), channel_id=1, source_target_pairs={{0,240},{16,0},{32,16},{48,32},{64,48},{80,64},{96,80},{112,96},{1... | collective-permute-start | bytes 626696 | tf_op jit(solution)/shard_map/ppermute | solution.py:280
  55.7 10.7 %collective-permute-start.4 = (bf16[3,272,128]{2,1,0:T(8,128)(2,1)S(1)}, bf16[3,272,128]{2,1,0:T(8,128)(2,1)S(1)}, u32[]{:S(2)}, u32[]{:S(2)}) collective-permute-start(bf16[3,272,128]{2,1,0:T(8,128)(2,1)S(1)} %get-tuple-element.25.s_ref), channel_id=1, source_target_pairs={{0,16},{16,32},{32,48},{48,64},{64,80},{80,96},{96,112},{112,128},... | collective-permute-start | bytes 626696 | tf_op jit(solution)/shard_map/ppermute | solution.py:280
  59.6 16.9 %collective-permute-start.10 = (bf16[3,272,128]{2,1,0:T(8,128)(2,1)S(1)}, bf16[3,272,128]{2,1,0:T(8,128)(2,1)S(1)}, u32[]{:S(2)}, u32[]{:S(2)}) collective-permute-start(bf16[3,272,128]{2,1,0:T(8,128)(2,1)S(1)} %get-tuple-element.25.s_ref), channel_id=1, source_target_pairs={{0,224},{16,240},{32,0},{48,16},{64,32},{80,48},{96,64},{112,80},{... | collective-permute-start | bytes 626696 | tf_op jit(solution)/shard_map/ppermute | solution.py:280
  61.6 15.3 %collective-permute-start.9 = (bf16[3,272,128]{2,1,0:T(8,128)(2,1)S(1)}, bf16[3,272,128]{2,1,0:T(8,128)(2,1)S(1)}, u32[]{:S(2)}, u32[]{:S(2)}) collective-permute-start(bf16[3,272,128]{2,1,0:T(8,128)(2,1)S(1)} %get-tuple-element.25.s_ref), channel_id=1, source_target_pairs={{0,32},{16,48},{32,64},{48,80},{64,96},{80,112},{96,128},{112,144}... | collective-permute-start | bytes 626696 | tf_op jit(solution)/shard_map/ppermute | solution.py:280
  71.9 19.5 %collective-permute-start.13 = (bf16[256,128]{1,0:T(8,128)(2,1)S(1)}, bf16[256,128]{1,0:T(8,128)(2,1)S(1)}, u32[]{:S(2)}, u32[]{:S(2)}) collective-permute-start(bf16[256,128]{1,0:T(8,128)(2,1)S(1)} %get-tuple-element.33), channel_id=1, source_target_pairs={{0,48},{16,224},{32,80},{48,0},{64,112},{80,32},{96,144},{112,64},... | collective-permute-start | bytes 196616 | tf_op jit(solution)/shard_map/ppermute | solution.py:285
  80.8 25.7 %collective-permute-start.14 = (bf16[2,128,512]{2,1,0:T(8,128)(2,1)S(1)}, bf16[2,128,512]{2,1,0:T(8,128)(2,1)S(1)}, u32[]{:S(2)}, u32[]{:S(2)}) collective-permute-start(bf16[2,128,512]{2,1,0:T(8,128)(2,1)S(1)} %get-tuple-element.35), channel_id=1, source_target_pairs={{0,8},{8,0},{1,9},{9,1},{2,10},{10,2},{3,11},{11,3},{4,12},{12,4},... | collective-permute-start | bytes 786440 | tf_op jit(solution)/shard_map/ppermute | solution.py:289
  82.7 12.6 %collective-permute-start.7 = (bf16[3,256,128]{2,1,0:T(8,128)(2,1)S(1)}, bf16[3,256,128]{2,1,0:T(8,128)(2,1)S(1)}, u32[]{:S(2)}, u32[]{:S(2)}) collective-permute-start(bf16[3,256,128]{2,1,0:T(8,128)(2,1)S(1)} %get-tuple-element.28), channel_id=1, source_target_pairs={{0,240},{16,0},{32,16},{48,32},{64,48},{80,64},{96,80},{112,96},{1... | collective-permute-start | bytes 589832 | tf_op jit(solution)/shard_map/ppermute | solution.py:280
  84.9 10.4 %collective-permute-start.8 = (bf16[3,256,128]{2,1,0:T(8,128)(2,1)S(1)}, bf16[3,256,128]{2,1,0:T(8,128)(2,1)S(1)}, u32[]{:S(2)}, u32[]{:S(2)}) collective-permute-start(bf16[3,256,128]{2,1,0:T(8,128)(2,1)S(1)} %get-tuple-element.29), channel_id=1, source_target_pairs={{0,16},{16,32},{32,48},{48,64},{64,80},{80,96},{96,112},{112,128},... | collective-permute-start | bytes 589832 | tf_op jit(solution)/shard_map/ppermute | solution.py:280
  88.5 12.7 %collective-permute-start.11 = (bf16[3,256,128]{2,1,0:T(8,128)(2,1)S(1)}, bf16[3,256,128]{2,1,0:T(8,128)(2,1)S(1)}, u32[]{:S(2)}, u32[]{:S(2)}) collective-permute-start(bf16[3,256,128]{2,1,0:T(8,128)(2,1)S(1)} %get-tuple-element.31), channel_id=1, source_target_pairs={{0,224},{16,240},{32,0},{48,16},{64,32},{80,48},{96,64},{112,80},{... | collective-permute-start | bytes 589832 | tf_op jit(solution)/shard_map/ppermute | solution.py:280
  91.4 15.0 %collective-permute-start.12 = (bf16[3,256,128]{2,1,0:T(8,128)(2,1)S(1)}, bf16[3,256,128]{2,1,0:T(8,128)(2,1)S(1)}, u32[]{:S(2)}, u32[]{:S(2)}) collective-permute-start(bf16[3,256,128]{2,1,0:T(8,128)(2,1)S(1)} %get-tuple-element.32), channel_id=1, source_target_pairs={{0,32},{16,48},{32,64},{48,80},{64,96},{80,112},{96,128},{112,144}... | collective-permute-start | bytes 589832 | tf_op jit(solution)/shard_map/ppermute | solution.py:280
  107.1 23.4 %collective-permute-start.17 = (bf16[128,512]{1,0:T(8,128)(2,1)S(1)}, bf16[128,512]{1,0:T(8,128)(2,1)S(1)}, u32[]{:S(2)}, u32[]{:S(2)}) collective-permute-start(bf16[128,512]{1,0:T(8,128)(2,1)S(1)} %get-tuple-element.40), channel_id=1, source_target_pairs={{0,256},{256,0},{1,257},{257,1},{2,258},{258,2},{3,259},{259,3},{4... | collective-permute-start | bytes 393224 | tf_op jit(solution)/shard_map/ppermute | solution.py:289
  111.1 13.8 %collective-permute-start.15 = (bf16[256,128]{1,0:T(8,128)(2,1)S(1)}, bf16[256,128]{1,0:T(8,128)(2,1)S(1)}, u32[]{:S(2)}, u32[]{:S(2)}) collective-permute-start(bf16[256,128]{1,0:T(8,128)(2,1)S(1)} %get-tuple-element.37), channel_id=1, source_target_pairs={{0,80},{16,96},{32,112},{48,128},{64,144},{80,160},{96,176},{112,1... | collective-permute-start | bytes 196616 | tf_op jit(solution)/shard_map/ppermute | solution.py:280
  117.5 13.0 %collective-permute-start.16 = (bf16[256,128]{1,0:T(8,128)(2,1)S(1)}, bf16[256,128]{1,0:T(8,128)(2,1)S(1)}, u32[]{:S(2)}, u32[]{:S(2)}) collective-permute-start(bf16[256,128]{1,0:T(8,128)(2,1)S(1)} %get-tuple-element.38), channel_id=1, source_target_pairs={{0,176},{16,192},{32,208},{48,224},{64,240},{80,0},{96,16},{112,32... | collective-permute-start | bytes 196616 | tf_op jit(solution)/shard_map/ppermute | solution.py:280
  130.5 0.7 copy-start.2

commit v5 on v4

--- a/solution.py
+++ b/solution.py
@@ -211,10 +211,13 @@
     start = pl.multiple_of(jnp.where(swapped, BLK, 0), BLK)
     lanes = lax.broadcasted_iota(jnp.int32, (BLK, HEAD), 1)
     c = jnp.minimum(pos[0], pos[BLK]) // BLK
+    lse = jnp.concatenate([lse_ref[...], jnp.zeros((HEAD - GROUP, TOK), F32)])
+    turned = jnp.transpose(lse)
+    turned = jnp.where(swapped, jnp.concatenate([turned[BLK:], turned[:BLK]]), turned)
     for i in range(2):
         rows = pl.ds(start if i == 0 else pl.multiple_of(BLK - start, BLK), BLK)
         q_out[i * BLK : (i + 1) * BLK, :wide] = q_ref[rows, :]
-        lse = lse_ref[rows, :]
+        lse = turned[i * BLK : (i + 1) * BLK, :]
         tail = in_terms([lse[:, h : h + 1] for h in range(GROUP)], lanes)
         tail = jnp.where(lanes == 24, c.astype(F32), tail)
         tail = jnp.where(lanes == 25, swapped.astype(F32), tail)
@@ -234,11 +237,10 @@
             g_out[twin * n_heads + d, :, wide:] = tail
 
 
-def join(info, own_ref, plus_ref, minus_ref, q_ref, qx_ref, grad_ref, s_out, e_out, x_out):
+def join(info, own_ref, u_ref, w_ref, q_ref, qx_ref, grad_ref, s_out, x_out):
     s_out[0] = own_ref[...]
-    s_out[1] = plus_ref[...]
-    s_out[2] = minus_ref[...]
-    e_out[...] = jnp.where(info[1] == 0, minus_ref[...], plus_ref[...])
+    s_out[1] = u_ref[...]
+    s_out[2] = w_ref[...]
     wide = (GROUP + 1) * HEAD
     x_out[0, :, :wide] = q_ref[...]
     x_out[1, :, :wide] = qx_ref[...]
@@ -246,24 +248,27 @@
     x_out[1, :, wide:] = grad_ref[1 - info[0]]
 
 
-def sum_near(info, own_ref, p1, m1, p2, m2, e_ref, dq_ref, core_ref, *outs):
-    own_out, plus_out, minus_out, dq_out, dqx_out = outs
-    extra = e_ref[...].astype(F32)
-    even = info[1] == 0
-    for i, out in enumerate((own_out, plus_out, minus_out)):
-        total = own_ref[i]
-        for ref in (p1, m1, p2, m2):
-            total = total + ref[i].astype(F32)
-        if i:
-            total = total + jnp.where(even == (i == 2), extra, 0.0)
-        out[...] = total.astype(out.dtype)
+def sum_first(own_ref, a_ref, b_ref, c_ref, d_ref, own_out, c_out, d_out):
+    own_out[...] = own_ref[...] + a_ref[...].astype(F32) + b_ref[...].astype(F32)
+    c_out[...] = c_ref[...]
+    d_out[...] = d_ref[...]
+
+
+def sum_near(own_ref, c_ref, d_ref, e_ref, own_out, u_out, w_out):
+    total = own_ref[...] + c_ref[...].astype(F32) + d_ref[...].astype(F32)
+    own_out[...] = total[0]
+    u_out[...] = total[1].astype(BF16)
+    w_out[...] = (total[2] + e_ref[...].astype(F32)).astype(BF16)
+
+
+def sum_cores(dq_ref, core_ref, dq_out, dqx_out):
     dq_out[...] = dq_ref[0] + core_ref[0].astype(F32)
     dqx_out[...] = (dq_ref[1] + core_ref[1].astype(F32)).astype(BF16)
 
 
-def finish(pos, own_ref, plus_ref, minus_ref, dq_ref, dqx_ref, q_out, k_out, v_out):
-    start = pl.multiple_of(jnp.where(pos[0] > pos[BLK], BLK, 0), BLK)
-    total = own_ref[...] + plus_ref[...].astype(F32) + minus_ref[...].astype(F32)
+def finish(info, own_ref, u_ref, w_ref, dq_ref, dqx_ref, q_out, k_out, v_out):
+    start = pl.multiple_of(info[1] * BLK, BLK)
+    total = own_ref[...] + u_ref[...].astype(F32) + w_ref[...].astype(F32)
     dq = dq_ref[...] + dqx_ref[...].astype(F32)
     for i in range(2):
         rows = pl.ds(start if i == 0 else pl.multiple_of(BLK - start, BLK), BLK)
@@ -275,14 +280,10 @@
 HEADS = ("xl", "y")
 
 
-def shifted(x, by):
+def by_parity(x, distance):
     n = lax.axis_size("z")
-    return lax.ppermute(x, "z", [(i, (i + by) % n) for i in range(n)])
-
-
-def by_parity(x, even):
-    n = lax.axis_size("z")
-    return lax.ppermute(x, "z", [(i, (i + (even if i % 2 == 0 else -even)) % n) for i in range(n)])
+    to = [(i + (distance if i % 2 == 0 else -distance)) % n for i in range(n)]
+    return lax.ppermute(x, "z", list(enumerate(to)))
 
 
 def swapped_with(x, axis):
@@ -312,28 +313,29 @@
 def shards(queries, keys, values, outputs, out_grad, lse, positions):
     n_heads = lax.axis_size(HEADS)
     wide = (GROUP + 1) * HEAD
-    info = jnp.stack([lax.axis_index("xh"), lax.axis_index("z") % 2]).astype(jnp.int32)
+    swapped = positions[0] > positions[BLK]
+    info = jnp.stack([lax.axis_index("xh"), swapped]).astype(jnp.int32)
 
     def like(shape, dtype=BF16):
         return jax.ShapeDtypeStruct(shape, dtype)
 
     packed, block = (4 * BLK + 16, HEAD), (4 * BLK, HEAD)
     own = local_call(pack_keys, like(packed), 56, stream_in=True)(positions, keys, values)
-    plus, minus = shifted(own, -5), shifted(own, 5)
+    u, w = by_parity(own, 5), by_parity(own, -5)
 
     own_q, send = local_call(
         pack_queries,
         (like((TOK, wide)), like((2 * n_heads, TOK // n_heads, wide))),
         56,
         stream_in=True,
-    )(positions, queries, lse, outputs, out_grad)
+    )(positions, queries, lse.T, outputs, out_grad)
     grad = lax.all_to_all(send, ("xh",) + HEADS, split_axis=0, concat_axis=0, tiled=True)
     other_q = swapped_with(own_q, "xh")
-    s_set, e_one, x = local_call(
-        join, (like((NEAR,) + packed), like(packed), like((2, TOK, 2 * wide))), 8, stream_in=True
-    )(info, own, plus, minus, own_q, other_q, grad.reshape(2, TOK, wide))
-    p1, m1, p2, m2 = [shifted(s_set, by) for by in (1, -1, 2, -2)]
-    e_one = by_parity(e_one, 3)
+    s_set, x = local_call(
+        join, (like((NEAR,) + packed), like((2, TOK, 2 * wide))), 8, stream_in=True
+    )(info, own, u, w, own_q, other_q, grad.reshape(2, TOK, wide))
+    p1, m1, p2, m2 = [by_parity(s_set, by) for by in (1, -1, 2, -2)]
+    e_one = by_parity(w, 3)
     y = swapped_with(x, "core")
 
     near, dq_shape = (NEAR,) + block, (2, TOK, GROUP * HEAD)
@@ -374,28 +376,24 @@
         ],
     )
 
-    p1_in, m1_in, e_in = shifted(p1_g, -1), shifted(m1_g, 1), by_parity(e_g, 3)
-    p2_in, m2_in = shifted(p2_g, -2), shifted(m2_g, 2)
+    p1_in, m1_in, e_in = by_parity(p1_g, 1), by_parity(m1_g, -1), by_parity(e_g, 3)
+    own_g, p2_g, m2_g = local_call(sum_first, (like(near, F32), like(near), like(near)), 8)(
+        own_g, p1_in, m1_in, p2_g, m2_g
+    )
+    p2_in, m2_in = by_parity(p2_g, -2), by_parity(m2_g, 2)
     dq_core = swapped_with(dq_core, "core")
-    own_g, plus_g, minus_g, dq, dqx = local_call(
-        sum_near,
-        (
-            like(block, F32),
-            like(block),
-            like(block),
-            like(dq_shape[1:], F32),
-            like(dq_shape[1:]),
-        ),
-        8,
-    )(info, own_g, p1_in, m1_in, p2_in, m2_in, e_in, dq, dq_core)
-    plus_g, minus_g = shifted(plus_g, 5), shifted(minus_g, -5)
+    dq, dqx = local_call(sum_cores, (like(dq_shape[1:], F32), like(dq_shape[1:])), 8)(dq, dq_core)
     dqx = swapped_with(dqx, "xh")
+    own_g, u_g, w_g = local_call(sum_near, (like(block, F32), like(block), like(block)), 8)(
+        own_g, p2_in, m2_in, e_in
+    )
+    u_g, w_g = by_parity(u_g, 5), by_parity(w_g, -5)
     return local_call(
         finish,
         (like(queries.shape), like(keys.shape), like(values.shape)),
         8,
         stream_out=True,
-    )(positions, own_g, plus_g, minus_g, dq, dqx)
+    )(info, own_g, u_g, w_g, dq, dqx)
 
 
 def solution(mesh):

time: 133 us -> 120 us (0.902)
  waiting for transfers between devices: 25.8 us -> 16.5 us
  starting transfers between devices: 87.1 us -> 83.8 us
  local copies, waits for them, and re-layouts: 2.96 us -> 1.47 us
    ppermute x14, waiting for transfers between devices: 25.8 us -> 16.2 us  [by_parity(): return lax.ppermute(x, 'z', list(enumerate(to)))]
    ppermute x14, starting transfers between devices: 66.6 us -> 63.8 us  [by_parity(): return lax.ppermute(x, 'z', list(enumerate(to)))]
    unnamed x7 -> x6, local copies, waits for them, and re-layouts: 2.96 us -> 0.89 us
    pallas_call x7 -> x9, Pallas kernels: 15.5 us -> 15.1 us  [call(): pl.pallas_call(body, out_shape=out_shape, in_specs=[smem if a.dtype == jn...]
  transfers between devices with their start and end apart: 19 -> 19, of which waited for: 7 -> 6; matrix products, arithmetic and copies ran while one was open for 0% -> 1% of each run, Pallas kernels for 8% -> 9%
where the time goes in v5:
time: 120 us; the launch traced here: 119 us
  starting transfers between devices  83.8 us (70%)
  waiting for transfers between devices  16.5 us (14%)
  Pallas kernels  15.1 us (13%)
  between operations  2.2 us (2%)
  local copies, waits for them, and re-layouts  1.47 us (1%)
    ppermute x14, starting transfers between devices, by_parity(): return lax.ppermute(x, 'z', list(enumerate(to)))  63.8 us
    ppermute x14, waiting for transfers between devices, by_parity(): return lax.ppermute(x, 'z', list(enumerate(to)))  16.2 us
    pallas_call x9, Pallas kernels, call(): pl.pallas_call(body, out_shape=out_shape, in_specs=[smem if a.dtype == jn...  15.1 us
    ppermute x4, starting transfers between devices, swapped_with(): return lax.ppermute(x, axis, [(0, 1), (1, 0)])  10.6 us
    all_to_all x1, starting transfers between devices, shards(): lax.all_to_all(send, ('xh',) + HEADS, split_axis=0, concat_axis=0, tiled=...  9.39 us
  transfers between devices with their start and end apart: 19, of which 6 were waited for; matrix products, arithmetic and copies ran while one was open for 1% of the time, Pallas kernels for 9%

profile of v5, /device:TPU:6, one launch (start us, length us, event | category | flops | bytes accessed | tf_op | source)
XLA Modules:
  0.0 119.1 jit_solution(9238258442323680766)
XLA Ops:
  0.6 2.2 %pack_queries.1 = (bf16[128,640]{1,0:T(8,128)(2,1)}, bf16[16,16,640]{2,1,0:T(8,128)(2,1)}) custom-call(s32[128]{0:T(128)} %pos.3, bf16[128,512]{1,0:T(8,128)(2,1)} %q_ref.1, f32[4,128]{1,0:T(4,128)} %bitcast.4, bf16[16,4096]{1,0:T(8,128)(2,1)} %o_ref.1, bf16[16,4096]{1,0:T(8,128)(2,1)} %g_ref.1), custom_call_target="tpu_custom_call" | custom-call | tf_op jit(solution)/shard_map/pack_queries/pallas_call | solution.py:298
  2.8 9.4 %all-to-all-start = ((bf16[16,16,640]{2,1,0:T(8,128)(2,1)}), bf16[16,16,640]{2,1,0:T(8,128)(2,1)S(1)}, u32[]{:S(2)}, u32[]{:S(2)}) async-start(bf16[16,16,640]{2,1,0:T(8,128)(2,1)} %get-tuple-element.25), calls=%async_computation | async-start | bytes 655360 | tf_op jit(solution)/shard_map/all_to_all | solution.py:332
  12.2 1.4 %pack_keys.1.own_ref = bf16[272,128]{1,0:T(8,128)(2,1)} custom-call(s32[128]{0:T(128)} %pos.3, bf16[128,128]{1,0:T(8,128)(2,1)} %k_ref.1, bf16[128,128]{1,0:T(8,128)(2,1)} %v_ref.1), custom_call_target="tpu_custom_call" | custom-call | tf_op jit(solution)/shard_map/pack_keys/pallas_call | solution.py:298
  13.7 12.7 %collective-permute-start.1 = (bf16[272,128]{1,0:T(8,128)(2,1)}, bf16[272,128]{1,0:T(8,128)(2,1)S(1)}, u32[]{:S(2)}, u32[]{:S(2)}) collective-permute-start(bf16[272,128]{1,0:T(8,128)(2,1)} %pack_keys.1.own_ref), channel_id=1, source_target_pairs={{0,176},{16,96},{32,208},{48,128},{64,240},{80,160},{96,16},{112,1... | collective-permute-start | bytes 208904 | tf_op jit(solution)/shard_map/ppermute | solution.py:286
  26.3 4.7 %collective-permute-start = (bf16[272,128]{1,0:T(8,128)(2,1)}, bf16[272,128]{1,0:T(8,128)(2,1)S(1)}, u32[]{:S(2)}, u32[]{:S(2)}) collective-permute-start(bf16[272,128]{1,0:T(8,128)(2,1)} %pack_keys.1.own_ref), channel_id=1, source_target_pairs={{0,80},{16,192},{32,112},{48,224},{64,144},{80,0},{96,176},{112,32... | collective-permute-start | bytes 208904 | tf_op jit(solution)/shard_map/ppermute | solution.py:286
  31.1 3.4 %collective-permute-start.2 = (bf16[128,640]{1,0:T(8,128)(2,1)S(1)}, bf16[128,640]{1,0:T(8,128)(2,1)S(1)}, u32[]{:S(2)}, u32[]{:S(2)}) collective-permute-start(bf16[128,640]{1,0:T(8,128)(2,1)S(1)} %copy-done.1), channel_id=1, source_target_pairs={{0,256},{256,0},{1,257},{257,1},{2,258},{258,2},{3,259},{259,3},{4... | collective-permute-start | bytes 491528 | tf_op jit(solution)/shard_map/ppermute | solution.py:290
  34.5 0.6 fusion
  36.4 3.1 %collective-permute-done.u_ref = bf16[272,128]{1,0:T(8,128)(2,1)S(1)} collective-permute-done((bf16[272,128]{1,0:T(8,128)(2,1)}, bf16[272,128]{1,0:T(8,128)(2,1)S(1)}, u32[]{:S(2)}, u32[]{:S(2)}) %collective-permute-start) | collective-permute-done | bytes 69664 | tf_op jit(solution)/shard_map/ppermute | solution.py:286
  39.5 0.3 collective-permute-done.2.qx_ref
  39.8 0.9 copy-done
  40.7 0.6 join.1
  41.3 1.9 %collective-permute-start.3 = (bf16[2,128,1280]{2,1,0:T(8,128)(2,1)S(1)}, bf16[2,128,1280]{2,1,0:T(8,128)(2,1)S(1)}, u32[]{:S(2)}, u32[]{:S(2)}) collective-permute-start(bf16[2,128,1280]{2,1,0:T(8,128)(2,1)S(1)} %get-tuple-element.26.x_ref), channel_id=1, source_target_pairs={{0,8},{8,0},{1,9},{9,1},{2,10},{10,2},{3,11},{11,3},{4,12},{12,4},... | collective-permute-start | bytes 1966088 | tf_op jit(solution)/shard_map/ppermute | solution.py:290
  43.2 3.8 %collective-permute-start.6 = (bf16[272,128]{1,0:T(8,128)(2,1)S(1)}, bf16[272,128]{1,0:T(8,128)(2,1)S(1)}, u32[]{:S(2)}, u32[]{:S(2)}) collective-permute-start(bf16[272,128]{1,0:T(8,128)(2,1)S(1)} %collective-permute-done.1.w_ref), channel_id=1, source_target_pairs={{0,48},{16,224},{32,80},{48,0},{64,112},{80,32},{96,144},{112,64},... | collective-permute-start | bytes 208904 | tf_op jit(solution)/shard_map/ppermute | solution.py:286
  47.0 1.9 %collective-permute-start.5 = (bf16[3,272,128]{2,1,0:T(8,128)(2,1)S(1)}, bf16[3,272,128]{2,1,0:T(8,128)(2,1)S(1)}, u32[]{:S(2)}, u32[]{:S(2)}) collective-permute-start(bf16[3,272,128]{2,1,0:T(8,128)(2,1)S(1)} %get-tuple-element.27.s_ref), channel_id=1, source_target_pairs={{0,240},{16,32},{32,16},{48,64},{64,48},{80,96},{96,80},{112,128},... | collective-permute-start | bytes 626696 | tf_op jit(solution)/shard_map/ppermute | solution.py:286
  49.0 5.1 %collective-permute-start.4 = (bf16[3,272,128]{2,1,0:T(8,128)(2,1)S(1)}, bf16[3,272,128]{2,1,0:T(8,128)(2,1)S(1)}, u32[]{:S(2)}, u32[]{:S(2)}) collective-permute-start(bf16[3,272,128]{2,1,0:T(8,128)(2,1)S(1)} %get-tuple-element.27.s_ref), channel_id=1, source_target_pairs={{0,16},{16,0},{32,48},{48,32},{64,80},{80,64},{96,112},{112,96},{1... | collective-permute-start | bytes 626696 | tf_op jit(solution)/shard_map/ppermute | solution.py:286
  54.1 3.4 %collective-permute-start.10 = (bf16[3,272,128]{2,1,0:T(8,128)(2,1)S(1)}, bf16[3,272,128]{2,1,0:T(8,128)(2,1)S(1)}, u32[]{:S(2)}, u32[]{:S(2)}) collective-permute-start(bf16[3,272,128]{2,1,0:T(8,128)(2,1)S(1)} %get-tuple-element.27.s_ref), channel_id=1, source_target_pairs={{0,224},{16,48},{32,0},{48,80},{64,32},{80,112},{96,64},{112,144},... | collective-permute-start | bytes 626696 | tf_op jit(solution)/shard_map/ppermute | solution.py:286
  57.5 3.4 %collective-permute-start.9 = (bf16[3,272,128]{2,1,0:T(8,128)(2,1)S(1)}, bf16[3,272,128]{2,1,0:T(8,128)(2,1)S(1)}, u32[]{:S(2)}, u32[]{:S(2)}) collective-permute-start(bf16[3,272,128]{2,1,0:T(8,128)(2,1)S(1)} %get-tuple-element.27.s_ref), channel_id=1, source_target_pairs={{0,32},{16,240},{32,64},{48,16},{64,96},{80,48},{96,128},{112,80},... | collective-permute-start | bytes 626696 | tf_op jit(solution)/shard_map/ppermute | solution.py:286
  60.9 3.0 %collective-permute-done.4.p_ref = bf16[3,272,128]{2,1,0:T(8,128)(2,1)S(1)} collective-permute-done((bf16[3,272,128]{2,1,0:T(8,128)(2,1)S(1)}, bf16[3,272,128]{2,1,0:T(8,128)(2,1)S(1)}, u32[]{:S(2)}, u32[]{:S(2)}) %collective-permute-start.4) | collective-permute-done | bytes 208928 | tf_op jit(solution)/shard_map/ppermute | solution.py:286
  63.9 5.5 %with_nearest.1 = (f32[3,256,128]{2,1,0:T(8,128)S(1)}, bf16[3,256,128]{2,1,0:T(8,128)(2,1)S(1)}, bf16[3,256,128]{2,1,0:T(8,128)(2,1)S(1)}, bf16[256,128]{1,0:T(8,128)(2,1)S(1)}, f32[4,128,512]{2,1,0:T(8,128)S(1)}) custom-call(bf16[2,128,1280]{2,1,0:T(8,128)(2,1)S(1)} %get-tuple-element.26.x_ref, bf16[2,128,1280]{2,1,0:T(8,128)(2,1)S(1)} %collective-permute-done.3.y_ref, ...), custom_call_target="tpu_custom_call" | custom-call | tf_op jit(solution)/shard_map/with_nearest/pallas_call | solution.py:298
  69.4 3.9 %collective-permute-start.7 = (bf16[3,256,128]{2,1,0:T(8,128)(2,1)S(1)}, bf16[3,256,128]{2,1,0:T(8,128)(2,1)S(1)}, u32[]{:S(2)}, u32[]{:S(2)}) collective-permute-start(bf16[3,256,128]{2,1,0:T(8,128)(2,1)S(1)} %get-tuple-element.29), channel_id=1, source_target_pairs={{0,16},{16,0},{32,48},{48,32},{64,80},{80,64},{96,112},{112,96},{1... | collective-permute-start | bytes 589832 | tf_op jit(solution)/shard_map/ppermute | solution.py:286
  73.3 2.7 %collective-permute-start.8 = (bf16[3,256,128]{2,1,0:T(8,128)(2,1)S(1)}, bf16[3,256,128]{2,1,0:T(8,128)(2,1)S(1)}, u32[]{:S(2)}, u32[]{:S(2)}) collective-permute-start(bf16[3,256,128]{2,1,0:T(8,128)(2,1)S(1)} %get-tuple-element.30), channel_id=1, source_target_pairs={{0,240},{16,32},{32,16},{48,64},{64,48},{80,96},{96,80},{112,128},... | collective-permute-start | bytes 589832 | tf_op jit(solution)/shard_map/ppermute | solution.py:286
  76.0 3.9 %with_next.1 = (bf16[3,256,128]{2,1,0:T(8,128)(2,1)S(1)}, bf16[3,256,128]{2,1,0:T(8,128)(2,1)S(1)}, f32[2,128,512]{2,1,0:T(8,128)S(1)}, bf16[2,128,512]{2,1,0:T(8,128)(2,1)S(1)}) custom-call(bf16[2,128,1280]{2,1,0:T(8,128)(2,1)S(1)} %get-tuple-element.26.x_ref, bf16[2,128,1280]{2,1,0:T(8,128)(2,1)S(1)} %collective-permute-done.3.y_ref, ...), custom_call_target="tpu_custom_call" | custom-call | tf_op jit(solution)/shard_map/with_next/pallas_call | solution.py:298
  79.9 1.9 %collective-permute-start.16 = (bf16[2,128,512]{2,1,0:T(8,128)(2,1)S(1)}, bf16[2,128,512]{2,1,0:T(8,128)(2,1)S(1)}, u32[]{:S(2)}, u32[]{:S(2)}) collective-permute-start(bf16[2,128,512]{2,1,0:T(8,128)(2,1)S(1)} %get-tuple-element.42), channel_id=1, source_target_pairs={{0,8},{8,0},{1,9},{9,1},{2,10},{10,2},{3,11},{11,3},{4,12},{12,4},... | collective-permute-start | bytes 786440 | tf_op jit(solution)/shard_map/ppermute | solution.py:290
  82.2 3.1 %collective-permute-start.11 = (bf16[3,256,128]{2,1,0:T(8,128)(2,1)S(1)}, bf16[3,256,128]{2,1,0:T(8,128)(2,1)S(1)}, u32[]{:S(2)}, u32[]{:S(2)}) collective-permute-start(bf16[3,256,128]{2,1,0:T(8,128)(2,1)S(1)} %get-tuple-element.35), channel_id=1, source_target_pairs={{0,224},{16,48},{32,0},{48,80},{64,32},{80,112},{96,64},{112,144},... | collective-permute-start | bytes 589832 | tf_op jit(solution)/shard_map/ppermute | solution.py:286
  85.3 3.6 %collective-permute-start.12 = (bf16[3,256,128]{2,1,0:T(8,128)(2,1)S(1)}, bf16[3,256,128]{2,1,0:T(8,128)(2,1)S(1)}, u32[]{:S(2)}, u32[]{:S(2)}) collective-permute-start(bf16[3,256,128]{2,1,0:T(8,128)(2,1)S(1)} %get-tuple-element.36), channel_id=1, source_target_pairs={{0,32},{16,240},{32,64},{48,16},{64,96},{80,48},{96,128},{112,80},... | collective-permute-start | bytes 589832 | tf_op jit(solution)/shard_map/ppermute | solution.py:286
  88.9 3.8 %collective-permute-start.13 = (bf16[256,128]{1,0:T(8,128)(2,1)S(1)}, bf16[256,128]{1,0:T(8,128)(2,1)S(1)}, u32[]{:S(2)}, u32[]{:S(2)}) collective-permute-start(bf16[256,128]{1,0:T(8,128)(2,1)S(1)} %get-tuple-element.37), channel_id=1, source_target_pairs={{0,48},{16,224},{32,80},{48,0},{64,112},{80,32},{96,144},{112,64},... | collective-permute-start | bytes 196616 | tf_op jit(solution)/shard_map/ppermute | solution.py:286
  92.8 3.4 %collective-permute-start.17 = (bf16[128,512]{1,0:T(8,128)(2,1)S(1)}, bf16[128,512]{1,0:T(8,128)(2,1)S(1)}, u32[]{:S(2)}, u32[]{:S(2)}) collective-permute-start(bf16[128,512]{1,0:T(8,128)(2,1)S(1)} %get-tuple-element.44), channel_id=1, source_target_pairs={{0,256},{256,0},{1,257},{257,1},{2,258},{258,2},{3,259},{259,3},{4... | collective-permute-start | bytes 393224 | tf_op jit(solution)/shard_map/ppermute | solution.py:290
  96.2 2.9 %collective-permute-done.13.e_ref = bf16[256,128]{1,0:T(8,128)(2,1)S(1)} collective-permute-done((bf16[256,128]{1,0:T(8,128)(2,1)S(1)}, bf16[256,128]{1,0:T(8,128)(2,1)S(1)}, u32[]{:S(2)}, u32[]{:S(2)}) %collective-permute-start.13) | collective-permute-done | bytes 65568 | tf_op jit(solution)/shard_map/ppermute | solution.py:286
  99.1 5.2 %collective-permute-start.14 = (bf16[256,128]{1,0:T(8,128)(2,1)S(1)}, bf16[256,128]{1,0:T(8,128)(2,1)S(1)}, u32[]{:S(2)}, u32[]{:S(2)}) collective-permute-start(bf16[256,128]{1,0:T(8,128)(2,1)S(1)} %get-tuple-element.39), channel_id=1, source_target_pairs={{0,80},{16,192},{32,112},{48,224},{64,144},{80,0},{96,176},{112,32... | collective-permute-start | bytes 196616 | tf_op jit(solution)/shard_map/ppermute | solution.py:286
  104.4 6.5 %collective-permute-start.15 = (bf16[256,128]{1,0:T(8,128)(2,1)S(1)}, bf16[256,128]{1,0:T(8,128)(2,1)S(1)}, u32[]{:S(2)}, u32[]{:S(2)}) collective-permute-start(bf16[256,128]{1,0:T(8,128)(2,1)S(1)} %get-tuple-element.40), channel_id=1, source_target_pairs={{0,176},{16,96},{32,208},{48,128},{64,240},{80,160},{96,16},{112,1... | collective-permute-start | bytes 196616 | tf_op jit(solution)/shard_map/ppermute | solution.py:286
  110.9 7.0 %collective-permute-done.15.w_ref = bf16[256,128]{1,0:T(8,128)(2,1)S(1)} collective-permute-done((bf16[256,128]{1,0:T(8,128)(2,1)S(1)}, bf16[256,128]{1,0:T(8,128)(2,1)S(1)}, u32[]{:S(2)}, u32[]{:S(2)}) %collective-permute-start.15) | collective-permute-done | bytes 65568 | tf_op jit(solution)/shard_map/ppermute | solution.py:286
  117.9 1.2 %finish.1 = (bf16[128,512]{1,0:T(8,128)(2,1)}, bf16[128,128]{1,0:T(8,128)(2,1)}, bf16[128,128]{1,0:T(8,128)(2,1)}) custom-call(s32[2]{0:T(128)S(1)} %pad_add_fusion.info, f32[256,128]{1,0:T(8,128)S(1)} %get-tuple-element.38.own_ref, bf16[256,128]{1,0:T(8,128)(2,1)S(1)} %collective-permute-done.14.u_ref, bf16[256,128]{1,0:T(8,128)(2,1)S(1)} %collective-permute-done.15.w_ref, ...), custom_call_target="tpu_custom_call" | custom-call | tf_op jit(solution)/shard_map/finish/pallas_call | solution.py:298
  (23 shorter events, 0.6 us)
Async XLA Ops:
  2.8 28.2 %copy-start.1 = (bf16[128,640]{1,0:T(8,128)(2,1)S(1)}, bf16[128,640]{1,0:T(8,128)(2,1)}, u32[]{:S(2)}) copy-start(bf16[128,640]{1,0:T(8,128)(2,1)} %get-tuple-element.24.q_ref) | copy-start | bytes 491524
  2.8 37.0 %all-to-all-start = ((bf16[16,16,640]{2,1,0:T(8,128)(2,1)}), bf16[16,16,640]{2,1,0:T(8,128)(2,1)S(1)}, u32[]{:S(2)}, u32[]{:S(2)}) async-start(bf16[16,16,640]{2,1,0:T(8,128)(2,1)} %get-tuple-element.25), calls=%async_computation | async-start | bytes 655360 | tf_op jit(solution)/shard_map/all_to_all | solution.py:332
  13.7 20.8 %copy-start.2 = (s32[128]{0:T(128)S(1)}, s32[128]{0:T(128)}, u32[]{:S(2)}) copy-start(s32[128]{0:T(128)} %pos.3) | copy-start | bytes 1540
  13.7 22.8 %collective-permute-start.1 = (bf16[272,128]{1,0:T(8,128)(2,1)}, bf16[272,128]{1,0:T(8,128)(2,1)S(1)}, u32[]{:S(2)}, u32[]{:S(2)}) collective-permute-start(bf16[272,128]{1,0:T(8,128)(2,1)} %pack_keys.1.own_ref), channel_id=1, source_target_pairs={{0,176},{16,96},{32,208},{48,128},{64,240},{80,160},{96,16},{112,1... | collective-permute-start | bytes 208904 | tf_op jit(solution)/shard_map/ppermute | solution.py:286
  26.3 13.2 %collective-permute-start = (bf16[272,128]{1,0:T(8,128)(2,1)}, bf16[272,128]{1,0:T(8,128)(2,1)S(1)}, u32[]{:S(2)}, u32[]{:S(2)}) collective-permute-start(bf16[272,128]{1,0:T(8,128)(2,1)} %pack_keys.1.own_ref), channel_id=1, source_target_pairs={{0,80},{16,192},{32,112},{48,224},{64,144},{80,0},{96,176},{112,32... | collective-permute-start | bytes 208904 | tf_op jit(solution)/shard_map/ppermute | solution.py:286
  31.1 8.7 %collective-permute-start.2 = (bf16[128,640]{1,0:T(8,128)(2,1)S(1)}, bf16[128,640]{1,0:T(8,128)(2,1)S(1)}, u32[]{:S(2)}, u32[]{:S(2)}) collective-permute-start(bf16[128,640]{1,0:T(8,128)(2,1)S(1)} %copy-done.1), channel_id=1, source_target_pairs={{0,256},{256,0},{1,257},{257,1},{2,258},{258,2},{3,259},{259,3},{4... | collective-permute-start | bytes 491528 | tf_op jit(solution)/shard_map/ppermute | solution.py:290
  39.8 0.9 copy-start
  41.3 22.6 %collective-permute-start.3 = (bf16[2,128,1280]{2,1,0:T(8,128)(2,1)S(1)}, bf16[2,128,1280]{2,1,0:T(8,128)(2,1)S(1)}, u32[]{:S(2)}, u32[]{:S(2)}) collective-permute-start(bf16[2,128,1280]{2,1,0:T(8,128)(2,1)S(1)} %get-tuple-element.26.x_ref), channel_id=1, source_target_pairs={{0,8},{8,0},{1,9},{9,1},{2,10},{10,2},{3,11},{11,3},{4,12},{12,4},... | collective-permute-start | bytes 1966088 | tf_op jit(solution)/shard_map/ppermute | solution.py:290
  43.2 14.3 %collective-permute-start.6 = (bf16[272,128]{1,0:T(8,128)(2,1)S(1)}, bf16[272,128]{1,0:T(8,128)(2,1)S(1)}, u32[]{:S(2)}, u32[]{:S(2)}) collective-permute-start(bf16[272,128]{1,0:T(8,128)(2,1)S(1)} %collective-permute-done.1.w_ref), channel_id=1, source_target_pairs={{0,48},{16,224},{32,80},{48,0},{64,112},{80,32},{96,144},{112,64},... | collective-permute-start | bytes 208904 | tf_op jit(solution)/shard_map/ppermute | solution.py:286
  47.0 13.9 %collective-permute-start.5 = (bf16[3,272,128]{2,1,0:T(8,128)(2,1)S(1)}, bf16[3,272,128]{2,1,0:T(8,128)(2,1)S(1)}, u32[]{:S(2)}, u32[]{:S(2)}) collective-permute-start(bf16[3,272,128]{2,1,0:T(8,128)(2,1)S(1)} %get-tuple-element.27.s_ref), channel_id=1, source_target_pairs={{0,240},{16,32},{32,16},{48,64},{64,48},{80,96},{96,80},{112,128},... | collective-permute-start | bytes 626696 | tf_op jit(solution)/shard_map/ppermute | solution.py:286
  49.0 14.9 %collective-permute-start.4 = (bf16[3,272,128]{2,1,0:T(8,128)(2,1)S(1)}, bf16[3,272,128]{2,1,0:T(8,128)(2,1)S(1)}, u32[]{:S(2)}, u32[]{:S(2)}) collective-permute-start(bf16[3,272,128]{2,1,0:T(8,128)(2,1)S(1)} %get-tuple-element.27.s_ref), channel_id=1, source_target_pairs={{0,16},{16,0},{32,48},{48,32},{64,80},{80,64},{96,112},{112,96},{1... | collective-permute-start | bytes 626696 | tf_op jit(solution)/shard_map/ppermute | solution.py:286
  54.1 21.9 %collective-permute-start.10 = (bf16[3,272,128]{2,1,0:T(8,128)(2,1)S(1)}, bf16[3,272,128]{2,1,0:T(8,128)(2,1)S(1)}, u32[]{:S(2)}, u32[]{:S(2)}) collective-permute-start(bf16[3,272,128]{2,1,0:T(8,128)(2,1)S(1)} %get-tuple-element.27.s_ref), channel_id=1, source_target_pairs={{0,224},{16,48},{32,0},{48,80},{64,32},{80,112},{96,64},{112,144},... | collective-permute-start | bytes 626696 | tf_op jit(solution)/shard_map/ppermute | solution.py:286
  57.5 18.5 %collective-permute-start.9 = (bf16[3,272,128]{2,1,0:T(8,128)(2,1)S(1)}, bf16[3,272,128]{2,1,0:T(8,128)(2,1)S(1)}, u32[]{:S(2)}, u32[]{:S(2)}) collective-permute-start(bf16[3,272,128]{2,1,0:T(8,128)(2,1)S(1)} %get-tuple-element.27.s_ref), channel_id=1, source_target_pairs={{0,32},{16,240},{32,64},{48,16},{64,96},{80,48},{96,128},{112,80},... | collective-permute-start | bytes 626696 | tf_op jit(solution)/shard_map/ppermute | solution.py:286
  69.4 12.4 %collective-permute-start.7 = (bf16[3,256,128]{2,1,0:T(8,128)(2,1)S(1)}, bf16[3,256,128]{2,1,0:T(8,128)(2,1)S(1)}, u32[]{:S(2)}, u32[]{:S(2)}) collective-permute-start(bf16[3,256,128]{2,1,0:T(8,128)(2,1)S(1)} %get-tuple-element.29), channel_id=1, source_target_pairs={{0,16},{16,0},{32,48},{48,32},{64,80},{80,64},{96,112},{112,96},{1... | collective-permute-start | bytes 589832 | tf_op jit(solution)/shard_map/ppermute | solution.py:286
  73.3 8.8 %collective-permute-start.8 = (bf16[3,256,128]{2,1,0:T(8,128)(2,1)S(1)}, bf16[3,256,128]{2,1,0:T(8,128)(2,1)S(1)}, u32[]{:S(2)}, u32[]{:S(2)}) collective-permute-start(bf16[3,256,128]{2,1,0:T(8,128)(2,1)S(1)} %get-tuple-element.30), channel_id=1, source_target_pairs={{0,240},{16,32},{32,16},{48,64},{64,48},{80,96},{96,80},{112,128},... | collective-permute-start | bytes 589832 | tf_op jit(solution)/shard_map/ppermute | solution.py:286
  79.9 12.9 %collective-permute-start.16 = (bf16[2,128,512]{2,1,0:T(8,128)(2,1)S(1)}, bf16[2,128,512]{2,1,0:T(8,128)(2,1)S(1)}, u32[]{:S(2)}, u32[]{:S(2)}) collective-permute-start(bf16[2,128,512]{2,1,0:T(8,128)(2,1)S(1)} %get-tuple-element.42), channel_id=1, source_target_pairs={{0,8},{8,0},{1,9},{9,1},{2,10},{10,2},{3,11},{11,3},{4,12},{12,4},... | collective-permute-start | bytes 786440 | tf_op jit(solution)/shard_map/ppermute | solution.py:290
  82.2 16.9 %collective-permute-start.11 = (bf16[3,256,128]{2,1,0:T(8,128)(2,1)S(1)}, bf16[3,256,128]{2,1,0:T(8,128)(2,1)S(1)}, u32[]{:S(2)}, u32[]{:S(2)}) collective-permute-start(bf16[3,256,128]{2,1,0:T(8,128)(2,1)S(1)} %get-tuple-element.35), channel_id=1, source_target_pairs={{0,224},{16,48},{32,0},{48,80},{64,32},{80,112},{96,64},{112,144},... | collective-permute-start | bytes 589832 | tf_op jit(solution)/shard_map/ppermute | solution.py:286
  85.3 13.7 %collective-permute-start.12 = (bf16[3,256,128]{2,1,0:T(8,128)(2,1)S(1)}, bf16[3,256,128]{2,1,0:T(8,128)(2,1)S(1)}, u32[]{:S(2)}, u32[]{:S(2)}) collective-permute-start(bf16[3,256,128]{2,1,0:T(8,128)(2,1)S(1)} %get-tuple-element.36), channel_id=1, source_target_pairs={{0,32},{16,240},{32,64},{48,16},{64,96},{80,48},{96,128},{112,80},... | collective-permute-start | bytes 589832 | tf_op jit(solution)/shard_map/ppermute | solution.py:286
  88.9 10.1 %collective-permute-start.13 = (bf16[256,128]{1,0:T(8,128)(2,1)S(1)}, bf16[256,128]{1,0:T(8,128)(2,1)S(1)}, u32[]{:S(2)}, u32[]{:S(2)}) collective-permute-start(bf16[256,128]{1,0:T(8,128)(2,1)S(1)} %get-tuple-element.37), channel_id=1, source_target_pairs={{0,48},{16,224},{32,80},{48,0},{64,112},{80,32},{96,144},{112,64},... | collective-permute-start | bytes 196616 | tf_op jit(solution)/shard_map/ppermute | solution.py:286
  92.8 18.0 %collective-permute-start.17 = (bf16[128,512]{1,0:T(8,128)(2,1)S(1)}, bf16[128,512]{1,0:T(8,128)(2,1)S(1)}, u32[]{:S(2)}, u32[]{:S(2)}) collective-permute-start(bf16[128,512]{1,0:T(8,128)(2,1)S(1)} %get-tuple-element.44), channel_id=1, source_target_pairs={{0,256},{256,0},{1,257},{257,1},{2,258},{258,2},{3,259},{259,3},{4... | collective-permute-start | bytes 393224 | tf_op jit(solution)/shard_map/ppermute | solution.py:290
  99.1 11.7 %collective-permute-start.14 = (bf16[256,128]{1,0:T(8,128)(2,1)S(1)}, bf16[256,128]{1,0:T(8,128)(2,1)S(1)}, u32[]{:S(2)}, u32[]{:S(2)}) collective-permute-start(bf16[256,128]{1,0:T(8,128)(2,1)S(1)} %get-tuple-element.39), channel_id=1, source_target_pairs={{0,80},{16,192},{32,112},{48,224},{64,144},{80,0},{96,176},{112,32... | collective-permute-start | bytes 196616 | tf_op jit(solution)/shard_map/ppermute | solution.py:286
  104.4 13.5 %collective-permute-start.15 = (bf16[256,128]{1,0:T(8,128)(2,1)S(1)}, bf16[256,128]{1,0:T(8,128)(2,1)S(1)}, u32[]{:S(2)}, u32[]{:S(2)}) collective-permute-start(bf16[256,128]{1,0:T(8,128)(2,1)S(1)} %get-tuple-element.40), channel_id=1, source_target_pairs={{0,176},{16,96},{32,208},{48,128},{64,240},{80,160},{96,16},{112,1... | collective-permute-start | bytes 196616 | tf_op jit(solution)/shard_map/ppermute | solution.py:286

commit v6 on v5

--- a/solution.py
+++ b/solution.py
@@ -157,28 +157,26 @@
     return jnp.concatenate([acc[rows, : 2 * BLK] * SCALE, acc[rows, 2 * BLK :]], axis=-2)
 
 
-def with_nearest(x_ref, y_ref, s_ref, p_ref, m_ref, e_ref, *rest):
-    own_out, p_out, m_out, e_out, dq_out, kv, acc = rest
+def with_next(x_ref, y_ref, p_ref, m_ref, e_ref, p_out, m_out, dq_out, kv, acc):
+    kv[:NEAR] = p_ref[...]
+    kv[NEAR : 2 * NEAR] = m_ref[...]
+    kv[2 * NEAR] = e_ref[...]
+    dq_out[...] = jnp.zeros_like(dq_out)
+    backward(x_ref, y_ref, kv, acc, dq_out, ((0, 4), (4, 7)), False)
+    p_out[...] = scaled(acc, slice(0, NEAR)).astype(BF16)
+    m_out[...] = scaled(acc, slice(NEAR, 2 * NEAR + 1)).astype(BF16)
+
+
+def with_nearest(x_ref, y_ref, s_ref, p_ref, m_ref, dq_ref, *rest):
+    own_out, p_out, m_out, dq_out, dq_core_out, kv, acc, dq = rest
     kv[:NEAR] = s_ref[...]
     kv[NEAR : 2 * NEAR] = p_ref[...]
-    kv[2 * NEAR : 3 * NEAR] = m_ref[...]
-    kv[3 * NEAR] = e_ref[...]
-    dq_out[...] = jnp.zeros_like(dq_out)
-    backward(x_ref, y_ref, kv, acc, dq_out, ((0, 5), (5, 10)), True)
+    kv[2 * NEAR :] = m_ref[...]
+    dq[...] = dq_ref[...]
+    backward(x_ref, y_ref, kv, acc, dq, ((0, 5), (5, 9)), True)
     own_out[...] = scaled(acc, slice(0, NEAR))
     p_out[...] = scaled(acc, slice(NEAR, 2 * NEAR)).astype(BF16)
     m_out[...] = scaled(acc, slice(2 * NEAR, 3 * NEAR)).astype(BF16)
-    e_out[...] = scaled(acc, 3 * NEAR).astype(BF16)
-
-
-def with_next(x_ref, y_ref, p_ref, m_ref, dq_ref, *rest):
-    p_out, m_out, dq_out, dq_core_out, kv, acc, dq = rest
-    kv[:NEAR] = p_ref[...]
-    kv[NEAR:] = m_ref[...]
-    dq[...] = dq_ref[...]
-    backward(x_ref, y_ref, kv, acc, dq, ((0, 3), (3, 6)), False)
-    p_out[...] = scaled(acc, slice(0, NEAR)).astype(BF16)
-    m_out[...] = scaled(acc, slice(NEAR, 2 * NEAR)).astype(BF16)
     dq_out[...] = dq[:2]
     dq_core_out[...] = dq[2:].astype(BF16)
 
@@ -237,44 +235,52 @@
             g_out[twin * n_heads + d, :, wide:] = tail
 
 
-def join(info, own_ref, u_ref, w_ref, q_ref, qx_ref, grad_ref, s_out, x_out):
+def join(own_ref, u_ref, w_ref, q_ref, qx_ref, grad_ref, s_out, x_out):
     s_out[0] = own_ref[...]
     s_out[1] = u_ref[...]
     s_out[2] = w_ref[...]
     wide = (GROUP + 1) * HEAD
     x_out[0, :, :wide] = q_ref[...]
     x_out[1, :, :wide] = qx_ref[...]
-    x_out[0, :, wide:] = grad_ref[info[0]]
-    x_out[1, :, wide:] = grad_ref[1 - info[0]]
-
-
-def sum_first(own_ref, a_ref, b_ref, c_ref, d_ref, own_out, c_out, d_out):
-    own_out[...] = own_ref[...] + a_ref[...].astype(F32) + b_ref[...].astype(F32)
-    c_out[...] = c_ref[...]
-    d_out[...] = d_ref[...]
-
-
-def sum_near(own_ref, c_ref, d_ref, e_ref, own_out, u_out, w_out):
-    total = own_ref[...] + c_ref[...].astype(F32) + d_ref[...].astype(F32)
+    half = lax.axis_index("xh")
+    x_out[0, :, wide:] = grad_ref[half]
+    x_out[1, :, wide:] = grad_ref[1 - half]
+
+
+def sum_first(own_ref, c_ref, d_ref, p_ref, m_ref, own_out, p_out, m_out):
+    own_out[...] = own_ref[...] + c_ref[...].astype(F32) + d_ref[:NEAR].astype(F32)
+    p_out[: NEAR - 1] = p_ref[: NEAR - 1]
+    last = p_ref[NEAR - 1].astype(F32) + d_ref[NEAR].astype(F32)
+    p_out[NEAR - 1] = last.astype(BF16)
+    m_out[...] = m_ref[...]
+
+
+def sum_near(own_ref, p_ref, m_ref, own_out, u_out, w_out):
+    total = own_ref[...] + p_ref[...].astype(F32) + m_ref[...].astype(F32)
     own_out[...] = total[0]
     u_out[...] = total[1].astype(BF16)
-    w_out[...] = (total[2] + e_ref[...].astype(F32)).astype(BF16)
-
-
-def sum_cores(dq_ref, core_ref, dq_out, dqx_out):
+    w_out[...] = total[2].astype(BF16)
+
+
+def sum_cores(dq_ref, core_ref, x_ref, dq_out, dqx_out, flag_out):
     dq_out[...] = dq_ref[0] + core_ref[0].astype(F32)
     dqx_out[...] = (dq_ref[1] + core_ref[1].astype(F32)).astype(BF16)
-
-
-def finish(info, own_ref, u_ref, w_ref, dq_ref, dqx_ref, q_out, k_out, v_out):
-    start = pl.multiple_of(info[1] * BLK, BLK)
+    at = GROUP * HEAD + 25
+    flag_out[...] = jnp.broadcast_to(x_ref[0, :BLK, at : at + 1].astype(F32), flag_out.shape)
+
+
+def finish(flag_ref, own_ref, u_ref, w_ref, dq_ref, dqx_ref, q_out, k_out, v_out):
+    swapped = flag_ref[...] > 0.5
     total = own_ref[...] + u_ref[...].astype(F32) + w_ref[...].astype(F32)
     dq = dq_ref[...] + dqx_ref[...].astype(F32)
     for i in range(2):
-        rows = pl.ds(start if i == 0 else pl.multiple_of(BLK - start, BLK), BLK)
-        q_out[rows, :] = dq[i * BLK : (i + 1) * BLK].astype(BF16)
-        k_out[rows, :] = total[i * BLK : (i + 1) * BLK].astype(BF16)
-        v_out[rows, :] = total[(2 + i) * BLK : (3 + i) * BLK].astype(BF16)
+        here, there = slice(i * BLK, (i + 1) * BLK), slice((1 - i) * BLK, (2 - i) * BLK)
+        for h in range(GROUP):
+            cols = slice(h * HEAD, (h + 1) * HEAD)
+            q_out[here, cols] = jnp.where(swapped, dq[there, cols], dq[here, cols]).astype(BF16)
+        k_out[here, :] = jnp.where(swapped, total[there], total[here]).astype(BF16)
+        there, of_v = slice((3 - i) * BLK, (4 - i) * BLK), slice((2 + i) * BLK, (3 + i) * BLK)
+        v_out[here, :] = jnp.where(swapped, total[there], total[of_v]).astype(BF16)
 
 
 HEADS = ("xl", "y")
@@ -313,8 +319,6 @@
 def shards(queries, keys, values, outputs, out_grad, lse, positions):
     n_heads = lax.axis_size(HEADS)
     wide = (GROUP + 1) * HEAD
-    swapped = positions[0] > positions[BLK]
-    info = jnp.stack([lax.axis_index("xh"), swapped]).astype(jnp.int32)
 
     def like(shape, dtype=BF16):
         return jax.ShapeDtypeStruct(shape, dtype)
@@ -333,21 +337,30 @@
     other_q = swapped_with(own_q, "xh")
     s_set, x = local_call(
         join, (like((NEAR,) + packed), like((2, TOK, 2 * wide))), 8, stream_in=True
-    )(info, own, u, w, own_q, other_q, grad.reshape(2, TOK, wide))
+    )(own, u, w, own_q, other_q, grad.reshape(2, TOK, wide))
     p1, m1, p2, m2 = [by_parity(s_set, by) for by in (1, -1, 2, -2)]
     e_one = by_parity(w, 3)
     y = swapped_with(x, "core")
 
     near, dq_shape = (NEAR,) + block, (2, TOK, GROUP * HEAD)
-    own_g, p1_g, m1_g, e_g, dq = local_call(
+    p2_g, m2_g, dq = local_call(
+        with_next,
+        (like(near), like((NEAR + 1,) + block), like((4,) + dq_shape[1:], F32)),
+        16,
+    )(
+        x,
+        y,
+        p2,
+        m2,
+        e_one,
+        scratch=[
+            pltpu.VMEM((2 * NEAR + 1,) + packed, BF16),
+            pltpu.VMEM((2 * NEAR + 1,) + block, F32),
+        ],
+    )
+    own_g, p1_g, m1_g, dq, dq_core = local_call(
         with_nearest,
-        (
-            like(near, F32),
-            like(near),
-            like(near),
-            like(block),
-            like((4,) + dq_shape[1:], F32),
-        ),
+        (like(near, F32), like(near), like(near), like(dq_shape, F32), like(dq_shape)),
         16,
     )(
         x,
@@ -355,37 +368,26 @@
         s_set,
         p1,
         m1,
-        e_one,
-        scratch=[
-            pltpu.VMEM((3 * NEAR + 1,) + packed, BF16),
-            pltpu.VMEM((3 * NEAR + 1,) + block, F32),
-        ],
-    )
-    p2_g, m2_g, dq, dq_core = local_call(
-        with_next, (like(near), like(near), like(dq_shape, F32), like(dq_shape)), 16
-    )(
-        x,
-        y,
-        p2,
-        m2,
         dq,
         scratch=[
-            pltpu.VMEM((2 * NEAR,) + packed, BF16),
-            pltpu.VMEM((2 * NEAR,) + block, F32),
+            pltpu.VMEM((3 * NEAR,) + packed, BF16),
+            pltpu.VMEM((3 * NEAR,) + block, F32),
             pltpu.VMEM((4,) + dq_shape[1:], F32),
         ],
     )
 
-    p1_in, m1_in, e_in = by_parity(p1_g, 1), by_parity(m1_g, -1), by_parity(e_g, 3)
-    own_g, p2_g, m2_g = local_call(sum_first, (like(near, F32), like(near), like(near)), 8)(
-        own_g, p1_in, m1_in, p2_g, m2_g
-    )
     p2_in, m2_in = by_parity(p2_g, -2), by_parity(m2_g, 2)
+    own_g, p1_g, m1_g = local_call(sum_first, (like(near, F32), like(near), like(near)), 8)(
+        own_g, p2_in, m2_in, p1_g, m1_g
+    )
+    p1_in, m1_in = by_parity(p1_g, 1), by_parity(m1_g, -1)
     dq_core = swapped_with(dq_core, "core")
-    dq, dqx = local_call(sum_cores, (like(dq_shape[1:], F32), like(dq_shape[1:])), 8)(dq, dq_core)
+    dq, dqx, flag = local_call(
+        sum_cores, (like(dq_shape[1:], F32), like(dq_shape[1:]), like((BLK, HEAD), F32)), 8
+    )(dq, dq_core, x)
     dqx = swapped_with(dqx, "xh")
     own_g, u_g, w_g = local_call(sum_near, (like(block, F32), like(block), like(block)), 8)(
-        own_g, p2_in, m2_in, e_in
+        own_g, p1_in, m1_in
     )
     u_g, w_g = by_parity(u_g, 5), by_parity(w_g, -5)
     return local_call(
@@ -393,7 +395,7 @@
         (like(queries.shape), like(keys.shape), like(values.shape)),
         8,
         stream_out=True,
-    )(info, own_g, u_g, w_g, dq, dqx)
+    )(flag, own_g, u_g, w_g, dq, dqx)
 
 
 def solution(mesh):

time: 120 us -> 119 us (level); the launches traced: 119 us -> 117 us
  waiting for transfers between devices: 16.5 us -> 20.6 us
  starting transfers between devices: 83.8 us -> 80.5 us
  Pallas kernels: 15.1 us -> 13.7 us
  between operations: 2.2 us -> 0.89 us
    ppermute x14 -> x13, waiting for transfers between devices: 16.2 us -> 20.5 us  [by_parity(): return lax.ppermute(x, 'z', list(enumerate(to)))]
    ppermute x14 -> x13, starting transfers between devices: 63.8 us -> 60 us  [by_parity(): return lax.ppermute(x, 'z', list(enumerate(to)))]
    pallas_call x9, Pallas kernels: 15.1 us -> 13.7 us  [call(): pl.pallas_call(body, out_shape=out_shape, in_specs=[smem if a.dtype == jn...]
  transfers between devices with their start and end apart: 19 -> 18, of which waited for: 6 -> 5; matrix products, arithmetic and copies ran while one was open for 1% -> 0% of each run, Pallas kernels for 9% -> 9%
where the time goes in v6:
time: 119 us; the launch traced here: 117 us
  starting transfers between devices  80.5 us (68%)
  waiting for transfers between devices  20.6 us (17%)
  Pallas kernels  13.7 us (12%)
    ppermute x13, starting transfers between devices, by_parity(): return lax.ppermute(x, 'z', list(enumerate(to)))  60 us
    ppermute x13, waiting for transfers between devices, by_parity(): return lax.ppermute(x, 'z', list(enumerate(to)))  20.5 us
    pallas_call x9, Pallas kernels, call(): pl.pallas_call(body, out_shape=out_shape, in_specs=[smem if a.dtype == jn...  13.7 us
    ppermute x4, starting transfers between devices, swapped_with(): return lax.ppermute(x, axis, [(0, 1), (1, 0)])  11.1 us
    all_to_all x1, starting transfers between devices, shards(): lax.all_to_all(send, ('xh',) + HEADS, split_axis=0, concat_axis=0, tiled=...  9.39 us
  transfers between devices with their start and end apart: 18, of which 5 were waited for; matrix products, arithmetic and copies ran while one was open for 0% of the time, Pallas kernels for 9%

profile of v6, /device:TPU:6, one launch (start us, length us, event | category | flops | bytes accessed | tf_op | source)
XLA Modules:
  0.0 116.6 jit_solution(1358889010972504217)
XLA Ops:
  0.6 2.2 %pack_queries.1 = (bf16[128,640]{1,0:T(8,128)(2,1)}, bf16[16,16,640]{2,1,0:T(8,128)(2,1)}) custom-call(s32[128]{0:T(128)} %pos.3, bf16[128,512]{1,0:T(8,128)(2,1)} %q_ref.1, f32[4,128]{1,0:T(4,128)} %bitcast.3, bf16[16,4096]{1,0:T(8,128)(2,1)} %o_ref.1, bf16[16,4096]{1,0:T(8,128)(2,1)} %g_ref.1), custom_call_target="tpu_custom_call" | custom-call | tf_op jit(solution)/shard_map/pack_queries/pallas_call | solution.py:304
  2.8 9.4 %all-to-all-start = ((bf16[16,16,640]{2,1,0:T(8,128)(2,1)}), bf16[16,16,640]{2,1,0:T(8,128)(2,1)S(1)}, u32[]{:S(2)}, u32[]{:S(2)}) async-start(bf16[16,16,640]{2,1,0:T(8,128)(2,1)} %get-tuple-element.25), calls=%async_computation | async-start | bytes 655360 | tf_op jit(solution)/shard_map/all_to_all | solution.py:336
  12.2 3.3 %collective-permute-start.2 = (bf16[128,640]{1,0:T(8,128)(2,1)S(1)}, bf16[128,640]{1,0:T(8,128)(2,1)S(1)}, u32[]{:S(2)}, u32[]{:S(2)}) collective-permute-start(bf16[128,640]{1,0:T(8,128)(2,1)S(1)} %copy-done.1), channel_id=1, source_target_pairs={{0,256},{256,0},{1,257},{257,1},{2,258},{258,2},{3,259},{259,3},{4... | collective-permute-start | bytes 491528 | tf_op jit(solution)/shard_map/ppermute | solution.py:296
  15.6 1.4 %pack_keys.1.own_ref = bf16[272,128]{1,0:T(8,128)(2,1)} custom-call(s32[128]{0:T(128)} %pos.3, bf16[128,128]{1,0:T(8,128)(2,1)} %k_ref.1, bf16[128,128]{1,0:T(8,128)(2,1)} %v_ref.1), custom_call_target="tpu_custom_call" | custom-call | tf_op jit(solution)/shard_map/pack_keys/pallas_call | solution.py:304
  17.0 12.6 %collective-permute-start.1 = (bf16[272,128]{1,0:T(8,128)(2,1)}, bf16[272,128]{1,0:T(8,128)(2,1)S(1)}, u32[]{:S(2)}, u32[]{:S(2)}) collective-permute-start(bf16[272,128]{1,0:T(8,128)(2,1)} %pack_keys.1.own_ref), channel_id=1, source_target_pairs={{0,176},{16,96},{32,208},{48,128},{64,240},{80,160},{96,16},{112,1... | collective-permute-start | bytes 208904 | tf_op jit(solution)/shard_map/ppermute | solution.py:292
  29.6 4.7 %collective-permute-start = (bf16[272,128]{1,0:T(8,128)(2,1)}, bf16[272,128]{1,0:T(8,128)(2,1)S(1)}, u32[]{:S(2)}, u32[]{:S(2)}) collective-permute-start(bf16[272,128]{1,0:T(8,128)(2,1)} %pack_keys.1.own_ref), channel_id=1, source_target_pairs={{0,80},{16,192},{32,112},{48,224},{64,144},{80,0},{96,176},{112,32... | collective-permute-start | bytes 208904 | tf_op jit(solution)/shard_map/ppermute | solution.py:292
  34.3 8.3 %collective-permute-done.u_ref = bf16[272,128]{1,0:T(8,128)(2,1)S(1)} collective-permute-done((bf16[272,128]{1,0:T(8,128)(2,1)}, bf16[272,128]{1,0:T(8,128)(2,1)S(1)}, u32[]{:S(2)}, u32[]{:S(2)}) %collective-permute-start) | collective-permute-done | bytes 69664 | tf_op jit(solution)/shard_map/ppermute | solution.py:292
  42.6 0.9 copy-done
  43.5 0.1 join.1
  43.6 1.9 %collective-permute-start.3 = (bf16[2,128,1280]{2,1,0:T(8,128)(2,1)S(1)}, bf16[2,128,1280]{2,1,0:T(8,128)(2,1)S(1)}, u32[]{:S(2)}, u32[]{:S(2)}) collective-permute-start(bf16[2,128,1280]{2,1,0:T(8,128)(2,1)S(1)} %get-tuple-element.26.x_ref), channel_id=1, source_target_pairs={{0,8},{8,0},{1,9},{9,1},{2,10},{10,2},{3,11},{11,3},{4,12},{12,4},... | collective-permute-start | bytes 1966088 | tf_op jit(solution)/shard_map/ppermute | solution.py:296
  45.5 2.6 %collective-permute-start.7 = (bf16[3,272,128]{2,1,0:T(8,128)(2,1)S(1)}, bf16[3,272,128]{2,1,0:T(8,128)(2,1)S(1)}, u32[]{:S(2)}, u32[]{:S(2)}) collective-permute-start(bf16[3,272,128]{2,1,0:T(8,128)(2,1)S(1)} %get-tuple-element.27.s_ref), channel_id=1, source_target_pairs={{0,224},{16,48},{32,0},{48,80},{64,32},{80,112},{96,64},{112,144},... | collective-permute-start | bytes 626696 | tf_op jit(solution)/shard_map/ppermute | solution.py:292
  48.1 4.1 %collective-permute-start.6 = (bf16[3,272,128]{2,1,0:T(8,128)(2,1)S(1)}, bf16[3,272,128]{2,1,0:T(8,128)(2,1)S(1)}, u32[]{:S(2)}, u32[]{:S(2)}) collective-permute-start(bf16[3,272,128]{2,1,0:T(8,128)(2,1)S(1)} %get-tuple-element.27.s_ref), channel_id=1, source_target_pairs={{0,32},{16,240},{32,64},{48,16},{64,96},{80,48},{96,128},{112,80},... | collective-permute-start | bytes 626696 | tf_op jit(solution)/shard_map/ppermute | solution.py:292
  52.3 2.2 %collective-permute-start.8 = (bf16[272,128]{1,0:T(8,128)(2,1)S(1)}, bf16[272,128]{1,0:T(8,128)(2,1)S(1)}, u32[]{:S(2)}, u32[]{:S(2)}) collective-permute-start(bf16[272,128]{1,0:T(8,128)(2,1)S(1)} %collective-permute-done.1.w_ref), channel_id=1, source_target_pairs={{0,48},{16,224},{32,80},{48,0},{64,112},{80,32},{96,144},{112,64},... | collective-permute-start | bytes 208904 | tf_op jit(solution)/shard_map/ppermute | solution.py:292
  54.5 2.5 %collective-permute-start.5 = (bf16[3,272,128]{2,1,0:T(8,128)(2,1)S(1)}, bf16[3,272,128]{2,1,0:T(8,128)(2,1)S(1)}, u32[]{:S(2)}, u32[]{:S(2)}) collective-permute-start(bf16[3,272,128]{2,1,0:T(8,128)(2,1)S(1)} %get-tuple-element.27.s_ref), channel_id=1, source_target_pairs={{0,240},{16,32},{32,16},{48,64},{64,48},{80,96},{96,80},{112,128},... | collective-permute-start | bytes 626696 | tf_op jit(solution)/shard_map/ppermute | solution.py:292
  57.0 5.0 %collective-permute-done.8.e_ref = bf16[272,128]{1,0:T(8,128)(2,1)S(1)} collective-permute-done((bf16[272,128]{1,0:T(8,128)(2,1)S(1)}, bf16[272,128]{1,0:T(8,128)(2,1)S(1)}, u32[]{:S(2)}, u32[]{:S(2)}) %collective-permute-start.8) | collective-permute-done | bytes 69664 | tf_op jit(solution)/shard_map/ppermute | solution.py:292
  62.1 3.8 %collective-permute-start.4 = (bf16[3,272,128]{2,1,0:T(8,128)(2,1)S(1)}, bf16[3,272,128]{2,1,0:T(8,128)(2,1)S(1)}, u32[]{:S(2)}, u32[]{:S(2)}) collective-permute-start(bf16[3,272,128]{2,1,0:T(8,128)(2,1)S(1)} %get-tuple-element.27.s_ref), channel_id=1, source_target_pairs={{0,16},{16,0},{32,48},{48,32},{64,80},{80,64},{96,112},{112,96},{1... | collective-permute-start | bytes 626696 | tf_op jit(solution)/shard_map/ppermute | solution.py:292
  65.9 3.8 %with_next.1 = (bf16[3,256,128]{2,1,0:T(8,128)(2,1)S(1)}, bf16[4,256,128]{2,1,0:T(8,128)(2,1)S(1)}, f32[4,128,512]{2,1,0:T(8,128)S(1)}) custom-call(bf16[2,128,1280]{2,1,0:T(8,128)(2,1)S(1)} %get-tuple-element.26.x_ref, bf16[2,128,1280]{2,1,0:T(8,128)(2,1)S(1)} %collective-permute-done.3.y_ref, bf16[3,272,128]{2,1,0:T(8,128)(2,1)S(1)} %collective-permute-done.6.p_ref, ...), custom_call_target="tpu_custom_call" | custom-call | tf_op jit(solution)/shard_map/with_next/pallas_call | solution.py:304
  69.7 3.8 %collective-permute-start.11 = (bf16[4,256,128]{2,1,0:T(8,128)(2,1)S(1)}, bf16[4,256,128]{2,1,0:T(8,128)(2,1)S(1)}, u32[]{:S(2)}, u32[]{:S(2)}) collective-permute-start(bf16[4,256,128]{2,1,0:T(8,128)(2,1)S(1)} %get-tuple-element.34), channel_id=1, source_target_pairs={{0,32},{16,240},{32,64},{48,16},{64,96},{80,48},{96,128},{112,80},... | collective-permute-start | bytes 786440 | tf_op jit(solution)/shard_map/ppermute | solution.py:292
  73.5 4.1 %collective-permute-start.10 = (bf16[3,256,128]{2,1,0:T(8,128)(2,1)S(1)}, bf16[3,256,128]{2,1,0:T(8,128)(2,1)S(1)}, u32[]{:S(2)}, u32[]{:S(2)}) collective-permute-start(bf16[3,256,128]{2,1,0:T(8,128)(2,1)S(1)} %get-tuple-element.33), channel_id=1, source_target_pairs={{0,224},{16,48},{32,0},{48,80},{64,32},{80,112},{96,64},{112,144},... | collective-permute-start | bytes 589832 | tf_op jit(solution)/shard_map/ppermute | solution.py:292
  77.7 5.2 %with_nearest.1 = (f32[3,256,128]{2,1,0:T(8,128)S(1)}, bf16[3,256,128]{2,1,0:T(8,128)(2,1)S(1)}, bf16[3,256,128]{2,1,0:T(8,128)(2,1)S(1)}, f32[2,128,512]{2,1,0:T(8,128)S(1)}, bf16[2,128,512]{2,1,0:T(8,128)(2,1)S(1)}) custom-call(bf16[2,128,1280]{2,1,0:T(8,128)(2,1)S(1)} %get-tuple-element.26.x_ref, bf16[2,128,1280]{2,1,0:T(8,128)(2,1)S(1)} %collective-permute-done.3.y_ref, ...), custom_call_target="tpu_custom_call" | custom-call | tf_op jit(solution)/shard_map/with_nearest/pallas_call | solution.py:304
  83.0 1.9 %collective-permute-start.9 = (bf16[2,128,512]{2,1,0:T(8,128)(2,1)S(1)}, bf16[2,128,512]{2,1,0:T(8,128)(2,1)S(1)}, u32[]{:S(2)}, u32[]{:S(2)}) collective-permute-start(bf16[2,128,512]{2,1,0:T(8,128)(2,1)S(1)} %get-tuple-element.30), channel_id=1, source_target_pairs={{0,8},{8,0},{1,9},{9,1},{2,10},{10,2},{3,11},{11,3},{4,12},{12,4},... | collective-permute-start | bytes 786440 | tf_op jit(solution)/shard_map/ppermute | solution.py:296
  84.9 0.1 sum_first.1
  85.0 3.8 %collective-permute-start.12 = (bf16[3,256,128]{2,1,0:T(8,128)(2,1)S(1)}, bf16[3,256,128]{2,1,0:T(8,128)(2,1)S(1)}, u32[]{:S(2)}, u32[]{:S(2)}) collective-permute-start(bf16[3,256,128]{2,1,0:T(8,128)(2,1)S(1)} %get-tuple-element.38), channel_id=1, source_target_pairs={{0,16},{16,0},{32,48},{48,32},{64,80},{80,64},{96,112},{112,96},{1... | collective-permute-start | bytes 589832 | tf_op jit(solution)/shard_map/ppermute | solution.py:292
  88.8 4.4 %collective-permute-start.13 = (bf16[3,256,128]{2,1,0:T(8,128)(2,1)S(1)}, bf16[3,256,128]{2,1,0:T(8,128)(2,1)S(1)}, u32[]{:S(2)}, u32[]{:S(2)}) collective-permute-start(bf16[3,256,128]{2,1,0:T(8,128)(2,1)S(1)} %get-tuple-element.39), channel_id=1, source_target_pairs={{0,240},{16,32},{32,16},{48,64},{64,48},{80,96},{96,80},{112,128},... | collective-permute-start | bytes 589832 | tf_op jit(solution)/shard_map/ppermute | solution.py:292
  93.3 0.1 sum_cores.1
  93.4 4.0 %collective-permute-start.16 = (bf16[128,512]{1,0:T(8,128)(2,1)S(1)}, bf16[128,512]{1,0:T(8,128)(2,1)S(1)}, u32[]{:S(2)}, u32[]{:S(2)}) collective-permute-start(bf16[128,512]{1,0:T(8,128)(2,1)S(1)} %get-tuple-element.44), channel_id=1, source_target_pairs={{0,256},{256,0},{1,257},{257,1},{2,258},{258,2},{3,259},{259,3},{4... | collective-permute-start | bytes 393224 | tf_op jit(solution)/shard_map/ppermute | solution.py:296
  97.3 0.7 collective-permute-done.13.m_ref
  98.1 4.6 %collective-permute-start.14 = (bf16[256,128]{1,0:T(8,128)(2,1)S(1)}, bf16[256,128]{1,0:T(8,128)(2,1)S(1)}, u32[]{:S(2)}, u32[]{:S(2)}) collective-permute-start(bf16[256,128]{1,0:T(8,128)(2,1)S(1)} %get-tuple-element.41), channel_id=1, source_target_pairs={{0,80},{16,192},{32,112},{48,224},{64,144},{80,0},{96,176},{112,32... | collective-permute-start | bytes 196616 | tf_op jit(solution)/shard_map/ppermute | solution.py:292
  102.7 6.7 %collective-permute-start.15 = (bf16[256,128]{1,0:T(8,128)(2,1)S(1)}, bf16[256,128]{1,0:T(8,128)(2,1)S(1)}, u32[]{:S(2)}, u32[]{:S(2)}) collective-permute-start(bf16[256,128]{1,0:T(8,128)(2,1)S(1)} %get-tuple-element.42), channel_id=1, source_target_pairs={{0,176},{16,96},{32,208},{48,128},{64,240},{80,160},{96,16},{112,1... | collective-permute-start | bytes 196616 | tf_op jit(solution)/shard_map/ppermute | solution.py:292
  109.3 0.4 collective-permute-done.14.u_ref
  109.7 6.1 %collective-permute-done.15.w_ref = bf16[256,128]{1,0:T(8,128)(2,1)S(1)} collective-permute-done((bf16[256,128]{1,0:T(8,128)(2,1)S(1)}, bf16[256,128]{1,0:T(8,128)(2,1)S(1)}, u32[]{:S(2)}, u32[]{:S(2)}) %collective-permute-start.15) | collective-permute-done | bytes 65568 | tf_op jit(solution)/shard_map/ppermute | solution.py:292
  115.9 0.7 finish.1
  (17 shorter events, 0.1 us)
Async XLA Ops:
  2.8 9.4 %copy-start.1 = (bf16[128,640]{1,0:T(8,128)(2,1)S(1)}, bf16[128,640]{1,0:T(8,128)(2,1)}, u32[]{:S(2)}) copy-start(bf16[128,640]{1,0:T(8,128)(2,1)} %get-tuple-element.24.q_ref) | copy-start | bytes 491524
  2.8 39.8 %all-to-all-start = ((bf16[16,16,640]{2,1,0:T(8,128)(2,1)}), bf16[16,16,640]{2,1,0:T(8,128)(2,1)S(1)}, u32[]{:S(2)}, u32[]{:S(2)}) async-start(bf16[16,16,640]{2,1,0:T(8,128)(2,1)} %get-tuple-element.25), calls=%async_computation | async-start | bytes 655360 | tf_op jit(solution)/shard_map/all_to_all | solution.py:336
  12.2 30.4 %collective-permute-start.2 = (bf16[128,640]{1,0:T(8,128)(2,1)S(1)}, bf16[128,640]{1,0:T(8,128)(2,1)S(1)}, u32[]{:S(2)}, u32[]{:S(2)}) collective-permute-start(bf16[128,640]{1,0:T(8,128)(2,1)S(1)} %copy-done.1), channel_id=1, source_target_pairs={{0,256},{256,0},{1,257},{257,1},{2,258},{258,2},{3,259},{259,3},{4... | collective-permute-start | bytes 491528 | tf_op jit(solution)/shard_map/ppermute | solution.py:296
  17.0 17.3 %collective-permute-start.1 = (bf16[272,128]{1,0:T(8,128)(2,1)}, bf16[272,128]{1,0:T(8,128)(2,1)S(1)}, u32[]{:S(2)}, u32[]{:S(2)}) collective-permute-start(bf16[272,128]{1,0:T(8,128)(2,1)} %pack_keys.1.own_ref), channel_id=1, source_target_pairs={{0,176},{16,96},{32,208},{48,128},{64,240},{80,160},{96,16},{112,1... | collective-permute-start | bytes 208904 | tf_op jit(solution)/shard_map/ppermute | solution.py:292
  29.6 13.0 %collective-permute-start = (bf16[272,128]{1,0:T(8,128)(2,1)}, bf16[272,128]{1,0:T(8,128)(2,1)S(1)}, u32[]{:S(2)}, u32[]{:S(2)}) collective-permute-start(bf16[272,128]{1,0:T(8,128)(2,1)} %pack_keys.1.own_ref), channel_id=1, source_target_pairs={{0,80},{16,192},{32,112},{48,224},{64,144},{80,0},{96,176},{112,32... | collective-permute-start | bytes 208904 | tf_op jit(solution)/shard_map/ppermute | solution.py:292
  42.6 0.9 copy-start
  43.6 22.3 %collective-permute-start.3 = (bf16[2,128,1280]{2,1,0:T(8,128)(2,1)S(1)}, bf16[2,128,1280]{2,1,0:T(8,128)(2,1)S(1)}, u32[]{:S(2)}, u32[]{:S(2)}) collective-permute-start(bf16[2,128,1280]{2,1,0:T(8,128)(2,1)S(1)} %get-tuple-element.26.x_ref), channel_id=1, source_target_pairs={{0,8},{8,0},{1,9},{9,1},{2,10},{10,2},{3,11},{11,3},{4,12},{12,4},... | collective-permute-start | bytes 1966088 | tf_op jit(solution)/shard_map/ppermute | solution.py:296
  45.5 20.3 %collective-permute-start.7 = (bf16[3,272,128]{2,1,0:T(8,128)(2,1)S(1)}, bf16[3,272,128]{2,1,0:T(8,128)(2,1)S(1)}, u32[]{:S(2)}, u32[]{:S(2)}) collective-permute-start(bf16[3,272,128]{2,1,0:T(8,128)(2,1)S(1)} %get-tuple-element.27.s_ref), channel_id=1, source_target_pairs={{0,224},{16,48},{32,0},{48,80},{64,32},{80,112},{96,64},{112,144},... | collective-permute-start | bytes 626696 | tf_op jit(solution)/shard_map/ppermute | solution.py:292
  48.1 17.7 %collective-permute-start.6 = (bf16[3,272,128]{2,1,0:T(8,128)(2,1)S(1)}, bf16[3,272,128]{2,1,0:T(8,128)(2,1)S(1)}, u32[]{:S(2)}, u32[]{:S(2)}) collective-permute-start(bf16[3,272,128]{2,1,0:T(8,128)(2,1)S(1)} %get-tuple-element.27.s_ref), channel_id=1, source_target_pairs={{0,32},{16,240},{32,64},{48,16},{64,96},{80,48},{96,128},{112,80},... | collective-permute-start | bytes 626696 | tf_op jit(solution)/shard_map/ppermute | solution.py:292
  52.3 9.8 %collective-permute-start.8 = (bf16[272,128]{1,0:T(8,128)(2,1)S(1)}, bf16[272,128]{1,0:T(8,128)(2,1)S(1)}, u32[]{:S(2)}, u32[]{:S(2)}) collective-permute-start(bf16[272,128]{1,0:T(8,128)(2,1)S(1)} %collective-permute-done.1.w_ref), channel_id=1, source_target_pairs={{0,48},{16,224},{32,80},{48,0},{64,112},{80,32},{96,144},{112,64},... | collective-permute-start | bytes 208904 | tf_op jit(solution)/shard_map/ppermute | solution.py:292
  54.5 23.2 %collective-permute-start.5 = (bf16[3,272,128]{2,1,0:T(8,128)(2,1)S(1)}, bf16[3,272,128]{2,1,0:T(8,128)(2,1)S(1)}, u32[]{:S(2)}, u32[]{:S(2)}) collective-permute-start(bf16[3,272,128]{2,1,0:T(8,128)(2,1)S(1)} %get-tuple-element.27.s_ref), channel_id=1, source_target_pairs={{0,240},{16,32},{32,16},{48,64},{64,48},{80,96},{96,80},{112,128},... | collective-permute-start | bytes 626696 | tf_op jit(solution)/shard_map/ppermute | solution.py:292
  62.1 15.6 %collective-permute-start.4 = (bf16[3,272,128]{2,1,0:T(8,128)(2,1)S(1)}, bf16[3,272,128]{2,1,0:T(8,128)(2,1)S(1)}, u32[]{:S(2)}, u32[]{:S(2)}) collective-permute-start(bf16[3,272,128]{2,1,0:T(8,128)(2,1)S(1)} %get-tuple-element.27.s_ref), channel_id=1, source_target_pairs={{0,16},{16,0},{32,48},{48,32},{64,80},{80,64},{96,112},{112,96},{1... | collective-permute-start | bytes 626696 | tf_op jit(solution)/shard_map/ppermute | solution.py:292
  69.7 15.2 %collective-permute-start.11 = (bf16[4,256,128]{2,1,0:T(8,128)(2,1)S(1)}, bf16[4,256,128]{2,1,0:T(8,128)(2,1)S(1)}, u32[]{:S(2)}, u32[]{:S(2)}) collective-permute-start(bf16[4,256,128]{2,1,0:T(8,128)(2,1)S(1)} %get-tuple-element.34), channel_id=1, source_target_pairs={{0,32},{16,240},{32,64},{48,16},{64,96},{80,48},{96,128},{112,80},... | collective-permute-start | bytes 786440 | tf_op jit(solution)/shard_map/ppermute | solution.py:292
  73.5 11.4 %collective-permute-start.10 = (bf16[3,256,128]{2,1,0:T(8,128)(2,1)S(1)}, bf16[3,256,128]{2,1,0:T(8,128)(2,1)S(1)}, u32[]{:S(2)}, u32[]{:S(2)}) collective-permute-start(bf16[3,256,128]{2,1,0:T(8,128)(2,1)S(1)} %get-tuple-element.33), channel_id=1, source_target_pairs={{0,224},{16,48},{32,0},{48,80},{64,32},{80,112},{96,64},{112,144},... | collective-permute-start | bytes 589832 | tf_op jit(solution)/shard_map/ppermute | solution.py:292
  83.0 10.3 %collective-permute-start.9 = (bf16[2,128,512]{2,1,0:T(8,128)(2,1)S(1)}, bf16[2,128,512]{2,1,0:T(8,128)(2,1)S(1)}, u32[]{:S(2)}, u32[]{:S(2)}) collective-permute-start(bf16[2,128,512]{2,1,0:T(8,128)(2,1)S(1)} %get-tuple-element.30), channel_id=1, source_target_pairs={{0,8},{8,0},{1,9},{9,1},{2,10},{10,2},{3,11},{11,3},{4,12},{12,4},... | collective-permute-start | bytes 786440 | tf_op jit(solution)/shard_map/ppermute | solution.py:296
  85.0 12.3 %collective-permute-start.12 = (bf16[3,256,128]{2,1,0:T(8,128)(2,1)S(1)}, bf16[3,256,128]{2,1,0:T(8,128)(2,1)S(1)}, u32[]{:S(2)}, u32[]{:S(2)}) collective-permute-start(bf16[3,256,128]{2,1,0:T(8,128)(2,1)S(1)} %get-tuple-element.38), channel_id=1, source_target_pairs={{0,16},{16,0},{32,48},{48,32},{64,80},{80,64},{96,112},{112,96},{1... | collective-permute-start | bytes 589832 | tf_op jit(solution)/shard_map/ppermute | solution.py:292
  88.8 9.2 %collective-permute-start.13 = (bf16[3,256,128]{2,1,0:T(8,128)(2,1)S(1)}, bf16[3,256,128]{2,1,0:T(8,128)(2,1)S(1)}, u32[]{:S(2)}, u32[]{:S(2)}) collective-permute-start(bf16[3,256,128]{2,1,0:T(8,128)(2,1)S(1)} %get-tuple-element.39), channel_id=1, source_target_pairs={{0,240},{16,32},{32,16},{48,64},{64,48},{80,96},{96,80},{112,128},... | collective-permute-start | bytes 589832 | tf_op jit(solution)/shard_map/ppermute | solution.py:292
  93.4 16.0 %collective-permute-start.16 = (bf16[128,512]{1,0:T(8,128)(2,1)S(1)}, bf16[128,512]{1,0:T(8,128)(2,1)S(1)}, u32[]{:S(2)}, u32[]{:S(2)}) collective-permute-start(bf16[128,512]{1,0:T(8,128)(2,1)S(1)} %get-tuple-element.44), channel_id=1, source_target_pairs={{0,256},{256,0},{1,257},{257,1},{2,258},{258,2},{3,259},{259,3},{4... | collective-permute-start | bytes 393224 | tf_op jit(solution)/shard_map/ppermute | solution.py:296
  98.1 11.7 %collective-permute-start.14 = (bf16[256,128]{1,0:T(8,128)(2,1)S(1)}, bf16[256,128]{1,0:T(8,128)(2,1)S(1)}, u32[]{:S(2)}, u32[]{:S(2)}) collective-permute-start(bf16[256,128]{1,0:T(8,128)(2,1)S(1)} %get-tuple-element.41), channel_id=1, source_target_pairs={{0,80},{16,192},{32,112},{48,224},{64,144},{80,0},{96,176},{112,32... | collective-permute-start | bytes 196616 | tf_op jit(solution)/shard_map/ppermute | solution.py:292
  102.7 13.2 %collective-permute-start.15 = (bf16[256,128]{1,0:T(8,128)(2,1)S(1)}, bf16[256,128]{1,0:T(8,128)(2,1)S(1)}, u32[]{:S(2)}, u32[]{:S(2)}) collective-permute-start(bf16[256,128]{1,0:T(8,128)(2,1)S(1)} %get-tuple-element.42), channel_id=1, source_target_pairs={{0,176},{16,96},{32,208},{48,128},{64,240},{80,160},{96,16},{112,1... | collective-permute-start | bytes 196616 | tf_op jit(solution)/shard_map/ppermute | solution.py:292

commit v7 on v6

--- a/solution.py
+++ b/solution.py
@@ -203,7 +203,7 @@
     out[4 * BLK :] = jnp.full((16, HEAD), c, jnp.int32).astype(F32).astype(BF16)
 
 
-def pack_queries(pos, q_ref, lse_ref, o_ref, g_ref, q_out, g_out):
+def pack_queries(pos, q_ref, lse_ref, o_ref, g_ref, after_ref, q_out, g_out):
     wide = GROUP * HEAD
     swapped = pos[0] > pos[BLK]
     start = pl.multiple_of(jnp.where(swapped, BLK, 0), BLK)
@@ -235,7 +235,7 @@
             g_out[twin * n_heads + d, :, wide:] = tail
 
 
-def join(own_ref, u_ref, w_ref, q_ref, qx_ref, grad_ref, s_out, x_out):
+def join(own_ref, u_ref, w_ref, e_ref, q_ref, qx_ref, grad_ref, s_out, x_out):
     s_out[0] = own_ref[...]
     s_out[1] = u_ref[...]
     s_out[2] = w_ref[...]
@@ -292,6 +292,11 @@
     return lax.ppermute(x, "z", list(enumerate(to)))
 
 
+def half_round(x):
+    n = lax.axis_size("z")
+    return lax.ppermute(x, "z", [(i, (i + n // 2) % n) for i in range(n)])
+
+
 def swapped_with(x, axis):
     return lax.ppermute(x, axis, [(0, 1), (1, 0)])
 
@@ -326,20 +331,20 @@
     packed, block = (4 * BLK + 16, HEAD), (4 * BLK, HEAD)
     own = local_call(pack_keys, like(packed), 56, stream_in=True)(positions, keys, values)
     u, w = by_parity(own, 5), by_parity(own, -5)
+    e_one = half_round(own)
 
     own_q, send = local_call(
         pack_queries,
         (like((TOK, wide)), like((2 * n_heads, TOK // n_heads, wide))),
         56,
         stream_in=True,
-    )(positions, queries, lse.T, outputs, out_grad)
+    )(positions, queries, lse.T, outputs, out_grad, own)
     grad = lax.all_to_all(send, ("xh",) + HEADS, split_axis=0, concat_axis=0, tiled=True)
     other_q = swapped_with(own_q, "xh")
     s_set, x = local_call(
         join, (like((NEAR,) + packed), like((2, TOK, 2 * wide))), 8, stream_in=True
-    )(own, u, w, own_q, other_q, grad.reshape(2, TOK, wide))
+    )(own, u, w, e_one, own_q, other_q, grad.reshape(2, TOK, wide))
     p1, m1, p2, m2 = [by_parity(s_set, by) for by in (1, -1, 2, -2)]
-    e_one = by_parity(w, 3)
     y = swapped_with(x, "core")
 
     near, dq_shape = (NEAR,) + block, (2, TOK, GROUP * HEAD)

time: 119 us -> 118 us (level)
    ppermute x13 -> x12, starting transfers between devices: 60 us -> 45.9 us  [by_parity(): return lax.ppermute(x, 'z', list(enumerate(to)))]
    ppermute x0 -> x1, starting transfers between devices: none -> 13.9 us  [half_round(): return lax.ppermute(x, 'z', [(i, (i + n // 2) % n) for i in range(n)])]
    ppermute x13 -> x12, waiting for transfers between devices: 20.5 us -> 21 us  [by_parity(): return lax.ppermute(x, 'z', list(enumerate(to)))]
  transfers between devices with their start and end apart: 18 -> 18, of which waited for: 5 -> 5; matrix products, arithmetic and copies ran while one was open for 0% -> 0% of each run, Pallas kernels for 9% -> 8%
where the time goes in v7:
time: 118 us; the launch traced here: 116 us
  starting transfers between devices  80.3 us (68%)
  waiting for transfers between devices  21 us (18%)
  Pallas kernels  13.8 us (12%)
    ppermute x12, starting transfers between devices, by_parity(): return lax.ppermute(x, 'z', list(enumerate(to)))  45.9 us
    ppermute x12, waiting for transfers between devices, by_parity(): return lax.ppermute(x, 'z', list(enumerate(to)))  21 us
    ppermute x1, starting transfers between devices, half_round(): return lax.ppermute(x, 'z', [(i, (i + n // 2) % n) for i in range(n)])  13.9 us
    pallas_call x9, Pallas kernels, call(): pl.pallas_call(body, out_shape=out_shape, in_specs=[smem if a.dtype == jn...  13.8 us
    ppermute x4, starting transfers between devices, swapped_with(): return lax.ppermute(x, axis, [(0, 1), (1, 0)])  11.1 us
    all_to_all x1, starting transfers between devices, shards(): lax.all_to_all(send, ('xh',) + HEADS, split_axis=0, concat_axis=0, tiled=...  9.39 us
  transfers between devices with their start and end apart: 18, of which 5 were waited for; matrix products, arithmetic and copies ran while one was open for 0% of the time, Pallas kernels for 8%

profile of v7, /device:TPU:6, one launch (start us, length us, event | category | flops | bytes accessed | tf_op | source)
XLA Modules:
  0.0 116.0 jit_solution(16509657636165311456)
XLA Ops:
  0.6 1.4 %pack_keys.1.after_ref.own_ref = bf16[272,128]{1,0:T(8,128)(2,1)} custom-call(s32[128]{0:T(128)} %pos.3, bf16[128,128]{1,0:T(8,128)(2,1)} %k_ref.1, bf16[128,128]{1,0:T(8,128)(2,1)} %v_ref.1), custom_call_target="tpu_custom_call" | custom-call | tf_op jit(solution)/shard_map/pack_keys/pallas_call | solution.py:309
  2.1 2.2 %pack_queries.1 = (bf16[128,640]{1,0:T(8,128)(2,1)}, bf16[16,16,640]{2,1,0:T(8,128)(2,1)}) custom-call(s32[128]{0:T(128)} %pos.3, bf16[128,512]{1,0:T(8,128)(2,1)} %q_ref.1, f32[4,128]{1,0:T(4,128)} %bitcast.3, bf16[16,4096]{1,0:T(8,128)(2,1)} %o_ref.1, bf16[16,4096]{1,0:T(8,128)(2,1)} %g_ref.1, bf16[272,128]{1,0:T(8,128)(2,1)} %pack_keys.1.after_ref.own_ref), custom_call_target="tpu_custom_call" | custom-call | tf_op jit(solution)/shard_map/pack_queries/pallas_call | solution.py:309
  4.3 9.4 %all-to-all-start = ((bf16[16,16,640]{2,1,0:T(8,128)(2,1)}), bf16[16,16,640]{2,1,0:T(8,128)(2,1)S(1)}, u32[]{:S(2)}, u32[]{:S(2)}) async-start(bf16[16,16,640]{2,1,0:T(8,128)(2,1)} %get-tuple-element.25), calls=%async_computation | async-start | bytes 655360 | tf_op jit(solution)/shard_map/all_to_all | solution.py:342
  13.7 3.3 %collective-permute-start.3 = (bf16[128,640]{1,0:T(8,128)(2,1)S(1)}, bf16[128,640]{1,0:T(8,128)(2,1)S(1)}, u32[]{:S(2)}, u32[]{:S(2)}) collective-permute-start(bf16[128,640]{1,0:T(8,128)(2,1)S(1)} %copy-done.1), channel_id=1, source_target_pairs={{0,256},{256,0},{1,257},{257,1},{2,258},{258,2},{3,259},{259,3},{4... | collective-permute-start | bytes 491528 | tf_op jit(solution)/shard_map/ppermute | solution.py:301
  17.0 13.9 %collective-permute-start.2 = (bf16[272,128]{1,0:T(8,128)(2,1)S(1)}, bf16[272,128]{1,0:T(8,128)(2,1)S(1)}, u32[]{:S(2)}, u32[]{:S(2)}) collective-permute-start(bf16[272,128]{1,0:T(8,128)(2,1)S(1)} %copy-done), channel_id=1, source_target_pairs={{0,128},{16,144},{32,160},{48,176},{64,192},{80,208},{96,224},{112... | collective-permute-start | bytes 208904 | tf_op jit(solution)/shard_map/ppermute | solution.py:297
  31.0 1.9 %collective-permute-start.1 = (bf16[272,128]{1,0:T(8,128)(2,1)S(1)}, bf16[272,128]{1,0:T(8,128)(2,1)S(1)}, u32[]{:S(2)}, u32[]{:S(2)}) collective-permute-start(bf16[272,128]{1,0:T(8,128)(2,1)S(1)} %copy-done), channel_id=1, source_target_pairs={{0,176},{16,96},{32,208},{48,128},{64,240},{80,160},{96,16},{112,1... | collective-permute-start | bytes 208904 | tf_op jit(solution)/shard_map/ppermute | solution.py:292
  32.9 4.7 %collective-permute-start = (bf16[272,128]{1,0:T(8,128)(2,1)S(1)}, bf16[272,128]{1,0:T(8,128)(2,1)S(1)}, u32[]{:S(2)}, u32[]{:S(2)}) collective-permute-start(bf16[272,128]{1,0:T(8,128)(2,1)S(1)} %copy-done), channel_id=1, source_target_pairs={{0,80},{16,192},{32,112},{48,224},{64,144},{80,0},{96,176},{112,32... | collective-permute-start | bytes 208904 | tf_op jit(solution)/shard_map/ppermute | solution.py:292
  37.7 9.0 %collective-permute-done.1.w_ref = bf16[272,128]{1,0:T(8,128)(2,1)S(1)} collective-permute-done((bf16[272,128]{1,0:T(8,128)(2,1)S(1)}, bf16[272,128]{1,0:T(8,128)(2,1)S(1)}, u32[]{:S(2)}, u32[]{:S(2)}) %collective-permute-start.1) | collective-permute-done | bytes 69664 | tf_op jit(solution)/shard_map/ppermute | solution.py:292
  46.7 0.1 join.1
  46.8 1.9 %collective-permute-start.4 = (bf16[2,128,1280]{2,1,0:T(8,128)(2,1)S(1)}, bf16[2,128,1280]{2,1,0:T(8,128)(2,1)S(1)}, u32[]{:S(2)}, u32[]{:S(2)}) collective-permute-start(bf16[2,128,1280]{2,1,0:T(8,128)(2,1)S(1)} %get-tuple-element.26.x_ref), channel_id=1, source_target_pairs={{0,8},{8,0},{1,9},{9,1},{2,10},{10,2},{3,11},{11,3},{4,12},{12,4},... | collective-permute-start | bytes 1966088 | tf_op jit(solution)/shard_map/ppermute | solution.py:301
  48.7 1.9 %collective-permute-start.8 = (bf16[3,272,128]{2,1,0:T(8,128)(2,1)S(1)}, bf16[3,272,128]{2,1,0:T(8,128)(2,1)S(1)}, u32[]{:S(2)}, u32[]{:S(2)}) collective-permute-start(bf16[3,272,128]{2,1,0:T(8,128)(2,1)S(1)} %get-tuple-element.27.s_ref), channel_id=1, source_target_pairs={{0,224},{16,48},{32,0},{48,80},{64,32},{80,112},{96,64},{112,144},... | collective-permute-start | bytes 626696 | tf_op jit(solution)/shard_map/ppermute | solution.py:292
  50.7 4.8 %collective-permute-start.7 = (bf16[3,272,128]{2,1,0:T(8,128)(2,1)S(1)}, bf16[3,272,128]{2,1,0:T(8,128)(2,1)S(1)}, u32[]{:S(2)}, u32[]{:S(2)}) collective-permute-start(bf16[3,272,128]{2,1,0:T(8,128)(2,1)S(1)} %get-tuple-element.27.s_ref), channel_id=1, source_target_pairs={{0,32},{16,240},{32,64},{48,16},{64,96},{80,48},{96,128},{112,80},... | collective-permute-start | bytes 626696 | tf_op jit(solution)/shard_map/ppermute | solution.py:292
  55.5 5.3 %collective-permute-start.6 = (bf16[3,272,128]{2,1,0:T(8,128)(2,1)S(1)}, bf16[3,272,128]{2,1,0:T(8,128)(2,1)S(1)}, u32[]{:S(2)}, u32[]{:S(2)}) collective-permute-start(bf16[3,272,128]{2,1,0:T(8,128)(2,1)S(1)} %get-tuple-element.27.s_ref), channel_id=1, source_target_pairs={{0,240},{16,32},{32,16},{48,64},{64,48},{80,96},{96,80},{112,128},... | collective-permute-start | bytes 626696 | tf_op jit(solution)/shard_map/ppermute | solution.py:292
  60.8 2.2 %collective-permute-start.5 = (bf16[3,272,128]{2,1,0:T(8,128)(2,1)S(1)}, bf16[3,272,128]{2,1,0:T(8,128)(2,1)S(1)}, u32[]{:S(2)}, u32[]{:S(2)}) collective-permute-start(bf16[3,272,128]{2,1,0:T(8,128)(2,1)S(1)} %get-tuple-element.27.s_ref), channel_id=1, source_target_pairs={{0,16},{16,0},{32,48},{48,32},{64,80},{80,64},{96,112},{112,96},{1... | collective-permute-start | bytes 626696 | tf_op jit(solution)/shard_map/ppermute | solution.py:292
  63.0 3.8 %collective-permute-done.7.p_ref = bf16[3,272,128]{2,1,0:T(8,128)(2,1)S(1)} collective-permute-done((bf16[3,272,128]{2,1,0:T(8,128)(2,1)S(1)}, bf16[3,272,128]{2,1,0:T(8,128)(2,1)S(1)}, u32[]{:S(2)}, u32[]{:S(2)}) %collective-permute-start.7) | collective-permute-done | bytes 208928 | tf_op jit(solution)/shard_map/ppermute | solution.py:292
  66.8 3.8 %with_next.1 = (bf16[3,256,128]{2,1,0:T(8,128)(2,1)S(1)}, bf16[4,256,128]{2,1,0:T(8,128)(2,1)S(1)}, f32[4,128,512]{2,1,0:T(8,128)S(1)}) custom-call(bf16[2,128,1280]{2,1,0:T(8,128)(2,1)S(1)} %get-tuple-element.26.x_ref, bf16[2,128,1280]{2,1,0:T(8,128)(2,1)S(1)} %collective-permute-done.4.y_ref, bf16[3,272,128]{2,1,0:T(8,128)(2,1)S(1)} %collective-permute-done.7.p_ref, ...), custom_call_target="tpu_custom_call" | custom-call | tf_op jit(solution)/shard_map/with_next/pallas_call | solution.py:309
  70.6 3.4 %collective-permute-start.11 = (bf16[4,256,128]{2,1,0:T(8,128)(2,1)S(1)}, bf16[4,256,128]{2,1,0:T(8,128)(2,1)S(1)}, u32[]{:S(2)}, u32[]{:S(2)}) collective-permute-start(bf16[4,256,128]{2,1,0:T(8,128)(2,1)S(1)} %get-tuple-element.34), channel_id=1, source_target_pairs={{0,32},{16,240},{32,64},{48,16},{64,96},{80,48},{96,128},{112,80},... | collective-permute-start | bytes 786440 | tf_op jit(solution)/shard_map/ppermute | solution.py:292
  74.0 4.6 %collective-permute-start.10 = (bf16[3,256,128]{2,1,0:T(8,128)(2,1)S(1)}, bf16[3,256,128]{2,1,0:T(8,128)(2,1)S(1)}, u32[]{:S(2)}, u32[]{:S(2)}) collective-permute-start(bf16[3,256,128]{2,1,0:T(8,128)(2,1)S(1)} %get-tuple-element.33), channel_id=1, source_target_pairs={{0,224},{16,48},{32,0},{48,80},{64,32},{80,112},{96,64},{112,144},... | collective-permute-start | bytes 589832 | tf_op jit(solution)/shard_map/ppermute | solution.py:292
  78.6 5.2 %with_nearest.1 = (f32[3,256,128]{2,1,0:T(8,128)S(1)}, bf16[3,256,128]{2,1,0:T(8,128)(2,1)S(1)}, bf16[3,256,128]{2,1,0:T(8,128)(2,1)S(1)}, f32[2,128,512]{2,1,0:T(8,128)S(1)}, bf16[2,128,512]{2,1,0:T(8,128)(2,1)S(1)}) custom-call(bf16[2,128,1280]{2,1,0:T(8,128)(2,1)S(1)} %get-tuple-element.26.x_ref, bf16[2,128,1280]{2,1,0:T(8,128)(2,1)S(1)} %collective-permute-done.4.y_ref, ...), custom_call_target="tpu_custom_call" | custom-call | tf_op jit(solution)/shard_map/with_nearest/pallas_call | solution.py:309
  83.9 1.9 %collective-permute-start.9 = (bf16[2,128,512]{2,1,0:T(8,128)(2,1)S(1)}, bf16[2,128,512]{2,1,0:T(8,128)(2,1)S(1)}, u32[]{:S(2)}, u32[]{:S(2)}) collective-permute-start(bf16[2,128,512]{2,1,0:T(8,128)(2,1)S(1)} %get-tuple-element.30), channel_id=1, source_target_pairs={{0,8},{8,0},{1,9},{9,1},{2,10},{10,2},{3,11},{11,3},{4,12},{12,4},... | collective-permute-start | bytes 786440 | tf_op jit(solution)/shard_map/ppermute | solution.py:301
  85.8 0.1 sum_first.1
  85.9 4.6 %collective-permute-start.12 = (bf16[3,256,128]{2,1,0:T(8,128)(2,1)S(1)}, bf16[3,256,128]{2,1,0:T(8,128)(2,1)S(1)}, u32[]{:S(2)}, u32[]{:S(2)}) collective-permute-start(bf16[3,256,128]{2,1,0:T(8,128)(2,1)S(1)} %get-tuple-element.38), channel_id=1, source_target_pairs={{0,16},{16,0},{32,48},{48,32},{64,80},{80,64},{96,112},{112,96},{1... | collective-permute-start | bytes 589832 | tf_op jit(solution)/shard_map/ppermute | solution.py:292
  90.6 3.4 %collective-permute-start.13 = (bf16[3,256,128]{2,1,0:T(8,128)(2,1)S(1)}, bf16[3,256,128]{2,1,0:T(8,128)(2,1)S(1)}, u32[]{:S(2)}, u32[]{:S(2)}) collective-permute-start(bf16[3,256,128]{2,1,0:T(8,128)(2,1)S(1)} %get-tuple-element.39), channel_id=1, source_target_pairs={{0,240},{16,32},{32,16},{48,64},{64,48},{80,96},{96,80},{112,128},... | collective-permute-start | bytes 589832 | tf_op jit(solution)/shard_map/ppermute | solution.py:292
  94.0 0.1 sum_cores.1
  94.1 4.0 %collective-permute-start.16 = (bf16[128,512]{1,0:T(8,128)(2,1)S(1)}, bf16[128,512]{1,0:T(8,128)(2,1)S(1)}, u32[]{:S(2)}, u32[]{:S(2)}) collective-permute-start(bf16[128,512]{1,0:T(8,128)(2,1)S(1)} %get-tuple-element.44), channel_id=1, source_target_pairs={{0,256},{256,0},{1,257},{257,1},{2,258},{258,2},{3,259},{259,3},{4... | collective-permute-start | bytes 393224 | tf_op jit(solution)/shard_map/ppermute | solution.py:301
  98.1 2.1 %collective-permute-done.13.m_ref = bf16[3,256,128]{2,1,0:T(8,128)(2,1)S(1)} collective-permute-done((bf16[3,256,128]{2,1,0:T(8,128)(2,1)S(1)}, bf16[3,256,128]{2,1,0:T(8,128)(2,1)S(1)}, u32[]{:S(2)}, u32[]{:S(2)}) %collective-permute-start.13) | collective-permute-done | bytes 196640 | tf_op jit(solution)/shard_map/ppermute | solution.py:292
  100.2 0.1 sum_near.1
  100.3 2.8 %collective-permute-start.14 = (bf16[256,128]{1,0:T(8,128)(2,1)S(1)}, bf16[256,128]{1,0:T(8,128)(2,1)S(1)}, u32[]{:S(2)}, u32[]{:S(2)}) collective-permute-start(bf16[256,128]{1,0:T(8,128)(2,1)S(1)} %get-tuple-element.41), channel_id=1, source_target_pairs={{0,80},{16,192},{32,112},{48,224},{64,144},{80,0},{96,176},{112,32... | collective-permute-start | bytes 196616 | tf_op jit(solution)/shard_map/ppermute | solution.py:292
  103.1 6.2 %collective-permute-start.15 = (bf16[256,128]{1,0:T(8,128)(2,1)S(1)}, bf16[256,128]{1,0:T(8,128)(2,1)S(1)}, u32[]{:S(2)}, u32[]{:S(2)}) collective-permute-start(bf16[256,128]{1,0:T(8,128)(2,1)S(1)} %get-tuple-element.42), channel_id=1, source_target_pairs={{0,176},{16,96},{32,208},{48,128},{64,240},{80,160},{96,16},{112,1... | collective-permute-start | bytes 196616 | tf_op jit(solution)/shard_map/ppermute | solution.py:292
  109.3 2.9 %collective-permute-done.14.u_ref = bf16[256,128]{1,0:T(8,128)(2,1)S(1)} collective-permute-done((bf16[256,128]{1,0:T(8,128)(2,1)S(1)}, bf16[256,128]{1,0:T(8,128)(2,1)S(1)}, u32[]{:S(2)}, u32[]{:S(2)}) %collective-permute-start.14) | collective-permute-done | bytes 65568 | tf_op jit(solution)/shard_map/ppermute | solution.py:292
  112.2 3.1 %collective-permute-done.15.w_ref = bf16[256,128]{1,0:T(8,128)(2,1)S(1)} collective-permute-done((bf16[256,128]{1,0:T(8,128)(2,1)S(1)}, bf16[256,128]{1,0:T(8,128)(2,1)S(1)}, u32[]{:S(2)}, u32[]{:S(2)}) %collective-permute-start.15) | collective-permute-done | bytes 65568 | tf_op jit(solution)/shard_map/ppermute | solution.py:292
  115.3 0.7 finish.1
  (17 shorter events, 0.0 us)
Async XLA Ops:
  4.3 9.4 %copy-start.1 = (bf16[128,640]{1,0:T(8,128)(2,1)S(1)}, bf16[128,640]{1,0:T(8,128)(2,1)}, u32[]{:S(2)}) copy-start(bf16[128,640]{1,0:T(8,128)(2,1)} %get-tuple-element.24.q_ref) | copy-start | bytes 491524
  4.3 12.7 %copy-start = (bf16[272,128]{1,0:T(8,128)(2,1)S(1)}, bf16[272,128]{1,0:T(8,128)(2,1)}, u32[]{:S(2)}) copy-start(bf16[272,128]{1,0:T(8,128)(2,1)} %pack_keys.1.after_ref.own_ref) | copy-start | bytes 208900
  4.3 42.4 %all-to-all-start = ((bf16[16,16,640]{2,1,0:T(8,128)(2,1)}), bf16[16,16,640]{2,1,0:T(8,128)(2,1)S(1)}, u32[]{:S(2)}, u32[]{:S(2)}) async-start(bf16[16,16,640]{2,1,0:T(8,128)(2,1)} %get-tuple-element.25), calls=%async_computation | async-start | bytes 655360 | tf_op jit(solution)/shard_map/all_to_all | solution.py:342
  13.7 33.0 %collective-permute-start.3 = (bf16[128,640]{1,0:T(8,128)(2,1)S(1)}, bf16[128,640]{1,0:T(8,128)(2,1)S(1)}, u32[]{:S(2)}, u32[]{:S(2)}) collective-permute-start(bf16[128,640]{1,0:T(8,128)(2,1)S(1)} %copy-done.1), channel_id=1, source_target_pairs={{0,256},{256,0},{1,257},{257,1},{2,258},{258,2},{3,259},{259,3},{4... | collective-permute-start | bytes 491528 | tf_op jit(solution)/shard_map/ppermute | solution.py:301
  17.0 20.6 %collective-permute-start.2 = (bf16[272,128]{1,0:T(8,128)(2,1)S(1)}, bf16[272,128]{1,0:T(8,128)(2,1)S(1)}, u32[]{:S(2)}, u32[]{:S(2)}) collective-permute-start(bf16[272,128]{1,0:T(8,128)(2,1)S(1)} %copy-done), channel_id=1, source_target_pairs={{0,128},{16,144},{32,160},{48,176},{64,192},{80,208},{96,224},{112... | collective-permute-start | bytes 208904 | tf_op jit(solution)/shard_map/ppermute | solution.py:297
  31.0 15.7 %collective-permute-start.1 = (bf16[272,128]{1,0:T(8,128)(2,1)S(1)}, bf16[272,128]{1,0:T(8,128)(2,1)S(1)}, u32[]{:S(2)}, u32[]{:S(2)}) collective-permute-start(bf16[272,128]{1,0:T(8,128)(2,1)S(1)} %copy-done), channel_id=1, source_target_pairs={{0,176},{16,96},{32,208},{48,128},{64,240},{80,160},{96,16},{112,1... | collective-permute-start | bytes 208904 | tf_op jit(solution)/shard_map/ppermute | solution.py:292
  32.9 13.8 %collective-permute-start = (bf16[272,128]{1,0:T(8,128)(2,1)S(1)}, bf16[272,128]{1,0:T(8,128)(2,1)S(1)}, u32[]{:S(2)}, u32[]{:S(2)}) collective-permute-start(bf16[272,128]{1,0:T(8,128)(2,1)S(1)} %copy-done), channel_id=1, source_target_pairs={{0,80},{16,192},{32,112},{48,224},{64,144},{80,0},{96,176},{112,32... | collective-permute-start | bytes 208904 | tf_op jit(solution)/shard_map/ppermute | solution.py:292
  46.8 20.0 %collective-permute-start.4 = (bf16[2,128,1280]{2,1,0:T(8,128)(2,1)S(1)}, bf16[2,128,1280]{2,1,0:T(8,128)(2,1)S(1)}, u32[]{:S(2)}, u32[]{:S(2)}) collective-permute-start(bf16[2,128,1280]{2,1,0:T(8,128)(2,1)S(1)} %get-tuple-element.26.x_ref), channel_id=1, source_target_pairs={{0,8},{8,0},{1,9},{9,1},{2,10},{10,2},{3,11},{11,3},{4,12},{12,4},... | collective-permute-start | bytes 1966088 | tf_op jit(solution)/shard_map/ppermute | solution.py:301
  48.7 14.3 %collective-permute-start.8 = (bf16[3,272,128]{2,1,0:T(8,128)(2,1)S(1)}, bf16[3,272,128]{2,1,0:T(8,128)(2,1)S(1)}, u32[]{:S(2)}, u32[]{:S(2)}) collective-permute-start(bf16[3,272,128]{2,1,0:T(8,128)(2,1)S(1)} %get-tuple-element.27.s_ref), channel_id=1, source_target_pairs={{0,224},{16,48},{32,0},{48,80},{64,32},{80,112},{96,64},{112,144},... | collective-permute-start | bytes 626696 | tf_op jit(solution)/shard_map/ppermute | solution.py:292
  50.7 16.1 %collective-permute-start.7 = (bf16[3,272,128]{2,1,0:T(8,128)(2,1)S(1)}, bf16[3,272,128]{2,1,0:T(8,128)(2,1)S(1)}, u32[]{:S(2)}, u32[]{:S(2)}) collective-permute-start(bf16[3,272,128]{2,1,0:T(8,128)(2,1)S(1)} %get-tuple-element.27.s_ref), channel_id=1, source_target_pairs={{0,32},{16,240},{32,64},{48,16},{64,96},{80,48},{96,128},{112,80},... | collective-permute-start | bytes 626696 | tf_op jit(solution)/shard_map/ppermute | solution.py:292
  55.5 23.1 %collective-permute-start.6 = (bf16[3,272,128]{2,1,0:T(8,128)(2,1)S(1)}, bf16[3,272,128]{2,1,0:T(8,128)(2,1)S(1)}, u32[]{:S(2)}, u32[]{:S(2)}) collective-permute-start(bf16[3,272,128]{2,1,0:T(8,128)(2,1)S(1)} %get-tuple-element.27.s_ref), channel_id=1, source_target_pairs={{0,240},{16,32},{32,16},{48,64},{64,48},{80,96},{96,80},{112,128},... | collective-permute-start | bytes 626696 | tf_op jit(solution)/shard_map/ppermute | solution.py:292
  60.8 17.8 %collective-permute-start.5 = (bf16[3,272,128]{2,1,0:T(8,128)(2,1)S(1)}, bf16[3,272,128]{2,1,0:T(8,128)(2,1)S(1)}, u32[]{:S(2)}, u32[]{:S(2)}) collective-permute-start(bf16[3,272,128]{2,1,0:T(8,128)(2,1)S(1)} %get-tuple-element.27.s_ref), channel_id=1, source_target_pairs={{0,16},{16,0},{32,48},{48,32},{64,80},{80,64},{96,112},{112,96},{1... | collective-permute-start | bytes 626696 | tf_op jit(solution)/shard_map/ppermute | solution.py:292
  70.6 15.2 %collective-permute-start.11 = (bf16[4,256,128]{2,1,0:T(8,128)(2,1)S(1)}, bf16[4,256,128]{2,1,0:T(8,128)(2,1)S(1)}, u32[]{:S(2)}, u32[]{:S(2)}) collective-permute-start(bf16[4,256,128]{2,1,0:T(8,128)(2,1)S(1)} %get-tuple-element.34), channel_id=1, source_target_pairs={{0,32},{16,240},{32,64},{48,16},{64,96},{80,48},{96,128},{112,80},... | collective-permute-start | bytes 786440 | tf_op jit(solution)/shard_map/ppermute | solution.py:292
  74.0 11.8 %collective-permute-start.10 = (bf16[3,256,128]{2,1,0:T(8,128)(2,1)S(1)}, bf16[3,256,128]{2,1,0:T(8,128)(2,1)S(1)}, u32[]{:S(2)}, u32[]{:S(2)}) collective-permute-start(bf16[3,256,128]{2,1,0:T(8,128)(2,1)S(1)} %get-tuple-element.33), channel_id=1, source_target_pairs={{0,224},{16,48},{32,0},{48,80},{64,32},{80,112},{96,64},{112,144},... | collective-permute-start | bytes 589832 | tf_op jit(solution)/shard_map/ppermute | solution.py:292
  83.9 10.1 %collective-permute-start.9 = (bf16[2,128,512]{2,1,0:T(8,128)(2,1)S(1)}, bf16[2,128,512]{2,1,0:T(8,128)(2,1)S(1)}, u32[]{:S(2)}, u32[]{:S(2)}) collective-permute-start(bf16[2,128,512]{2,1,0:T(8,128)(2,1)S(1)} %get-tuple-element.30), channel_id=1, source_target_pairs={{0,8},{8,0},{1,9},{9,1},{2,10},{10,2},{3,11},{11,3},{4,12},{12,4},... | collective-permute-start | bytes 786440 | tf_op jit(solution)/shard_map/ppermute | solution.py:301
  85.9 12.1 %collective-permute-start.12 = (bf16[3,256,128]{2,1,0:T(8,128)(2,1)S(1)}, bf16[3,256,128]{2,1,0:T(8,128)(2,1)S(1)}, u32[]{:S(2)}, u32[]{:S(2)}) collective-permute-start(bf16[3,256,128]{2,1,0:T(8,128)(2,1)S(1)} %get-tuple-element.38), channel_id=1, source_target_pairs={{0,16},{16,0},{32,48},{48,32},{64,80},{80,64},{96,112},{112,96},{1... | collective-permute-start | bytes 589832 | tf_op jit(solution)/shard_map/ppermute | solution.py:292
  90.6 9.6 %collective-permute-start.13 = (bf16[3,256,128]{2,1,0:T(8,128)(2,1)S(1)}, bf16[3,256,128]{2,1,0:T(8,128)(2,1)S(1)}, u32[]{:S(2)}, u32[]{:S(2)}) collective-permute-start(bf16[3,256,128]{2,1,0:T(8,128)(2,1)S(1)} %get-tuple-element.39), channel_id=1, source_target_pairs={{0,240},{16,32},{32,16},{48,64},{64,48},{80,96},{96,80},{112,128},... | collective-permute-start | bytes 589832 | tf_op jit(solution)/shard_map/ppermute | solution.py:292
  94.1 15.2 %collective-permute-start.16 = (bf16[128,512]{1,0:T(8,128)(2,1)S(1)}, bf16[128,512]{1,0:T(8,128)(2,1)S(1)}, u32[]{:S(2)}, u32[]{:S(2)}) collective-permute-start(bf16[128,512]{1,0:T(8,128)(2,1)S(1)} %get-tuple-element.44), channel_id=1, source_target_pairs={{0,256},{256,0},{1,257},{257,1},{2,258},{258,2},{3,259},{259,3},{4... | collective-permute-start | bytes 393224 | tf_op jit(solution)/shard_map/ppermute | solution.py:301
  100.3 12.0 %collective-permute-start.14 = (bf16[256,128]{1,0:T(8,128)(2,1)S(1)}, bf16[256,128]{1,0:T(8,128)(2,1)S(1)}, u32[]{:S(2)}, u32[]{:S(2)}) collective-permute-start(bf16[256,128]{1,0:T(8,128)(2,1)S(1)} %get-tuple-element.41), channel_id=1, source_target_pairs={{0,80},{16,192},{32,112},{48,224},{64,144},{80,0},{96,176},{112,32... | collective-permute-start | bytes 196616 | tf_op jit(solution)/shard_map/ppermute | solution.py:292
  103.1 12.2 %collective-permute-start.15 = (bf16[256,128]{1,0:T(8,128)(2,1)S(1)}, bf16[256,128]{1,0:T(8,128)(2,1)S(1)}, u32[]{:S(2)}, u32[]{:S(2)}) collective-permute-start(bf16[256,128]{1,0:T(8,128)(2,1)S(1)} %get-tuple-element.42), channel_id=1, source_target_pairs={{0,176},{16,96},{32,208},{48,128},{64,240},{80,160},{96,16},{112,1... | collective-permute-start | bytes 196616 | tf_op jit(solution)/shard_map/ppermute | solution.py:292

commit v8 on v7

--- a/solution.py
+++ b/solution.py
@@ -203,7 +203,7 @@
     out[4 * BLK :] = jnp.full((16, HEAD), c, jnp.int32).astype(F32).astype(BF16)
 
 
-def pack_queries(pos, q_ref, lse_ref, o_ref, g_ref, after_ref, q_out, g_out):
+def pack_queries(pos, q_ref, lse_ref, o_ref, g_ref, u_ref, w_ref, q_out, g_out):
     wide = GROUP * HEAD
     swapped = pos[0] > pos[BLK]
     start = pl.multiple_of(jnp.where(swapped, BLK, 0), BLK)
@@ -292,11 +292,6 @@
     return lax.ppermute(x, "z", list(enumerate(to)))
 
 
-def half_round(x):
-    n = lax.axis_size("z")
-    return lax.ppermute(x, "z", [(i, (i + n // 2) % n) for i in range(n)])
-
-
 def swapped_with(x, axis):
     return lax.ppermute(x, axis, [(0, 1), (1, 0)])
 
@@ -331,14 +326,14 @@
     packed, block = (4 * BLK + 16, HEAD), (4 * BLK, HEAD)
     own = local_call(pack_keys, like(packed), 56, stream_in=True)(positions, keys, values)
     u, w = by_parity(own, 5), by_parity(own, -5)
-    e_one = half_round(own)
+    e_one = by_parity(w, 3)
 
     own_q, send = local_call(
         pack_queries,
         (like((TOK, wide)), like((2 * n_heads, TOK // n_heads, wide))),
-        56,
+        8,
         stream_in=True,
-    )(positions, queries, lse.T, outputs, out_grad, own)
+    )(positions, queries, lse.T, outputs, out_grad, u, w)
     grad = lax.all_to_all(send, ("xh",) + HEADS, split_axis=0, concat_axis=0, tiled=True)
     other_q = swapped_with(own_q, "xh")
     s_set, x = local_call(

time: 118 us -> 121 us (1.025)
  waiting for transfers between devices: 21 us -> 25.8 us
  starting transfers between devices: 80.3 us -> 77.5 us
  local copies, waits for them, and re-layouts: 0.01 us -> 1.82 us
    ppermute x1 -> x0, starting transfers between devices: 13.9 us -> none  [half_round(): return lax.ppermute(x, 'z', [(i, (i + n // 2) % n) for i in range(n)])]
    ppermute x12 -> x13, starting transfers between devices: 45.9 us -> 58.8 us  [by_parity(): return lax.ppermute(x, 'z', list(enumerate(to)))]
    ppermute x12 -> x13, waiting for transfers between devices: 21 us -> 25.8 us  [by_parity(): return lax.ppermute(x, 'z', list(enumerate(to)))]
    all_to_all x1, starting transfers between devices: 9.39 us -> 7.56 us  [shards(): lax.all_to_all(send, ('xh',) + HEADS, split_axis=0, concat_axis=0, tiled=...]
    unnamed x4 -> x12, local copies, waits for them, and re-layouts: 0.01 us -> 1.82 us
  transfers between devices with their start and end apart: 18 -> 18, of which waited for: 5 -> 7; matrix products, arithmetic and copies ran while one was open for 0% -> 0% of each run, Pallas kernels for 8% -> 8%
where the time goes in v8:
time: 121 us; the launch traced here: 119 us
  starting transfers between devices  77.5 us (64%)
  waiting for transfers between devices  25.8 us (21%)
  Pallas kernels  13.2 us (11%)
  local copies, waits for them, and re-layouts  1.82 us (2%)
    ppermute x13, starting transfers between devices, by_parity(): return lax.ppermute(x, 'z', list(enumerate(to)))  58.8 us
    ppermute x13, waiting for transfers between devices, by_parity(): return lax.ppermute(x, 'z', list(enumerate(to)))  25.8 us
    pallas_call x9, Pallas kernels, call(): pl.pallas_call(body, out_shape=out_shape, in_specs=[smem if a.dtype == jn...  13.2 us
    ppermute x4, starting transfers between devices, swapped_with(): return lax.ppermute(x, axis, [(0, 1), (1, 0)])  11.2 us
    all_to_all x1, starting transfers between devices, shards(): lax.all_to_all(send, ('xh',) + HEADS, split_axis=0, concat_axis=0, tiled=...  7.56 us
  transfers between devices with their start and end apart: 18, of which 7 were waited for; matrix products, arithmetic and copies ran while one was open for 0% of the time, Pallas kernels for 8%

profile of v8, /device:TPU:6, one launch (start us, length us, event | category | flops | bytes accessed | tf_op | source)
XLA Modules:
  0.0 119.2 jit_solution(15675010405424202776)
XLA Ops:
  0.7 1.5 %pack_keys.1.own_ref = bf16[272,128]{1,0:T(8,128)(2,1)} custom-call(s32[128]{0:T(128)} %pos.3, bf16[128,128]{1,0:T(8,128)(2,1)} %k_ref.1, bf16[128,128]{1,0:T(8,128)(2,1)} %v_ref.1), custom_call_target="tpu_custom_call" | custom-call | tf_op jit(solution)/shard_map/pack_keys/pallas_call | solution.py:304
  2.1 14.5 %collective-permute-start.1 = (bf16[272,128]{1,0:T(8,128)(2,1)}, bf16[272,128]{1,0:T(8,128)(2,1)S(1)}, u32[]{:S(2)}, u32[]{:S(2)}) collective-permute-start(bf16[272,128]{1,0:T(8,128)(2,1)} %pack_keys.1.own_ref), channel_id=1, source_target_pairs={{0,176},{16,96},{32,208},{48,128},{64,240},{80,160},{96,16},{112,1... | collective-permute-start | bytes 208904 | tf_op jit(solution)/shard_map/ppermute | solution.py:292
  16.6 4.7 %collective-permute-start = (bf16[272,128]{1,0:T(8,128)(2,1)}, bf16[272,128]{1,0:T(8,128)(2,1)S(1)}, u32[]{:S(2)}, u32[]{:S(2)}) collective-permute-start(bf16[272,128]{1,0:T(8,128)(2,1)} %pack_keys.1.own_ref), channel_id=1, source_target_pairs={{0,80},{16,192},{32,112},{48,224},{64,144},{80,0},{96,176},{112,32... | collective-permute-start | bytes 208904 | tf_op jit(solution)/shard_map/ppermute | solution.py:292
  21.4 7.3 %collective-permute-done.u_ref = bf16[272,128]{1,0:T(8,128)(2,1)S(1)} collective-permute-done((bf16[272,128]{1,0:T(8,128)(2,1)}, bf16[272,128]{1,0:T(8,128)(2,1)S(1)}, u32[]{:S(2)}, u32[]{:S(2)}) %collective-permute-start) | collective-permute-done | bytes 69664 | tf_op jit(solution)/shard_map/ppermute | solution.py:292
  28.7 0.9 copy-done.2
  29.6 0.9 copy-done.3
  30.5 1.7 %pack_queries.1 = (bf16[128,640]{1,0:T(8,128)(2,1)S(1)}, bf16[16,16,640]{2,1,0:T(8,128)(2,1)}) custom-call(s32[128]{0:T(128)S(1)} %copy-done.5, bf16[128,512]{1,0:T(8,128)(2,1)S(1)} %copy-done.1, f32[4,128]{1,0:T(4,128)S(1)} %bitcast.3, bf16[16,4096]{1,0:T(8,128)(2,1)S(1)} %copy-done.2, bf16[16,4096]{1,0:T(8,128)(2,1)S(1)} %copy-done.3, ...), custom_call_target="tpu_custom_call" | custom-call | tf_op jit(solution)/shard_map/pack_queries/pallas_call | solution.py:304
  32.2 7.6 %all-to-all-start = ((bf16[16,16,640]{2,1,0:T(8,128)(2,1)}), bf16[16,16,640]{2,1,0:T(8,128)(2,1)S(1)}, u32[]{:S(2)}, u32[]{:S(2)}) async-start(bf16[16,16,640]{2,1,0:T(8,128)(2,1)} %get-tuple-element.25), calls=%async_computation | async-start | bytes 655360 | tf_op jit(solution)/shard_map/all_to_all | solution.py:337
  39.8 3.4 %collective-permute-start.3 = (bf16[128,640]{1,0:T(8,128)(2,1)S(1)}, bf16[128,640]{1,0:T(8,128)(2,1)S(1)}, u32[]{:S(2)}, u32[]{:S(2)}) collective-permute-start(bf16[128,640]{1,0:T(8,128)(2,1)S(1)} %get-tuple-element.24.q_ref), channel_id=1, source_target_pairs={{0,256},{256,0},{1,257},{257,1},{2,258},{258,2},{3,259},{259,3},{4... | collective-permute-start | bytes 491528 | tf_op jit(solution)/shard_map/ppermute | solution.py:296
  43.1 4.1 %collective-permute-start.2 = (bf16[272,128]{1,0:T(8,128)(2,1)S(1)}, bf16[272,128]{1,0:T(8,128)(2,1)S(1)}, u32[]{:S(2)}, u32[]{:S(2)}) collective-permute-start(bf16[272,128]{1,0:T(8,128)(2,1)S(1)} %collective-permute-done.1.w_ref), channel_id=1, source_target_pairs={{0,48},{16,224},{32,80},{48,0},{64,112},{80,32},{96,144},{112,64},... | collective-permute-start | bytes 208904 | tf_op jit(solution)/shard_map/ppermute | solution.py:292
  47.3 4.6 %collective-permute-done.2.e_ref = bf16[272,128]{1,0:T(8,128)(2,1)S(1)} collective-permute-done((bf16[272,128]{1,0:T(8,128)(2,1)S(1)}, bf16[272,128]{1,0:T(8,128)(2,1)S(1)}, u32[]{:S(2)}, u32[]{:S(2)}) %collective-permute-start.2) | collective-permute-done | bytes 69664 | tf_op jit(solution)/shard_map/ppermute | solution.py:292
  52.0 1.9 %collective-permute-start.4 = (bf16[2,128,1280]{2,1,0:T(8,128)(2,1)S(1)}, bf16[2,128,1280]{2,1,0:T(8,128)(2,1)S(1)}, u32[]{:S(2)}, u32[]{:S(2)}) collective-permute-start(bf16[2,128,1280]{2,1,0:T(8,128)(2,1)S(1)} %get-tuple-element.26.x_ref), channel_id=1, source_target_pairs={{0,8},{8,0},{1,9},{9,1},{2,10},{10,2},{3,11},{11,3},{4,12},{12,4},... | collective-permute-start | bytes 1966088 | tf_op jit(solution)/shard_map/ppermute | solution.py:296
  53.9 6.2 %collective-permute-start.8 = (bf16[3,272,128]{2,1,0:T(8,128)(2,1)S(1)}, bf16[3,272,128]{2,1,0:T(8,128)(2,1)S(1)}, u32[]{:S(2)}, u32[]{:S(2)}) collective-permute-start(bf16[3,272,128]{2,1,0:T(8,128)(2,1)S(1)} %get-tuple-element.27.s_ref), channel_id=1, source_target_pairs={{0,224},{16,48},{32,0},{48,80},{64,32},{80,112},{96,64},{112,144},... | collective-permute-start | bytes 626696 | tf_op jit(solution)/shard_map/ppermute | solution.py:292
  60.1 1.9 %collective-permute-start.7 = (bf16[3,272,128]{2,1,0:T(8,128)(2,1)S(1)}, bf16[3,272,128]{2,1,0:T(8,128)(2,1)S(1)}, u32[]{:S(2)}, u32[]{:S(2)}) collective-permute-start(bf16[3,272,128]{2,1,0:T(8,128)(2,1)S(1)} %get-tuple-element.27.s_ref), channel_id=1, source_target_pairs={{0,32},{16,240},{32,64},{48,16},{64,96},{80,48},{96,128},{112,80},... | collective-permute-start | bytes 626696 | tf_op jit(solution)/shard_map/ppermute | solution.py:292
  62.1 1.9 %collective-permute-start.6 = (bf16[3,272,128]{2,1,0:T(8,128)(2,1)S(1)}, bf16[3,272,128]{2,1,0:T(8,128)(2,1)S(1)}, u32[]{:S(2)}, u32[]{:S(2)}) collective-permute-start(bf16[3,272,128]{2,1,0:T(8,128)(2,1)S(1)} %get-tuple-element.27.s_ref), channel_id=1, source_target_pairs={{0,240},{16,32},{32,16},{48,64},{64,48},{80,96},{96,80},{112,128},... | collective-permute-start | bytes 626696 | tf_op jit(solution)/shard_map/ppermute | solution.py:292
  64.0 2.5 %collective-permute-start.5 = (bf16[3,272,128]{2,1,0:T(8,128)(2,1)S(1)}, bf16[3,272,128]{2,1,0:T(8,128)(2,1)S(1)}, u32[]{:S(2)}, u32[]{:S(2)}) collective-permute-start(bf16[3,272,128]{2,1,0:T(8,128)(2,1)S(1)} %get-tuple-element.27.s_ref), channel_id=1, source_target_pairs={{0,16},{16,0},{32,48},{48,32},{64,80},{80,64},{96,112},{112,96},{1... | collective-permute-start | bytes 626696 | tf_op jit(solution)/shard_map/ppermute | solution.py:292
  66.5 3.6 %collective-permute-done.8.m_ref = bf16[3,272,128]{2,1,0:T(8,128)(2,1)S(1)} collective-permute-done((bf16[3,272,128]{2,1,0:T(8,128)(2,1)S(1)}, bf16[3,272,128]{2,1,0:T(8,128)(2,1)S(1)}, u32[]{:S(2)}, u32[]{:S(2)}) %collective-permute-start.8) | collective-permute-done | bytes 208928 | tf_op jit(solution)/shard_map/ppermute | solution.py:292
  70.1 1.7 %collective-permute-done.7.p_ref = bf16[3,272,128]{2,1,0:T(8,128)(2,1)S(1)} collective-permute-done((bf16[3,272,128]{2,1,0:T(8,128)(2,1)S(1)}, bf16[3,272,128]{2,1,0:T(8,128)(2,1)S(1)}, u32[]{:S(2)}, u32[]{:S(2)}) %collective-permute-start.7) | collective-permute-done | bytes 208928 | tf_op jit(solution)/shard_map/ppermute | solution.py:292
  71.8 3.8 %with_next.1 = (bf16[3,256,128]{2,1,0:T(8,128)(2,1)S(1)}, bf16[4,256,128]{2,1,0:T(8,128)(2,1)S(1)}, f32[4,128,512]{2,1,0:T(8,128)S(1)}) custom-call(bf16[2,128,1280]{2,1,0:T(8,128)(2,1)S(1)} %get-tuple-element.26.x_ref, bf16[2,128,1280]{2,1,0:T(8,128)(2,1)S(1)} %collective-permute-done.4.y_ref, bf16[3,272,128]{2,1,0:T(8,128)(2,1)S(1)} %collective-permute-done.7.p_ref, ...), custom_call_target="tpu_custom_call" | custom-call | tf_op jit(solution)/shard_map/with_next/pallas_call | solution.py:304
  75.6 1.9 %collective-permute-start.11 = (bf16[4,256,128]{2,1,0:T(8,128)(2,1)S(1)}, bf16[4,256,128]{2,1,0:T(8,128)(2,1)S(1)}, u32[]{:S(2)}, u32[]{:S(2)}) collective-permute-start(bf16[4,256,128]{2,1,0:T(8,128)(2,1)S(1)} %get-tuple-element.34), channel_id=1, source_target_pairs={{0,32},{16,240},{32,64},{48,16},{64,96},{80,48},{96,128},{112,80},... | collective-permute-start | bytes 786440 | tf_op jit(solution)/shard_map/ppermute | solution.py:292
  77.6 6.0 %collective-permute-start.10 = (bf16[3,256,128]{2,1,0:T(8,128)(2,1)S(1)}, bf16[3,256,128]{2,1,0:T(8,128)(2,1)S(1)}, u32[]{:S(2)}, u32[]{:S(2)}) collective-permute-start(bf16[3,256,128]{2,1,0:T(8,128)(2,1)S(1)} %get-tuple-element.33), channel_id=1, source_target_pairs={{0,224},{16,48},{32,0},{48,80},{64,32},{80,112},{96,64},{112,144},... | collective-permute-start | bytes 589832 | tf_op jit(solution)/shard_map/ppermute | solution.py:292
  83.6 5.2 %with_nearest.1 = (f32[3,256,128]{2,1,0:T(8,128)S(1)}, bf16[3,256,128]{2,1,0:T(8,128)(2,1)S(1)}, bf16[3,256,128]{2,1,0:T(8,128)(2,1)S(1)}, f32[2,128,512]{2,1,0:T(8,128)S(1)}, bf16[2,128,512]{2,1,0:T(8,128)(2,1)S(1)}) custom-call(bf16[2,128,1280]{2,1,0:T(8,128)(2,1)S(1)} %get-tuple-element.26.x_ref, bf16[2,128,1280]{2,1,0:T(8,128)(2,1)S(1)} %collective-permute-done.4.y_ref, ...), custom_call_target="tpu_custom_call" | custom-call | tf_op jit(solution)/shard_map/with_nearest/pallas_call | solution.py:304
  88.8 1.9 %collective-permute-start.9 = (bf16[2,128,512]{2,1,0:T(8,128)(2,1)S(1)}, bf16[2,128,512]{2,1,0:T(8,128)(2,1)S(1)}, u32[]{:S(2)}, u32[]{:S(2)}) collective-permute-start(bf16[2,128,512]{2,1,0:T(8,128)(2,1)S(1)} %get-tuple-element.30), channel_id=1, source_target_pairs={{0,8},{8,0},{1,9},{9,1},{2,10},{10,2},{3,11},{11,3},{4,12},{12,4},... | collective-permute-start | bytes 786440 | tf_op jit(solution)/shard_map/ppermute | solution.py:296
  90.9 3.7 %collective-permute-start.12 = (bf16[3,256,128]{2,1,0:T(8,128)(2,1)S(1)}, bf16[3,256,128]{2,1,0:T(8,128)(2,1)S(1)}, u32[]{:S(2)}, u32[]{:S(2)}) collective-permute-start(bf16[3,256,128]{2,1,0:T(8,128)(2,1)S(1)} %get-tuple-element.38), channel_id=1, source_target_pairs={{0,16},{16,0},{32,48},{48,32},{64,80},{80,64},{96,112},{112,96},{1... | collective-permute-start | bytes 589832 | tf_op jit(solution)/shard_map/ppermute | solution.py:292
  94.6 2.9 %collective-permute-start.13 = (bf16[3,256,128]{2,1,0:T(8,128)(2,1)S(1)}, bf16[3,256,128]{2,1,0:T(8,128)(2,1)S(1)}, u32[]{:S(2)}, u32[]{:S(2)}) collective-permute-start(bf16[3,256,128]{2,1,0:T(8,128)(2,1)S(1)} %get-tuple-element.39), channel_id=1, source_target_pairs={{0,240},{16,32},{32,16},{48,64},{64,48},{80,96},{96,80},{112,128},... | collective-permute-start | bytes 589832 | tf_op jit(solution)/shard_map/ppermute | solution.py:292
  97.6 4.0 %collective-permute-start.16 = (bf16[128,512]{1,0:T(8,128)(2,1)S(1)}, bf16[128,512]{1,0:T(8,128)(2,1)S(1)}, u32[]{:S(2)}, u32[]{:S(2)}) collective-permute-start(bf16[128,512]{1,0:T(8,128)(2,1)S(1)} %get-tuple-element.44), channel_id=1, source_target_pairs={{0,256},{256,0},{1,257},{257,1},{2,258},{258,2},{3,259},{259,3},{4... | collective-permute-start | bytes 393224 | tf_op jit(solution)/shard_map/ppermute | solution.py:296
  101.6 2.7 %collective-permute-done.13.m_ref = bf16[3,256,128]{2,1,0:T(8,128)(2,1)S(1)} collective-permute-done((bf16[3,256,128]{2,1,0:T(8,128)(2,1)S(1)}, bf16[3,256,128]{2,1,0:T(8,128)(2,1)S(1)}, u32[]{:S(2)}, u32[]{:S(2)}) %collective-permute-start.13) | collective-permute-done | bytes 196640 | tf_op jit(solution)/shard_map/ppermute | solution.py:292
  104.3 2.0 %collective-permute-start.14 = (bf16[256,128]{1,0:T(8,128)(2,1)S(1)}, bf16[256,128]{1,0:T(8,128)(2,1)S(1)}, u32[]{:S(2)}, u32[]{:S(2)}) collective-permute-start(bf16[256,128]{1,0:T(8,128)(2,1)S(1)} %get-tuple-element.41), channel_id=1, source_target_pairs={{0,80},{16,192},{32,112},{48,224},{64,144},{80,0},{96,176},{112,32... | collective-permute-start | bytes 196616 | tf_op jit(solution)/shard_map/ppermute | solution.py:292
  106.3 6.4 %collective-permute-start.15 = (bf16[256,128]{1,0:T(8,128)(2,1)S(1)}, bf16[256,128]{1,0:T(8,128)(2,1)S(1)}, u32[]{:S(2)}, u32[]{:S(2)}) collective-permute-start(bf16[256,128]{1,0:T(8,128)(2,1)S(1)} %get-tuple-element.42), channel_id=1, source_target_pairs={{0,176},{16,96},{32,208},{48,128},{64,240},{80,160},{96,16},{112,1... | collective-permute-start | bytes 196616 | tf_op jit(solution)/shard_map/ppermute | solution.py:292
  112.7 3.8 %collective-permute-done.14.u_ref = bf16[256,128]{1,0:T(8,128)(2,1)S(1)} collective-permute-done((bf16[256,128]{1,0:T(8,128)(2,1)S(1)}, bf16[256,128]{1,0:T(8,128)(2,1)S(1)}, u32[]{:S(2)}, u32[]{:S(2)}) %collective-permute-start.14) | collective-permute-done | bytes 65568 | tf_op jit(solution)/shard_map/ppermute | solution.py:292
  116.5 2.0 %collective-permute-done.15.w_ref = bf16[256,128]{1,0:T(8,128)(2,1)S(1)} collective-permute-done((bf16[256,128]{1,0:T(8,128)(2,1)S(1)}, bf16[256,128]{1,0:T(8,128)(2,1)S(1)}, u32[]{:S(2)}, u32[]{:S(2)}) %collective-permute-start.15) | collective-permute-done | bytes 65568 | tf_op jit(solution)/shard_map/ppermute | solution.py:292
  118.5 0.7 finish.1
  (25 shorter events, 0.3 us)
Async XLA Ops:
  0.6 28.1 %copy-start.1 = (bf16[128,512]{1,0:T(8,128)(2,1)S(1)}, bf16[128,512]{1,0:T(8,128)(2,1)}, u32[]{:S(2)}) copy-start(bf16[128,512]{1,0:T(8,128)(2,1)} %q_ref.1) | copy-start | bytes 393220
  0.6 28.1 %copy-start.4 = (f32[128,4]{0,1:T(4,128)S(1)}, f32[128,4]{0,1:T(4,128)}, u32[]{:S(2)}) copy-start(f32[128,4]{0,1:T(4,128)} %param.12) | copy-start | bytes 6148
  2.1 26.6 %copy-start.5 = (s32[128]{0:T(128)S(1)}, s32[128]{0:T(128)}, u32[]{:S(2)}) copy-start(s32[128]{0:T(128)} %pos.3) | copy-start | bytes 1540
  2.1 19.2 %collective-permute-start.1 = (bf16[272,128]{1,0:T(8,128)(2,1)}, bf16[272,128]{1,0:T(8,128)(2,1)S(1)}, u32[]{:S(2)}, u32[]{:S(2)}) collective-permute-start(bf16[272,128]{1,0:T(8,128)(2,1)} %pack_keys.1.own_ref), channel_id=1, source_target_pairs={{0,176},{16,96},{32,208},{48,128},{64,240},{80,160},{96,16},{112,1... | collective-permute-start | bytes 208904 | tf_op jit(solution)/shard_map/ppermute | solution.py:292
  16.6 12.1 %collective-permute-start = (bf16[272,128]{1,0:T(8,128)(2,1)}, bf16[272,128]{1,0:T(8,128)(2,1)S(1)}, u32[]{:S(2)}, u32[]{:S(2)}) collective-permute-start(bf16[272,128]{1,0:T(8,128)(2,1)} %pack_keys.1.own_ref), channel_id=1, source_target_pairs={{0,80},{16,192},{32,112},{48,224},{64,144},{80,0},{96,176},{112,32... | collective-permute-start | bytes 208904 | tf_op jit(solution)/shard_map/ppermute | solution.py:292
  28.7 0.9 copy-start.2
  29.6 0.9 copy-start.3
  32.2 19.7 %copy-start = (bf16[272,128]{1,0:T(8,128)(2,1)S(1)}, bf16[272,128]{1,0:T(8,128)(2,1)}, u32[]{:S(2)}) copy-start(bf16[272,128]{1,0:T(8,128)(2,1)} %pack_keys.1.own_ref) | copy-start | bytes 208900
  32.2 19.7 %all-to-all-start = ((bf16[16,16,640]{2,1,0:T(8,128)(2,1)}), bf16[16,16,640]{2,1,0:T(8,128)(2,1)S(1)}, u32[]{:S(2)}, u32[]{:S(2)}) async-start(bf16[16,16,640]{2,1,0:T(8,128)(2,1)} %get-tuple-element.25), calls=%async_computation | async-start | bytes 655360 | tf_op jit(solution)/shard_map/all_to_all | solution.py:337
  39.8 12.1 %collective-permute-start.3 = (bf16[128,640]{1,0:T(8,128)(2,1)S(1)}, bf16[128,640]{1,0:T(8,128)(2,1)S(1)}, u32[]{:S(2)}, u32[]{:S(2)}) collective-permute-start(bf16[128,640]{1,0:T(8,128)(2,1)S(1)} %get-tuple-element.24.q_ref), channel_id=1, source_target_pairs={{0,256},{256,0},{1,257},{257,1},{2,258},{258,2},{3,259},{259,3},{4... | collective-permute-start | bytes 491528 | tf_op jit(solution)/shard_map/ppermute | solution.py:296
  43.1 8.8 %collective-permute-start.2 = (bf16[272,128]{1,0:T(8,128)(2,1)S(1)}, bf16[272,128]{1,0:T(8,128)(2,1)S(1)}, u32[]{:S(2)}, u32[]{:S(2)}) collective-permute-start(bf16[272,128]{1,0:T(8,128)(2,1)S(1)} %collective-permute-done.1.w_ref), channel_id=1, source_target_pairs={{0,48},{16,224},{32,80},{48,0},{64,112},{80,32},{96,144},{112,64},... | collective-permute-start | bytes 208904 | tf_op jit(solution)/shard_map/ppermute | solution.py:292
  52.0 19.8 %collective-permute-start.4 = (bf16[2,128,1280]{2,1,0:T(8,128)(2,1)S(1)}, bf16[2,128,1280]{2,1,0:T(8,128)(2,1)S(1)}, u32[]{:S(2)}, u32[]{:S(2)}) collective-permute-start(bf16[2,128,1280]{2,1,0:T(8,128)(2,1)S(1)} %get-tuple-element.26.x_ref), channel_id=1, source_target_pairs={{0,8},{8,0},{1,9},{9,1},{2,10},{10,2},{3,11},{11,3},{4,12},{12,4},... | collective-permute-start | bytes 1966088 | tf_op jit(solution)/shard_map/ppermute | solution.py:296
  53.9 16.1 %collective-permute-start.8 = (bf16[3,272,128]{2,1,0:T(8,128)(2,1)S(1)}, bf16[3,272,128]{2,1,0:T(8,128)(2,1)S(1)}, u32[]{:S(2)}, u32[]{:S(2)}) collective-permute-start(bf16[3,272,128]{2,1,0:T(8,128)(2,1)S(1)} %get-tuple-element.27.s_ref), channel_id=1, source_target_pairs={{0,224},{16,48},{32,0},{48,80},{64,32},{80,112},{96,64},{112,144},... | collective-permute-start | bytes 626696 | tf_op jit(solution)/shard_map/ppermute | solution.py:292
  60.1 11.7 %collective-permute-start.7 = (bf16[3,272,128]{2,1,0:T(8,128)(2,1)S(1)}, bf16[3,272,128]{2,1,0:T(8,128)(2,1)S(1)}, u32[]{:S(2)}, u32[]{:S(2)}) collective-permute-start(bf16[3,272,128]{2,1,0:T(8,128)(2,1)S(1)} %get-tuple-element.27.s_ref), channel_id=1, source_target_pairs={{0,32},{16,240},{32,64},{48,16},{64,96},{80,48},{96,128},{112,80},... | collective-permute-start | bytes 626696 | tf_op jit(solution)/shard_map/ppermute | solution.py:292
  62.1 21.5 %collective-permute-start.6 = (bf16[3,272,128]{2,1,0:T(8,128)(2,1)S(1)}, bf16[3,272,128]{2,1,0:T(8,128)(2,1)S(1)}, u32[]{:S(2)}, u32[]{:S(2)}) collective-permute-start(bf16[3,272,128]{2,1,0:T(8,128)(2,1)S(1)} %get-tuple-element.27.s_ref), channel_id=1, source_target_pairs={{0,240},{16,32},{32,16},{48,64},{64,48},{80,96},{96,80},{112,128},... | collective-permute-start | bytes 626696 | tf_op jit(solution)/shard_map/ppermute | solution.py:292
  64.0 19.6 %collective-permute-start.5 = (bf16[3,272,128]{2,1,0:T(8,128)(2,1)S(1)}, bf16[3,272,128]{2,1,0:T(8,128)(2,1)S(1)}, u32[]{:S(2)}, u32[]{:S(2)}) collective-permute-start(bf16[3,272,128]{2,1,0:T(8,128)(2,1)S(1)} %get-tuple-element.27.s_ref), channel_id=1, source_target_pairs={{0,16},{16,0},{32,48},{48,32},{64,80},{80,64},{96,112},{112,96},{1... | collective-permute-start | bytes 626696 | tf_op jit(solution)/shard_map/ppermute | solution.py:292
  75.6 15.1 %collective-permute-start.11 = (bf16[4,256,128]{2,1,0:T(8,128)(2,1)S(1)}, bf16[4,256,128]{2,1,0:T(8,128)(2,1)S(1)}, u32[]{:S(2)}, u32[]{:S(2)}) collective-permute-start(bf16[4,256,128]{2,1,0:T(8,128)(2,1)S(1)} %get-tuple-element.34), channel_id=1, source_target_pairs={{0,32},{16,240},{32,64},{48,16},{64,96},{80,48},{96,128},{112,80},... | collective-permute-start | bytes 786440 | tf_op jit(solution)/shard_map/ppermute | solution.py:292
  77.6 13.2 %collective-permute-start.10 = (bf16[3,256,128]{2,1,0:T(8,128)(2,1)S(1)}, bf16[3,256,128]{2,1,0:T(8,128)(2,1)S(1)}, u32[]{:S(2)}, u32[]{:S(2)}) collective-permute-start(bf16[3,256,128]{2,1,0:T(8,128)(2,1)S(1)} %get-tuple-element.33), channel_id=1, source_target_pairs={{0,224},{16,48},{32,0},{48,80},{64,32},{80,112},{96,64},{112,144},... | collective-permute-start | bytes 589832 | tf_op jit(solution)/shard_map/ppermute | solution.py:292
  88.8 8.7 %collective-permute-start.9 = (bf16[2,128,512]{2,1,0:T(8,128)(2,1)S(1)}, bf16[2,128,512]{2,1,0:T(8,128)(2,1)S(1)}, u32[]{:S(2)}, u32[]{:S(2)}) collective-permute-start(bf16[2,128,512]{2,1,0:T(8,128)(2,1)S(1)} %get-tuple-element.30), channel_id=1, source_target_pairs={{0,8},{8,0},{1,9},{9,1},{2,10},{10,2},{3,11},{11,3},{4,12},{12,4},... | collective-permute-start | bytes 786440 | tf_op jit(solution)/shard_map/ppermute | solution.py:296
  90.9 10.7 %collective-permute-start.12 = (bf16[3,256,128]{2,1,0:T(8,128)(2,1)S(1)}, bf16[3,256,128]{2,1,0:T(8,128)(2,1)S(1)}, u32[]{:S(2)}, u32[]{:S(2)}) collective-permute-start(bf16[3,256,128]{2,1,0:T(8,128)(2,1)S(1)} %get-tuple-element.38), channel_id=1, source_target_pairs={{0,16},{16,0},{32,48},{48,32},{64,80},{80,64},{96,112},{112,96},{1... | collective-permute-start | bytes 589832 | tf_op jit(solution)/shard_map/ppermute | solution.py:292
  94.6 9.6 %collective-permute-start.13 = (bf16[3,256,128]{2,1,0:T(8,128)(2,1)S(1)}, bf16[3,256,128]{2,1,0:T(8,128)(2,1)S(1)}, u32[]{:S(2)}, u32[]{:S(2)}) collective-permute-start(bf16[3,256,128]{2,1,0:T(8,128)(2,1)S(1)} %get-tuple-element.39), channel_id=1, source_target_pairs={{0,240},{16,32},{32,16},{48,64},{64,48},{80,96},{96,80},{112,128},... | collective-permute-start | bytes 589832 | tf_op jit(solution)/shard_map/ppermute | solution.py:292
  97.6 15.1 %collective-permute-start.16 = (bf16[128,512]{1,0:T(8,128)(2,1)S(1)}, bf16[128,512]{1,0:T(8,128)(2,1)S(1)}, u32[]{:S(2)}, u32[]{:S(2)}) collective-permute-start(bf16[128,512]{1,0:T(8,128)(2,1)S(1)} %get-tuple-element.44), channel_id=1, source_target_pairs={{0,256},{256,0},{1,257},{257,1},{2,258},{258,2},{3,259},{259,3},{4... | collective-permute-start | bytes 393224 | tf_op jit(solution)/shard_map/ppermute | solution.py:296
  104.3 12.2 %collective-permute-start.14 = (bf16[256,128]{1,0:T(8,128)(2,1)S(1)}, bf16[256,128]{1,0:T(8,128)(2,1)S(1)}, u32[]{:S(2)}, u32[]{:S(2)}) collective-permute-start(bf16[256,128]{1,0:T(8,128)(2,1)S(1)} %get-tuple-element.41), channel_id=1, source_target_pairs={{0,80},{16,192},{32,112},{48,224},{64,144},{80,0},{96,176},{112,32... | collective-permute-start | bytes 196616 | tf_op jit(solution)/shard_map/ppermute | solution.py:292
  106.3 12.2 %collective-permute-start.15 = (bf16[256,128]{1,0:T(8,128)(2,1)S(1)}, bf16[256,128]{1,0:T(8,128)(2,1)S(1)}, u32[]{:S(2)}, u32[]{:S(2)}) collective-permute-start(bf16[256,128]{1,0:T(8,128)(2,1)S(1)} %get-tuple-element.42), channel_id=1, source_target_pairs={{0,176},{16,96},{32,208},{48,128},{64,240},{80,160},{96,16},{112,1... | collective-permute-start | bytes 196616 | tf_op jit(solution)/shard_map/ppermute | solution.py:292

commit v9 on v7

--- a/solution.py
+++ b/solution.py
@@ -157,21 +157,29 @@
     return jnp.concatenate([acc[rows, : 2 * BLK] * SCALE, acc[rows, 2 * BLK :]], axis=-2)
 
 
-def with_next(x_ref, y_ref, p_ref, m_ref, e_ref, p_out, m_out, dq_out, kv, acc):
-    kv[:NEAR] = p_ref[...]
-    kv[NEAR : 2 * NEAR] = m_ref[...]
-    kv[2 * NEAR] = e_ref[...]
+GATHERED = ((0, 4, -4, 8), (1, -3, 5, -7), (-1, -5, 3, 7), (2, 6, -2, -6))
+NEXT = (-2, 3, -7, 2, 7, -3, 8)
+NEAREST = (0, 5, -5, 1, -4, 6, -1, -6, 4)
+
+
+def arrange(kv, sets, order):
+    at = {d: (ref, i) for ref, held in zip(sets, GATHERED) for i, d in enumerate(held)}
+    for j, d in enumerate(order):
+        ref, i = at[d]
+        kv[j] = ref[i]
+
+
+def with_next(x_ref, y_ref, s_ref, p_ref, m_ref, h_ref, p_out, m_out, dq_out, kv, acc):
+    arrange(kv, (s_ref, p_ref, m_ref, h_ref), NEXT)
     dq_out[...] = jnp.zeros_like(dq_out)
     backward(x_ref, y_ref, kv, acc, dq_out, ((0, 4), (4, 7)), False)
     p_out[...] = scaled(acc, slice(0, NEAR)).astype(BF16)
     m_out[...] = scaled(acc, slice(NEAR, 2 * NEAR + 1)).astype(BF16)
 
 
-def with_nearest(x_ref, y_ref, s_ref, p_ref, m_ref, dq_ref, *rest):
+def with_nearest(x_ref, y_ref, s_ref, p_ref, m_ref, h_ref, dq_ref, *rest):
     own_out, p_out, m_out, dq_out, dq_core_out, kv, acc, dq = rest
-    kv[:NEAR] = s_ref[...]
-    kv[NEAR : 2 * NEAR] = p_ref[...]
-    kv[2 * NEAR :] = m_ref[...]
+    arrange(kv, (s_ref, p_ref, m_ref, h_ref), NEAREST)
     dq[...] = dq_ref[...]
     backward(x_ref, y_ref, kv, acc, dq, ((0, 5), (5, 9)), True)
     own_out[...] = scaled(acc, slice(0, NEAR))
@@ -235,10 +243,9 @@
             g_out[twin * n_heads + d, :, wide:] = tail
 
 
-def join(own_ref, u_ref, w_ref, e_ref, q_ref, qx_ref, grad_ref, s_out, x_out):
-    s_out[0] = own_ref[...]
-    s_out[1] = u_ref[...]
-    s_out[2] = w_ref[...]
+def join(own_ref, a_ref, b_ref, c_ref, q_ref, qx_ref, grad_ref, s_out, x_out):
+    for i, ref in enumerate((own_ref, a_ref, b_ref, c_ref)):
+        s_out[i] = ref[...]
     wide = (GROUP + 1) * HEAD
     x_out[0, :, :wide] = q_ref[...]
     x_out[1, :, :wide] = qx_ref[...]
@@ -330,8 +337,7 @@
 
     packed, block = (4 * BLK + 16, HEAD), (4 * BLK, HEAD)
     own = local_call(pack_keys, like(packed), 56, stream_in=True)(positions, keys, values)
-    u, w = by_parity(own, 5), by_parity(own, -5)
-    e_one = half_round(own)
+    far = [by_parity(own, -4), by_parity(own, 4), half_round(own)]
 
     own_q, send = local_call(
         pack_queries,
@@ -342,9 +348,9 @@
     grad = lax.all_to_all(send, ("xh",) + HEADS, split_axis=0, concat_axis=0, tiled=True)
     other_q = swapped_with(own_q, "xh")
     s_set, x = local_call(
-        join, (like((NEAR,) + packed), like((2, TOK, 2 * wide))), 8, stream_in=True
-    )(own, u, w, e_one, own_q, other_q, grad.reshape(2, TOK, wide))
-    p1, m1, p2, m2 = [by_parity(s_set, by) for by in (1, -1, 2, -2)]
+        join, (like((4,) + packed), like((2, TOK, 2 * wide))), 8, stream_in=True
+    )(own, *far, own_q, other_q, grad.reshape(2, TOK, wide))
+    sets = [s_set] + [by_parity(s_set, by) for by in (1, -1, -2)]
     y = swapped_with(x, "core")
 
     near, dq_shape = (NEAR,) + block, (2, TOK, GROUP * HEAD)
@@ -355,9 +361,7 @@
     )(
         x,
         y,
-        p2,
-        m2,
-        e_one,
+        *sets,
         scratch=[
             pltpu.VMEM((2 * NEAR + 1,) + packed, BF16),
             pltpu.VMEM((2 * NEAR + 1,) + block, F32),
@@ -370,9 +374,7 @@
     )(
         x,
         y,
-        s_set,
-        p1,
-        m1,
+        *sets,
         dq,
         scratch=[
             pltpu.VMEM((3 * NEAR,) + packed, BF16),

time: 118 us -> 119 us (level)
  waiting for transfers between devices: 21 us -> 23.3 us
  starting transfers between devices: 80.3 us -> 79.1 us
    ppermute x12 -> x11, waiting for transfers between devices: 21 us -> 23.3 us  [by_parity(): return lax.ppermute(x, 'z', list(enumerate(to)))]
    ppermute x12 -> x11, starting transfers between devices: 45.9 us -> 44.7 us  [by_parity(): return lax.ppermute(x, 'z', list(enumerate(to)))]
  transfers between devices with their start and end apart: 18 -> 17, of which waited for: 5 -> 8; matrix products, arithmetic and copies ran while one was open for 0% -> 0% of each run, Pallas kernels for 8% -> 5%
where the time goes in v9:
time: 119 us; the launch traced here: 117 us
  starting transfers between devices  79.1 us (66%)
  waiting for transfers between devices  23.3 us (20%)
  Pallas kernels  13.7 us (12%)
    ppermute x11, starting transfers between devices, by_parity(): return lax.ppermute(x, 'z', list(enumerate(to)))  44.7 us
    ppermute x11, waiting for transfers between devices, by_parity(): return lax.ppermute(x, 'z', list(enumerate(to)))  23.3 us
    ppermute x1, starting transfers between devices, half_round(): return lax.ppermute(x, 'z', [(i, (i + n // 2) % n) for i in range(n)])  13.9 us
    pallas_call x9, Pallas kernels, call(): pl.pallas_call(body, out_shape=out_shape, in_specs=[smem if a.dtype == jn...  13.7 us
    ppermute x4, starting transfers between devices, swapped_with(): return lax.ppermute(x, axis, [(0, 1), (1, 0)])  11.1 us
    all_to_all x1, starting transfers between devices, shards(): lax.all_to_all(send, ('xh',) + HEADS, split_axis=0, concat_axis=0, tiled=...  9.39 us
  transfers between devices with their start and end apart: 17, of which 8 were waited for; matrix products, arithmetic and copies ran while one was open for 0% of the time, Pallas kernels for 5%

profile of v9, /device:TPU:6, one launch (start us, length us, event | category | flops | bytes accessed | tf_op | source)
XLA Modules:
  0.0 117.0 jit_solution(4514661346007066335)
XLA Ops:
  0.6 1.4 %pack_keys.1.after_ref.own_ref = bf16[272,128]{1,0:T(8,128)(2,1)} custom-call(s32[128]{0:T(128)} %pos.3, bf16[128,128]{1,0:T(8,128)(2,1)} %k_ref.1, bf16[128,128]{1,0:T(8,128)(2,1)} %v_ref.1), custom_call_target="tpu_custom_call" | custom-call | tf_op jit(solution)/shard_map/pack_keys/pallas_call | solution.py:316
  2.1 2.3 %pack_queries.1 = (bf16[128,640]{1,0:T(8,128)(2,1)}, bf16[16,16,640]{2,1,0:T(8,128)(2,1)}) custom-call(s32[128]{0:T(128)} %pos.3, bf16[128,512]{1,0:T(8,128)(2,1)} %q_ref.1, f32[4,128]{1,0:T(4,128)} %bitcast.3, bf16[16,4096]{1,0:T(8,128)(2,1)} %o_ref.1, bf16[16,4096]{1,0:T(8,128)(2,1)} %g_ref.1, bf16[272,128]{1,0:T(8,128)(2,1)} %pack_keys.1.after_ref.own_ref), custom_call_target="tpu_custom_call" | custom-call | tf_op jit(solution)/shard_map/pack_queries/pallas_call | solution.py:316
  4.3 9.4 %all-to-all-start = ((bf16[16,16,640]{2,1,0:T(8,128)(2,1)}), bf16[16,16,640]{2,1,0:T(8,128)(2,1)S(1)}, u32[]{:S(2)}, u32[]{:S(2)}) async-start(bf16[16,16,640]{2,1,0:T(8,128)(2,1)} %get-tuple-element.25), calls=%async_computation | async-start | bytes 655360 | tf_op jit(solution)/shard_map/all_to_all | solution.py:348
  13.7 3.3 %collective-permute-start.3 = (bf16[128,640]{1,0:T(8,128)(2,1)S(1)}, bf16[128,640]{1,0:T(8,128)(2,1)S(1)}, u32[]{:S(2)}, u32[]{:S(2)}) collective-permute-start(bf16[128,640]{1,0:T(8,128)(2,1)S(1)} %copy-done.1), channel_id=1, source_target_pairs={{0,256},{256,0},{1,257},{257,1},{2,258},{258,2},{3,259},{259,3},{4... | collective-permute-start | bytes 491528 | tf_op jit(solution)/shard_map/ppermute | solution.py:308
  17.0 13.9 %collective-permute-start.2 = (bf16[272,128]{1,0:T(8,128)(2,1)S(1)}, bf16[272,128]{1,0:T(8,128)(2,1)S(1)}, u32[]{:S(2)}, u32[]{:S(2)}) collective-permute-start(bf16[272,128]{1,0:T(8,128)(2,1)S(1)} %copy-done), channel_id=1, source_target_pairs={{0,128},{16,144},{32,160},{48,176},{64,192},{80,208},{96,224},{112... | collective-permute-start | bytes 208904 | tf_op jit(solution)/shard_map/ppermute | solution.py:304
  31.0 4.3 %collective-permute-start.1 = (bf16[272,128]{1,0:T(8,128)(2,1)S(1)}, bf16[272,128]{1,0:T(8,128)(2,1)S(1)}, u32[]{:S(2)}, u32[]{:S(2)}) collective-permute-start(bf16[272,128]{1,0:T(8,128)(2,1)S(1)} %copy-done), channel_id=1, source_target_pairs={{0,64},{16,208},{32,96},{48,240},{64,128},{80,16},{96,160},{112,48... | collective-permute-start | bytes 208904 | tf_op jit(solution)/shard_map/ppermute | solution.py:299
  35.3 5.5 %collective-permute-start = (bf16[272,128]{1,0:T(8,128)(2,1)S(1)}, bf16[272,128]{1,0:T(8,128)(2,1)S(1)}, u32[]{:S(2)}, u32[]{:S(2)}) collective-permute-start(bf16[272,128]{1,0:T(8,128)(2,1)S(1)} %copy-done), channel_id=1, source_target_pairs={{0,192},{16,80},{32,224},{48,112},{64,0},{80,144},{96,32},{112,176... | collective-permute-start | bytes 208904 | tf_op jit(solution)/shard_map/ppermute | solution.py:299
  40.8 2.5 %collective-permute-done.1.b_ref = bf16[272,128]{1,0:T(8,128)(2,1)S(1)} collective-permute-done((bf16[272,128]{1,0:T(8,128)(2,1)S(1)}, bf16[272,128]{1,0:T(8,128)(2,1)S(1)}, u32[]{:S(2)}, u32[]{:S(2)}) %collective-permute-start.1) | collective-permute-done | bytes 69664 | tf_op jit(solution)/shard_map/ppermute | solution.py:299
  43.2 2.2 %collective-permute-done.a_ref = bf16[272,128]{1,0:T(8,128)(2,1)S(1)} collective-permute-done((bf16[272,128]{1,0:T(8,128)(2,1)S(1)}, bf16[272,128]{1,0:T(8,128)(2,1)S(1)}, u32[]{:S(2)}, u32[]{:S(2)}) %collective-permute-start) | collective-permute-done | bytes 69664 | tf_op jit(solution)/shard_map/ppermute | solution.py:299
  45.5 1.9 %collective-permute-start.4 = (bf16[2,128,1280]{2,1,0:T(8,128)(2,1)S(1)}, bf16[2,128,1280]{2,1,0:T(8,128)(2,1)S(1)}, u32[]{:S(2)}, u32[]{:S(2)}) collective-permute-start(bf16[2,128,1280]{2,1,0:T(8,128)(2,1)S(1)} %get-tuple-element.26.x_ref), channel_id=1, source_target_pairs={{0,8},{8,0},{1,9},{9,1},{2,10},{10,2},{3,11},{11,3},{4,12},{12,4},... | collective-permute-start | bytes 1966088 | tf_op jit(solution)/shard_map/ppermute | solution.py:308
  47.4 4.6 %collective-permute-start.7 = (bf16[4,272,128]{2,1,0:T(8,128)(2,1)S(1)}, bf16[4,272,128]{2,1,0:T(8,128)(2,1)S(1)}, u32[]{:S(2)}, u32[]{:S(2)}) collective-permute-start(bf16[4,272,128]{2,1,0:T(8,128)(2,1)S(1)} %get-tuple-element.27.s_ref), channel_id=1, source_target_pairs={{0,224},{16,48},{32,0},{48,80},{64,32},{80,112},{96,64},{112,144},... | collective-permute-start | bytes 835592 | tf_op jit(solution)/shard_map/ppermute | solution.py:299
  52.0 2.7 %collective-permute-start.6 = (bf16[4,272,128]{2,1,0:T(8,128)(2,1)S(1)}, bf16[4,272,128]{2,1,0:T(8,128)(2,1)S(1)}, u32[]{:S(2)}, u32[]{:S(2)}) collective-permute-start(bf16[4,272,128]{2,1,0:T(8,128)(2,1)S(1)} %get-tuple-element.27.s_ref), channel_id=1, source_target_pairs={{0,240},{16,32},{32,16},{48,64},{64,48},{80,96},{96,80},{112,128},... | collective-permute-start | bytes 835592 | tf_op jit(solution)/shard_map/ppermute | solution.py:299
  54.7 1.9 %collective-permute-start.5 = (bf16[4,272,128]{2,1,0:T(8,128)(2,1)S(1)}, bf16[4,272,128]{2,1,0:T(8,128)(2,1)S(1)}, u32[]{:S(2)}, u32[]{:S(2)}) collective-permute-start(bf16[4,272,128]{2,1,0:T(8,128)(2,1)S(1)} %get-tuple-element.27.s_ref), channel_id=1, source_target_pairs={{0,16},{16,0},{32,48},{48,32},{64,80},{80,64},{96,112},{112,96},{1... | collective-permute-start | bytes 835592 | tf_op jit(solution)/shard_map/ppermute | solution.py:299
  56.7 3.0 %collective-permute-done.7.h_ref = bf16[4,272,128]{2,1,0:T(8,128)(2,1)S(1)} collective-permute-done((bf16[4,272,128]{2,1,0:T(8,128)(2,1)S(1)}, bf16[4,272,128]{2,1,0:T(8,128)(2,1)S(1)}, u32[]{:S(2)}, u32[]{:S(2)}) %collective-permute-start.7) | collective-permute-done | bytes 278560 | tf_op jit(solution)/shard_map/ppermute | solution.py:299
  59.7 6.1 %collective-permute-done.6.m_ref = bf16[4,272,128]{2,1,0:T(8,128)(2,1)S(1)} collective-permute-done((bf16[4,272,128]{2,1,0:T(8,128)(2,1)S(1)}, bf16[4,272,128]{2,1,0:T(8,128)(2,1)S(1)}, u32[]{:S(2)}, u32[]{:S(2)}) %collective-permute-start.6) | collective-permute-done | bytes 278560 | tf_op jit(solution)/shard_map/ppermute | solution.py:299
  65.8 3.8 %with_next.1 = (bf16[3,256,128]{2,1,0:T(8,128)(2,1)S(1)}, bf16[4,256,128]{2,1,0:T(8,128)(2,1)S(1)}, f32[4,128,512]{2,1,0:T(8,128)S(1)}) custom-call(bf16[2,128,1280]{2,1,0:T(8,128)(2,1)S(1)} %get-tuple-element.26.x_ref, bf16[2,128,1280]{2,1,0:T(8,128)(2,1)S(1)} %collective-permute-done.4.y_ref, bf16[4,272,128]{2,1,0:T(8,128)(2,1)S(1)} %get-tuple-element.27.s_ref, ...), custom_call_target="tpu_custom_call" | custom-call | tf_op jit(solution)/shard_map/with_next/pallas_call | solution.py:316
  69.6 4.3 %collective-permute-start.10 = (bf16[4,256,128]{2,1,0:T(8,128)(2,1)S(1)}, bf16[4,256,128]{2,1,0:T(8,128)(2,1)S(1)}, u32[]{:S(2)}, u32[]{:S(2)}) collective-permute-start(bf16[4,256,128]{2,1,0:T(8,128)(2,1)S(1)} %get-tuple-element.34), channel_id=1, source_target_pairs={{0,32},{16,240},{32,64},{48,16},{64,96},{80,48},{96,128},{112,80},... | collective-permute-start | bytes 786440 | tf_op jit(solution)/shard_map/ppermute | solution.py:299
  73.9 3.7 %collective-permute-start.9 = (bf16[3,256,128]{2,1,0:T(8,128)(2,1)S(1)}, bf16[3,256,128]{2,1,0:T(8,128)(2,1)S(1)}, u32[]{:S(2)}, u32[]{:S(2)}) collective-permute-start(bf16[3,256,128]{2,1,0:T(8,128)(2,1)S(1)} %get-tuple-element.33), channel_id=1, source_target_pairs={{0,224},{16,48},{32,0},{48,80},{64,32},{80,112},{96,64},{112,144},... | collective-permute-start | bytes 589832 | tf_op jit(solution)/shard_map/ppermute | solution.py:299
  77.6 5.2 %with_nearest.1 = (f32[3,256,128]{2,1,0:T(8,128)S(1)}, bf16[3,256,128]{2,1,0:T(8,128)(2,1)S(1)}, bf16[3,256,128]{2,1,0:T(8,128)(2,1)S(1)}, f32[2,128,512]{2,1,0:T(8,128)S(1)}, bf16[2,128,512]{2,1,0:T(8,128)(2,1)S(1)}) custom-call(bf16[2,128,1280]{2,1,0:T(8,128)(2,1)S(1)} %get-tuple-element.26.x_ref, bf16[2,128,1280]{2,1,0:T(8,128)(2,1)S(1)} %collective-permute-done.4.y_ref, ...), custom_call_target="tpu_custom_call" | custom-call | tf_op jit(solution)/shard_map/with_nearest/pallas_call | solution.py:316
  82.8 1.9 %collective-permute-start.8 = (bf16[2,128,512]{2,1,0:T(8,128)(2,1)S(1)}, bf16[2,128,512]{2,1,0:T(8,128)(2,1)S(1)}, u32[]{:S(2)}, u32[]{:S(2)}) collective-permute-start(bf16[2,128,512]{2,1,0:T(8,128)(2,1)S(1)} %get-tuple-element.30), channel_id=1, source_target_pairs={{0,8},{8,0},{1,9},{9,1},{2,10},{10,2},{3,11},{11,3},{4,12},{12,4},... | collective-permute-start | bytes 786440 | tf_op jit(solution)/shard_map/ppermute | solution.py:308
  84.7 1.1 collective-permute-done.9.c_ref
  85.8 0.1 sum_first.1
  85.8 3.5 %collective-permute-start.11 = (bf16[3,256,128]{2,1,0:T(8,128)(2,1)S(1)}, bf16[3,256,128]{2,1,0:T(8,128)(2,1)S(1)}, u32[]{:S(2)}, u32[]{:S(2)}) collective-permute-start(bf16[3,256,128]{2,1,0:T(8,128)(2,1)S(1)} %get-tuple-element.38), channel_id=1, source_target_pairs={{0,16},{16,0},{32,48},{48,32},{64,80},{80,64},{96,112},{112,96},{1... | collective-permute-start | bytes 589832 | tf_op jit(solution)/shard_map/ppermute | solution.py:299
  89.3 4.3 %collective-permute-start.12 = (bf16[3,256,128]{2,1,0:T(8,128)(2,1)S(1)}, bf16[3,256,128]{2,1,0:T(8,128)(2,1)S(1)}, u32[]{:S(2)}, u32[]{:S(2)}) collective-permute-start(bf16[3,256,128]{2,1,0:T(8,128)(2,1)S(1)} %get-tuple-element.39), channel_id=1, source_target_pairs={{0,240},{16,32},{32,16},{48,64},{64,48},{80,96},{96,80},{112,128},... | collective-permute-start | bytes 589832 | tf_op jit(solution)/shard_map/ppermute | solution.py:299
  93.6 0.1 sum_cores.1
  93.7 4.0 %collective-permute-start.15 = (bf16[128,512]{1,0:T(8,128)(2,1)S(1)}, bf16[128,512]{1,0:T(8,128)(2,1)S(1)}, u32[]{:S(2)}, u32[]{:S(2)}) collective-permute-start(bf16[128,512]{1,0:T(8,128)(2,1)S(1)} %get-tuple-element.44), channel_id=1, source_target_pairs={{0,256},{256,0},{1,257},{257,1},{2,258},{258,2},{3,259},{259,3},{4... | collective-permute-start | bytes 393224 | tf_op jit(solution)/shard_map/ppermute | solution.py:308
  97.7 1.3 %collective-permute-done.12.m_ref = bf16[3,256,128]{2,1,0:T(8,128)(2,1)S(1)} collective-permute-done((bf16[3,256,128]{2,1,0:T(8,128)(2,1)S(1)}, bf16[3,256,128]{2,1,0:T(8,128)(2,1)S(1)}, u32[]{:S(2)}, u32[]{:S(2)}) %collective-permute-start.12) | collective-permute-done | bytes 196640 | tf_op jit(solution)/shard_map/ppermute | solution.py:299
  99.0 4.8 %collective-permute-start.13 = (bf16[256,128]{1,0:T(8,128)(2,1)S(1)}, bf16[256,128]{1,0:T(8,128)(2,1)S(1)}, u32[]{:S(2)}, u32[]{:S(2)}) collective-permute-start(bf16[256,128]{1,0:T(8,128)(2,1)S(1)} %get-tuple-element.41), channel_id=1, source_target_pairs={{0,80},{16,192},{32,112},{48,224},{64,144},{80,0},{96,176},{112,32... | collective-permute-start | bytes 196616 | tf_op jit(solution)/shard_map/ppermute | solution.py:299
  103.9 5.2 %collective-permute-start.14 = (bf16[256,128]{1,0:T(8,128)(2,1)S(1)}, bf16[256,128]{1,0:T(8,128)(2,1)S(1)}, u32[]{:S(2)}, u32[]{:S(2)}) collective-permute-start(bf16[256,128]{1,0:T(8,128)(2,1)S(1)} %get-tuple-element.42), channel_id=1, source_target_pairs={{0,176},{16,96},{32,208},{48,128},{64,240},{80,160},{96,16},{112,1... | collective-permute-start | bytes 196616 | tf_op jit(solution)/shard_map/ppermute | solution.py:299
  109.1 1.3 %collective-permute-done.13.u_ref = bf16[256,128]{1,0:T(8,128)(2,1)S(1)} collective-permute-done((bf16[256,128]{1,0:T(8,128)(2,1)S(1)}, bf16[256,128]{1,0:T(8,128)(2,1)S(1)}, u32[]{:S(2)}, u32[]{:S(2)}) %collective-permute-start.13) | collective-permute-done | bytes 65568 | tf_op jit(solution)/shard_map/ppermute | solution.py:299
  110.3 5.9 %collective-permute-done.14.w_ref = bf16[256,128]{1,0:T(8,128)(2,1)S(1)} collective-permute-done((bf16[256,128]{1,0:T(8,128)(2,1)S(1)}, bf16[256,128]{1,0:T(8,128)(2,1)S(1)}, u32[]{:S(2)}, u32[]{:S(2)}) %collective-permute-start.14) | collective-permute-done | bytes 65568 | tf_op jit(solution)/shard_map/ppermute | solution.py:299
  116.3 0.7 finish.1
  (15 shorter events, 0.2 us)
Async XLA Ops:
  4.3 9.4 %copy-start.1 = (bf16[128,640]{1,0:T(8,128)(2,1)S(1)}, bf16[128,640]{1,0:T(8,128)(2,1)}, u32[]{:S(2)}) copy-start(bf16[128,640]{1,0:T(8,128)(2,1)} %get-tuple-element.24.q_ref) | copy-start | bytes 491524
  4.3 12.7 %copy-start = (bf16[272,128]{1,0:T(8,128)(2,1)S(1)}, bf16[272,128]{1,0:T(8,128)(2,1)}, u32[]{:S(2)}) copy-start(bf16[272,128]{1,0:T(8,128)(2,1)} %pack_keys.1.after_ref.own_ref) | copy-start | bytes 208900
  4.3 41.1 %all-to-all-start = ((bf16[16,16,640]{2,1,0:T(8,128)(2,1)}), bf16[16,16,640]{2,1,0:T(8,128)(2,1)S(1)}, u32[]{:S(2)}, u32[]{:S(2)}) async-start(bf16[16,16,640]{2,1,0:T(8,128)(2,1)} %get-tuple-element.25), calls=%async_computation | async-start | bytes 655360 | tf_op jit(solution)/shard_map/all_to_all | solution.py:348
  13.7 31.7 %collective-permute-start.3 = (bf16[128,640]{1,0:T(8,128)(2,1)S(1)}, bf16[128,640]{1,0:T(8,128)(2,1)S(1)}, u32[]{:S(2)}, u32[]{:S(2)}) collective-permute-start(bf16[128,640]{1,0:T(8,128)(2,1)S(1)} %copy-done.1), channel_id=1, source_target_pairs={{0,256},{256,0},{1,257},{257,1},{2,258},{258,2},{3,259},{259,3},{4... | collective-permute-start | bytes 491528 | tf_op jit(solution)/shard_map/ppermute | solution.py:308
  17.0 23.7 %collective-permute-start.2 = (bf16[272,128]{1,0:T(8,128)(2,1)S(1)}, bf16[272,128]{1,0:T(8,128)(2,1)S(1)}, u32[]{:S(2)}, u32[]{:S(2)}) collective-permute-start(bf16[272,128]{1,0:T(8,128)(2,1)S(1)} %copy-done), channel_id=1, source_target_pairs={{0,128},{16,144},{32,160},{48,176},{64,192},{80,208},{96,224},{112... | collective-permute-start | bytes 208904 | tf_op jit(solution)/shard_map/ppermute | solution.py:304
  31.0 12.2 %collective-permute-start.1 = (bf16[272,128]{1,0:T(8,128)(2,1)S(1)}, bf16[272,128]{1,0:T(8,128)(2,1)S(1)}, u32[]{:S(2)}, u32[]{:S(2)}) collective-permute-start(bf16[272,128]{1,0:T(8,128)(2,1)S(1)} %copy-done), channel_id=1, source_target_pairs={{0,64},{16,208},{32,96},{48,240},{64,128},{80,16},{96,160},{112,48... | collective-permute-start | bytes 208904 | tf_op jit(solution)/shard_map/ppermute | solution.py:299
  35.3 10.1 %collective-permute-start = (bf16[272,128]{1,0:T(8,128)(2,1)S(1)}, bf16[272,128]{1,0:T(8,128)(2,1)S(1)}, u32[]{:S(2)}, u32[]{:S(2)}) collective-permute-start(bf16[272,128]{1,0:T(8,128)(2,1)S(1)} %copy-done), channel_id=1, source_target_pairs={{0,192},{16,80},{32,224},{48,112},{64,0},{80,144},{96,32},{112,176... | collective-permute-start | bytes 208904 | tf_op jit(solution)/shard_map/ppermute | solution.py:299
  45.5 20.3 %collective-permute-start.4 = (bf16[2,128,1280]{2,1,0:T(8,128)(2,1)S(1)}, bf16[2,128,1280]{2,1,0:T(8,128)(2,1)S(1)}, u32[]{:S(2)}, u32[]{:S(2)}) collective-permute-start(bf16[2,128,1280]{2,1,0:T(8,128)(2,1)S(1)} %get-tuple-element.26.x_ref), channel_id=1, source_target_pairs={{0,8},{8,0},{1,9},{9,1},{2,10},{10,2},{3,11},{11,3},{4,12},{12,4},... | collective-permute-start | bytes 1966088 | tf_op jit(solution)/shard_map/ppermute | solution.py:308
  47.4 12.2 %collective-permute-start.7 = (bf16[4,272,128]{2,1,0:T(8,128)(2,1)S(1)}, bf16[4,272,128]{2,1,0:T(8,128)(2,1)S(1)}, u32[]{:S(2)}, u32[]{:S(2)}) collective-permute-start(bf16[4,272,128]{2,1,0:T(8,128)(2,1)S(1)} %get-tuple-element.27.s_ref), channel_id=1, source_target_pairs={{0,224},{16,48},{32,0},{48,80},{64,32},{80,112},{96,64},{112,144},... | collective-permute-start | bytes 835592 | tf_op jit(solution)/shard_map/ppermute | solution.py:299
  52.0 13.8 %collective-permute-start.6 = (bf16[4,272,128]{2,1,0:T(8,128)(2,1)S(1)}, bf16[4,272,128]{2,1,0:T(8,128)(2,1)S(1)}, u32[]{:S(2)}, u32[]{:S(2)}) collective-permute-start(bf16[4,272,128]{2,1,0:T(8,128)(2,1)S(1)} %get-tuple-element.27.s_ref), channel_id=1, source_target_pairs={{0,240},{16,32},{32,16},{48,64},{64,48},{80,96},{96,80},{112,128},... | collective-permute-start | bytes 835592 | tf_op jit(solution)/shard_map/ppermute | solution.py:299
  54.7 11.1 %collective-permute-start.5 = (bf16[4,272,128]{2,1,0:T(8,128)(2,1)S(1)}, bf16[4,272,128]{2,1,0:T(8,128)(2,1)S(1)}, u32[]{:S(2)}, u32[]{:S(2)}) collective-permute-start(bf16[4,272,128]{2,1,0:T(8,128)(2,1)S(1)} %get-tuple-element.27.s_ref), channel_id=1, source_target_pairs={{0,16},{16,0},{32,48},{48,32},{64,80},{80,64},{96,112},{112,96},{1... | collective-permute-start | bytes 835592 | tf_op jit(solution)/shard_map/ppermute | solution.py:299
  69.6 16.2 %collective-permute-start.10 = (bf16[4,256,128]{2,1,0:T(8,128)(2,1)S(1)}, bf16[4,256,128]{2,1,0:T(8,128)(2,1)S(1)}, u32[]{:S(2)}, u32[]{:S(2)}) collective-permute-start(bf16[4,256,128]{2,1,0:T(8,128)(2,1)S(1)} %get-tuple-element.34), channel_id=1, source_target_pairs={{0,32},{16,240},{32,64},{48,16},{64,96},{80,48},{96,128},{112,80},... | collective-permute-start | bytes 786440 | tf_op jit(solution)/shard_map/ppermute | solution.py:299
  73.9 11.9 %collective-permute-start.9 = (bf16[3,256,128]{2,1,0:T(8,128)(2,1)S(1)}, bf16[3,256,128]{2,1,0:T(8,128)(2,1)S(1)}, u32[]{:S(2)}, u32[]{:S(2)}) collective-permute-start(bf16[3,256,128]{2,1,0:T(8,128)(2,1)S(1)} %get-tuple-element.33), channel_id=1, source_target_pairs={{0,224},{16,48},{32,0},{48,80},{64,32},{80,112},{96,64},{112,144},... | collective-permute-start | bytes 589832 | tf_op jit(solution)/shard_map/ppermute | solution.py:299
  82.8 10.8 %collective-permute-start.8 = (bf16[2,128,512]{2,1,0:T(8,128)(2,1)S(1)}, bf16[2,128,512]{2,1,0:T(8,128)(2,1)S(1)}, u32[]{:S(2)}, u32[]{:S(2)}) collective-permute-start(bf16[2,128,512]{2,1,0:T(8,128)(2,1)S(1)} %get-tuple-element.30), channel_id=1, source_target_pairs={{0,8},{8,0},{1,9},{9,1},{2,10},{10,2},{3,11},{11,3},{4,12},{12,4},... | collective-permute-start | bytes 786440 | tf_op jit(solution)/shard_map/ppermute | solution.py:308
  85.8 11.8 %collective-permute-start.11 = (bf16[3,256,128]{2,1,0:T(8,128)(2,1)S(1)}, bf16[3,256,128]{2,1,0:T(8,128)(2,1)S(1)}, u32[]{:S(2)}, u32[]{:S(2)}) collective-permute-start(bf16[3,256,128]{2,1,0:T(8,128)(2,1)S(1)} %get-tuple-element.38), channel_id=1, source_target_pairs={{0,16},{16,0},{32,48},{48,32},{64,80},{80,64},{96,112},{112,96},{1... | collective-permute-start | bytes 589832 | tf_op jit(solution)/shard_map/ppermute | solution.py:299
  89.3 9.6 %collective-permute-start.12 = (bf16[3,256,128]{2,1,0:T(8,128)(2,1)S(1)}, bf16[3,256,128]{2,1,0:T(8,128)(2,1)S(1)}, u32[]{:S(2)}, u32[]{:S(2)}) collective-permute-start(bf16[3,256,128]{2,1,0:T(8,128)(2,1)S(1)} %get-tuple-element.39), channel_id=1, source_target_pairs={{0,240},{16,32},{32,16},{48,64},{64,48},{80,96},{96,80},{112,128},... | collective-permute-start | bytes 589832 | tf_op jit(solution)/shard_map/ppermute | solution.py:299
  93.7 15.4 %collective-permute-start.15 = (bf16[128,512]{1,0:T(8,128)(2,1)S(1)}, bf16[128,512]{1,0:T(8,128)(2,1)S(1)}, u32[]{:S(2)}, u32[]{:S(2)}) collective-permute-start(bf16[128,512]{1,0:T(8,128)(2,1)S(1)} %get-tuple-element.44), channel_id=1, source_target_pairs={{0,256},{256,0},{1,257},{257,1},{2,258},{258,2},{3,259},{259,3},{4... | collective-permute-start | bytes 393224 | tf_op jit(solution)/shard_map/ppermute | solution.py:308
  99.0 11.3 %collective-permute-start.13 = (bf16[256,128]{1,0:T(8,128)(2,1)S(1)}, bf16[256,128]{1,0:T(8,128)(2,1)S(1)}, u32[]{:S(2)}, u32[]{:S(2)}) collective-permute-start(bf16[256,128]{1,0:T(8,128)(2,1)S(1)} %get-tuple-element.41), channel_id=1, source_target_pairs={{0,80},{16,192},{32,112},{48,224},{64,144},{80,0},{96,176},{112,32... | collective-permute-start | bytes 196616 | tf_op jit(solution)/shard_map/ppermute | solution.py:299
  103.9 12.4 %collective-permute-start.14 = (bf16[256,128]{1,0:T(8,128)(2,1)S(1)}, bf16[256,128]{1,0:T(8,128)(2,1)S(1)}, u32[]{:S(2)}, u32[]{:S(2)}) collective-permute-start(bf16[256,128]{1,0:T(8,128)(2,1)S(1)} %get-tuple-element.42), channel_id=1, source_target_pairs={{0,176},{16,96},{32,208},{48,128},{64,240},{80,160},{96,16},{112,1... | collective-permute-start | bytes 196616 | tf_op jit(solution)/shard_map/ppermute | solution.py:299

commit v10 on v9

--- a/solution.py
+++ b/solution.py
@@ -157,9 +157,10 @@
     return jnp.concatenate([acc[rows, : 2 * BLK] * SCALE, acc[rows, 2 * BLK :]], axis=-2)
 
 
-GATHERED = ((0, 4, -4, 8), (1, -3, 5, -7), (-1, -5, 3, 7), (2, 6, -2, -6))
-NEXT = (-2, 3, -7, 2, 7, -3, 8)
-NEAREST = (0, 5, -5, 1, -4, 6, -1, -6, 4)
+OWN = (0, 4, -4, 8)
+GATHERED = ((1, -3, 5, -7), (-1, -5, 3, 7), (2, 6, -2, -6))
+NEXT = (-2, 3, -7, 2, 7, -3)
+NEAREST = (5, -5, 1, 6, -1, -6)
 
 
 def arrange(kv, sets, order):
@@ -169,22 +170,30 @@
         kv[j] = ref[i]
 
 
-def with_next(x_ref, y_ref, s_ref, p_ref, m_ref, h_ref, p_out, m_out, dq_out, kv, acc):
-    arrange(kv, (s_ref, p_ref, m_ref, h_ref), NEXT)
+def with_own(x_ref, y_ref, s_ref, grad_out, dq_out, acc):
     dq_out[...] = jnp.zeros_like(dq_out)
-    backward(x_ref, y_ref, kv, acc, dq_out, ((0, 4), (4, 7)), False)
+    backward(x_ref, y_ref, s_ref, acc, dq_out, ((0, 4),), True)
+    grad_out[...] = scaled(acc, slice(0, 4))
+
+
+def with_next(x_ref, y_ref, p_ref, m_ref, h_ref, g_ref, dq_ref, p_out, m_out, dq_out, kv, acc):
+    arrange(kv, (p_ref, m_ref, h_ref), NEXT)
+    dq_out[...] = dq_ref[...]
+    backward(x_ref, y_ref, kv, acc, dq_out, ((0, 3), (3, 6)), False)
     p_out[...] = scaled(acc, slice(0, NEAR)).astype(BF16)
-    m_out[...] = scaled(acc, slice(NEAR, 2 * NEAR + 1)).astype(BF16)
-
-
-def with_nearest(x_ref, y_ref, s_ref, p_ref, m_ref, h_ref, dq_ref, *rest):
+    m_out[:NEAR] = scaled(acc, slice(NEAR, 2 * NEAR)).astype(BF16)
+    m_out[NEAR] = g_ref[OWN.index(8)].astype(BF16)
+
+
+def with_nearest(x_ref, y_ref, p_ref, m_ref, h_ref, g_ref, dq_ref, *rest):
     own_out, p_out, m_out, dq_out, dq_core_out, kv, acc, dq = rest
-    arrange(kv, (s_ref, p_ref, m_ref, h_ref), NEAREST)
+    arrange(kv, (p_ref, m_ref, h_ref), NEAREST)
     dq[...] = dq_ref[...]
-    backward(x_ref, y_ref, kv, acc, dq, ((0, 5), (5, 9)), True)
-    own_out[...] = scaled(acc, slice(0, NEAR))
-    p_out[...] = scaled(acc, slice(NEAR, 2 * NEAR)).astype(BF16)
-    m_out[...] = scaled(acc, slice(2 * NEAR, 3 * NEAR)).astype(BF16)
+    backward(x_ref, y_ref, kv, acc, dq, ((0, 3), (3, 6)), False)
+    for out, held in ((own_out, (0, 5, -5)), (p_out, (1, -4, 6)), (m_out, (-1, -6, 4))):
+        for i, d in enumerate(held):
+            grad = g_ref[OWN.index(d)] if d in OWN else scaled(acc, NEAREST.index(d))
+            out[i] = grad.astype(out.dtype)
     dq_out[...] = dq[:2]
     dq_core_out[...] = dq[2:].astype(BF16)
 
@@ -350,10 +359,13 @@
     s_set, x = local_call(
         join, (like((4,) + packed), like((2, TOK, 2 * wide))), 8, stream_in=True
     )(own, *far, own_q, other_q, grad.reshape(2, TOK, wide))
-    sets = [s_set] + [by_parity(s_set, by) for by in (1, -1, -2)]
+    sets = [by_parity(s_set, by) for by in (1, -1, -2)]
     y = swapped_with(x, "core")
 
     near, dq_shape = (NEAR,) + block, (2, TOK, GROUP * HEAD)
+    own_g, dq = local_call(
+        with_own, (like((4,) + block, F32), like((4,) + dq_shape[1:], F32)), 16
+    )(x, y, s_set, scratch=[pltpu.VMEM((4,) + block, F32)])
     p2_g, m2_g, dq = local_call(
         with_next,
         (like(near), like((NEAR + 1,) + block), like((4,) + dq_shape[1:], F32)),
@@ -362,9 +374,11 @@
         x,
         y,
         *sets,
+        own_g,
+        dq,
         scratch=[
-            pltpu.VMEM((2 * NEAR + 1,) + packed, BF16),
-            pltpu.VMEM((2 * NEAR + 1,) + block, F32),
+            pltpu.VMEM((2 * NEAR,) + packed, BF16),
+            pltpu.VMEM((2 * NEAR,) + block, F32),
         ],
     )
     own_g, p1_g, m1_g, dq, dq_core = local_call(
@@ -375,10 +389,11 @@
         x,
         y,
         *sets,
+        own_g,
         dq,
         scratch=[
-            pltpu.VMEM((3 * NEAR,) + packed, BF16),
-            pltpu.VMEM((3 * NEAR,) + block, F32),
+            pltpu.VMEM((2 * NEAR,) + packed, BF16),
+            pltpu.VMEM((2 * NEAR,) + block, F32),
             pltpu.VMEM((4,) + dq_shape[1:], F32),
         ],
     )

time: 119 us -> 119 us (level)
  Pallas kernels: 13.7 us -> 15.1 us
  waiting for transfers between devices: 23.3 us -> 22 us
    ppermute x11, waiting for transfers between devices: 23.3 us -> 21.9 us  [by_parity(): return lax.ppermute(x, 'z', list(enumerate(to)))]
    pallas_call x9 -> x10, Pallas kernels: 13.7 us -> 15.1 us  [call(): pl.pallas_call(body, out_shape=out_shape, in_specs=[smem if a.dtype == jn...]
  transfers between devices with their start and end apart: 17 -> 17, of which waited for: 8 -> 8; matrix products, arithmetic and copies ran while one was open for 0% -> 0% of each run, Pallas kernels for 5% -> 6%
where the time goes in v10:
time: 119 us; the launch traced here: 117 us
  starting transfers between devices  79.1 us (66%)
  waiting for transfers between devices  22 us (18%)
  Pallas kernels  15.1 us (13%)
    ppermute x11, starting transfers between devices, by_parity(): return lax.ppermute(x, 'z', list(enumerate(to)))  44.7 us
    ppermute x11, waiting for transfers between devices, by_parity(): return lax.ppermute(x, 'z', list(enumerate(to)))  21.9 us
    pallas_call x10, Pallas kernels, call(): pl.pallas_call(body, out_shape=out_shape, in_specs=[smem if a.dtype == jn...  15.1 us
    ppermute x1, starting transfers between devices, half_round(): return lax.ppermute(x, 'z', [(i, (i + n // 2) % n) for i in range(n)])  13.9 us
    ppermute x4, starting transfers between devices, swapped_with(): return lax.ppermute(x, axis, [(0, 1), (1, 0)])  11.1 us
    all_to_all x1, starting transfers between devices, shards(): lax.all_to_all(send, ('xh',) + HEADS, split_axis=0, concat_axis=0, tiled=...  9.39 us
  transfers between devices with their start and end apart: 17, of which 8 were waited for; matrix products, arithmetic and copies ran while one was open for 0% of the time, Pallas kernels for 6%

profile of v10, /device:TPU:6, one launch (start us, length us, event | category | flops | bytes accessed | tf_op | source)
XLA Modules:
  0.0 117.0 jit_solution(6663141652188868018)
XLA Ops:
  0.6 1.4 %pack_keys.1.after_ref.own_ref = bf16[272,128]{1,0:T(8,128)(2,1)} custom-call(s32[128]{0:T(128)} %pos.3, bf16[128,128]{1,0:T(8,128)(2,1)} %k_ref.1, bf16[128,128]{1,0:T(8,128)(2,1)} %v_ref.1), custom_call_target="tpu_custom_call" | custom-call | tf_op jit(solution)/shard_map/pack_keys/pallas_call | solution.py:325
  2.1 2.2 %pack_queries.1 = (bf16[128,640]{1,0:T(8,128)(2,1)}, bf16[16,16,640]{2,1,0:T(8,128)(2,1)}) custom-call(s32[128]{0:T(128)} %pos.3, bf16[128,512]{1,0:T(8,128)(2,1)} %q_ref.1, f32[4,128]{1,0:T(4,128)} %bitcast.3, bf16[16,4096]{1,0:T(8,128)(2,1)} %o_ref.1, bf16[16,4096]{1,0:T(8,128)(2,1)} %g_ref.1, bf16[272,128]{1,0:T(8,128)(2,1)} %pack_keys.1.after_ref.own_ref), custom_call_target="tpu_custom_call" | custom-call | tf_op jit(solution)/shard_map/pack_queries/pallas_call | solution.py:325
  4.3 9.4 %all-to-all-start = ((bf16[16,16,640]{2,1,0:T(8,128)(2,1)}), bf16[16,16,640]{2,1,0:T(8,128)(2,1)S(1)}, u32[]{:S(2)}, u32[]{:S(2)}) async-start(bf16[16,16,640]{2,1,0:T(8,128)(2,1)} %get-tuple-element.27), calls=%async_computation | async-start | bytes 655360 | tf_op jit(solution)/shard_map/all_to_all | solution.py:357
  13.7 3.3 %collective-permute-start.3 = (bf16[128,640]{1,0:T(8,128)(2,1)S(1)}, bf16[128,640]{1,0:T(8,128)(2,1)S(1)}, u32[]{:S(2)}, u32[]{:S(2)}) collective-permute-start(bf16[128,640]{1,0:T(8,128)(2,1)S(1)} %copy-done.1), channel_id=1, source_target_pairs={{0,256},{256,0},{1,257},{257,1},{2,258},{258,2},{3,259},{259,3},{4... | collective-permute-start | bytes 491528 | tf_op jit(solution)/shard_map/ppermute | solution.py:317
  17.0 13.9 %collective-permute-start.2 = (bf16[272,128]{1,0:T(8,128)(2,1)S(1)}, bf16[272,128]{1,0:T(8,128)(2,1)S(1)}, u32[]{:S(2)}, u32[]{:S(2)}) collective-permute-start(bf16[272,128]{1,0:T(8,128)(2,1)S(1)} %copy-done), channel_id=1, source_target_pairs={{0,128},{16,144},{32,160},{48,176},{64,192},{80,208},{96,224},{112... | collective-permute-start | bytes 208904 | tf_op jit(solution)/shard_map/ppermute | solution.py:313
  31.0 4.3 %collective-permute-start.1 = (bf16[272,128]{1,0:T(8,128)(2,1)S(1)}, bf16[272,128]{1,0:T(8,128)(2,1)S(1)}, u32[]{:S(2)}, u32[]{:S(2)}) collective-permute-start(bf16[272,128]{1,0:T(8,128)(2,1)S(1)} %copy-done), channel_id=1, source_target_pairs={{0,64},{16,208},{32,96},{48,240},{64,128},{80,16},{96,160},{112,48... | collective-permute-start | bytes 208904 | tf_op jit(solution)/shard_map/ppermute | solution.py:308
  35.3 5.5 %collective-permute-start = (bf16[272,128]{1,0:T(8,128)(2,1)S(1)}, bf16[272,128]{1,0:T(8,128)(2,1)S(1)}, u32[]{:S(2)}, u32[]{:S(2)}) collective-permute-start(bf16[272,128]{1,0:T(8,128)(2,1)S(1)} %copy-done), channel_id=1, source_target_pairs={{0,192},{16,80},{32,224},{48,112},{64,0},{80,144},{96,32},{112,176... | collective-permute-start | bytes 208904 | tf_op jit(solution)/shard_map/ppermute | solution.py:308
  40.8 2.5 %collective-permute-done.1.b_ref = bf16[272,128]{1,0:T(8,128)(2,1)S(1)} collective-permute-done((bf16[272,128]{1,0:T(8,128)(2,1)S(1)}, bf16[272,128]{1,0:T(8,128)(2,1)S(1)}, u32[]{:S(2)}, u32[]{:S(2)}) %collective-permute-start.1) | collective-permute-done | bytes 69664 | tf_op jit(solution)/shard_map/ppermute | solution.py:308
  43.2 2.2 %collective-permute-done.a_ref = bf16[272,128]{1,0:T(8,128)(2,1)S(1)} collective-permute-done((bf16[272,128]{1,0:T(8,128)(2,1)S(1)}, bf16[272,128]{1,0:T(8,128)(2,1)S(1)}, u32[]{:S(2)}, u32[]{:S(2)}) %collective-permute-start) | collective-permute-done | bytes 69664 | tf_op jit(solution)/shard_map/ppermute | solution.py:308
  45.5 1.9 %collective-permute-start.4 = (bf16[2,128,1280]{2,1,0:T(8,128)(2,1)S(1)}, bf16[2,128,1280]{2,1,0:T(8,128)(2,1)S(1)}, u32[]{:S(2)}, u32[]{:S(2)}) collective-permute-start(bf16[2,128,1280]{2,1,0:T(8,128)(2,1)S(1)} %get-tuple-element.28.x_ref), channel_id=1, source_target_pairs={{0,8},{8,0},{1,9},{9,1},{2,10},{10,2},{3,11},{11,3},{4,12},{12,4},... | collective-permute-start | bytes 1966088 | tf_op jit(solution)/shard_map/ppermute | solution.py:317
  47.4 4.6 %collective-permute-start.7 = (bf16[4,272,128]{2,1,0:T(8,128)(2,1)S(1)}, bf16[4,272,128]{2,1,0:T(8,128)(2,1)S(1)}, u32[]{:S(2)}, u32[]{:S(2)}) collective-permute-start(bf16[4,272,128]{2,1,0:T(8,128)(2,1)S(1)} %get-tuple-element.29.s_ref), channel_id=1, source_target_pairs={{0,224},{16,48},{32,0},{48,80},{64,32},{80,112},{96,64},{112,144},... | collective-permute-start | bytes 835592 | tf_op jit(solution)/shard_map/ppermute | solution.py:308
  52.0 2.7 %collective-permute-start.6 = (bf16[4,272,128]{2,1,0:T(8,128)(2,1)S(1)}, bf16[4,272,128]{2,1,0:T(8,128)(2,1)S(1)}, u32[]{:S(2)}, u32[]{:S(2)}) collective-permute-start(bf16[4,272,128]{2,1,0:T(8,128)(2,1)S(1)} %get-tuple-element.29.s_ref), channel_id=1, source_target_pairs={{0,240},{16,32},{32,16},{48,64},{64,48},{80,96},{96,80},{112,128},... | collective-permute-start | bytes 835592 | tf_op jit(solution)/shard_map/ppermute | solution.py:308
  54.7 1.9 %collective-permute-start.5 = (bf16[4,272,128]{2,1,0:T(8,128)(2,1)S(1)}, bf16[4,272,128]{2,1,0:T(8,128)(2,1)S(1)}, u32[]{:S(2)}, u32[]{:S(2)}) collective-permute-start(bf16[4,272,128]{2,1,0:T(8,128)(2,1)S(1)} %get-tuple-element.29.s_ref), channel_id=1, source_target_pairs={{0,16},{16,0},{32,48},{48,32},{64,80},{80,64},{96,112},{112,96},{1... | collective-permute-start | bytes 835592 | tf_op jit(solution)/shard_map/ppermute | solution.py:308
  56.7 2.6 %with_own.1 = (f32[4,256,128]{2,1,0:T(8,128)S(1)}, f32[4,128,512]{2,1,0:T(8,128)S(1)}) custom-call(bf16[2,128,1280]{2,1,0:T(8,128)(2,1)S(1)} %get-tuple-element.28.x_ref, bf16[2,128,1280]{2,1,0:T(8,128)(2,1)S(1)} %collective-permute-done.4.y_ref, bf16[4,272,128]{2,1,0:T(8,128)(2,1)S(1)} %get-tuple-element.29.s_ref), custom_call_target="tpu_custom_call" | custom-call | tf_op jit(solution)/shard_map/with_own/pallas_call | solution.py:325
  59.3 0.3 collective-permute-done.7.h_ref
  59.7 6.1 %collective-permute-done.6.m_ref = bf16[4,272,128]{2,1,0:T(8,128)(2,1)S(1)} collective-permute-done((bf16[4,272,128]{2,1,0:T(8,128)(2,1)S(1)}, bf16[4,272,128]{2,1,0:T(8,128)(2,1)S(1)}, u32[]{:S(2)}, u32[]{:S(2)}) %collective-permute-start.6) | collective-permute-done | bytes 278560 | tf_op jit(solution)/shard_map/ppermute | solution.py:308
  65.8 3.8 %with_next.1 = (bf16[3,256,128]{2,1,0:T(8,128)(2,1)S(1)}, bf16[4,256,128]{2,1,0:T(8,128)(2,1)S(1)}, f32[4,128,512]{2,1,0:T(8,128)S(1)}) custom-call(bf16[2,128,1280]{2,1,0:T(8,128)(2,1)S(1)} %get-tuple-element.28.x_ref, bf16[2,128,1280]{2,1,0:T(8,128)(2,1)S(1)} %collective-permute-done.4.y_ref, bf16[4,272,128]{2,1,0:T(8,128)(2,1)S(1)} %collective-permute-done.5.p_ref, ...), custom_call_target="tpu_custom_call" | custom-call | tf_op jit(solution)/shard_map/with_next/pallas_call | solution.py:325
  69.6 4.3 %collective-permute-start.10 = (bf16[4,256,128]{2,1,0:T(8,128)(2,1)S(1)}, bf16[4,256,128]{2,1,0:T(8,128)(2,1)S(1)}, u32[]{:S(2)}, u32[]{:S(2)}) collective-permute-start(bf16[4,256,128]{2,1,0:T(8,128)(2,1)S(1)} %get-tuple-element.38), channel_id=1, source_target_pairs={{0,32},{16,240},{32,64},{48,16},{64,96},{80,48},{96,128},{112,80},... | collective-permute-start | bytes 786440 | tf_op jit(solution)/shard_map/ppermute | solution.py:308
  73.9 3.7 %collective-permute-start.9 = (bf16[3,256,128]{2,1,0:T(8,128)(2,1)S(1)}, bf16[3,256,128]{2,1,0:T(8,128)(2,1)S(1)}, u32[]{:S(2)}, u32[]{:S(2)}) collective-permute-start(bf16[3,256,128]{2,1,0:T(8,128)(2,1)S(1)} %get-tuple-element.37), channel_id=1, source_target_pairs={{0,224},{16,48},{32,0},{48,80},{64,32},{80,112},{96,64},{112,144},... | collective-permute-start | bytes 589832 | tf_op jit(solution)/shard_map/ppermute | solution.py:308
  77.6 3.9 %with_nearest.1 = (f32[3,256,128]{2,1,0:T(8,128)S(1)}, bf16[3,256,128]{2,1,0:T(8,128)(2,1)S(1)}, bf16[3,256,128]{2,1,0:T(8,128)(2,1)S(1)}, f32[2,128,512]{2,1,0:T(8,128)S(1)}, bf16[2,128,512]{2,1,0:T(8,128)(2,1)S(1)}) custom-call(bf16[2,128,1280]{2,1,0:T(8,128)(2,1)S(1)} %get-tuple-element.28.x_ref, bf16[2,128,1280]{2,1,0:T(8,128)(2,1)S(1)} %collective-permute-done.4.y_ref, ...), custom_call_target="tpu_custom_call" | custom-call | tf_op jit(solution)/shard_map/with_nearest/pallas_call | solution.py:325
  81.5 1.9 %collective-permute-start.8 = (bf16[2,128,512]{2,1,0:T(8,128)(2,1)S(1)}, bf16[2,128,512]{2,1,0:T(8,128)(2,1)S(1)}, u32[]{:S(2)}, u32[]{:S(2)}) collective-permute-start(bf16[2,128,512]{2,1,0:T(8,128)(2,1)S(1)} %get-tuple-element.34), channel_id=1, source_target_pairs={{0,8},{8,0},{1,9},{9,1},{2,10},{10,2},{3,11},{11,3},{4,12},{12,4},... | collective-permute-start | bytes 786440 | tf_op jit(solution)/shard_map/ppermute | solution.py:317
  83.4 2.3 %collective-permute-done.9.c_ref = bf16[3,256,128]{2,1,0:T(8,128)(2,1)S(1)} collective-permute-done((bf16[3,256,128]{2,1,0:T(8,128)(2,1)S(1)}, bf16[3,256,128]{2,1,0:T(8,128)(2,1)S(1)}, u32[]{:S(2)}, u32[]{:S(2)}) %collective-permute-start.9) | collective-permute-done | bytes 196640 | tf_op jit(solution)/shard_map/ppermute | solution.py:308
  85.8 0.1 sum_first.1
  85.9 3.5 %collective-permute-start.11 = (bf16[3,256,128]{2,1,0:T(8,128)(2,1)S(1)}, bf16[3,256,128]{2,1,0:T(8,128)(2,1)S(1)}, u32[]{:S(2)}, u32[]{:S(2)}) collective-permute-start(bf16[3,256,128]{2,1,0:T(8,128)(2,1)S(1)} %get-tuple-element.42), channel_id=1, source_target_pairs={{0,16},{16,0},{32,48},{48,32},{64,80},{80,64},{96,112},{112,96},{1... | collective-permute-start | bytes 589832 | tf_op jit(solution)/shard_map/ppermute | solution.py:308
  89.3 4.3 %collective-permute-start.12 = (bf16[3,256,128]{2,1,0:T(8,128)(2,1)S(1)}, bf16[3,256,128]{2,1,0:T(8,128)(2,1)S(1)}, u32[]{:S(2)}, u32[]{:S(2)}) collective-permute-start(bf16[3,256,128]{2,1,0:T(8,128)(2,1)S(1)} %get-tuple-element.43), channel_id=1, source_target_pairs={{0,240},{16,32},{32,16},{48,64},{64,48},{80,96},{96,80},{112,128},... | collective-permute-start | bytes 589832 | tf_op jit(solution)/shard_map/ppermute | solution.py:308
  93.7 4.0 %collective-permute-start.15 = (bf16[128,512]{1,0:T(8,128)(2,1)S(1)}, bf16[128,512]{1,0:T(8,128)(2,1)S(1)}, u32[]{:S(2)}, u32[]{:S(2)}) collective-permute-start(bf16[128,512]{1,0:T(8,128)(2,1)S(1)} %get-tuple-element.48), channel_id=1, source_target_pairs={{0,256},{256,0},{1,257},{257,1},{2,258},{258,2},{3,259},{259,3},{4... | collective-permute-start | bytes 393224 | tf_op jit(solution)/shard_map/ppermute | solution.py:317
  97.7 1.3 %collective-permute-done.12.m_ref = bf16[3,256,128]{2,1,0:T(8,128)(2,1)S(1)} collective-permute-done((bf16[3,256,128]{2,1,0:T(8,128)(2,1)S(1)}, bf16[3,256,128]{2,1,0:T(8,128)(2,1)S(1)}, u32[]{:S(2)}, u32[]{:S(2)}) %collective-permute-start.12) | collective-permute-done | bytes 196640 | tf_op jit(solution)/shard_map/ppermute | solution.py:308
  99.0 4.8 %collective-permute-start.13 = (bf16[256,128]{1,0:T(8,128)(2,1)S(1)}, bf16[256,128]{1,0:T(8,128)(2,1)S(1)}, u32[]{:S(2)}, u32[]{:S(2)}) collective-permute-start(bf16[256,128]{1,0:T(8,128)(2,1)S(1)} %get-tuple-element.45), channel_id=1, source_target_pairs={{0,80},{16,192},{32,112},{48,224},{64,144},{80,0},{96,176},{112,32... | collective-permute-start | bytes 196616 | tf_op jit(solution)/shard_map/ppermute | solution.py:308
  103.9 5.2 %collective-permute-start.14 = (bf16[256,128]{1,0:T(8,128)(2,1)S(1)}, bf16[256,128]{1,0:T(8,128)(2,1)S(1)}, u32[]{:S(2)}, u32[]{:S(2)}) collective-permute-start(bf16[256,128]{1,0:T(8,128)(2,1)S(1)} %get-tuple-element.46), channel_id=1, source_target_pairs={{0,176},{16,96},{32,208},{48,128},{64,240},{80,160},{96,16},{112,1... | collective-permute-start | bytes 196616 | tf_op jit(solution)/shard_map/ppermute | solution.py:308
  109.1 1.3 %collective-permute-done.13.u_ref = bf16[256,128]{1,0:T(8,128)(2,1)S(1)} collective-permute-done((bf16[256,128]{1,0:T(8,128)(2,1)S(1)}, bf16[256,128]{1,0:T(8,128)(2,1)S(1)}, u32[]{:S(2)}, u32[]{:S(2)}) %collective-permute-start.13) | collective-permute-done | bytes 65568 | tf_op jit(solution)/shard_map/ppermute | solution.py:308
  110.4 5.9 %collective-permute-done.14.w_ref = bf16[256,128]{1,0:T(8,128)(2,1)S(1)} collective-permute-done((bf16[256,128]{1,0:T(8,128)(2,1)S(1)}, bf16[256,128]{1,0:T(8,128)(2,1)S(1)}, u32[]{:S(2)}, u32[]{:S(2)}) %collective-permute-start.14) | collective-permute-done | bytes 65568 | tf_op jit(solution)/shard_map/ppermute | solution.py:308
  116.3 0.7 finish.1
  (16 shorter events, 0.2 us)
Async XLA Ops:
  4.3 9.4 %copy-start.1 = (bf16[128,640]{1,0:T(8,128)(2,1)S(1)}, bf16[128,640]{1,0:T(8,128)(2,1)}, u32[]{:S(2)}) copy-start(bf16[128,640]{1,0:T(8,128)(2,1)} %get-tuple-element.26.q_ref) | copy-start | bytes 491524
  4.3 12.7 %copy-start = (bf16[272,128]{1,0:T(8,128)(2,1)S(1)}, bf16[272,128]{1,0:T(8,128)(2,1)}, u32[]{:S(2)}) copy-start(bf16[272,128]{1,0:T(8,128)(2,1)} %pack_keys.1.after_ref.own_ref) | copy-start | bytes 208900
  4.3 41.1 %all-to-all-start = ((bf16[16,16,640]{2,1,0:T(8,128)(2,1)}), bf16[16,16,640]{2,1,0:T(8,128)(2,1)S(1)}, u32[]{:S(2)}, u32[]{:S(2)}) async-start(bf16[16,16,640]{2,1,0:T(8,128)(2,1)} %get-tuple-element.27), calls=%async_computation | async-start | bytes 655360 | tf_op jit(solution)/shard_map/all_to_all | solution.py:357
  13.7 31.7 %collective-permute-start.3 = (bf16[128,640]{1,0:T(8,128)(2,1)S(1)}, bf16[128,640]{1,0:T(8,128)(2,1)S(1)}, u32[]{:S(2)}, u32[]{:S(2)}) collective-permute-start(bf16[128,640]{1,0:T(8,128)(2,1)S(1)} %copy-done.1), channel_id=1, source_target_pairs={{0,256},{256,0},{1,257},{257,1},{2,258},{258,2},{3,259},{259,3},{4... | collective-permute-start | bytes 491528 | tf_op jit(solution)/shard_map/ppermute | solution.py:317
  17.0 23.7 %collective-permute-start.2 = (bf16[272,128]{1,0:T(8,128)(2,1)S(1)}, bf16[272,128]{1,0:T(8,128)(2,1)S(1)}, u32[]{:S(2)}, u32[]{:S(2)}) collective-permute-start(bf16[272,128]{1,0:T(8,128)(2,1)S(1)} %copy-done), channel_id=1, source_target_pairs={{0,128},{16,144},{32,160},{48,176},{64,192},{80,208},{96,224},{112... | collective-permute-start | bytes 208904 | tf_op jit(solution)/shard_map/ppermute | solution.py:313
  31.0 12.2 %collective-permute-start.1 = (bf16[272,128]{1,0:T(8,128)(2,1)S(1)}, bf16[272,128]{1,0:T(8,128)(2,1)S(1)}, u32[]{:S(2)}, u32[]{:S(2)}) collective-permute-start(bf16[272,128]{1,0:T(8,128)(2,1)S(1)} %copy-done), channel_id=1, source_target_pairs={{0,64},{16,208},{32,96},{48,240},{64,128},{80,16},{96,160},{112,48... | collective-permute-start | bytes 208904 | tf_op jit(solution)/shard_map/ppermute | solution.py:308
  35.3 10.1 %collective-permute-start = (bf16[272,128]{1,0:T(8,128)(2,1)S(1)}, bf16[272,128]{1,0:T(8,128)(2,1)S(1)}, u32[]{:S(2)}, u32[]{:S(2)}) collective-permute-start(bf16[272,128]{1,0:T(8,128)(2,1)S(1)} %copy-done), channel_id=1, source_target_pairs={{0,192},{16,80},{32,224},{48,112},{64,0},{80,144},{96,32},{112,176... | collective-permute-start | bytes 208904 | tf_op jit(solution)/shard_map/ppermute | solution.py:308
  45.5 11.2 %collective-permute-start.4 = (bf16[2,128,1280]{2,1,0:T(8,128)(2,1)S(1)}, bf16[2,128,1280]{2,1,0:T(8,128)(2,1)S(1)}, u32[]{:S(2)}, u32[]{:S(2)}) collective-permute-start(bf16[2,128,1280]{2,1,0:T(8,128)(2,1)S(1)} %get-tuple-element.28.x_ref), channel_id=1, source_target_pairs={{0,8},{8,0},{1,9},{9,1},{2,10},{10,2},{3,11},{11,3},{4,12},{12,4},... | collective-permute-start | bytes 1966088 | tf_op jit(solution)/shard_map/ppermute | solution.py:317
  47.4 12.2 %collective-permute-start.7 = (bf16[4,272,128]{2,1,0:T(8,128)(2,1)S(1)}, bf16[4,272,128]{2,1,0:T(8,128)(2,1)S(1)}, u32[]{:S(2)}, u32[]{:S(2)}) collective-permute-start(bf16[4,272,128]{2,1,0:T(8,128)(2,1)S(1)} %get-tuple-element.29.s_ref), channel_id=1, source_target_pairs={{0,224},{16,48},{32,0},{48,80},{64,32},{80,112},{96,64},{112,144},... | collective-permute-start | bytes 835592 | tf_op jit(solution)/shard_map/ppermute | solution.py:308
  52.0 13.8 %collective-permute-start.6 = (bf16[4,272,128]{2,1,0:T(8,128)(2,1)S(1)}, bf16[4,272,128]{2,1,0:T(8,128)(2,1)S(1)}, u32[]{:S(2)}, u32[]{:S(2)}) collective-permute-start(bf16[4,272,128]{2,1,0:T(8,128)(2,1)S(1)} %get-tuple-element.29.s_ref), channel_id=1, source_target_pairs={{0,240},{16,32},{32,16},{48,64},{64,48},{80,96},{96,80},{112,128},... | collective-permute-start | bytes 835592 | tf_op jit(solution)/shard_map/ppermute | solution.py:308
  54.7 11.1 %collective-permute-start.5 = (bf16[4,272,128]{2,1,0:T(8,128)(2,1)S(1)}, bf16[4,272,128]{2,1,0:T(8,128)(2,1)S(1)}, u32[]{:S(2)}, u32[]{:S(2)}) collective-permute-start(bf16[4,272,128]{2,1,0:T(8,128)(2,1)S(1)} %get-tuple-element.29.s_ref), channel_id=1, source_target_pairs={{0,16},{16,0},{32,48},{48,32},{64,80},{80,64},{96,112},{112,96},{1... | collective-permute-start | bytes 835592 | tf_op jit(solution)/shard_map/ppermute | solution.py:308
  69.6 16.2 %collective-permute-start.10 = (bf16[4,256,128]{2,1,0:T(8,128)(2,1)S(1)}, bf16[4,256,128]{2,1,0:T(8,128)(2,1)S(1)}, u32[]{:S(2)}, u32[]{:S(2)}) collective-permute-start(bf16[4,256,128]{2,1,0:T(8,128)(2,1)S(1)} %get-tuple-element.38), channel_id=1, source_target_pairs={{0,32},{16,240},{32,64},{48,16},{64,96},{80,48},{96,128},{112,80},... | collective-permute-start | bytes 786440 | tf_op jit(solution)/shard_map/ppermute | solution.py:308
  73.9 11.9 %collective-permute-start.9 = (bf16[3,256,128]{2,1,0:T(8,128)(2,1)S(1)}, bf16[3,256,128]{2,1,0:T(8,128)(2,1)S(1)}, u32[]{:S(2)}, u32[]{:S(2)}) collective-permute-start(bf16[3,256,128]{2,1,0:T(8,128)(2,1)S(1)} %get-tuple-element.37), channel_id=1, source_target_pairs={{0,224},{16,48},{32,0},{48,80},{64,32},{80,112},{96,64},{112,144},... | collective-permute-start | bytes 589832 | tf_op jit(solution)/shard_map/ppermute | solution.py:308
  81.5 12.1 %collective-permute-start.8 = (bf16[2,128,512]{2,1,0:T(8,128)(2,1)S(1)}, bf16[2,128,512]{2,1,0:T(8,128)(2,1)S(1)}, u32[]{:S(2)}, u32[]{:S(2)}) collective-permute-start(bf16[2,128,512]{2,1,0:T(8,128)(2,1)S(1)} %get-tuple-element.34), channel_id=1, source_target_pairs={{0,8},{8,0},{1,9},{9,1},{2,10},{10,2},{3,11},{11,3},{4,12},{12,4},... | collective-permute-start | bytes 786440 | tf_op jit(solution)/shard_map/ppermute | solution.py:317
  85.9 11.8 %collective-permute-start.11 = (bf16[3,256,128]{2,1,0:T(8,128)(2,1)S(1)}, bf16[3,256,128]{2,1,0:T(8,128)(2,1)S(1)}, u32[]{:S(2)}, u32[]{:S(2)}) collective-permute-start(bf16[3,256,128]{2,1,0:T(8,128)(2,1)S(1)} %get-tuple-element.42), channel_id=1, source_target_pairs={{0,16},{16,0},{32,48},{48,32},{64,80},{80,64},{96,112},{112,96},{1... | collective-permute-start | bytes 589832 | tf_op jit(solution)/shard_map/ppermute | solution.py:308
  89.3 9.6 %collective-permute-start.12 = (bf16[3,256,128]{2,1,0:T(8,128)(2,1)S(1)}, bf16[3,256,128]{2,1,0:T(8,128)(2,1)S(1)}, u32[]{:S(2)}, u32[]{:S(2)}) collective-permute-start(bf16[3,256,128]{2,1,0:T(8,128)(2,1)S(1)} %get-tuple-element.43), channel_id=1, source_target_pairs={{0,240},{16,32},{32,16},{48,64},{64,48},{80,96},{96,80},{112,128},... | collective-permute-start | bytes 589832 | tf_op jit(solution)/shard_map/ppermute | solution.py:308
  93.7 15.4 %collective-permute-start.15 = (bf16[128,512]{1,0:T(8,128)(2,1)S(1)}, bf16[128,512]{1,0:T(8,128)(2,1)S(1)}, u32[]{:S(2)}, u32[]{:S(2)}) collective-permute-start(bf16[128,512]{1,0:T(8,128)(2,1)S(1)} %get-tuple-element.48), channel_id=1, source_target_pairs={{0,256},{256,0},{1,257},{257,1},{2,258},{258,2},{3,259},{259,3},{4... | collective-permute-start | bytes 393224 | tf_op jit(solution)/shard_map/ppermute | solution.py:317
  99.0 11.3 %collective-permute-start.13 = (bf16[256,128]{1,0:T(8,128)(2,1)S(1)}, bf16[256,128]{1,0:T(8,128)(2,1)S(1)}, u32[]{:S(2)}, u32[]{:S(2)}) collective-permute-start(bf16[256,128]{1,0:T(8,128)(2,1)S(1)} %get-tuple-element.45), channel_id=1, source_target_pairs={{0,80},{16,192},{32,112},{48,224},{64,144},{80,0},{96,176},{112,32... | collective-permute-start | bytes 196616 | tf_op jit(solution)/shard_map/ppermute | solution.py:308
  103.9 12.4 %collective-permute-start.14 = (bf16[256,128]{1,0:T(8,128)(2,1)S(1)}, bf16[256,128]{1,0:T(8,128)(2,1)S(1)}, u32[]{:S(2)}, u32[]{:S(2)}) collective-permute-start(bf16[256,128]{1,0:T(8,128)(2,1)S(1)} %get-tuple-element.46), channel_id=1, source_target_pairs={{0,176},{16,96},{32,208},{48,128},{64,240},{80,160},{96,16},{112,1... | collective-permute-start | bytes 196616 | tf_op jit(solution)/shard_map/ppermute | solution.py:308

commit v11 on v10

--- a/solution.py
+++ b/solution.py
@@ -263,12 +263,11 @@
     x_out[1, :, wide:] = grad_ref[1 - half]
 
 
-def sum_first(own_ref, c_ref, d_ref, p_ref, m_ref, own_out, p_out, m_out):
+def sum_first(own_ref, c_ref, d_ref, p_ref, own_out, p_out):
     own_out[...] = own_ref[...] + c_ref[...].astype(F32) + d_ref[:NEAR].astype(F32)
     p_out[: NEAR - 1] = p_ref[: NEAR - 1]
     last = p_ref[NEAR - 1].astype(F32) + d_ref[NEAR].astype(F32)
     p_out[NEAR - 1] = last.astype(BF16)
-    m_out[...] = m_ref[...]
 
 
 def sum_near(own_ref, p_ref, m_ref, own_out, u_out, w_out):
@@ -399,10 +398,11 @@
     )
 
     p2_in, m2_in = by_parity(p2_g, -2), by_parity(m2_g, 2)
-    own_g, p1_g, m1_g = local_call(sum_first, (like(near, F32), like(near), like(near)), 8)(
-        own_g, p2_in, m2_in, p1_g, m1_g
-    )
-    p1_in, m1_in = by_parity(p1_g, 1), by_parity(m1_g, -1)
+    m1_in = by_parity(m1_g, -1)
+    own_g, p1_g = local_call(sum_first, (like(near, F32), like(near)), 8)(
+        own_g, p2_in, m2_in, p1_g
+    )
+    p1_in = by_parity(p1_g, 1)
     dq_core = swapped_with(dq_core, "core")
     dq, dqx, flag = local_call(
         sum_cores, (like(dq_shape[1:], F32), like(dq_shape[1:]), like((BLK, HEAD), F32)), 8

time: 119 us -> 117 us (0.983)
  waiting for transfers between devices: 22 us -> 20.8 us
  transfers between devices with their start and end apart: 17 -> 17, of which waited for: 8 -> 7; matrix products, arithmetic and copies ran while one was open for 0% -> 0% of each run, Pallas kernels for 6% -> 6%
where the time goes in v11:
time: 117 us; the launch traced here: 115 us
  starting transfers between devices  78 us (67%)
  waiting for transfers between devices  20.8 us (18%)
  Pallas kernels  15.1 us (13%)
    ppermute x11, starting transfers between devices, by_parity(): return lax.ppermute(x, 'z', list(enumerate(to)))  43.5 us
    ppermute x11, waiting for transfers between devices, by_parity(): return lax.ppermute(x, 'z', list(enumerate(to)))  20.8 us
    pallas_call x10, Pallas kernels, call(): pl.pallas_call(body, out_shape=out_shape, in_specs=[smem if a.dtype == jn...  15.1 us
    ppermute x1, starting transfers between devices, half_round(): return lax.ppermute(x, 'z', [(i, (i + n // 2) % n) for i in range(n)])  13.9 us
    ppermute x4, starting transfers between devices, swapped_with(): return lax.ppermute(x, axis, [(0, 1), (1, 0)])  11.1 us
    all_to_all x1, starting transfers between devices, shards(): lax.all_to_all(send, ('xh',) + HEADS, split_axis=0, concat_axis=0, tiled=...  9.39 us
  transfers between devices with their start and end apart: 17, of which 7 were waited for; matrix products, arithmetic and copies ran while one was open for 0% of the time, Pallas kernels for 6%

profile of v11, /device:TPU:6, one launch (start us, length us, event | category | flops | bytes accessed | tf_op | source)
XLA Modules:
  0.0 114.7 jit_solution(8624033020996246452)
XLA Ops:
  0.6 1.4 %pack_keys.1.after_ref.own_ref = bf16[272,128]{1,0:T(8,128)(2,1)} custom-call(s32[128]{0:T(128)} %pos.3, bf16[128,128]{1,0:T(8,128)(2,1)} %k_ref.1, bf16[128,128]{1,0:T(8,128)(2,1)} %v_ref.1), custom_call_target="tpu_custom_call" | custom-call | tf_op jit(solution)/shard_map/pack_keys/pallas_call | solution.py:324
  2.1 2.2 %pack_queries.1 = (bf16[128,640]{1,0:T(8,128)(2,1)}, bf16[16,16,640]{2,1,0:T(8,128)(2,1)}) custom-call(s32[128]{0:T(128)} %pos.3, bf16[128,512]{1,0:T(8,128)(2,1)} %q_ref.1, f32[4,128]{1,0:T(4,128)} %bitcast.3, bf16[16,4096]{1,0:T(8,128)(2,1)} %o_ref.1, bf16[16,4096]{1,0:T(8,128)(2,1)} %g_ref.1, bf16[272,128]{1,0:T(8,128)(2,1)} %pack_keys.1.after_ref.own_ref), custom_call_target="tpu_custom_call" | custom-call | tf_op jit(solution)/shard_map/pack_queries/pallas_call | solution.py:324
  4.3 9.4 %all-to-all-start = ((bf16[16,16,640]{2,1,0:T(8,128)(2,1)}), bf16[16,16,640]{2,1,0:T(8,128)(2,1)S(1)}, u32[]{:S(2)}, u32[]{:S(2)}) async-start(bf16[16,16,640]{2,1,0:T(8,128)(2,1)} %get-tuple-element.26), calls=%async_computation | async-start | bytes 655360 | tf_op jit(solution)/shard_map/all_to_all | solution.py:356
  13.7 3.3 %collective-permute-start.3 = (bf16[128,640]{1,0:T(8,128)(2,1)S(1)}, bf16[128,640]{1,0:T(8,128)(2,1)S(1)}, u32[]{:S(2)}, u32[]{:S(2)}) collective-permute-start(bf16[128,640]{1,0:T(8,128)(2,1)S(1)} %copy-done.1), channel_id=1, source_target_pairs={{0,256},{256,0},{1,257},{257,1},{2,258},{258,2},{3,259},{259,3},{4... | collective-permute-start | bytes 491528 | tf_op jit(solution)/shard_map/ppermute | solution.py:316
  17.0 13.9 %collective-permute-start.2 = (bf16[272,128]{1,0:T(8,128)(2,1)S(1)}, bf16[272,128]{1,0:T(8,128)(2,1)S(1)}, u32[]{:S(2)}, u32[]{:S(2)}) collective-permute-start(bf16[272,128]{1,0:T(8,128)(2,1)S(1)} %copy-done), channel_id=1, source_target_pairs={{0,128},{16,144},{32,160},{48,176},{64,192},{80,208},{96,224},{112... | collective-permute-start | bytes 208904 | tf_op jit(solution)/shard_map/ppermute | solution.py:312
  31.0 4.3 %collective-permute-start.1 = (bf16[272,128]{1,0:T(8,128)(2,1)S(1)}, bf16[272,128]{1,0:T(8,128)(2,1)S(1)}, u32[]{:S(2)}, u32[]{:S(2)}) collective-permute-start(bf16[272,128]{1,0:T(8,128)(2,1)S(1)} %copy-done), channel_id=1, source_target_pairs={{0,64},{16,208},{32,96},{48,240},{64,128},{80,16},{96,160},{112,48... | collective-permute-start | bytes 208904 | tf_op jit(solution)/shard_map/ppermute | solution.py:307
  35.3 5.5 %collective-permute-start = (bf16[272,128]{1,0:T(8,128)(2,1)S(1)}, bf16[272,128]{1,0:T(8,128)(2,1)S(1)}, u32[]{:S(2)}, u32[]{:S(2)}) collective-permute-start(bf16[272,128]{1,0:T(8,128)(2,1)S(1)} %copy-done), channel_id=1, source_target_pairs={{0,192},{16,80},{32,224},{48,112},{64,0},{80,144},{96,32},{112,176... | collective-permute-start | bytes 208904 | tf_op jit(solution)/shard_map/ppermute | solution.py:307
  40.8 2.5 %collective-permute-done.1.b_ref = bf16[272,128]{1,0:T(8,128)(2,1)S(1)} collective-permute-done((bf16[272,128]{1,0:T(8,128)(2,1)S(1)}, bf16[272,128]{1,0:T(8,128)(2,1)S(1)}, u32[]{:S(2)}, u32[]{:S(2)}) %collective-permute-start.1) | collective-permute-done | bytes 69664 | tf_op jit(solution)/shard_map/ppermute | solution.py:307
  43.2 2.2 %collective-permute-done.a_ref = bf16[272,128]{1,0:T(8,128)(2,1)S(1)} collective-permute-done((bf16[272,128]{1,0:T(8,128)(2,1)S(1)}, bf16[272,128]{1,0:T(8,128)(2,1)S(1)}, u32[]{:S(2)}, u32[]{:S(2)}) %collective-permute-start) | collective-permute-done | bytes 69664 | tf_op jit(solution)/shard_map/ppermute | solution.py:307
  45.5 1.9 %collective-permute-start.4 = (bf16[2,128,1280]{2,1,0:T(8,128)(2,1)S(1)}, bf16[2,128,1280]{2,1,0:T(8,128)(2,1)S(1)}, u32[]{:S(2)}, u32[]{:S(2)}) collective-permute-start(bf16[2,128,1280]{2,1,0:T(8,128)(2,1)S(1)} %get-tuple-element.27.x_ref), channel_id=1, source_target_pairs={{0,8},{8,0},{1,9},{9,1},{2,10},{10,2},{3,11},{11,3},{4,12},{12,4},... | collective-permute-start | bytes 1966088 | tf_op jit(solution)/shard_map/ppermute | solution.py:316
  47.4 4.6 %collective-permute-start.7 = (bf16[4,272,128]{2,1,0:T(8,128)(2,1)S(1)}, bf16[4,272,128]{2,1,0:T(8,128)(2,1)S(1)}, u32[]{:S(2)}, u32[]{:S(2)}) collective-permute-start(bf16[4,272,128]{2,1,0:T(8,128)(2,1)S(1)} %get-tuple-element.28.s_ref), channel_id=1, source_target_pairs={{0,224},{16,48},{32,0},{48,80},{64,32},{80,112},{96,64},{112,144},... | collective-permute-start | bytes 835592 | tf_op jit(solution)/shard_map/ppermute | solution.py:307
  52.0 2.7 %collective-permute-start.6 = (bf16[4,272,128]{2,1,0:T(8,128)(2,1)S(1)}, bf16[4,272,128]{2,1,0:T(8,128)(2,1)S(1)}, u32[]{:S(2)}, u32[]{:S(2)}) collective-permute-start(bf16[4,272,128]{2,1,0:T(8,128)(2,1)S(1)} %get-tuple-element.28.s_ref), channel_id=1, source_target_pairs={{0,240},{16,32},{32,16},{48,64},{64,48},{80,96},{96,80},{112,128},... | collective-permute-start | bytes 835592 | tf_op jit(solution)/shard_map/ppermute | solution.py:307
  54.7 1.9 %collective-permute-start.5 = (bf16[4,272,128]{2,1,0:T(8,128)(2,1)S(1)}, bf16[4,272,128]{2,1,0:T(8,128)(2,1)S(1)}, u32[]{:S(2)}, u32[]{:S(2)}) collective-permute-start(bf16[4,272,128]{2,1,0:T(8,128)(2,1)S(1)} %get-tuple-element.28.s_ref), channel_id=1, source_target_pairs={{0,16},{16,0},{32,48},{48,32},{64,80},{80,64},{96,112},{112,96},{1... | collective-permute-start | bytes 835592 | tf_op jit(solution)/shard_map/ppermute | solution.py:307
  56.7 2.6 %with_own.1 = (f32[4,256,128]{2,1,0:T(8,128)S(1)}, f32[4,128,512]{2,1,0:T(8,128)S(1)}) custom-call(bf16[2,128,1280]{2,1,0:T(8,128)(2,1)S(1)} %get-tuple-element.27.x_ref, bf16[2,128,1280]{2,1,0:T(8,128)(2,1)S(1)} %collective-permute-done.4.y_ref, bf16[4,272,128]{2,1,0:T(8,128)(2,1)S(1)} %get-tuple-element.28.s_ref), custom_call_target="tpu_custom_call" | custom-call | tf_op jit(solution)/shard_map/with_own/pallas_call | solution.py:324
  59.3 0.3 collective-permute-done.7.h_ref
  59.7 6.1 %collective-permute-done.6.m_ref = bf16[4,272,128]{2,1,0:T(8,128)(2,1)S(1)} collective-permute-done((bf16[4,272,128]{2,1,0:T(8,128)(2,1)S(1)}, bf16[4,272,128]{2,1,0:T(8,128)(2,1)S(1)}, u32[]{:S(2)}, u32[]{:S(2)}) %collective-permute-start.6) | collective-permute-done | bytes 278560 | tf_op jit(solution)/shard_map/ppermute | solution.py:307
  65.8 3.8 %with_next.1 = (bf16[3,256,128]{2,1,0:T(8,128)(2,1)S(1)}, bf16[4,256,128]{2,1,0:T(8,128)(2,1)S(1)}, f32[4,128,512]{2,1,0:T(8,128)S(1)}) custom-call(bf16[2,128,1280]{2,1,0:T(8,128)(2,1)S(1)} %get-tuple-element.27.x_ref, bf16[2,128,1280]{2,1,0:T(8,128)(2,1)S(1)} %collective-permute-done.4.y_ref, bf16[4,272,128]{2,1,0:T(8,128)(2,1)S(1)} %collective-permute-done.5.p_ref, ...), custom_call_target="tpu_custom_call" | custom-call | tf_op jit(solution)/shard_map/with_next/pallas_call | solution.py:324
  69.6 4.3 %collective-permute-start.10 = (bf16[4,256,128]{2,1,0:T(8,128)(2,1)S(1)}, bf16[4,256,128]{2,1,0:T(8,128)(2,1)S(1)}, u32[]{:S(2)}, u32[]{:S(2)}) collective-permute-start(bf16[4,256,128]{2,1,0:T(8,128)(2,1)S(1)} %get-tuple-element.37), channel_id=1, source_target_pairs={{0,32},{16,240},{32,64},{48,16},{64,96},{80,48},{96,128},{112,80},... | collective-permute-start | bytes 786440 | tf_op jit(solution)/shard_map/ppermute | solution.py:307
  73.9 3.7 %collective-permute-start.9 = (bf16[3,256,128]{2,1,0:T(8,128)(2,1)S(1)}, bf16[3,256,128]{2,1,0:T(8,128)(2,1)S(1)}, u32[]{:S(2)}, u32[]{:S(2)}) collective-permute-start(bf16[3,256,128]{2,1,0:T(8,128)(2,1)S(1)} %get-tuple-element.36), channel_id=1, source_target_pairs={{0,224},{16,48},{32,0},{48,80},{64,32},{80,112},{96,64},{112,144},... | collective-permute-start | bytes 589832 | tf_op jit(solution)/shard_map/ppermute | solution.py:307
  77.6 3.9 %with_nearest.1 = (f32[3,256,128]{2,1,0:T(8,128)S(1)}, bf16[3,256,128]{2,1,0:T(8,128)(2,1)S(1)}, bf16[3,256,128]{2,1,0:T(8,128)(2,1)S(1)}, f32[2,128,512]{2,1,0:T(8,128)S(1)}, bf16[2,128,512]{2,1,0:T(8,128)(2,1)S(1)}) custom-call(bf16[2,128,1280]{2,1,0:T(8,128)(2,1)S(1)} %get-tuple-element.27.x_ref, bf16[2,128,1280]{2,1,0:T(8,128)(2,1)S(1)} %collective-permute-done.4.y_ref, ...), custom_call_target="tpu_custom_call" | custom-call | tf_op jit(solution)/shard_map/with_nearest/pallas_call | solution.py:324
  81.5 1.9 %collective-permute-start.8 = (bf16[2,128,512]{2,1,0:T(8,128)(2,1)S(1)}, bf16[2,128,512]{2,1,0:T(8,128)(2,1)S(1)}, u32[]{:S(2)}, u32[]{:S(2)}) collective-permute-start(bf16[2,128,512]{2,1,0:T(8,128)(2,1)S(1)} %get-tuple-element.33), channel_id=1, source_target_pairs={{0,8},{8,0},{1,9},{9,1},{2,10},{10,2},{3,11},{11,3},{4,12},{12,4},... | collective-permute-start | bytes 786440 | tf_op jit(solution)/shard_map/ppermute | solution.py:316
  83.4 4.4 %collective-permute-start.12 = (bf16[3,256,128]{2,1,0:T(8,128)(2,1)S(1)}, bf16[3,256,128]{2,1,0:T(8,128)(2,1)S(1)}, u32[]{:S(2)}, u32[]{:S(2)}) collective-permute-start(bf16[3,256,128]{2,1,0:T(8,128)(2,1)S(1)} %get-tuple-element.41), channel_id=1, source_target_pairs={{0,240},{16,32},{32,16},{48,64},{64,48},{80,96},{96,80},{112,128},... | collective-permute-start | bytes 589832 | tf_op jit(solution)/shard_map/ppermute | solution.py:307
  87.8 0.1 sum_first.1
  87.9 1.9 %collective-permute-start.11 = (bf16[3,256,128]{2,1,0:T(8,128)(2,1)S(1)}, bf16[3,256,128]{2,1,0:T(8,128)(2,1)S(1)}, u32[]{:S(2)}, u32[]{:S(2)}) collective-permute-start(bf16[3,256,128]{2,1,0:T(8,128)(2,1)S(1)} %get-tuple-element.40), channel_id=1, source_target_pairs={{0,16},{16,0},{32,48},{48,32},{64,80},{80,64},{96,112},{112,96},{1... | collective-permute-start | bytes 589832 | tf_op jit(solution)/shard_map/ppermute | solution.py:307
  89.9 0.1 sum_cores.1
  89.9 4.0 %collective-permute-start.15 = (bf16[128,512]{1,0:T(8,128)(2,1)S(1)}, bf16[128,512]{1,0:T(8,128)(2,1)S(1)}, u32[]{:S(2)}, u32[]{:S(2)}) collective-permute-start(bf16[128,512]{1,0:T(8,128)(2,1)S(1)} %get-tuple-element.46), channel_id=1, source_target_pairs={{0,256},{256,0},{1,257},{257,1},{2,258},{258,2},{3,259},{259,3},{4... | collective-permute-start | bytes 393224 | tf_op jit(solution)/shard_map/ppermute | solution.py:316
  93.9 2.9 %collective-permute-done.11.p_ref = bf16[3,256,128]{2,1,0:T(8,128)(2,1)S(1)} collective-permute-done((bf16[3,256,128]{2,1,0:T(8,128)(2,1)S(1)}, bf16[3,256,128]{2,1,0:T(8,128)(2,1)S(1)}, u32[]{:S(2)}, u32[]{:S(2)}) %collective-permute-start.11) | collective-permute-done | bytes 196640 | tf_op jit(solution)/shard_map/ppermute | solution.py:307
  96.9 4.7 %collective-permute-start.13 = (bf16[256,128]{1,0:T(8,128)(2,1)S(1)}, bf16[256,128]{1,0:T(8,128)(2,1)S(1)}, u32[]{:S(2)}, u32[]{:S(2)}) collective-permute-start(bf16[256,128]{1,0:T(8,128)(2,1)S(1)} %get-tuple-element.43), channel_id=1, source_target_pairs={{0,80},{16,192},{32,112},{48,224},{64,144},{80,0},{96,176},{112,32... | collective-permute-start | bytes 196616 | tf_op jit(solution)/shard_map/ppermute | solution.py:307
  101.6 5.5 %collective-permute-start.14 = (bf16[256,128]{1,0:T(8,128)(2,1)S(1)}, bf16[256,128]{1,0:T(8,128)(2,1)S(1)}, u32[]{:S(2)}, u32[]{:S(2)}) collective-permute-start(bf16[256,128]{1,0:T(8,128)(2,1)S(1)} %get-tuple-element.44), channel_id=1, source_target_pairs={{0,176},{16,96},{32,208},{48,128},{64,240},{80,160},{96,16},{112,1... | collective-permute-start | bytes 196616 | tf_op jit(solution)/shard_map/ppermute | solution.py:307
  107.2 1.2 %collective-permute-done.13.u_ref = bf16[256,128]{1,0:T(8,128)(2,1)S(1)} collective-permute-done((bf16[256,128]{1,0:T(8,128)(2,1)S(1)}, bf16[256,128]{1,0:T(8,128)(2,1)S(1)}, u32[]{:S(2)}, u32[]{:S(2)}) %collective-permute-start.13) | collective-permute-done | bytes 65568 | tf_op jit(solution)/shard_map/ppermute | solution.py:307
  108.4 5.5 %collective-permute-done.14.w_ref = bf16[256,128]{1,0:T(8,128)(2,1)S(1)} collective-permute-done((bf16[256,128]{1,0:T(8,128)(2,1)S(1)}, bf16[256,128]{1,0:T(8,128)(2,1)S(1)}, u32[]{:S(2)}, u32[]{:S(2)}) %collective-permute-start.14) | collective-permute-done | bytes 65568 | tf_op jit(solution)/shard_map/ppermute | solution.py:307
  113.9 0.7 finish.1
  (16 shorter events, 0.2 us)
Async XLA Ops:
  4.3 9.4 %copy-start.1 = (bf16[128,640]{1,0:T(8,128)(2,1)S(1)}, bf16[128,640]{1,0:T(8,128)(2,1)}, u32[]{:S(2)}) copy-start(bf16[128,640]{1,0:T(8,128)(2,1)} %get-tuple-element.25.q_ref) | copy-start | bytes 491524
  4.3 12.7 %copy-start = (bf16[272,128]{1,0:T(8,128)(2,1)S(1)}, bf16[272,128]{1,0:T(8,128)(2,1)}, u32[]{:S(2)}) copy-start(bf16[272,128]{1,0:T(8,128)(2,1)} %pack_keys.1.after_ref.own_ref) | copy-start | bytes 208900
  4.3 41.1 %all-to-all-start = ((bf16[16,16,640]{2,1,0:T(8,128)(2,1)}), bf16[16,16,640]{2,1,0:T(8,128)(2,1)S(1)}, u32[]{:S(2)}, u32[]{:S(2)}) async-start(bf16[16,16,640]{2,1,0:T(8,128)(2,1)} %get-tuple-element.26), calls=%async_computation | async-start | bytes 655360 | tf_op jit(solution)/shard_map/all_to_all | solution.py:356
  13.7 31.7 %collective-permute-start.3 = (bf16[128,640]{1,0:T(8,128)(2,1)S(1)}, bf16[128,640]{1,0:T(8,128)(2,1)S(1)}, u32[]{:S(2)}, u32[]{:S(2)}) collective-permute-start(bf16[128,640]{1,0:T(8,128)(2,1)S(1)} %copy-done.1), channel_id=1, source_target_pairs={{0,256},{256,0},{1,257},{257,1},{2,258},{258,2},{3,259},{259,3},{4... | collective-permute-start | bytes 491528 | tf_op jit(solution)/shard_map/ppermute | solution.py:316
  17.0 23.7 %collective-permute-start.2 = (bf16[272,128]{1,0:T(8,128)(2,1)S(1)}, bf16[272,128]{1,0:T(8,128)(2,1)S(1)}, u32[]{:S(2)}, u32[]{:S(2)}) collective-permute-start(bf16[272,128]{1,0:T(8,128)(2,1)S(1)} %copy-done), channel_id=1, source_target_pairs={{0,128},{16,144},{32,160},{48,176},{64,192},{80,208},{96,224},{112... | collective-permute-start | bytes 208904 | tf_op jit(solution)/shard_map/ppermute | solution.py:312
  31.0 12.2 %collective-permute-start.1 = (bf16[272,128]{1,0:T(8,128)(2,1)S(1)}, bf16[272,128]{1,0:T(8,128)(2,1)S(1)}, u32[]{:S(2)}, u32[]{:S(2)}) collective-permute-start(bf16[272,128]{1,0:T(8,128)(2,1)S(1)} %copy-done), channel_id=1, source_target_pairs={{0,64},{16,208},{32,96},{48,240},{64,128},{80,16},{96,160},{112,48... | collective-permute-start | bytes 208904 | tf_op jit(solution)/shard_map/ppermute | solution.py:307
  35.3 10.1 %collective-permute-start = (bf16[272,128]{1,0:T(8,128)(2,1)S(1)}, bf16[272,128]{1,0:T(8,128)(2,1)S(1)}, u32[]{:S(2)}, u32[]{:S(2)}) collective-permute-start(bf16[272,128]{1,0:T(8,128)(2,1)S(1)} %copy-done), channel_id=1, source_target_pairs={{0,192},{16,80},{32,224},{48,112},{64,0},{80,144},{96,32},{112,176... | collective-permute-start | bytes 208904 | tf_op jit(solution)/shard_map/ppermute | solution.py:307
  45.5 11.2 %collective-permute-start.4 = (bf16[2,128,1280]{2,1,0:T(8,128)(2,1)S(1)}, bf16[2,128,1280]{2,1,0:T(8,128)(2,1)S(1)}, u32[]{:S(2)}, u32[]{:S(2)}) collective-permute-start(bf16[2,128,1280]{2,1,0:T(8,128)(2,1)S(1)} %get-tuple-element.27.x_ref), channel_id=1, source_target_pairs={{0,8},{8,0},{1,9},{9,1},{2,10},{10,2},{3,11},{11,3},{4,12},{12,4},... | collective-permute-start | bytes 1966088 | tf_op jit(solution)/shard_map/ppermute | solution.py:316
  47.4 12.2 %collective-permute-start.7 = (bf16[4,272,128]{2,1,0:T(8,128)(2,1)S(1)}, bf16[4,272,128]{2,1,0:T(8,128)(2,1)S(1)}, u32[]{:S(2)}, u32[]{:S(2)}) collective-permute-start(bf16[4,272,128]{2,1,0:T(8,128)(2,1)S(1)} %get-tuple-element.28.s_ref), channel_id=1, source_target_pairs={{0,224},{16,48},{32,0},{48,80},{64,32},{80,112},{96,64},{112,144},... | collective-permute-start | bytes 835592 | tf_op jit(solution)/shard_map/ppermute | solution.py:307
  52.0 13.8 %collective-permute-start.6 = (bf16[4,272,128]{2,1,0:T(8,128)(2,1)S(1)}, bf16[4,272,128]{2,1,0:T(8,128)(2,1)S(1)}, u32[]{:S(2)}, u32[]{:S(2)}) collective-permute-start(bf16[4,272,128]{2,1,0:T(8,128)(2,1)S(1)} %get-tuple-element.28.s_ref), channel_id=1, source_target_pairs={{0,240},{16,32},{32,16},{48,64},{64,48},{80,96},{96,80},{112,128},... | collective-permute-start | bytes 835592 | tf_op jit(solution)/shard_map/ppermute | solution.py:307
  54.7 11.1 %collective-permute-start.5 = (bf16[4,272,128]{2,1,0:T(8,128)(2,1)S(1)}, bf16[4,272,128]{2,1,0:T(8,128)(2,1)S(1)}, u32[]{:S(2)}, u32[]{:S(2)}) collective-permute-start(bf16[4,272,128]{2,1,0:T(8,128)(2,1)S(1)} %get-tuple-element.28.s_ref), channel_id=1, source_target_pairs={{0,16},{16,0},{32,48},{48,32},{64,80},{80,64},{96,112},{112,96},{1... | collective-permute-start | bytes 835592 | tf_op jit(solution)/shard_map/ppermute | solution.py:307
  69.6 18.2 %collective-permute-start.10 = (bf16[4,256,128]{2,1,0:T(8,128)(2,1)S(1)}, bf16[4,256,128]{2,1,0:T(8,128)(2,1)S(1)}, u32[]{:S(2)}, u32[]{:S(2)}) collective-permute-start(bf16[4,256,128]{2,1,0:T(8,128)(2,1)S(1)} %get-tuple-element.37), channel_id=1, source_target_pairs={{0,32},{16,240},{32,64},{48,16},{64,96},{80,48},{96,128},{112,80},... | collective-permute-start | bytes 786440 | tf_op jit(solution)/shard_map/ppermute | solution.py:307
  73.9 13.9 %collective-permute-start.9 = (bf16[3,256,128]{2,1,0:T(8,128)(2,1)S(1)}, bf16[3,256,128]{2,1,0:T(8,128)(2,1)S(1)}, u32[]{:S(2)}, u32[]{:S(2)}) collective-permute-start(bf16[3,256,128]{2,1,0:T(8,128)(2,1)S(1)} %get-tuple-element.36), channel_id=1, source_target_pairs={{0,224},{16,48},{32,0},{48,80},{64,32},{80,112},{96,64},{112,144},... | collective-permute-start | bytes 589832 | tf_op jit(solution)/shard_map/ppermute | solution.py:307
  81.5 8.3 %collective-permute-start.8 = (bf16[2,128,512]{2,1,0:T(8,128)(2,1)S(1)}, bf16[2,128,512]{2,1,0:T(8,128)(2,1)S(1)}, u32[]{:S(2)}, u32[]{:S(2)}) collective-permute-start(bf16[2,128,512]{2,1,0:T(8,128)(2,1)S(1)} %get-tuple-element.33), channel_id=1, source_target_pairs={{0,8},{8,0},{1,9},{9,1},{2,10},{10,2},{3,11},{11,3},{4,12},{12,4},... | collective-permute-start | bytes 786440 | tf_op jit(solution)/shard_map/ppermute | solution.py:316
  83.4 10.5 %collective-permute-start.12 = (bf16[3,256,128]{2,1,0:T(8,128)(2,1)S(1)}, bf16[3,256,128]{2,1,0:T(8,128)(2,1)S(1)}, u32[]{:S(2)}, u32[]{:S(2)}) collective-permute-start(bf16[3,256,128]{2,1,0:T(8,128)(2,1)S(1)} %get-tuple-element.41), channel_id=1, source_target_pairs={{0,240},{16,32},{32,16},{48,64},{64,48},{80,96},{96,80},{112,128},... | collective-permute-start | bytes 589832 | tf_op jit(solution)/shard_map/ppermute | solution.py:307
  87.9 8.9 %collective-permute-start.11 = (bf16[3,256,128]{2,1,0:T(8,128)(2,1)S(1)}, bf16[3,256,128]{2,1,0:T(8,128)(2,1)S(1)}, u32[]{:S(2)}, u32[]{:S(2)}) collective-permute-start(bf16[3,256,128]{2,1,0:T(8,128)(2,1)S(1)} %get-tuple-element.40), channel_id=1, source_target_pairs={{0,16},{16,0},{32,48},{48,32},{64,80},{80,64},{96,112},{112,96},{1... | collective-permute-start | bytes 589832 | tf_op jit(solution)/shard_map/ppermute | solution.py:307
  89.9 17.3 %collective-permute-start.15 = (bf16[128,512]{1,0:T(8,128)(2,1)S(1)}, bf16[128,512]{1,0:T(8,128)(2,1)S(1)}, u32[]{:S(2)}, u32[]{:S(2)}) collective-permute-start(bf16[128,512]{1,0:T(8,128)(2,1)S(1)} %get-tuple-element.46), channel_id=1, source_target_pairs={{0,256},{256,0},{1,257},{257,1},{2,258},{258,2},{3,259},{259,3},{4... | collective-permute-start | bytes 393224 | tf_op jit(solution)/shard_map/ppermute | solution.py:316
  96.9 11.5 %collective-permute-start.13 = (bf16[256,128]{1,0:T(8,128)(2,1)S(1)}, bf16[256,128]{1,0:T(8,128)(2,1)S(1)}, u32[]{:S(2)}, u32[]{:S(2)}) collective-permute-start(bf16[256,128]{1,0:T(8,128)(2,1)S(1)} %get-tuple-element.43), channel_id=1, source_target_pairs={{0,80},{16,192},{32,112},{48,224},{64,144},{80,0},{96,176},{112,32... | collective-permute-start | bytes 196616 | tf_op jit(solution)/shard_map/ppermute | solution.py:307
  101.6 12.3 %collective-permute-start.14 = (bf16[256,128]{1,0:T(8,128)(2,1)S(1)}, bf16[256,128]{1,0:T(8,128)(2,1)S(1)}, u32[]{:S(2)}, u32[]{:S(2)}) collective-permute-start(bf16[256,128]{1,0:T(8,128)(2,1)S(1)} %get-tuple-element.44), channel_id=1, source_target_pairs={{0,176},{16,96},{32,208},{48,128},{64,240},{80,160},{96,16},{112,1... | collective-permute-start | bytes 196616 | tf_op jit(solution)/shard_map/ppermute | solution.py:307
